TPU v7x, 32 devices: a whole 2x2x4 slice. The times are simulated.
32 devices in a mesh: pts: 8 (over z, x), cams: 4 (over y, core).
Axes of the slice: x: 2, y: 2, z: 4, core: 2. Of those that a mesh axis runs over, the one named last changes fastest.
Arguments:
- camera_jacobian: float32 [18, 131072], P(None, ('pts', 'cams')), may hold values from -3 to 3
- point_jacobian: float32 [6, 131072], P(None, ('pts', 'cams')), may hold values from -6 to 6
- residual: float32 [2, 131072], P(None, ('pts', 'cams')), may hold values from -6 to 6
- observed_slot: int32 [131072], P(('pts', 'cams')), may hold values from 0 to 1023, as said below
- observed_point: int32 [131072], P(('pts', 'cams')), may hold values from 0 to 4095, as said below
- send_list: int32 [32, 4, 256], P(('pts', 'cams')), may hold values from 0 to 8191, as said below
Outputs:
- camera_step: float32 [9, 32768], P(None, 'cams')
- point_step: float32 [3, 131072], P(None, ('pts', 'cams'))
Inputs may be any that keep to these rules, and one draw needn't show every extreme that they name: `observed_slot`: an observation on device d = p * 4 + c with value s names entry s % 256 of send_list[p * 4 + s // 256, c]. In each such list only a leading run of entries is named, at least 64 long; for every device one list is named up to its last entry. `observed_point`: on every device both the first and the last of its 4096 points are observed. `send_list`: entry j of every list lies in the (j % 8)-th of 8 equal runs of an owner's 8192 cameras, that is, its value v has v // 1024 == j % 8.
All inputs are finite; a program needn't handle non-finite values.
Results may differ from a plain program's by a relative error of at most 0.0001.
Values sent between devices are 32-bit elements; how exact they have to be, the bound alone decides.
No kernel may reach another device: no remote copies, remote signals or barrier semaphores. Data moves between devices by JAX's collectives and lax.ppermute only.
A program may use at most 64 MiB of HBM per device.

v0:
```python
import jax
import jax.numpy as jnp
from jax import lax
from jax.sharding import PartitionSpec as P

CAM_OWN = 8192
SLOT = 256
PT_DEV = 4096
ITERS = 3


damping_camera = 1.0
damping_point = 1.0


def spread(values, index, count):
    return jnp.zeros((values.shape[0], count), values.dtype).at[:, index].add(values)


def camera_apply(jacobian, gathered):
    return jnp.sum(jacobian.reshape(2, 9, -1) * gathered[None], axis=1)


def camera_transpose(jacobian, errors):
    return jnp.sum(jacobian.reshape(2, 9, -1) * errors[:, None], axis=0)


def point_apply(jacobian, values):
    return jnp.sum(jacobian.reshape(2, 3, -1) * values[None], axis=1)


def point_transpose(jacobian, errors):
    return jnp.sum(jacobian.reshape(2, 3, -1) * errors[:, None], axis=0)


def point_inverse(jacobian, points, count):
    blocks = jacobian.reshape(2, 3, -1)
    first, second, third = (blocks[:, 0], blocks[:, 1], blocks[:, 2])
    outer = jnp.stack(
        [
            first * first,
            first * second,
            first * third,
            second * second,
            second * third,
            third * third,
        ]
    ).sum(axis=1)
    normal = spread(outer, points, count)
    top_left = normal[0] + damping_point
    top_mid = normal[1]
    top_right = normal[2]
    mid_mid = normal[3] + damping_point
    mid_right = normal[4]
    low_right = normal[5] + damping_point
    adjugate = jnp.stack(
        [
            mid_mid * low_right - mid_right * mid_right,
            top_right * mid_right - top_mid * low_right,
            top_mid * mid_right - top_right * mid_mid,
            top_left * low_right - top_right * top_right,
            top_mid * top_right - top_left * mid_right,
            top_left * mid_mid - top_mid * top_mid,
        ]
    )
    determinant = top_left * adjugate[0] + top_mid * adjugate[1] + top_right * adjugate[2]
    return adjugate / determinant[None]


def point_solve(inverse, values):
    first = inverse[0] * values[0] + inverse[1] * values[1] + inverse[2] * values[2]
    second = inverse[1] * values[0] + inverse[3] * values[1] + inverse[4] * values[2]
    third = inverse[2] * values[0] + inverse[4] * values[1] + inverse[5] * values[2]
    return jnp.stack([first, second, third])


def owner_total(dense):
    return lax.psum(dense, "pts")


def inner(left, right):
    return lax.psum(jnp.sum(left * right), "cams")


def body(camera_jacobian, point_jacobian, residual, observed_slot, observed_point, send_list):
    owners = lax.axis_size("cams")
    inverse = point_inverse(point_jacobian, observed_point, PT_DEV)
    width = CAM_OWN
    send_order = send_list[0].reshape(-1)

    def fetch(owned):
        received = lax.all_to_all(
            owned[:, send_order], "cams", split_axis=1, concat_axis=1, tiled=True
        )
        return received[:, observed_slot]

    def collect(terms):
        slots = spread(terms, observed_slot, owners * SLOT)
        back = lax.all_to_all(slots, "cams", split_axis=1, concat_axis=1, tiled=True)
        return owner_total(spread(back, send_order, CAM_OWN))

    point_gradient = spread(point_transpose(point_jacobian, residual), observed_point, PT_DEV)
    eliminated = point_solve(inverse, point_gradient)
    errors = residual - point_apply(point_jacobian, eliminated[:, observed_point])
    blocks = camera_jacobian.reshape(2, 9, -1)
    squares = jnp.sum(blocks * blocks, axis=0)
    combined = collect(
        jnp.concatenate([camera_transpose(camera_jacobian, errors), squares], axis=0)
    )
    right_side = -combined[:9]
    precondition = 1.0 / (combined[9:] + damping_camera)
    solution = jnp.zeros((9, width), jnp.float32)
    remainder = right_side
    scaled = precondition * remainder
    direction = scaled
    product = inner(remainder, scaled)
    for iteration in range(ITERS):
        schur_gathered = camera_apply(camera_jacobian, fetch(direction))
        folded = point_solve(
            inverse, spread(point_transpose(point_jacobian, schur_gathered), observed_point, PT_DEV)
        )
        schur_errors = schur_gathered - point_apply(point_jacobian, folded[:, observed_point])
        image = (
            collect(camera_transpose(camera_jacobian, schur_errors)) + damping_camera * direction
        )
        step_size = product / inner(direction, image)
        solution = solution + step_size * direction
        remainder = remainder - step_size * image
        scaled = precondition * remainder
        renewed = inner(remainder, scaled)
        direction = scaled + renewed / product * direction
        product = renewed
    gathered = camera_apply(camera_jacobian, fetch(solution))
    point_step = -point_solve(
        inverse,
        point_gradient + spread(point_transpose(point_jacobian, gathered), observed_point, PT_DEV),
    )
    return (solution, point_step)


def solution(mesh):
    return jax.shard_map(
        body,
        mesh=mesh,
        in_specs=(
            P(None, ("pts", "cams")),
            P(None, ("pts", "cams")),
            P(None, ("pts", "cams")),
            P(("pts", "cams")),
            P(("pts", "cams")),
            P(("pts", "cams"), None, None),
        ),
        out_specs=(P(None, "cams"), P(None, ("pts", "cams"))),
        check_vma=False,
    )
```

profile of v0, /device:TPU:0, one launch (start us, length us, event | category | flops | bytes accessed | tf_op | source)
XLA Modules:
  0.0 1036.1 jit_solution(16210610747607985872)
XLA Ops:
  10.6 23.2 %scatter_custom_fusion = f32[6,4096]{0,1:T(8,128)S(1)} fusion(s32[4096]{0:T(1024)S(1)} %get-tuple-element.75, f32[4096,6]{1,0:T(8,128)} %copy.451, f32[]{:T(128)} %constant.6.clone.1), kind=kCustom, calls=%fused_computation.42 | custom fusion | flops 24576 | bytes 98816 | tf_op jit(solution)/shard_map/scatter-add | solution.py:17
  53.7 23.4 %scatter_custom_fusion.1 = f32[3,4096]{0,1:T(8,128)S(1)} fusion(s32[4096]{0:T(1024)S(1)} %get-tuple-element.75, f32[4096,3]{1,0:T(8,128)} %copy.458, f32[]{:T(128)} %constant.6.clone.1), kind=kCustom, calls=%fused_computation.40 | custom fusion | flops 12288 | bytes 49664 | tf_op jit(solution)/shard_map/scatter-add | solution.py:17
  90.0 15.7 %gather_fusion = f32[4096,3]{1,0:T(8,128)} fusion(f32[3,4096]{0,1:T(8,128)} %copy.462, s32[4096]{0:T(1024)S(1)} %get-tuple-element.74), kind=kCustom, calls=%fused_computation | custom fusion | bytes 114688 | tf_op jit(solution)/shard_map/gather | solution.py:104
  110.2 22.8 %scatter_custom_fusion.2 = f32[18,1024]{0,1:T(8,128)S(1)} fusion(s32[4096]{0:T(1024)S(1)} %get-tuple-element.73, f32[4096,18]{1,0:T(8,128)} %copy.464, f32[]{:T(128)} %constant.6.clone.1), kind=kCustom, calls=%fused_computation.76 | custom fusion | flops 73728 | bytes 74240 | tf_op jit(solution)/shard_map/scatter-add | solution.py:17
  154.6 75.6 %all-reduce.6.cloned.1.call-done = f32[18,8192]{1,0:T(8,128)} async-done(((f32[18,8192]{1,0:T(8,128)}), f32[18,8192]{1,0:T(8,128)}) %all-reduce.6.cloned.1.call-update) | async-done | bytes 589840 | tf_op jit(solution)/shard_map/psum | solution.py:78
  246.6 14.1 %gather_fusion.2 = f32[4096,9]{1,0:T(8,128)} fusion(f32[9,1024]{0,1:T(8,128)S(1)} %bitcast.76, s32[4096]{0:T(1024)S(1)} %get-tuple-element.72), kind=kCustom, calls=%fused_computation.2 | custom fusion | bytes 311296 | tf_op jit(solution)/shard_map/gather | solution.py:95
  265.0 24.1 %scatter_custom_fusion.4 = f32[3,4096]{0,1:T(8,128)} fusion(s32[4096]{0:T(1024)} %copy-done.14, f32[4096,3]{1,0:T(8,128)} %copy.473, f32[]{:T(128)} %constant.6.clone.1), kind=kCustom, calls=%fused_computation.38 | custom fusion | flops 12288 | bytes 49664 | tf_op jit(solution)/shard_map/scatter-add | solution.py:17
  304.6 15.7 %gather_fusion.3 = f32[4096,3]{1,0:T(8,128)} fusion(f32[3,4096]{0,1:T(8,128)} %copy.477, s32[4096]{0:T(1024)S(1)} %copy-done.7), kind=kCustom, calls=%fused_computation.3 | custom fusion | bytes 114688 | tf_op jit(solution)/shard_map/gather | solution.py:122
  324.6 22.8 %scatter_custom_fusion.5 = f32[9,1024]{0,1:T(8,128)S(1)} fusion(s32[4096]{0:T(1024)} %copy-done.18, f32[4096,9]{1,0:T(8,128)} %copy.479, f32[]{:T(128)} %constant.6.clone.1), kind=kCustom, calls=%fused_computation.74 | custom fusion | flops 36864 | bytes 37376 | tf_op jit(solution)/shard_map/scatter-add | solution.py:17
  366.4 70.6 %all-reduce.8.cloned.1.call-done = f32[9,8192]{1,0:T(8,128)} async-done(((f32[9,8192]{1,0:T(8,128)}), f32[9,8192]{1,0:T(8,128)}) %all-reduce.8.cloned.1.call-update) | async-done | bytes 294928 | tf_op jit(solution)/shard_map/psum | solution.py:78
  482.2 15.1 %gather_fusion.5 = f32[4096,9]{1,0:T(8,128)} fusion(f32[9,1024]{0,1:T(8,128)} %bitcast.78, s32[4096]{0:T(1024)S(1)} %get-tuple-element.72), kind=kCustom, calls=%fused_computation.5 | custom fusion | bytes 311296 | tf_op jit(solution)/shard_map/gather | solution.py:95
  505.5 24.1 %scatter_custom_fusion.7 = f32[3,4096]{0,1:T(8,128)} fusion(s32[4096]{0:T(1024)} %copy-done.14, f32[4096,3]{1,0:T(8,128)} %copy.488, f32[]{:T(128)} %constant.6.clone.1), kind=kCustom, calls=%fused_computation.36 | custom fusion | flops 12288 | bytes 49664 | tf_op jit(solution)/shard_map/scatter-add | solution.py:17
  549.8 17.0 %gather_fusion.6 = f32[4096,3]{1,0:T(8,128)} fusion(f32[3,4096]{0,1:T(8,128)} %copy.492, s32[4096]{0:T(1024)} %copy-done.6), kind=kCustom, calls=%fused_computation.6 | custom fusion | bytes 114688 | tf_op jit(solution)/shard_map/gather | solution.py:122
  575.1 23.4 %scatter_custom_fusion.8 = f32[9,1024]{0,1:T(8,128)} fusion(s32[4096]{0:T(1024)} %copy-done.18, f32[4096,9]{1,0:T(8,128)} %copy.494, f32[]{:T(128)} %constant.6.clone.1), kind=kCustom, calls=%fused_computation.72 | custom fusion | flops 36864 | bytes 37376 | tf_op jit(solution)/shard_map/scatter-add | solution.py:17
  610.5 8.6 scatter_custom_fusion.9
  622.6 70.8 %all-reduce.10.cloned.1.call-done = f32[9,8192]{1,0:T(8,128)} async-done(((f32[9,8192]{1,0:T(8,128)}), f32[9,8192]{1,0:T(8,128)}) %all-reduce.10.cloned.1.call-update) | async-done | bytes 294928 | tf_op jit(solution)/shard_map/psum | solution.py:78
  738.2 15.1 %gather_fusion.8 = f32[4096,9]{1,0:T(8,128)} fusion(f32[9,1024]{0,1:T(8,128)} %bitcast.79, s32[4096]{0:T(1024)S(1)} %get-tuple-element.72), kind=kCustom, calls=%fused_computation.8 | custom fusion | bytes 311296 | tf_op jit(solution)/shard_map/gather | solution.py:95
  761.5 24.3 %scatter_custom_fusion.10 = f32[3,4096]{0,1:T(8,128)} fusion(s32[4096]{0:T(1024)} %copy-done.14, f32[4096,3]{1,0:T(8,128)} %copy.503, f32[]{:T(128)} %constant.6.clone.1), kind=kCustom, calls=%fused_computation.34 | custom fusion | flops 12288 | bytes 49664 | tf_op jit(solution)/shard_map/scatter-add | solution.py:17
  806.0 17.0 %gather_fusion.9 = f32[4096,3]{1,0:T(8,128)} fusion(f32[3,4096]{0,1:T(8,128)} %copy.507, s32[4096]{0:T(1024)} %copy-done.6), kind=kCustom, calls=%fused_computation.9 | custom fusion | bytes 114688 | tf_op jit(solution)/shard_map/gather | solution.py:122
  831.3 23.4 %scatter_custom_fusion.11 = f32[9,1024]{0,1:T(8,128)} fusion(s32[4096]{0:T(1024)} %copy-done.18, f32[4096,9]{1,0:T(8,128)} %copy.509, f32[]{:T(128)} %constant.6.clone.1), kind=kCustom, calls=%fused_computation.70 | custom fusion | flops 36864 | bytes 37376 | tf_op jit(solution)/shard_map/scatter-add | solution.py:17
  866.5 8.6 scatter_custom_fusion.12
  878.6 70.9 %all-reduce.12.cloned.1.call-done = f32[9,8192]{1,0:T(8,128)} async-done(((f32[9,8192]{1,0:T(8,128)}), f32[9,8192]{1,0:T(8,128)}) %all-reduce.12.cloned.1.call-update) | async-done | bytes 294928 | tf_op jit(solution)/shard_map/psum | solution.py:78
  977.1 14.1 %gather_fusion.11 = f32[4096,9]{1,0:T(8,128)} fusion(f32[9,1024]{0,1:T(8,128)S(1)} %bitcast.77, s32[4096]{0:T(1024)S(1)} %get-tuple-element.72), kind=kCustom, calls=%fused_computation.11 | custom fusion | bytes 311296 | tf_op jit(solution)/shard_map/gather | solution.py:95
  995.6 23.7 %scatter_fusion = f32[3,4096]{0,1:T(8,128)S(1)} fusion(f32[3,4096]{0,1:T(8,128)S(1)} %scatter_custom_fusion.1, s32[4096]{0:T(1024)S(1)} %copy-done.15, f32[4096,3]{1,0:T(8,128)} %copy.518), kind=kCustom, calls=%fused_computation.25 | custom fusion | flops 12288 | bytes 163840 | tf_op jit(solution)/shard_map/scatter-add | solution.py:17
  (209 shorter events, 351.2 us)
Async XLA Ops:
  7.2 3.4 copy-start.16
  10.6 43.0 %copy-start.14 = (s32[4096]{0:T(1024)}, s32[4096]{0:T(1024)S(1)}, u32[]{:S(2)}) copy-start(s32[4096]{0:T(1024)S(1)} %get-tuple-element.75) | copy-start | bytes 49156
  10.6 79.3 %copy-start.6 = (s32[4096]{0:T(1024)}, s32[4096]{0:T(1024)S(1)}, u32[]{:S(2)}) copy-start(s32[4096]{0:T(1024)S(1)} %get-tuple-element.74) | copy-start | bytes 49156
  41.2 4.6 copy-start.2
  46.4 4.6 copy-start.1
  48.7 2.9 copy-start.11
  87.8 214.6 %copy-start.4 = (f32[6,4096]{1,0:T(8,128)}, f32[6,4096]{1,0:T(8,128)S(1)}, u32[]{:S(2)}) copy-start(f32[6,4096]{1,0:T(8,128)S(1)} %broadcast_divide_fusion) | copy-start | bytes 294916
  87.9 20.0 %copy-start.8 = (f32[18,4096]{1,0:T(8,128)S(1)}, f32[18,4096]{1,0:T(8,128)}, u32[]{:S(2)}) copy-start(f32[18,4096]{1,0:T(8,128)} %param.6) | copy-start | bytes 884740
  108.0 2.2 copy-start.17
  108.2 29.9 %copy-start.20 = (s32[1,4,256]{2,1,0:T(4,128)S(1)}, s32[1,4,256]{2,1,0:T(4,128)}, u32[]{:S(2)}) copy-start(s32[1,4,256]{2,1,0:T(4,128)} %param.11) | copy-start | bytes 12292
  110.2 23.6 %copy-start.18 = (s32[4096]{0:T(1024)}, s32[4096]{0:T(1024)S(1)}, u32[]{:S(2)}) copy-start(s32[4096]{0:T(1024)S(1)} %get-tuple-element.73) | copy-start | bytes 49156
  133.9 8.5 all-to-all-start
  138.1 92.1 %all-reduce.6.cloned.1.call-start = ((), (), s32[]{:S(2)}) async-start(), calls=%async_computation.8 | async-start | bytes 1572864 | tf_op jit(solution)/shard_map/psum | solution.py:78
  138.1 16.4 %copy-start.19 = (s32[1024,1]{0,1:T(1,128)}, s32[1024,1]{0,1:T(1,128)S(1)}, u32[]{:S(2)}) copy-start(s32[1024,1]{0,1:T(1,128)S(1)} %compare_select_fusion.2) | copy-start | bytes 12292
  154.5 282.5 %all-reduce.8.cloned.1.call-start = ((), (), s32[]{:S(2)}) async-start(), calls=%async_computation.9 | async-start | bytes 1048576 | tf_op jit(solution)/shard_map/psum | solution.py:78
  154.6 79.5 %copy-start.12 = (s32[1024]{0:T(1024)}, s32[1024]{0:T(1024)S(1)}, u32[]{:S(2)}) copy-start(s32[1024]{0:T(1024)S(1)} %broadcast_clamp_fusion.2) | copy-start | bytes 12292
  300.1 4.4 copy-start.7
  362.7 74.3 %copy-start = (f32[18,8192]{1,0:T(8,128)S(1)}, f32[18,8192]{1,0:T(8,128)}, u32[]{:S(2)}) copy-start(f32[18,8192]{1,0:T(8,128)} %all-reduce.6.cloned.1.call-done) | copy-start | bytes 1769476
  366.3 327.2 %all-reduce.10.cloned.1.call-start = ((), (), s32[]{:S(2)}) async-start(), calls=%async_computation.10 | async-start | bytes 1048576 | tf_op jit(solution)/shard_map/psum | solution.py:78
  622.6 326.9 %all-reduce.12.cloned.1.call-start = ((), (), s32[]{:S(2)}) async-start(), calls=%async_computation.11 | async-start | bytes 1048576 | tf_op jit(solution)/shard_map/psum | solution.py:78
  961.2 3.5 copy-start.13
  993.4 2.2 copy-start.15
  1023.1 4.6 copy-start.3
  1025.4 2.9 copy-start.5
  (2 other events, 1.2 us)
Sparse Core Ops, SparseCore 0:
  154.6 75.5 all-reduce.5
  366.4 70.5 all-reduce.7
  622.7 70.7 all-reduce.9
  878.7 70.7 all-reduce.11
where the time goes:
time: 1050 us; the launch traced here: 1040 us
  local copies, waits for them, and re-layouts  330 us (31%)
  other arithmetic  304 us (29%)
  waiting for transfers between devices  292 us (28%)
  blocking collectives  84.9 us (8%)
  between operations  21 us (2%)
    psum x4, waiting for transfers between devices, owner_total(): return lax.psum(dense, 'pts')  288 us
    scatter-add x14, other arithmetic, spread(): jnp.zeros((values.shape[0], count), values.dtype).at[:, index].add(values)  269 us
    gather x8, local copies, waits for them, and re-layouts, fetch(): return received[:, observed_slot]  68.7 us
    gather x6, local copies, waits for them, and re-layouts, body(): folded[:, observed_point]  57.6 us
    unnamed x72, local copies, waits for them, and re-layouts  48.4 us
    psum x5, blocking collectives, inner(): return lax.psum(jnp.sum(left * right), 'cams')  33.4 us
    all_to_all x4, blocking collectives, fetch(): lax.all_to_all(owned[:, send_order], 'cams', split_axis=1, concat_axis=1,...  30.1 us
    slice x5, local copies, waits for them, and re-layouts, point_solve(): values[0]  27.4 us
  transfers between devices with their start and end apart: 5, of which 5 were waited for; matrix products, arithmetic and copies ran while one was open for 0% of the time, Pallas kernels for 0%

commit v1 on v0

v1 whole, which is shorter than its diff:
```python
import functools

import jax
import jax.numpy as jnp
from jax import lax
from jax.experimental import pallas as pl
from jax.experimental.pallas import tpu as pltpu
from jax.sharding import PartitionSpec as P

CP = 9
CAM_OWN = 8192
PT_DEV = 4096
ITERS = 3
LANES = 128
SUB = 8
PT_LO = 256
PT_HI = PT_DEV // PT_LO
PT_ROWS = PT_DEV // LANES
PIECES = 3
VMEM_LIMIT = 40 * 1024 * 1024

damping_camera = 1.0
damping_point = 1.0

f32 = jnp.float32
bf16 = jnp.bfloat16


class Sizes:
    def __init__(self, pts, cams, slot, obs):
        self.pts, self.cams, self.slot, self.obs = pts, cams, slot, obs
        self.devices = pts * cams
        self.block = slot // pts
        assert cams * self.block == LANES and LANES % pts == 0
        self.rows = obs // LANES
        self.run = CAM_OWN // pts
        self.run_rows = self.run // LANES
        self.own_rows = max(SUB, self.run_rows)
        self.groups = -(-CP // cams)
        self.first_groups = -(-2 * CP // cams)
        self.message = 4
        self.first_message = 4 if self.first_groups < 4 else 8
        assert self.groups * cams > CP


def sub_iota(rows):
    return lax.broadcasted_iota(jnp.int32, (rows, LANES), 0)


def lane_iota(rows):
    return lax.broadcasted_iota(jnp.int32, (rows, LANES), 1)


def cut(value):
    parts = []
    for _ in range(PIECES - 1):
        part = value.astype(bf16).astype(f32)
        parts.append(part)
        value = value - part
    parts.append(value)
    return parts


def swap_blocks(rows, block, wanted):
    which = lane_iota(rows[0].shape[0]) // block
    result = []
    for q in range(wanted):
        total = None
        for c, value in enumerate(rows):
            shift = ((c - q) * block) % LANES
            moved = pltpu.roll(value, shift, axis=1) if shift else value
            total = jnp.where(which == c, moved, 0.0 if total is None else total)
        result.append(total)
    return result


def gather_rows(row, count, high, low, comps):
    result = [None] * comps
    for k in range(count):
        here = high == k
        for c in range(comps):
            source = jnp.broadcast_to(row(c, k), high.shape)
            found = jnp.take_along_axis(source, low, axis=1, mode="promise_in_bounds")
            result[c] = found if k == 0 else jnp.where(here, found, result[c])
    return result


def build(index, parts, high, low, high_count, low_count, spread_ref, place_ref):
    columns = pl.ds(pl.multiple_of(index * LANES, LANES), LANES)
    mask = jnp.broadcast_to(high, (high_count, LANES)) == sub_iota(high_count)
    together = max(1, 16 // high_count)
    for start in range(0, len(parts), together):
        pieces = [
            jnp.where(mask, jnp.broadcast_to(part, (high_count, LANES)), 0.0)
            for part in parts[start : start + together]
        ]
        while len(pieces) < together:
            pieces.append(jnp.zeros((high_count, LANES), f32))
        tile = pieces[0] if together == 1 else jnp.concatenate(pieces, axis=0)
        spread_ref[start * high_count : start * high_count + tile.shape[0], columns] = tile.astype(bf16)
    place = jnp.broadcast_to(low, (low_count, LANES)) == sub_iota(low_count)
    place_ref[:low_count, columns] = jnp.where(place, 1.0, 0.0).astype(bf16)


def spread_rows(parts, high_count):
    return -(-parts * high_count // 16) * 16


def scatter(parts, entries, high_count, low_count, spread_ref, place_ref):
    rows = spread_rows(parts, high_count)
    return lax.dot_general(
        spread_ref[:rows, :entries],
        place_ref[:low_count, :entries],
        (((1,), (1,)), ((), ())),
        preferred_element_type=f32,
    )


def joined(result, comp, high_count, pieces=PIECES):
    first = comp * pieces * high_count
    total = result[first + (pieces - 1) * high_count : first + pieces * high_count]
    for piece in reversed(range(pieces - 1)):
        total = total + result[first + piece * high_count : first + (piece + 1) * high_count]
    return total


def point_rows(value):
    return jnp.concatenate([value[:, :LANES], value[:, LANES:]], axis=0)


def point_place(point):
    high = point >> 8
    return high + ((point >> 7) & 1) * PT_HI, point & (LANES - 1), high, point & (PT_LO - 1)


def slot_place(slot, sizes):
    within = slot % sizes.slot
    return within % sizes.pts, (slot // sizes.slot) * sizes.block + within // sizes.pts


def solve(inverse, values):
    first = inverse[0] * values[0] + inverse[1] * values[1] + inverse[2] * values[2]
    second = inverse[1] * values[0] + inverse[3] * values[1] + inverse[4] * values[2]
    third = inverse[2] * values[0] + inverse[4] * values[1] + inverse[5] * values[2]
    return first, second, third


def write_messages(fields, scalar, groups, message, out_ref, sizes, extra=None):
    which = lane_iota(sizes.pts) // sizes.block
    for g in range(groups):
        rows = fields[g * sizes.cams : (g + 1) * sizes.cams]
        moved = swap_partial(rows, sizes)
        for c in range(sizes.cams):
            value = moved[c]
            if g == groups - 1 and scalar is not None:
                value = jnp.where(which == sizes.cams - 1, scalar, value)
            out_ref[pl.ds(c * message + g, sizes.pts, stride=sizes.cams * message), :] = value
    for g in range(groups, message):
        for c in range(sizes.cams):
            value = extra if (extra is not None and g == groups) else jnp.zeros((sizes.pts, LANES), f32)
            out_ref[pl.ds(c * message + g, sizes.pts, stride=sizes.cams * message), :] = value


def swap_partial(rows, sizes):
    return swap_blocks(rows, sizes.block, sizes.cams)


def read_row(in_ref, c, g, message, sizes):
    return in_ref[pl.ds(c * message + g, sizes.pts, stride=sizes.cams * message), :]


def read_messages(in_ref, count, message, sizes):
    fields = []
    group = 0
    while len(fields) < count:
        rows = [read_row(in_ref, c, group, message, sizes) for c in range(sizes.cams)]
        fields += swap_blocks(rows, sizes.block, min(sizes.cams, count - len(fields)))
        group += 1
    return fields


def read_scalar(in_ref, groups, message, sizes):
    total = read_row(in_ref, 0, groups - 1, message, sizes)
    for c in range(1, sizes.cams):
        total = total + read_row(in_ref, c, groups - 1, message, sizes)
    chosen = jnp.where(lane_iota(sizes.pts) == LANES - 1, total, 0.0)
    return jnp.sum(chosen, keepdims=True)


def setup_kernel(sizes, jac_ref, pjac_ref, res_ref, slot_ref, point_ref, list_ref,
                 out_ref, a_ref, b_ref, inv_ref, grad_ref,
                 r_ref, table_ref, spread_ref, place_ref):
    rows = sizes.rows
    for j in range(rows):
        columns = slice(j * LANES, (j + 1) * LANES)
        for start in range(0, 2 * CP, SUB):
            size = min(SUB, 2 * CP - start)
            a_ref[pl.ds(start * rows + j, size, stride=rows), :] = jac_ref[start : start + size, columns]
        b_ref[pl.ds(j, 6, stride=rows), :] = pjac_ref[:, columns]
        r_ref[pl.ds(j, 2, stride=rows), :] = res_ref[:, columns]

    def at(ref, comp, group):
        return ref[pl.ds(pl.multiple_of(comp * rows + group * SUB, SUB), SUB), :]

    def first(group, carry):
        b = [at(b_ref, k, group) for k in range(6)]
        r = [at(r_ref, k, group) for k in range(2)]
        point = point_ref[pl.ds(pl.multiple_of(group * SUB, SUB), SUB), :]
        _, _, high, low = point_place(point)
        values = [b[i] * b[j] + b[3 + i] * b[3 + j] for i, j in ((0, 0), (0, 1), (0, 2), (1, 1), (1, 2), (2, 2))]
        values += [b[i] * r[0] + b[3 + i] * r[1] for i in range(3)]
        parts = [part for value in values for part in cut(value)]
        for s in range(SUB):
            build(group * SUB + s, [part[s : s + 1] for part in parts], high[s : s + 1], low[s : s + 1],
                  PT_HI, PT_LO, spread_ref, place_ref)
        return carry

    lax.fori_loop(0, rows // SUB, first, 0)
    result = scatter(9 * PIECES, sizes.obs, PT_HI, PT_LO, spread_ref, place_ref)
    normal = [point_rows(joined(result, k, PT_HI)) for k in range(9)]
    top_left = normal[0] + damping_point
    top_mid = normal[1]
    top_right = normal[2]
    mid_mid = normal[3] + damping_point
    mid_right = normal[4]
    low_right = normal[5] + damping_point
    adjugate = [
        mid_mid * low_right - mid_right * mid_right,
        top_right * mid_right - top_mid * low_right,
        top_mid * mid_right - top_right * mid_mid,
        top_left * low_right - top_right * top_right,
        top_mid * top_right - top_left * mid_right,
        top_left * mid_mid - top_mid * top_mid,
    ]
    determinant = top_left * adjugate[0] + top_mid * adjugate[1] + top_right * adjugate[2]
    inverse = [value / determinant for value in adjugate]
    for k in range(6):
        inv_ref[k] = inverse[k]
    for k in range(3):
        grad_ref[k] = normal[6 + k]
    eliminated = solve(inverse, normal[6:])
    for k in range(3):
        table_ref[k] = eliminated[k]

    def second(group, carry):
        point = point_ref[pl.ds(pl.multiple_of(group * SUB, SUB), SUB), :]
        high, low, _, _ = point_place(point)
        at_point = gather_rows(lambda c, k: table_ref[c, k : k + 1, :], PT_ROWS, high, low, 3)
        b = [at(b_ref, k, group) for k in range(6)]
        errors = [at(r_ref, i, group) - sum(b[3 * i + k] * at_point[k] for k in range(3)) for i in range(2)]
        a = [at(a_ref, k, group) for k in range(2 * CP)]
        values = [a[k] * errors[0] + a[CP + k] * errors[1] for k in range(CP)]
        values += [a[k] * a[k] + a[CP + k] * a[CP + k] for k in range(CP)]
        parts = [part for value in values for part in cut(value)]
        high, low = slot_place(slot_ref[pl.ds(pl.multiple_of(group * SUB, SUB), SUB), :], sizes)
        for s in range(SUB):
            build(group * SUB + s, [part[s : s + 1] for part in parts], high[s : s + 1], low[s : s + 1],
                  sizes.pts, LANES, spread_ref, place_ref)
        return carry

    lax.fori_loop(0, rows // SUB, second, 0)
    result = scatter(2 * CP * PIECES, sizes.obs, sizes.pts, LANES, spread_ref, place_ref)
    fields = [joined(result, k, sizes.pts) for k in range(2 * CP)]

    pieces = sizes.slot // LANES
    lane = lane_iota(1)
    for c in range(sizes.cams):
        for half in range(pieces):
            value = list_ref[c : c + 1, half * LANES : (half + 1) * LANES]
            low = c * sizes.block + half * (LANES // sizes.pts) + lane // sizes.pts
            build(c * pieces + half, [(value >> 8).astype(f32), (value & 255).astype(f32)], lane % sizes.pts, low,
                  sizes.pts, LANES, spread_ref, place_ref)
    result = scatter(2, sizes.cams * sizes.slot, sizes.pts, LANES, spread_ref, place_ref)
    listed = result[: sizes.pts] * 256.0 + result[sizes.pts : 2 * sizes.pts]
    write_messages(fields, None, sizes.first_groups, sizes.first_message, out_ref, sizes, extra=listed)


def entries_scatter(fields, entry, sizes, spread_ref, place_ref):
    high, low = entry // LANES, entry % LANES
    parts = [part for value in fields for part in cut(value)]
    for p in range(sizes.pts):
        build(p, [part[p : p + 1] for part in parts], high[p : p + 1], low[p : p + 1],
              sizes.own_rows, LANES, spread_ref, place_ref)
    result = scatter(len(parts), sizes.pts * LANES, sizes.own_rows, LANES, spread_ref, place_ref)
    return [joined(result, k, sizes.own_rows) for k in range(len(fields))]


def send_owned(scaled, partial, entry, out_ref, table_ref, sizes):
    for k in range(CP):
        table_ref[k] = scaled[k]
    fields = gather_rows(lambda c, k: table_ref[c, k : k + 1, :], sizes.run_rows, entry // LANES, entry % LANES, CP)
    write_messages(fields, partial, sizes.groups, sizes.message, out_ref, sizes)


def dot_fields(left, right):
    return jnp.sum(sum(a * b for a, b in zip(left, right)), keepdims=True)


def first_owner_kernel(sizes, column_ref, in_ref, out_ref, entry_ref, pre_ref, rem_ref,
                       table_ref, spread_ref, place_ref):
    listed = jnp.zeros((sizes.pts, LANES), f32)
    for c in range(sizes.cams):
        row = read_row(in_ref, c, sizes.first_groups, sizes.first_message, sizes)
        listed = jnp.where(column_ref[0] == c, row, listed)
    entry = listed.astype(jnp.int32) % sizes.run
    entry_ref[...] = entry
    fields = read_messages(in_ref, 2 * CP, sizes.first_message, sizes)
    sums = entries_scatter(fields, entry, sizes, spread_ref, place_ref)
    remainder = [-value for value in sums[:CP]]
    precondition = [1.0 / (value + damping_camera) for value in sums[CP:]]
    scaled = [p * r for p, r in zip(precondition, remainder)]
    for k in range(CP):
        pre_ref[k] = precondition[k]
        rem_ref[k] = remainder[k]
    send_owned(scaled, dot_fields(remainder, scaled), entry, out_ref, table_ref, sizes)


def owner_kernel(sizes, start, in_ref, entry_ref, pre_ref, rem_ref, dir_ref, product_ref, *refs):
    if start:
        out_ref, new_rem_ref, new_sol_ref, step_ref, table_ref, spread_ref, place_ref = refs
    else:
        sol_ref, out_ref, new_rem_ref, new_sol_ref, step_ref, table_ref, spread_ref, place_ref = refs
    entry = entry_ref[...]
    fields = read_messages(in_ref, CP, sizes.message, sizes)
    curvature = read_scalar(in_ref, sizes.groups, sizes.message, sizes)
    step = product_ref[...] / jnp.broadcast_to(curvature, (SUB, LANES))
    step_ref[...] = step
    sums = entries_scatter(fields, entry, sizes, spread_ref, place_ref)
    remainder, scaled = [], []
    for k in range(CP):
        direction = dir_ref[k]
        moved = step[:1] * direction
        new_sol_ref[k] = moved if start else sol_ref[k] + moved
        value = rem_ref[k] - step[:1] * (sums[k] + damping_camera * direction)
        new_rem_ref[k] = value
        remainder.append(value)
        scaled.append(pre_ref[k] * value)
    send_owned(scaled, dot_fields(remainder, scaled), entry, out_ref, table_ref, sizes)


def schur_kernel(sizes, start, last, in_ref, a_ref, b_ref, inv_ref, slot_ref, point_ref, pre_ref, rem_ref, grad_ref, *refs):
    refs = list(refs)
    if not start:
        product_ref, at_slot_ref, dir_ref, step_ref, sum_ref = refs[:5]
        refs = refs[5:]
    out_ref, new_product_ref, new_at_slot_ref, new_dir_ref, new_sum_ref = refs[:5]
    new_grad_ref = None
    refs = refs[5:]
    if not start:
        new_grad_ref = refs.pop(0)
    q_ref, table_ref, spread_ref, place_ref = refs
    rows = sizes.rows

    def at(ref, comp, group):
        return ref[pl.ds(pl.multiple_of(comp * rows + group * SUB, SUB), SUB), :]

    def index(ref, group):
        return ref[pl.ds(pl.multiple_of(group * SUB, SUB), SUB), :]

    renewed = jnp.broadcast_to(read_scalar(in_ref, sizes.groups, sizes.message, sizes), (SUB, LANES))
    new_product_ref[...] = renewed
    fields = read_messages(in_ref, CP, sizes.message, sizes)
    beta = None if start else (renewed / product_ref[...])[:1]
    squares = None
    for k in range(CP):
        direction = pre_ref[k] * rem_ref[k]
        if start:
            new_at_slot_ref[k] = fields[k]
        else:
            new_at_slot_ref[k] = fields[k] + beta * at_slot_ref[k]
            direction = direction + beta * dir_ref[k]
        new_dir_ref[k] = direction
        squares = direction * direction if squares is None else squares + direction * direction

    def first(group, carry):
        high, low = slot_place(index(slot_ref, group), sizes)
        gathered = gather_rows(lambda c, k: new_at_slot_ref[c, k : k + 1, :], sizes.pts, high, low, CP)
        q = [sum(at(a_ref, i * CP + k, group) * gathered[k] for k in range(CP)) for i in range(2)]
        for i in range(2):
            q_ref[pl.ds(pl.multiple_of(i * rows + group * SUB, SUB), SUB), :] = q[i]
        values = [at(b_ref, k, group) * q[0] + at(b_ref, 3 + k, group) * q[1] for k in range(3)]
        parts = [part for value in values for part in cut(value)]
        _, _, high, low = point_place(index(point_ref, group))
        for s in range(SUB):
            build(group * SUB + s, [part[s : s + 1] for part in parts], high[s : s + 1], low[s : s + 1],
                  PT_HI, PT_LO, spread_ref, place_ref)
        return carry

    lax.fori_loop(0, rows // SUB, first, 0)
    result = scatter(3 * PIECES, sizes.obs, PT_HI, PT_LO, spread_ref, place_ref)
    sums = [point_rows(joined(result, k, PT_HI)) for k in range(3)]
    folded = solve([inv_ref[k] for k in range(6)], sums)
    for k in range(3):
        table_ref[k] = folded[k]
        new_sum_ref[k] = sums[k]
        if not start:
            new_grad_ref[k] = grad_ref[k] + step_ref[:1, :] * sum_ref[k]

    def second(group, inner):
        high, low, _, _ = point_place(index(point_ref, group))
        at_point = gather_rows(lambda c, k: table_ref[c, k : k + 1, :], PT_ROWS, high, low, 3)
        q = [at(q_ref, i, group) for i in range(2)]
        errors = [q[i] - sum(at(b_ref, 3 * i + k, group) * at_point[k] for k in range(3)) for i in range(2)]
        inner = inner + q[0] * errors[0] + q[1] * errors[1]
        if not last:
            values = [at(a_ref, k, group) * errors[0] + at(a_ref, CP + k, group) * errors[1] for k in range(CP)]
            parts = [part for value in values for part in cut(value)]
            high, low = slot_place(index(slot_ref, group), sizes)
            for s in range(SUB):
                build(group * SUB + s, [part[s : s + 1] for part in parts], high[s : s + 1], low[s : s + 1],
                      sizes.pts, LANES, spread_ref, place_ref)
        return inner

    inner = lax.fori_loop(0, rows // SUB, second, jnp.zeros((SUB, LANES), f32))
    partial = jnp.sum(inner, keepdims=True) + damping_camera * jnp.sum(squares, keepdims=True)
    if last:
        out_ref[...] = jnp.broadcast_to(partial, (sizes.devices, LANES))
        return
    result = scatter(CP * PIECES, sizes.obs, sizes.pts, LANES, spread_ref, place_ref)
    fields = [joined(result, k, sizes.pts) for k in range(CP)]
    write_messages(fields, partial, sizes.groups, sizes.message, out_ref, sizes)


def final_kernel(sizes, in_ref, product_ref, all_ref, inv_ref, grad_ref, sum_ref, cam_ref, pt_ref, table_ref):
    curvature = jnp.sum(jnp.where(lane_iota(sizes.devices) == 0, in_ref[...], 0.0), keepdims=True)
    step = (product_ref[...] / jnp.broadcast_to(curvature, (SUB, LANES)))[:1]
    per = 2 * CP * sizes.own_rows
    for r in range(sizes.pts):
        for h in range(sizes.run_rows):
            columns = slice((r * sizes.run_rows + h) * LANES, (r * sizes.run_rows + h + 1) * LANES)
            for start in range(0, CP, SUB):
                size = min(SUB, CP - start)
                first = r * per + start * sizes.own_rows + h
                base = all_ref[pl.ds(first, size, stride=sizes.own_rows), :]
                direction = all_ref[pl.ds(first + CP * sizes.own_rows, size, stride=sizes.own_rows), :]
                cam_ref[start : start + size, columns] = base + step * direction
    total = [grad_ref[k] + step * sum_ref[k] for k in range(3)]
    solved = solve([inv_ref[k] for k in range(6)], total)
    for k in range(3):
        table_ref[k * PT_ROWS : (k + 1) * PT_ROWS, :] = -solved[k]
    for row in range(PT_ROWS):
        half, high = row // PT_HI, row % PT_HI
        chunk = high * (PT_LO // LANES) + half
        pt_ref[:, chunk * LANES : (chunk + 1) * LANES] = table_ref[pl.ds(row, 3, stride=PT_ROWS), :]


def shape(*dims, dtype=f32):
    return jax.ShapeDtypeStruct(dims, dtype)


def call(kernel, name, inputs, outputs, scratch, scalars=()):
    vmem = pl.BlockSpec(memory_space=pltpu.VMEM)
    smem = pl.BlockSpec(memory_space=pltpu.SMEM)
    return pl.pallas_call(
        kernel,
        name=name,
        out_shape=outputs,
        in_specs=[smem] * len(scalars) + [vmem] * len(inputs),
        out_specs=[vmem] * len(outputs),
        scratch_shapes=scratch,
        compiler_params=pltpu.CompilerParams(vmem_limit_bytes=VMEM_LIMIT),
    )(*scalars, *inputs)


def body(camera_jacobian, point_jacobian, residual, observed_slot, observed_point, send_list):
    sizes = Sizes(lax.axis_size("pts"), lax.axis_size("cams"), send_list.shape[2], camera_jacobian.shape[1])
    axes = ("pts", "cams")
    rows = sizes.rows
    slot = observed_slot.reshape(rows, LANES)
    point = observed_point.reshape(rows, LANES)
    column = lax.axis_index("cams").astype(jnp.int32).reshape(1)

    def exchange(messages):
        return lax.all_to_all(messages, axes, split_axis=0, concat_axis=0, tiled=True)

    def factors(high_rows, low_rows, entries):
        return [pltpu.VMEM((high_rows, entries), bf16), pltpu.VMEM((low_rows, entries), bf16)]

    point_table = shape(3, PT_ROWS, LANES)
    owned = shape(CP, sizes.own_rows, LANES)
    messages = shape(sizes.devices * sizes.message, LANES)
    scalar = shape(SUB, LANES)
    owned_scratch = pltpu.VMEM((CP, sizes.own_rows, LANES), f32)
    point_scratch = pltpu.VMEM((3, PT_ROWS, LANES), f32)
    entries = sizes.pts * LANES

    first, a, b, inverse, gradient = call(
        functools.partial(setup_kernel, sizes),
        "setup",
        [camera_jacobian, point_jacobian, residual, slot, point, send_list[0]],
        [
            shape(sizes.devices * sizes.first_message, LANES),
            shape(2 * CP * rows, LANES),
            shape(6 * rows, LANES),
            shape(6, PT_ROWS, LANES),
            point_table,
        ],
        [pltpu.VMEM((2 * rows, LANES), f32), point_scratch]
        + factors(max(spread_rows(9 * PIECES, PT_HI), spread_rows(2 * CP * PIECES, sizes.pts)), PT_LO, sizes.obs),
    )
    out, entry, precondition, remainder = call(
        functools.partial(first_owner_kernel, sizes),
        "first_owner",
        [exchange(first)],
        [messages, shape(sizes.pts, LANES, dtype=jnp.int32), owned, owned],
        [owned_scratch] + factors(spread_rows(2 * CP * PIECES, sizes.own_rows), LANES, entries),
        scalars=[column],
    )
    schur_scratch = [pltpu.VMEM((2 * rows, LANES), f32), point_scratch] + factors(
        max(spread_rows(3 * PIECES, PT_HI), spread_rows(CP * PIECES, sizes.pts)), PT_LO, sizes.obs
    )
    at_slot = shape(CP, sizes.pts, LANES)
    product = slots = direction = step = sums = solution_ = None
    for iteration in range(ITERS):
        start, last = iteration == 0, iteration == ITERS - 1
        earlier = [] if start else [product, slots, direction, step, sums]
        results = call(
            functools.partial(schur_kernel, sizes, start, last),
            "schur_last" if last else "schur",
            [exchange(out), a, b, inverse, slot, point, precondition, remainder, gradient] + earlier,
            [shape(sizes.devices, LANES) if last else messages, scalar, at_slot, owned, point_table]
            + ([] if start else [point_table]),
            schur_scratch,
        )
        out, product, slots, direction, sums = results[:5]
        if not start:
            gradient = results[5]
        if last:
            break
        out, remainder, solution_, step = call(
            functools.partial(owner_kernel, sizes, start),
            "owner",
            [exchange(out), entry, precondition, remainder, direction, product] + ([] if start else [solution_]),
            [messages, owned, owned, scalar],
            [owned_scratch] + factors(spread_rows(CP * PIECES, sizes.own_rows), LANES, entries),
        )
    both = jnp.concatenate([solution_, direction]).reshape(2 * CP * sizes.own_rows, LANES)
    gathered = lax.all_gather(both, "pts", axis=0, tiled=True)
    return call(
        functools.partial(final_kernel, sizes),
        "final",
        [exchange(out), product, gathered, inverse, gradient, sums],
        [shape(CP, CAM_OWN), shape(3, PT_DEV)],
        [pltpu.VMEM((3 * PT_ROWS, LANES), f32)],
    )


def solution(mesh):
    return jax.shard_map(
        lambda *arguments: tuple(body(*arguments)),
        mesh=mesh,
        in_specs=(
            P(None, ("pts", "cams")),
            P(None, ("pts", "cams")),
            P(None, ("pts", "cams")),
            P(("pts", "cams")),
            P(("pts", "cams")),
            P(("pts", "cams"), None, None),
        ),
        out_specs=(P(None, "cams"), P(None, ("pts", "cams"))),
        check_vma=False,
    )
```

time: 1050 us -> 129 us (0.12); the launches traced: 1040 us -> 129 us
  local copies, waits for them, and re-layouts: 330 us -> 4.78 us
  other arithmetic: 304 us -> 0.01 us
  waiting for transfers between devices: 292 us -> 8.23 us
  Pallas kernels: 0 us -> 27.7 us
  between operations: 21 us -> 0.71 us
    psum x4 -> x0, waiting for transfers between devices: 288 us -> none  [owner_total(): return lax.psum(dense, 'pts')]
    scatter-add x14 -> x0, other arithmetic: 269 us -> none  [spread(): jnp.zeros((values.shape[0], count), values.dtype).at[:, index].add(values)]
    gather x20 -> x0, local copies, waits for them, and re-layouts: 167 us -> none  [the longest x8 68.7 us: fetch(): return received[:, observed_slot]]
    unnamed x72 -> x16, local copies, waits for them, and re-layouts: 48.4 us -> 4.78 us
    slice x6 -> x0, local copies, waits for them, and re-layouts: 34.8 us -> none  [the longest x5 27.4 us: point_solve(): values[0]]
    psum x5 -> x0, blocking collectives: 33.4 us -> none  [inner(): return lax.psum(jnp.sum(left * right), 'cams')]
    all_gather x0 -> x1, blocking collectives: none -> 31.9 us  [body(): gathered = lax.all_gather(both, 'pts', axis=0, tiled=True)]
    pallas_call x0 -> x8, Pallas kernels: none -> 27.7 us  [call(): pl.pallas_call(kernel, name=name, out_shape=outputs, in_specs=[smem] * le...]
  transfers between devices with their start and end apart: 5 -> 2, of which waited for: 5 -> 1; matrix products, arithmetic and copies ran while one was open for 0% -> 0% of each run, Pallas kernels for 0% -> 0%
where the time goes in v1:
time: 129 us
  blocking collectives  77.5 us (60%)
  Pallas kernels  27.7 us (21%)
  starting transfers between devices  9.84 us (8%)
  waiting for transfers between devices  8.23 us (6%)
  local copies, waits for them, and re-layouts  4.78 us (4%)
    all_to_all x5, blocking collectives, exchange(): lax.all_to_all(messages, axes, split_axis=0, concat_axis=0, tiled=True)  45.6 us
    all_gather x1, blocking collectives, body(): gathered = lax.all_gather(both, 'pts', axis=0, tiled=True)  31.9 us
    pallas_call x8, Pallas kernels, call(): pl.pallas_call(kernel, name=name, out_shape=outputs, in_specs=[smem] * le...  27.7 us
    all_to_all x2, starting transfers between devices, exchange(): lax.all_to_all(messages, axes, split_axis=0, concat_axis=0, tiled=True)  9.84 us
    all_to_all x2, waiting for transfers between devices, exchange(): lax.all_to_all(messages, axes, split_axis=0, concat_axis=0, tiled=True)  8.23 us
    unnamed x16, local copies, waits for them, and re-layouts  4.78 us
  transfers between devices with their start and end apart: 2, of which 1 were waited for; matrix products, arithmetic and copies ran while one was open for 0% of the time, Pallas kernels for 0%

profile of v1, /device:TPU:0, one launch (start us, length us, event | category | flops | bytes accessed | tf_op | source)
XLA Modules:
  0.0 128.8 jit_solution(18007745510111123091)
XLA Ops:
  0.6 0.7 copy-done.7
  1.3 1.0 copy-done
  2.3 0.7 copy-done.1
  3.0 0.7 copy-done.3
  3.8 0.9 copy-done.5
  4.7 0.8 copy-done.6
  5.4 9.9 %setup.1 = (f32[256,128]{1,0:T(8,128)}, f32[576,128]{1,0:T(8,128)S(1)}, f32[192,128]{1,0:T(8,128)S(1)}, f32[6,32,128]{2,1,0:T(8,128)S(1)}, f32[3,32,128]{2,1,0:T(8,128)S(1)}) custom-call(f32[18,4096]{1,0:T(8,128)S(1)} %copy-done, f32[6,4096]{1,0:T(8,128)S(1)} %copy-done.5, f32[2,4096]{1,0:T(2,128)S(1)} %copy-done.6, s32[32,128]{1,0:T(8,128)S(1)} %bitcast.23, ...), custom_call_target="tpu_custom_call" | custom-call | tf_op jit(solution)/shard_map/setup/pallas_call | solution.py:454
  15.3 7.3 %all-to-all-start = ((f32[32,8,128]{2,1,0:T(8,128)}), f32[32,8,128]{2,1,0:T(8,128)S(1)}, u32[]{:S(2)}, u32[]{:S(2)}) async-start(f32[32,8,128]{2,1,0:T(8,128)} %bitcast.4), calls=%async_computation | async-start | bytes 262144 | tf_op jit(solution)/shard_map/all_to_all | solution.py:474
  22.6 8.2 %all-to-all-done = f32[32,8,128]{2,1,0:T(8,128)S(1)} async-done(((f32[32,8,128]{2,1,0:T(8,128)}), f32[32,8,128]{2,1,0:T(8,128)S(1)}, u32[]{:S(2)}, u32[]{:S(2)}) %all-to-all-start) | async-done | bytes 131104 | tf_op jit(solution)/shard_map/all_to_all | solution.py:474
  30.8 0.8 first_owner.1
  31.7 0.0 copy-start.4
  31.7 9.2 %all_to_all.77 = f32[32,4,128]{2,1,0:T(4,128)S(1)} all-to-all(f32[32,4,128]{2,1,0:T(4,128)S(1)} %bitcast.39), channel_id=1, replica_groups=mesh['pts'=8,'cams'=4] {'pts','cams'}, dimensions={0} | all-to-all | bytes 131072 | tf_op jit(solution)/shard_map/all_to_all | solution.py:474
  40.9 5.4 %schur.2 = (f32[128,128]{1,0:T(8,128)S(1)}, f32[8,128]{1,0:T(8,128)S(1)}, f32[9,8,128]{2,1,0:T(8,128)S(1)}, f32[9,8,128]{2,1,0:T(8,128)S(1)}, f32[3,32,128]{2,1,0:T(8,128)S(1)}) custom-call(f32[128,128]{1,0:T(8,128)S(1)} %bitcast.35, f32[576,128]{1,0:T(8,128)S(1)} %get-tuple-element.37.a_ref, f32[192,128]{1,0:T(8,128)S(1)} %get-tuple-element.38.b_ref, ...), custom_call_target="tpu_custom_call" | custom-call | tf_op jit(solution)/shard_map/schur/pallas_call | solution.py:454
  46.3 9.1 %all_to_all.78 = f32[32,4,128]{2,1,0:T(4,128)S(1)} all-to-all(f32[32,4,128]{2,1,0:T(4,128)S(1)} %bitcast.40), channel_id=1, replica_groups=mesh['pts'=8,'cams'=4] {'pts','cams'}, dimensions={0} | all-to-all | bytes 131072 | tf_op jit(solution)/shard_map/all_to_all | solution.py:474
  55.4 0.6 owner.2
  56.0 9.1 %all_to_all.79 = f32[32,4,128]{2,1,0:T(4,128)S(1)} all-to-all(f32[32,4,128]{2,1,0:T(4,128)S(1)} %bitcast.41), channel_id=1, replica_groups=mesh['pts'=8,'cams'=4] {'pts','cams'}, dimensions={0} | all-to-all | bytes 131072 | tf_op jit(solution)/shard_map/all_to_all | solution.py:474
  65.1 5.4 %schur.3 = (f32[128,128]{1,0:T(8,128)S(1)}, f32[8,128]{1,0:T(8,128)S(1)}, f32[9,8,128]{2,1,0:T(8,128)S(1)}, f32[9,8,128]{2,1,0:T(8,128)S(1)}, f32[3,32,128]{2,1,0:T(8,128)S(1)}, /*index=5*/f32[3,32,128]{2,1,0:T(8,128)S(1)}) custom-call(f32[128,128]{1,0:T(8,128)S(1)} %bitcast.32, f32[576,128]{1,0:T(8,128)S(1)} %get-tuple-element.37.a_ref, ...), custom_call_target="tpu_custom_call" | custom-call | tf_op jit(solution)/shard_map/schur/pallas_call | solution.py:454
  70.6 9.1 %all_to_all.80 = f32[32,4,128]{2,1,0:T(4,128)S(1)} all-to-all(f32[32,4,128]{2,1,0:T(4,128)S(1)} %bitcast.37), channel_id=1, replica_groups=mesh['pts'=8,'cams'=4] {'pts','cams'}, dimensions={0} | all-to-all | bytes 131072 | tf_op jit(solution)/shard_map/all_to_all | solution.py:474
  79.7 0.6 owner.3
  80.3 9.1 %all_to_all.81 = f32[32,4,128]{2,1,0:T(4,128)S(1)} all-to-all(f32[32,4,128]{2,1,0:T(4,128)S(1)} %bitcast.38), channel_id=1, replica_groups=mesh['pts'=8,'cams'=4] {'pts','cams'}, dimensions={0} | all-to-all | bytes 131072 | tf_op jit(solution)/shard_map/all_to_all | solution.py:474
  89.4 3.9 %schur_last.1 = (f32[32,128]{1,0:T(8,128)}, f32[8,128]{1,0:T(8,128)S(1)}, f32[9,8,128]{2,1,0:T(8,128)}, f32[9,8,128]{2,1,0:T(8,128)S(1)}, f32[3,32,128]{2,1,0:T(8,128)S(1)}, /*index=5*/f32[3,32,128]{2,1,0:T(8,128)S(1)}) custom-call(f32[128,128]{1,0:T(8,128)S(1)} %bitcast.31, f32[576,128]{1,0:T(8,128)S(1)} %get-tuple-element.37.a_ref, ...), custom_call_target="tpu_custom_call" | custom-call | tf_op jit(solution)/shard_map/schur_last/pallas_call | solution.py:454
  93.3 2.5 %all-to-all-start.6 = ((f32[32,1,128]{2,1,0:T(1,128)}), f32[32,1,128]{2,1,0:T(1,128)S(1)}, u32[]{:S(2)}, u32[]{:S(2)}) async-start(f32[32,1,128]{2,1,0:T(1,128)} %bitcast.17), calls=%async_computation.6 | async-start | bytes 32768 | tf_op jit(solution)/shard_map/all_to_all | solution.py:474
  95.8 31.9 %all_gather.3.all_ref = f32[1152,128]{1,0:T(8,128)S(1)} all-gather(f32[144,128]{1,0:T(8,128)S(1)} %maximum_bitcast_fusion), channel_id=1, replica_groups=mesh['pts'=8,'cams'=4] {'pts'}, dimensions={0}, use_global_device_ids=true | all-gather | bytes 663552 | tf_op jit(solution)/shard_map/all_gather | solution.py:538
  127.8 1.0 final.1
  (11 shorter events, 0.0 us)
Async XLA Ops:
  0.6 0.7 copy-start.7
  1.3 1.0 copy-start
  2.3 0.7 copy-start.1
  3.0 0.7 copy-start.3
  3.8 0.9 copy-start.5
  4.7 0.8 copy-start.6
  15.3 15.5 %all-to-all-start = ((f32[32,8,128]{2,1,0:T(8,128)}), f32[32,8,128]{2,1,0:T(8,128)S(1)}, u32[]{:S(2)}, u32[]{:S(2)}) async-start(f32[32,8,128]{2,1,0:T(8,128)} %bitcast.4), calls=%async_computation | async-start | bytes 262144 | tf_op jit(solution)/shard_map/all_to_all | solution.py:474
  31.7 9.2 %copy-start.2 = (s32[4096]{0:T(1024)S(1)}, s32[4096]{0:T(1024)}, u32[]{:S(2)}) copy-start(s32[4096]{0:T(1024)} %param.9) | copy-start | bytes 49156
  31.7 9.2 %copy-start.4 = (s32[4096]{0:T(1024)S(1)}, s32[4096]{0:T(1024)}, u32[]{:S(2)}) copy-start(s32[4096]{0:T(1024)} %param.10) | copy-start | bytes 49156
  93.3 34.5 %all-to-all-start.6 = ((f32[32,1,128]{2,1,0:T(1,128)}), f32[32,1,128]{2,1,0:T(1,128)S(1)}, u32[]{:S(2)}, u32[]{:S(2)}) async-start(f32[32,1,128]{2,1,0:T(1,128)} %bitcast.17), calls=%async_computation.6 | async-start | bytes 32768 | tf_op jit(solution)/shard_map/all_to_all | solution.py:474

commit v2 on v1

--- a/solution.py
+++ b/solution.py
@@ -38,8 +38,8 @@
         self.own_rows = max(SUB, self.run_rows)
         self.groups = -(-CP // cams)
         self.first_groups = -(-2 * CP // cams)
-        self.message = 4
-        self.first_message = 4 if self.first_groups < 4 else 8
+        self.message = self.groups
+        self.first_message = self.first_groups + 1
         assert self.groups * cams > CP
 
 
@@ -187,10 +187,18 @@
     return jnp.sum(chosen, keepdims=True)
 
 
-def setup_kernel(sizes, jac_ref, pjac_ref, res_ref, slot_ref, point_ref, list_ref,
-                 out_ref, a_ref, b_ref, inv_ref, grad_ref,
-                 r_ref, table_ref, spread_ref, place_ref):
+def setup_kernel(sizes, *refs):
+    sources, refs = refs[:6], refs[6:]
+    out_ref, a_ref, b_ref, inv_ref, grad_ref = refs[:5]
+    r_ref, table_ref, spread_ref, place_ref = refs[5:9]
+    jac_ref, pjac_ref, res_ref, slot_ref, point_ref, list_ref = refs[9:15]
+    semaphores = refs[15]
     rows = sizes.rows
+    copies = [pltpu.make_async_copy(source, target, semaphores.at[k]) for k, (source, target) in enumerate(zip(sources, refs[9:15]))]
+    for copy in copies:
+        copy.start()
+    for copy in copies:
+        copy.wait()
     for j in range(rows):
         columns = slice(j * LANES, (j + 1) * LANES)
         for start in range(0, 2 * CP, SUB):
@@ -421,6 +429,18 @@
     write_messages(fields, partial, sizes.groups, sizes.message, out_ref, sizes)
 
 
+def tail_kernel(sizes, in_ref, pre_ref, rem_ref, dir_ref, product_ref, sol_ref, out_ref):
+    renewed = jnp.broadcast_to(read_scalar(in_ref, sizes.groups, sizes.message, sizes), (SUB, LANES))
+    beta = (renewed / product_ref[...])[:1]
+    for k in range(CP):
+        direction = pre_ref[k] * rem_ref[k] + beta * dir_ref[k]
+        for p in range(sizes.pts):
+            first = (p * 2 * CP + k) * sizes.own_rows
+            out_ref[first : first + sizes.own_rows, :] = sol_ref[k]
+            first += CP * sizes.own_rows
+            out_ref[first : first + sizes.own_rows, :] = direction
+
+
 def final_kernel(sizes, in_ref, product_ref, all_ref, inv_ref, grad_ref, sum_ref, cam_ref, pt_ref, table_ref):
     curvature = jnp.sum(jnp.where(lane_iota(sizes.devices) == 0, in_ref[...], 0.0), keepdims=True)
     step = (product_ref[...] / jnp.broadcast_to(curvature, (SUB, LANES)))[:1]
@@ -448,16 +468,18 @@
     return jax.ShapeDtypeStruct(dims, dtype)
 
 
-def call(kernel, name, inputs, outputs, scratch, scalars=()):
+def call(kernel, name, inputs, outputs, scratch, scalars=(), inputs_at=pltpu.VMEM, cost=None):
     vmem = pl.BlockSpec(memory_space=pltpu.VMEM)
+    given = pl.BlockSpec(memory_space=inputs_at)
     smem = pl.BlockSpec(memory_space=pltpu.SMEM)
     return pl.pallas_call(
         kernel,
         name=name,
         out_shape=outputs,
-        in_specs=[smem] * len(scalars) + [vmem] * len(inputs),
+        in_specs=[smem] * len(scalars) + [given] * len(inputs),
         out_specs=[vmem] * len(outputs),
         scratch_shapes=scratch,
+        cost_estimate=cost,
         compiler_params=pltpu.CompilerParams(vmem_limit_bytes=VMEM_LIMIT),
     )(*scalars, *inputs)
 
@@ -471,7 +493,9 @@
     column = lax.axis_index("cams").astype(jnp.int32).reshape(1)
 
     def exchange(messages):
-        return lax.all_to_all(messages, axes, split_axis=0, concat_axis=0, tiled=True)
+        width = messages.size // sizes.devices
+        flat = messages.reshape(sizes.devices, 1, width)
+        return lax.all_to_all(flat, axes, split_axis=0, concat_axis=0, tiled=True).reshape(messages.shape)
 
     def factors(high_rows, low_rows, entries):
         return [pltpu.VMEM((high_rows, entries), bf16), pltpu.VMEM((low_rows, entries), bf16)]
@@ -484,10 +508,11 @@
     point_scratch = pltpu.VMEM((3, PT_ROWS, LANES), f32)
     entries = sizes.pts * LANES
 
+    given = [camera_jacobian, point_jacobian, residual, slot, point, send_list[0]]
     first, a, b, inverse, gradient = call(
         functools.partial(setup_kernel, sizes),
         "setup",
-        [camera_jacobian, point_jacobian, residual, slot, point, send_list[0]],
+        given,
         [
             shape(sizes.devices * sizes.first_message, LANES),
             shape(2 * CP * rows, LANES),
@@ -496,7 +521,10 @@
             point_table,
         ],
         [pltpu.VMEM((2 * rows, LANES), f32), point_scratch]
-        + factors(max(spread_rows(9 * PIECES, PT_HI), spread_rows(2 * CP * PIECES, sizes.pts)), PT_LO, sizes.obs),
+        + factors(max(spread_rows(9 * PIECES, PT_HI), spread_rows(2 * CP * PIECES, sizes.pts)), PT_LO, sizes.obs)
+        + [pltpu.VMEM(value.shape, value.dtype) for value in given]
+        + [pltpu.SemaphoreType.DMA((len(given),))],
+        inputs_at=pltpu.HBM,
     )
     out, entry, precondition, remainder = call(
         functools.partial(first_owner_kernel, sizes),
@@ -514,13 +542,26 @@
     for iteration in range(ITERS):
         start, last = iteration == 0, iteration == ITERS - 1
         earlier = [] if start else [product, slots, direction, step, sums]
+        arrived = exchange(out)
+        if last:
+            (both,) = call(
+                functools.partial(tail_kernel, sizes),
+                "tail",
+                [arrived, precondition, remainder, direction, product, solution_],
+                [shape(sizes.pts * 2 * CP * sizes.own_rows, LANES)],
+                [],
+            )
+            gathered = lax.all_to_all(
+                both.reshape(sizes.pts, -1, LANES), "pts", split_axis=0, concat_axis=0, tiled=True
+            ).reshape(both.shape)
         results = call(
             functools.partial(schur_kernel, sizes, start, last),
             "schur_last" if last else "schur",
-            [exchange(out), a, b, inverse, slot, point, precondition, remainder, gradient] + earlier,
+            [arrived, a, b, inverse, slot, point, precondition, remainder, gradient] + earlier,
             [shape(sizes.devices, LANES) if last else messages, scalar, at_slot, owned, point_table]
             + ([] if start else [point_table]),
             schur_scratch,
+            cost=pl.CostEstimate(flops=2_000_000_000, bytes_accessed=10_000_000, transcendentals=0),
         )
         out, product, slots, direction, sums = results[:5]
         if not start:
@@ -534,8 +575,6 @@
             [messages, owned, owned, scalar],
             [owned_scratch] + factors(spread_rows(CP * PIECES, sizes.own_rows), LANES, entries),
         )
-    both = jnp.concatenate([solution_, direction]).reshape(2 * CP * sizes.own_rows, LANES)
-    gathered = lax.all_gather(both, "pts", axis=0, tiled=True)
     return call(
         functools.partial(final_kernel, sizes),
         "final",

time: 129 us -> 123 us (0.953)
  blocking collectives: 77.5 us -> 64.4 us
  waiting for transfers between devices: 8.23 us -> 14.8 us
    all_gather x1 -> x0, blocking collectives: 31.9 us -> none  [body(): gathered = lax.all_gather(both, 'pts', axis=0, tiled=True)]
    all_to_all x5 -> x6, blocking collectives: 45.6 us -> 64.4 us  [the longest x5 45.1 us: exchange(): lax.all_to_all(flat, axes, split_axis=0, concat_axis=0, tiled=True)]
    all_to_all x2, waiting for transfers between devices: 8.23 us -> 14.8 us  [exchange(): lax.all_to_all(flat, axes, split_axis=0, concat_axis=0, tiled=True)]
    pallas_call x8 -> x9, Pallas kernels: 27.7 us -> 28.2 us  [call(): pl.pallas_call(kernel, name=name, out_shape=outputs, in_specs=[smem] * le...]
  transfers between devices with their start and end apart: 2 -> 2, of which waited for: 1 -> 2; matrix products, arithmetic and copies ran while one was open for 0% -> 0% of each run, Pallas kernels for 0% -> 0%
where the time goes in v2:
time: 123 us
  blocking collectives  64.4 us (52%)
  Pallas kernels  28.2 us (23%)
  waiting for transfers between devices  14.8 us (12%)
  starting transfers between devices  9.87 us (8%)
  local copies, waits for them, and re-layouts  4.78 us (4%)
    all_to_all x5, blocking collectives, exchange(): lax.all_to_all(flat, axes, split_axis=0, concat_axis=0, tiled=True)  45.1 us
    pallas_call x9, Pallas kernels, call(): pl.pallas_call(kernel, name=name, out_shape=outputs, in_specs=[smem] * le...  28.2 us
    all_to_all x1, blocking collectives, body(): lax.all_to_all(both.reshape(sizes.pts, -1, LANES), 'pts', split_axis=0, c...  19.2 us
    all_to_all x2, waiting for transfers between devices, exchange(): lax.all_to_all(flat, axes, split_axis=0, concat_axis=0, tiled=True)  14.8 us
    all_to_all x2, starting transfers between devices, exchange(): lax.all_to_all(flat, axes, split_axis=0, concat_axis=0, tiled=True)  9.87 us
    unnamed x16, local copies, waits for them, and re-layouts  4.78 us
  transfers between devices with their start and end apart: 2, of which 2 were waited for; matrix products, arithmetic and copies ran while one was open for 0% of the time, Pallas kernels for 0%

profile of v2, /device:TPU:0, one launch (start us, length us, event | category | flops | bytes accessed | tf_op | source)
XLA Modules:
  0.0 122.7 jit_solution(9698152152461093510)
XLA Ops:
  0.6 0.7 copy-done.7
  1.3 1.0 copy-done
  2.3 0.9 copy-done.1
  3.2 0.8 copy-done.2
  4.0 0.7 copy-done.3
  4.7 0.7 copy-done.5
  5.4 10.4 %setup.1 = (f32[192,128]{1,0:T(8,128)}, f32[576,128]{1,0:T(8,128)S(1)}, f32[192,128]{1,0:T(8,128)S(1)}, f32[6,32,128]{2,1,0:T(8,128)S(1)}, f32[3,32,128]{2,1,0:T(8,128)S(1)}) custom-call(f32[18,4096]{1,0:T(8,128)S(1)} %copy-done, f32[6,4096]{1,0:T(8,128)S(1)} %copy-done.1, f32[2,4096]{1,0:T(2,128)S(1)} %copy-done.2, s32[32,128]{1,0:T(8,128)S(1)} %bitcast.37, ...), custom_call_target="tpu_custom_call" | custom-call | tf_op jit(solution)/shard_map/setup/pallas_call | solution.py:475
  15.8 7.3 %all-to-all-start = ((f32[32,1,768]{2,1,0:T(1,128)}), f32[32,1,768]{2,1,0:T(1,128)S(1)}, u32[]{:S(2)}, u32[]{:S(2)}) async-start(f32[32,1,768]{2,1,0:T(1,128)} %bitcast.4), calls=%async_computation | async-start | bytes 196608 | tf_op jit(solution)/shard_map/all_to_all | solution.py:498
  23.1 7.8 %all-to-all-done = f32[32,1,768]{2,1,0:T(1,128)S(1)} async-done(((f32[32,1,768]{2,1,0:T(1,128)}), f32[32,1,768]{2,1,0:T(1,128)S(1)}, u32[]{:S(2)}, u32[]{:S(2)}) %all-to-all-start) | async-done | bytes 98336 | tf_op jit(solution)/shard_map/all_to_all | solution.py:498
  30.9 0.8 first_owner.1
  31.7 9.0 %all_to_all.40 = f32[32,1,384]{2,1,0:T(1,128)S(1)} all-to-all(f32[32,1,384]{2,1,0:T(1,128)S(1)} %bitcast.34), channel_id=1, replica_groups=mesh['pts'=8,'cams'=4] {'pts','cams'}, dimensions={0} | all-to-all | bytes 98304 | tf_op jit(solution)/shard_map/all_to_all | solution.py:498
  40.8 5.4 %schur.2 = (f32[96,128]{1,0:T(8,128)S(1)}, f32[8,128]{1,0:T(8,128)S(1)}, f32[9,8,128]{2,1,0:T(8,128)S(1)}, f32[9,8,128]{2,1,0:T(8,128)S(1)}, f32[3,32,128]{2,1,0:T(8,128)S(1)}) custom-call(f32[96,128]{1,0:T(8,128)S(1)} %bitcast.33, f32[576,128]{1,0:T(8,128)S(1)} %get-tuple-element.36.a_ref, f32[192,128]{1,0:T(8,128)S(1)} %get-tuple-element.37.b_ref, ...), custom_call_target="tpu_custom_call" | custom-call | flops 2000000000 | bytes 10000000 | tf_op jit(solution)/shard_map/schur/pallas_call | solution.py:475
  46.2 9.0 %all_to_all.41 = f32[32,1,384]{2,1,0:T(1,128)S(1)} all-to-all(f32[32,1,384]{2,1,0:T(1,128)S(1)} %bitcast.35), channel_id=1, replica_groups=mesh['pts'=8,'cams'=4] {'pts','cams'}, dimensions={0} | all-to-all | bytes 98304 | tf_op jit(solution)/shard_map/all_to_all | solution.py:498
  55.2 0.6 owner.2
  55.8 9.0 %all_to_all.42 = f32[32,1,384]{2,1,0:T(1,128)S(1)} all-to-all(f32[32,1,384]{2,1,0:T(1,128)S(1)} %bitcast.36), channel_id=1, replica_groups=mesh['pts'=8,'cams'=4] {'pts','cams'}, dimensions={0} | all-to-all | bytes 98304 | tf_op jit(solution)/shard_map/all_to_all | solution.py:498
  64.8 5.4 %schur.3 = (f32[96,128]{1,0:T(8,128)S(1)}, f32[8,128]{1,0:T(8,128)S(1)}, f32[9,8,128]{2,1,0:T(8,128)S(1)}, f32[9,8,128]{2,1,0:T(8,128)S(1)}, f32[3,32,128]{2,1,0:T(8,128)S(1)}, /*index=5*/f32[3,32,128]{2,1,0:T(8,128)S(1)}) custom-call(f32[96,128]{1,0:T(8,128)S(1)} %bitcast.30, f32[576,128]{1,0:T(8,128)S(1)} %get-tuple-element.36.a_ref, ...), custom_call_target="tpu_custom_call" | custom-call | flops 2000000000 | bytes 10000000 | tf_op jit(solution)/shard_map/schur/pallas_call | solution.py:475
  70.3 9.0 %all_to_all.43 = f32[32,1,384]{2,1,0:T(1,128)S(1)} all-to-all(f32[32,1,384]{2,1,0:T(1,128)S(1)} %bitcast.31), channel_id=1, replica_groups=mesh['pts'=8,'cams'=4] {'pts','cams'}, dimensions={0} | all-to-all | bytes 98304 | tf_op jit(solution)/shard_map/all_to_all | solution.py:498
  79.3 0.6 owner.3
  79.9 9.0 %all_to_all.44 = f32[32,1,384]{2,1,0:T(1,128)S(1)} all-to-all(f32[32,1,384]{2,1,0:T(1,128)S(1)} %bitcast.32), channel_id=1, replica_groups=mesh['pts'=8,'cams'=4] {'pts','cams'}, dimensions={0} | all-to-all | bytes 98304 | tf_op jit(solution)/shard_map/all_to_all | solution.py:498
  88.9 3.9 %schur_last.1 = (f32[32,128]{1,0:T(8,128)}, f32[8,128]{1,0:T(8,128)S(1)}, f32[9,8,128]{2,1,0:T(8,128)}, f32[9,8,128]{2,1,0:T(8,128)}, f32[3,32,128]{2,1,0:T(8,128)S(1)}, /*index=5*/f32[3,32,128]{2,1,0:T(8,128)S(1)}) custom-call(f32[96,128]{1,0:T(8,128)S(1)} %bitcast.25, f32[576,128]{1,0:T(8,128)S(1)} %get-tuple-element.36.a_ref, ...), custom_call_target="tpu_custom_call" | custom-call | flops 2000000000 | bytes 10000000 | tf_op jit(solution)/shard_map/schur_last/pallas_call | solution.py:475
  92.8 2.6 %all-to-all-start.6 = ((f32[32,1,128]{2,1,0:T(1,128)}), f32[32,1,128]{2,1,0:T(1,128)S(1)}, u32[]{:S(2)}, u32[]{:S(2)}) async-start(f32[32,1,128]{2,1,0:T(1,128)} %bitcast.17), calls=%async_computation.6 | async-start | bytes 32768 | tf_op jit(solution)/shard_map/all_to_all | solution.py:498
  95.5 7.0 %all-to-all-done.6 = f32[32,1,128]{2,1,0:T(1,128)S(1)} async-done(((f32[32,1,128]{2,1,0:T(1,128)}), f32[32,1,128]{2,1,0:T(1,128)S(1)}, u32[]{:S(2)}, u32[]{:S(2)}) %all-to-all-start.6) | async-done | bytes 16416 | tf_op jit(solution)/shard_map/all_to_all | solution.py:498
  102.5 19.2 %all_to_all.45 = f32[8,144,128]{2,1,0:T(8,128)S(1)} all-to-all(f32[8,144,128]{2,1,0:T(8,128)S(1)} %bitcast.22), channel_id=1, replica_groups=mesh['pts'=8,'cams'=4] {'pts'}, dimensions={0} | all-to-all | bytes 1179648 | tf_op jit(solution)/shard_map/all_to_all | solution.py:554
  121.7 1.0 final.1
  (11 shorter events, 0.2 us)
Async XLA Ops:
  0.6 0.7 copy-start.7
  1.3 1.0 copy-start
  2.3 0.9 copy-start.1
  3.2 0.8 copy-start.2
  4.0 0.7 copy-start.3
  4.7 0.7 copy-start.5
  15.8 15.1 %all-to-all-start = ((f32[32,1,768]{2,1,0:T(1,128)}), f32[32,1,768]{2,1,0:T(1,128)S(1)}, u32[]{:S(2)}, u32[]{:S(2)}) async-start(f32[32,1,768]{2,1,0:T(1,128)} %bitcast.4), calls=%async_computation | async-start | bytes 196608 | tf_op jit(solution)/shard_map/all_to_all | solution.py:498
  31.7 9.1 %copy-start.4 = (s32[4096]{0:T(1024)S(1)}, s32[4096]{0:T(1024)}, u32[]{:S(2)}) copy-start(s32[4096]{0:T(1024)} %param.9) | copy-start | bytes 49156
  31.7 9.0 %copy-start.6 = (s32[4096]{0:T(1024)S(1)}, s32[4096]{0:T(1024)}, u32[]{:S(2)}) copy-start(s32[4096]{0:T(1024)} %param.10) | copy-start | bytes 49156
  92.8 9.7 %all-to-all-start.6 = ((f32[32,1,128]{2,1,0:T(1,128)}), f32[32,1,128]{2,1,0:T(1,128)S(1)}, u32[]{:S(2)}, u32[]{:S(2)}) async-start(f32[32,1,128]{2,1,0:T(1,128)} %bitcast.17), calls=%async_computation.6 | async-start | bytes 32768 | tf_op jit(solution)/shard_map/all_to_all | solution.py:498

commit v3 on v2

--- a/solution.py
+++ b/solution.py
@@ -434,23 +434,24 @@
     beta = (renewed / product_ref[...])[:1]
     for k in range(CP):
         direction = pre_ref[k] * rem_ref[k] + beta * dir_ref[k]
-        for p in range(sizes.pts):
-            first = (p * 2 * CP + k) * sizes.own_rows
-            out_ref[first : first + sizes.own_rows, :] = sol_ref[k]
-            first += CP * sizes.own_rows
-            out_ref[first : first + sizes.own_rows, :] = direction
-
-
-def final_kernel(sizes, in_ref, product_ref, all_ref, inv_ref, grad_ref, sum_ref, cam_ref, pt_ref, table_ref):
+        first = k * sizes.own_rows
+        out_ref[first : first + sizes.own_rows, :] = sol_ref[k]
+        first += CP * sizes.own_rows
+        out_ref[first : first + sizes.own_rows, :] = direction
+
+
+def final_kernel(sizes, run_ref, in_ref, product_ref, inv_ref, grad_ref, sum_ref, *refs):
+    all_refs = refs[: sizes.pts]
+    cam_ref, pt_ref, table_ref = refs[sizes.pts :]
     curvature = jnp.sum(jnp.where(lane_iota(sizes.devices) == 0, in_ref[...], 0.0), keepdims=True)
     step = (product_ref[...] / jnp.broadcast_to(curvature, (SUB, LANES)))[:1]
-    per = 2 * CP * sizes.own_rows
-    for r in range(sizes.pts):
+    for k, all_ref in enumerate(all_refs):
+        base_column = (run_ref[0] ^ k) * sizes.run
         for h in range(sizes.run_rows):
-            columns = slice((r * sizes.run_rows + h) * LANES, (r * sizes.run_rows + h + 1) * LANES)
+            columns = pl.ds(pl.multiple_of(base_column + h * LANES, LANES), LANES)
             for start in range(0, CP, SUB):
                 size = min(SUB, CP - start)
-                first = r * per + start * sizes.own_rows + h
+                first = start * sizes.own_rows + h
                 base = all_ref[pl.ds(first, size, stride=sizes.own_rows), :]
                 direction = all_ref[pl.ds(first + CP * sizes.own_rows, size, stride=sizes.own_rows), :]
                 cam_ref[start : start + size, columns] = base + step * direction
@@ -508,7 +509,10 @@
     point_scratch = pltpu.VMEM((3, PT_ROWS, LANES), f32)
     entries = sizes.pts * LANES
 
-    given = [camera_jacobian, point_jacobian, residual, slot, point, send_list[0]]
+    given = [
+        pltpu.with_memory_space_constraint(value, pltpu.HBM)
+        for value in (camera_jacobian, point_jacobian, residual, slot, point, send_list[0])
+    ]
     first, a, b, inverse, gradient = call(
         functools.partial(setup_kernel, sizes),
         "setup",
@@ -524,7 +528,7 @@
         + factors(max(spread_rows(9 * PIECES, PT_HI), spread_rows(2 * CP * PIECES, sizes.pts)), PT_LO, sizes.obs)
         + [pltpu.VMEM(value.shape, value.dtype) for value in given]
         + [pltpu.SemaphoreType.DMA((len(given),))],
-        inputs_at=pltpu.HBM,
+        inputs_at=pl.ANY,
     )
     out, entry, precondition, remainder = call(
         functools.partial(first_owner_kernel, sizes),
@@ -548,12 +552,12 @@
                 functools.partial(tail_kernel, sizes),
                 "tail",
                 [arrived, precondition, remainder, direction, product, solution_],
-                [shape(sizes.pts * 2 * CP * sizes.own_rows, LANES)],
+                [shape(2 * CP * sizes.own_rows, LANES)],
                 [],
             )
-            gathered = lax.all_to_all(
-                both.reshape(sizes.pts, -1, LANES), "pts", split_axis=0, concat_axis=0, tiled=True
-            ).reshape(both.shape)
+            gathered = [both] + [
+                lax.ppermute(both, "pts", [(p, p ^ k) for p in range(sizes.pts)]) for k in range(1, sizes.pts)
+            ]
         results = call(
             functools.partial(schur_kernel, sizes, start, last),
             "schur_last" if last else "schur",
@@ -578,9 +582,10 @@
     return call(
         functools.partial(final_kernel, sizes),
         "final",
-        [exchange(out), product, gathered, inverse, gradient, sums],
+        [exchange(out), product, inverse, gradient, sums] + gathered,
         [shape(CP, CAM_OWN), shape(3, PT_DEV)],
         [pltpu.VMEM((3 * PT_ROWS, LANES), f32)],
+        scalars=[lax.axis_index("pts").astype(jnp.int32).reshape(1)],
     )
 
 

time: 123 us -> 113 us (0.919)
  blocking collectives: 64.4 us -> 45.1 us
  starting transfers between devices: 9.87 us -> 23 us
  local copies, waits for them, and re-layouts: 4.78 us -> 0.01 us
    all_to_all x1 -> x0, blocking collectives: 19.2 us -> none  [body(): lax.all_to_all(both.reshape(sizes.pts, -1, LANES), 'pts', split_axis=0, c...]
    ppermute x0 -> x7, starting transfers between devices: none -> 13.1 us  [body(): lax.ppermute(both, 'pts', [(p, p ^ k) for p in range(sizes.pts)])]
    unnamed x16 -> x4, local copies, waits for them, and re-layouts: 4.78 us -> 0.01 us
  transfers between devices with their start and end apart: 2 -> 9, of which waited for: 2 -> 3; matrix products, arithmetic and copies ran while one was open for 0% -> 0% of each run, Pallas kernels for 0% -> 3%
where the time goes in v3:
time: 113 us
  blocking collectives  45.1 us (40%)
  Pallas kernels  28.8 us (25%)
  starting transfers between devices  23 us (20%)
  waiting for transfers between devices  15.2 us (13%)
    all_to_all x5, blocking collectives, exchange(): lax.all_to_all(flat, axes, split_axis=0, concat_axis=0, tiled=True)  45.1 us
    pallas_call x9, Pallas kernels, call(): pl.pallas_call(kernel, name=name, out_shape=outputs, in_specs=[smem] * le...  28.8 us
    all_to_all x2, waiting for transfers between devices, exchange(): lax.all_to_all(flat, axes, split_axis=0, concat_axis=0, tiled=True)  14.9 us
    ppermute x7, starting transfers between devices, body(): lax.ppermute(both, 'pts', [(p, p ^ k) for p in range(sizes.pts)])  13.1 us
    all_to_all x2, starting transfers between devices, exchange(): lax.all_to_all(flat, axes, split_axis=0, concat_axis=0, tiled=True)  9.86 us
  transfers between devices with their start and end apart: 9, of which 3 were waited for; matrix products, arithmetic and copies ran while one was open for 0% of the time, Pallas kernels for 3%

profile of v3, /device:TPU:0, one launch (start us, length us, event | category | flops | bytes accessed | tf_op | source)
XLA Modules:
  0.0 112.9 jit_solution(8792992381183933798)
XLA Ops:
  0.6 10.9 %setup.1 = (f32[192,128]{1,0:T(8,128)}, f32[576,128]{1,0:T(8,128)S(1)}, f32[192,128]{1,0:T(8,128)S(1)}, f32[6,32,128]{2,1,0:T(8,128)S(1)}, f32[3,32,128]{2,1,0:T(8,128)S(1)}) custom-call(f32[18,4096]{1,0:T(8,128)} %refs_0_.1, f32[6,4096]{1,0:T(8,128)} %refs_1_.1, f32[2,4096]{1,0:T(2,128)} %refs_2_.1, s32[32,128]{1,0:T(8,128)} %bitcast.34, ...), custom_call_target="tpu_custom_call" | custom-call | tf_op jit(solution)/shard_map/setup/pallas_call | solution.py:476
  11.6 7.3 %all-to-all-start = ((f32[32,1,768]{2,1,0:T(1,128)}), f32[32,1,768]{2,1,0:T(1,128)S(1)}, u32[]{:S(2)}, u32[]{:S(2)}) async-start(f32[32,1,768]{2,1,0:T(1,128)} %bitcast.5), calls=%async_computation | async-start | bytes 196608 | tf_op jit(solution)/shard_map/all_to_all | solution.py:499
  18.9 7.8 %all-to-all-done = f32[32,1,768]{2,1,0:T(1,128)S(1)} async-done(((f32[32,1,768]{2,1,0:T(1,128)}), f32[32,1,768]{2,1,0:T(1,128)S(1)}, u32[]{:S(2)}, u32[]{:S(2)}) %all-to-all-start) | async-done | bytes 98336 | tf_op jit(solution)/shard_map/all_to_all | solution.py:499
  26.7 0.8 first_owner.1
  27.5 9.0 %all_to_all.35 = f32[32,1,384]{2,1,0:T(1,128)S(1)} all-to-all(f32[32,1,384]{2,1,0:T(1,128)S(1)} %bitcast.31), channel_id=1, replica_groups=mesh['pts'=8,'cams'=4] {'pts','cams'}, dimensions={0} | all-to-all | bytes 98304 | tf_op jit(solution)/shard_map/all_to_all | solution.py:499
  36.6 5.4 %schur.2 = (f32[96,128]{1,0:T(8,128)S(1)}, f32[8,128]{1,0:T(8,128)S(1)}, f32[9,8,128]{2,1,0:T(8,128)S(1)}, f32[9,8,128]{2,1,0:T(8,128)S(1)}, f32[3,32,128]{2,1,0:T(8,128)S(1)}) custom-call(f32[96,128]{1,0:T(8,128)S(1)} %bitcast.30, f32[576,128]{1,0:T(8,128)S(1)} %get-tuple-element.36.a_ref, f32[192,128]{1,0:T(8,128)S(1)} %get-tuple-element.37.b_ref, ...), custom_call_target="tpu_custom_call" | custom-call | flops 2000000000 | bytes 10000000 | tf_op jit(solution)/shard_map/schur/pallas_call | solution.py:476
  42.0 9.0 %all_to_all.36 = f32[32,1,384]{2,1,0:T(1,128)S(1)} all-to-all(f32[32,1,384]{2,1,0:T(1,128)S(1)} %bitcast.32), channel_id=1, replica_groups=mesh['pts'=8,'cams'=4] {'pts','cams'}, dimensions={0} | all-to-all | bytes 98304 | tf_op jit(solution)/shard_map/all_to_all | solution.py:499
  51.0 0.6 owner.2
  51.6 9.0 %all_to_all.37 = f32[32,1,384]{2,1,0:T(1,128)S(1)} all-to-all(f32[32,1,384]{2,1,0:T(1,128)S(1)} %bitcast.33), channel_id=1, replica_groups=mesh['pts'=8,'cams'=4] {'pts','cams'}, dimensions={0} | all-to-all | bytes 98304 | tf_op jit(solution)/shard_map/all_to_all | solution.py:499
  60.6 5.4 %schur.3 = (f32[96,128]{1,0:T(8,128)S(1)}, f32[8,128]{1,0:T(8,128)S(1)}, f32[9,8,128]{2,1,0:T(8,128)S(1)}, f32[9,8,128]{2,1,0:T(8,128)S(1)}, f32[3,32,128]{2,1,0:T(8,128)S(1)}, /*index=5*/f32[3,32,128]{2,1,0:T(8,128)S(1)}) custom-call(f32[96,128]{1,0:T(8,128)S(1)} %bitcast.27, f32[576,128]{1,0:T(8,128)S(1)} %get-tuple-element.36.a_ref, ...), custom_call_target="tpu_custom_call" | custom-call | flops 2000000000 | bytes 10000000 | tf_op jit(solution)/shard_map/schur/pallas_call | solution.py:476
  66.0 9.0 %all_to_all.38 = f32[32,1,384]{2,1,0:T(1,128)S(1)} all-to-all(f32[32,1,384]{2,1,0:T(1,128)S(1)} %bitcast.28), channel_id=1, replica_groups=mesh['pts'=8,'cams'=4] {'pts','cams'}, dimensions={0} | all-to-all | bytes 98304 | tf_op jit(solution)/shard_map/all_to_all | solution.py:499
  75.1 0.6 owner.3
  75.7 9.0 %all_to_all.39 = f32[32,1,384]{2,1,0:T(1,128)S(1)} all-to-all(f32[32,1,384]{2,1,0:T(1,128)S(1)} %bitcast.29), channel_id=1, replica_groups=mesh['pts'=8,'cams'=4] {'pts','cams'}, dimensions={0} | all-to-all | bytes 98304 | tf_op jit(solution)/shard_map/all_to_all | solution.py:499
  84.7 0.1 tail.1.refs_0_
  84.8 0.7 collective-permute-start.6
  85.5 3.2 %collective-permute-start.5 = (f32[144,128]{1,0:T(8,128)S(1)}, f32[144,128]{1,0:T(8,128)S(1)}, u32[]{:S(2)}, u32[]{:S(2)}) collective-permute-start(f32[144,128]{1,0:T(8,128)S(1)} %tail.1.refs_0_), channel_id=1, source_target_pairs={{0,24},{4,28},{8,16},{12,20},{16,8},{20,12},{24,0},{28,4},{1,25},{... | collective-permute-start | bytes 221192 | tf_op jit(solution)/shard_map/ppermute | solution.py:559
  88.8 3.8 %collective-permute-start.3 = (f32[144,128]{1,0:T(8,128)S(1)}, f32[144,128]{1,0:T(8,128)S(1)}, u32[]{:S(2)}, u32[]{:S(2)}) collective-permute-start(f32[144,128]{1,0:T(8,128)S(1)} %tail.1.refs_0_), channel_id=1, source_target_pairs={{0,16},{4,20},{8,24},{12,28},{16,0},{20,4},{24,8},{28,12},{1,17},{... | collective-permute-start | bytes 221192 | tf_op jit(solution)/shard_map/ppermute | solution.py:559
  92.6 0.3 collective-permute-done.6.refs_7_
  92.8 1.8 %collective-permute-start.1 = (f32[144,128]{1,0:T(8,128)S(1)}, f32[144,128]{1,0:T(8,128)S(1)}, u32[]{:S(2)}, u32[]{:S(2)}) collective-permute-start(f32[144,128]{1,0:T(8,128)S(1)} %tail.1.refs_0_), channel_id=1, source_target_pairs={{0,8},{4,12},{8,0},{12,4},{16,24},{20,28},{24,16},{28,20},{1,9},{5... | collective-permute-start | bytes 221192 | tf_op jit(solution)/shard_map/ppermute | solution.py:559
  94.6 3.6 %collective-permute-start = (f32[144,128]{1,0:T(8,128)S(1)}, f32[144,128]{1,0:T(8,128)S(1)}, u32[]{:S(2)}, u32[]{:S(2)}) collective-permute-start(f32[144,128]{1,0:T(8,128)S(1)} %tail.1.refs_0_), channel_id=1, source_target_pairs={{0,4},{4,0},{8,12},{12,8},{16,20},{20,16},{24,28},{28,24},{1,5},{5... | collective-permute-start | bytes 221192 | tf_op jit(solution)/shard_map/ppermute | solution.py:559
  98.2 3.9 %schur_last.1 = (f32[32,128]{1,0:T(8,128)}, f32[8,128]{1,0:T(8,128)S(1)}, f32[9,8,128]{2,1,0:T(8,128)}, f32[9,8,128]{2,1,0:T(8,128)}, f32[3,32,128]{2,1,0:T(8,128)S(1)}, /*index=5*/f32[3,32,128]{2,1,0:T(8,128)S(1)}) custom-call(f32[96,128]{1,0:T(8,128)S(1)} %bitcast.25, f32[576,128]{1,0:T(8,128)S(1)} %get-tuple-element.36.a_ref, ...), custom_call_target="tpu_custom_call" | custom-call | flops 2000000000 | bytes 10000000 | tf_op jit(solution)/shard_map/schur_last/pallas_call | solution.py:476
  102.1 2.6 %all-to-all-start.6 = ((f32[32,1,128]{2,1,0:T(1,128)}), f32[32,1,128]{2,1,0:T(1,128)S(1)}, u32[]{:S(2)}, u32[]{:S(2)}) async-start(f32[32,1,128]{2,1,0:T(1,128)} %bitcast.18), calls=%async_computation.6 | async-start | bytes 32768 | tf_op jit(solution)/shard_map/all_to_all | solution.py:499
  104.7 7.1 %all-to-all-done.6 = f32[32,1,128]{2,1,0:T(1,128)S(1)} async-done(((f32[32,1,128]{2,1,0:T(1,128)}), f32[32,1,128]{2,1,0:T(1,128)S(1)}, u32[]{:S(2)}, u32[]{:S(2)}) %all-to-all-start.6) | async-done | bytes 16416 | tf_op jit(solution)/shard_map/all_to_all | solution.py:499
  111.8 1.1 final.1
  (12 shorter events, 0.0 us)
Async XLA Ops:
  11.6 15.1 %all-to-all-start = ((f32[32,1,768]{2,1,0:T(1,128)}), f32[32,1,768]{2,1,0:T(1,128)S(1)}, u32[]{:S(2)}, u32[]{:S(2)}) async-start(f32[32,1,768]{2,1,0:T(1,128)} %bitcast.5), calls=%async_computation | async-start | bytes 196608 | tf_op jit(solution)/shard_map/all_to_all | solution.py:499
  27.5 9.1 %copy-start = (s32[4096]{0:T(1024)S(1)}, s32[4096]{0:T(1024)}, u32[]{:S(2)}) copy-start(s32[4096]{0:T(1024)} %param.9) | copy-start | bytes 49156
  27.5 9.0 %copy-start.1 = (s32[4096]{0:T(1024)S(1)}, s32[4096]{0:T(1024)}, u32[]{:S(2)}) copy-start(s32[4096]{0:T(1024)} %param.10) | copy-start | bytes 49156
  84.8 8.0 %collective-permute-start.6 = (f32[144,128]{1,0:T(8,128)S(1)}, f32[144,128]{1,0:T(8,128)S(1)}, u32[]{:S(2)}, u32[]{:S(2)}) collective-permute-start(f32[144,128]{1,0:T(8,128)S(1)} %tail.1.refs_0_), channel_id=1, source_target_pairs={{0,28},{4,24},{8,20},{12,16},{16,12},{20,8},{24,4},{28,0},{1,29},{... | collective-permute-start | bytes 221192 | tf_op jit(solution)/shard_map/ppermute | solution.py:559
  85.5 9.1 %collective-permute-start.5 = (f32[144,128]{1,0:T(8,128)S(1)}, f32[144,128]{1,0:T(8,128)S(1)}, u32[]{:S(2)}, u32[]{:S(2)}) collective-permute-start(f32[144,128]{1,0:T(8,128)S(1)} %tail.1.refs_0_), channel_id=1, source_target_pairs={{0,24},{4,28},{8,16},{12,20},{16,8},{20,12},{24,0},{28,4},{1,25},{... | collective-permute-start | bytes 221192 | tf_op jit(solution)/shard_map/ppermute | solution.py:559
  88.8 23.0 %collective-permute-start.4 = (f32[144,128]{1,0:T(8,128)S(1)}, f32[144,128]{1,0:T(8,128)S(1)}, u32[]{:S(2)}, u32[]{:S(2)}) collective-permute-start(f32[144,128]{1,0:T(8,128)S(1)} %tail.1.refs_0_), channel_id=1, source_target_pairs={{0,20},{4,16},{8,28},{12,24},{16,4},{20,0},{24,12},{28,8},{1,21},{... | collective-permute-start | bytes 221192 | tf_op jit(solution)/shard_map/ppermute | solution.py:559
  88.8 23.0 %collective-permute-start.3 = (f32[144,128]{1,0:T(8,128)S(1)}, f32[144,128]{1,0:T(8,128)S(1)}, u32[]{:S(2)}, u32[]{:S(2)}) collective-permute-start(f32[144,128]{1,0:T(8,128)S(1)} %tail.1.refs_0_), channel_id=1, source_target_pairs={{0,16},{4,20},{8,24},{12,28},{16,0},{20,4},{24,8},{28,12},{1,17},{... | collective-permute-start | bytes 221192 | tf_op jit(solution)/shard_map/ppermute | solution.py:559
  92.6 19.2 %collective-permute-start.2 = (f32[144,128]{1,0:T(8,128)S(1)}, f32[144,128]{1,0:T(8,128)S(1)}, u32[]{:S(2)}, u32[]{:S(2)}) collective-permute-start(f32[144,128]{1,0:T(8,128)S(1)} %tail.1.refs_0_), channel_id=1, source_target_pairs={{0,12},{4,8},{8,4},{12,0},{16,28},{20,24},{24,20},{28,16},{1,13},{... | collective-permute-start | bytes 221192 | tf_op jit(solution)/shard_map/ppermute | solution.py:559
  92.8 19.0 %collective-permute-start.1 = (f32[144,128]{1,0:T(8,128)S(1)}, f32[144,128]{1,0:T(8,128)S(1)}, u32[]{:S(2)}, u32[]{:S(2)}) collective-permute-start(f32[144,128]{1,0:T(8,128)S(1)} %tail.1.refs_0_), channel_id=1, source_target_pairs={{0,8},{4,12},{8,0},{12,4},{16,24},{20,28},{24,16},{28,20},{1,9},{5... | collective-permute-start | bytes 221192 | tf_op jit(solution)/shard_map/ppermute | solution.py:559
  94.6 17.2 %collective-permute-start = (f32[144,128]{1,0:T(8,128)S(1)}, f32[144,128]{1,0:T(8,128)S(1)}, u32[]{:S(2)}, u32[]{:S(2)}) collective-permute-start(f32[144,128]{1,0:T(8,128)S(1)} %tail.1.refs_0_), channel_id=1, source_target_pairs={{0,4},{4,0},{8,12},{12,8},{16,20},{20,16},{24,28},{28,24},{1,5},{5... | collective-permute-start | bytes 221192 | tf_op jit(solution)/shard_map/ppermute | solution.py:559
  102.1 9.7 %all-to-all-start.6 = ((f32[32,1,128]{2,1,0:T(1,128)}), f32[32,1,128]{2,1,0:T(1,128)S(1)}, u32[]{:S(2)}, u32[]{:S(2)}) async-start(f32[32,1,128]{2,1,0:T(1,128)} %bitcast.18), calls=%async_computation.6 | async-start | bytes 32768 | tf_op jit(solution)/shard_map/all_to_all | solution.py:499

commit v4 on v3

--- a/solution.py
+++ b/solution.py
@@ -17,6 +17,7 @@
 PT_HI = PT_DEV // PT_LO
 PT_ROWS = PT_DEV // LANES
 PIECES = 3
+NEAR = 2
 VMEM_LIMIT = 40 * 1024 * 1024
 
 damping_camera = 1.0
@@ -323,11 +324,12 @@
     send_owned(scaled, dot_fields(remainder, scaled), entry, out_ref, table_ref, sizes)
 
 
-def owner_kernel(sizes, start, in_ref, entry_ref, pre_ref, rem_ref, dir_ref, product_ref, *refs):
-    if start:
-        out_ref, new_rem_ref, new_sol_ref, step_ref, table_ref, spread_ref, place_ref = refs
-    else:
-        sol_ref, out_ref, new_rem_ref, new_sol_ref, step_ref, table_ref, spread_ref, place_ref = refs
+def owner_kernel(sizes, start, final, in_ref, entry_ref, pre_ref, rem_ref, dir_ref, product_ref, *refs):
+    refs = list(refs)
+    sol_ref = None if start else refs.pop(0)
+    out_ref, new_rem_ref, new_sol_ref, step_ref = refs[:4]
+    fields_ref = refs[4] if final else None
+    table_ref, spread_ref, place_ref = refs[-3:]
     entry = entry_ref[...]
     fields = read_messages(in_ref, CP, sizes.message, sizes)
     curvature = read_scalar(in_ref, sizes.groups, sizes.message, sizes)
@@ -338,11 +340,16 @@
     for k in range(CP):
         direction = dir_ref[k]
         moved = step[:1] * direction
-        new_sol_ref[k] = moved if start else sol_ref[k] + moved
+        moved = moved if start else sol_ref[k] + moved
+        new_sol_ref[k] = moved
         value = rem_ref[k] - step[:1] * (sums[k] + damping_camera * direction)
         new_rem_ref[k] = value
         remainder.append(value)
         scaled.append(pre_ref[k] * value)
+        if final:
+            for j, field in enumerate((moved, direction, scaled[k])):
+                first = (j * CP + k) * sizes.own_rows
+                fields_ref[first : first + sizes.own_rows, :] = field
     send_owned(scaled, dot_fields(remainder, scaled), entry, out_ref, table_ref, sizes)
 
 
@@ -429,32 +436,32 @@
     write_messages(fields, partial, sizes.groups, sizes.message, out_ref, sizes)
 
 
-def tail_kernel(sizes, in_ref, pre_ref, rem_ref, dir_ref, product_ref, sol_ref, out_ref):
+def tail_kernel(sizes, in_ref, product_ref, own_ref, other_ref, out_ref):
     renewed = jnp.broadcast_to(read_scalar(in_ref, sizes.groups, sizes.message, sizes), (SUB, LANES))
     beta = (renewed / product_ref[...])[:1]
-    for k in range(CP):
-        direction = pre_ref[k] * rem_ref[k] + beta * dir_ref[k]
-        first = k * sizes.own_rows
-        out_ref[first : first + sizes.own_rows, :] = sol_ref[k]
-        first += CP * sizes.own_rows
-        out_ref[first : first + sizes.own_rows, :] = direction
-
-
-def final_kernel(sizes, run_ref, in_ref, product_ref, inv_ref, grad_ref, sum_ref, *refs):
-    all_refs = refs[: sizes.pts]
-    cam_ref, pt_ref, table_ref = refs[sizes.pts :]
+    field = CP * sizes.own_rows
+    for j, ref in enumerate((own_ref, other_ref)):
+        first = j * 2 * field
+        out_ref[first : first + field, :] = ref[:field, :]
+        out_ref[first + field : first + 2 * field, :] = ref[2 * field :, :] + beta * ref[field : 2 * field, :]
+
+
+def final_kernel(sizes, masks, run_ref, in_ref, product_ref, inv_ref, grad_ref, sum_ref, *refs):
+    all_refs = refs[: len(masks)]
+    cam_ref, pt_ref, table_ref = refs[len(masks) :]
     curvature = jnp.sum(jnp.where(lane_iota(sizes.devices) == 0, in_ref[...], 0.0), keepdims=True)
     step = (product_ref[...] / jnp.broadcast_to(curvature, (SUB, LANES)))[:1]
-    for k, all_ref in enumerate(all_refs):
-        base_column = (run_ref[0] ^ k) * sizes.run
-        for h in range(sizes.run_rows):
-            columns = pl.ds(pl.multiple_of(base_column + h * LANES, LANES), LANES)
-            for start in range(0, CP, SUB):
-                size = min(SUB, CP - start)
-                first = start * sizes.own_rows + h
-                base = all_ref[pl.ds(first, size, stride=sizes.own_rows), :]
-                direction = all_ref[pl.ds(first + CP * sizes.own_rows, size, stride=sizes.own_rows), :]
-                cam_ref[start : start + size, columns] = base + step * direction
+    for all_ref, pair in zip(all_refs, masks):
+        for j, mask in enumerate(pair):
+            base_column = (run_ref[0] ^ mask) * sizes.run
+            for h in range(sizes.run_rows):
+                columns = pl.ds(pl.multiple_of(base_column + h * LANES, LANES), LANES)
+                for start in range(0, CP, SUB):
+                    size = min(SUB, CP - start)
+                    first = (j * 2 * CP + start) * sizes.own_rows + h
+                    base = all_ref[pl.ds(first, size, stride=sizes.own_rows), :]
+                    direction = all_ref[pl.ds(first + CP * sizes.own_rows, size, stride=sizes.own_rows), :]
+                    cam_ref[start : start + size, columns] = base + step * direction
     total = [grad_ref[k] + step * sum_ref[k] for k in range(3)]
     solved = solve([inv_ref[k] for k in range(6)], total)
     for k in range(3):
@@ -497,6 +504,9 @@
         width = messages.size // sizes.devices
         flat = messages.reshape(sizes.devices, 1, width)
         return lax.all_to_all(flat, axes, split_axis=0, concat_axis=0, tiled=True).reshape(messages.shape)
+
+    def flipped(value, flip):
+        return lax.ppermute(value, "pts", [(p, p ^ flip) for p in range(sizes.pts)])
 
     def factors(high_rows, low_rows, entries):
         return [pltpu.VMEM((high_rows, entries), bf16), pltpu.VMEM((low_rows, entries), bf16)]
@@ -546,18 +556,20 @@
     for iteration in range(ITERS):
         start, last = iteration == 0, iteration == ITERS - 1
         earlier = [] if start else [product, slots, direction, step, sums]
+        if last:
+            neighbour = flipped(fields, NEAR)
         arrived = exchange(out)
         if last:
             (both,) = call(
                 functools.partial(tail_kernel, sizes),
                 "tail",
-                [arrived, precondition, remainder, direction, product, solution_],
-                [shape(2 * CP * sizes.own_rows, LANES)],
+                [arrived, product, fields, neighbour],
+                [shape(4 * CP * sizes.own_rows, LANES)],
                 [],
             )
-            gathered = [both] + [
-                lax.ppermute(both, "pts", [(p, p ^ k) for p in range(sizes.pts)]) for k in range(1, sizes.pts)
-            ]
+            flips = [1 << bit for bit in range(sizes.pts.bit_length() - 1) if 1 << bit != NEAR]
+            flips = flips[1:] + flips[:1]
+            early = {flip: flipped(both, flip) for flip in (flips[0], flips[-1])}
         results = call(
             functools.partial(schur_kernel, sizes, start, last),
             "schur_last" if last else "schur",
@@ -571,16 +583,23 @@
         if not start:
             gradient = results[5]
         if last:
+            early[flips[0]], out = lax.optimization_barrier((early[flips[0]], out))
+            gathered, masks = [both], [(0, NEAR)]
+            for flip in flips:
+                gathered += [early[flip] if value is both and flip in early else flipped(value, flip) for value in gathered]
+                masks += [tuple(mask ^ flip for mask in pair) for pair in masks]
             break
-        out, remainder, solution_, step = call(
-            functools.partial(owner_kernel, sizes, start),
-            "owner",
+        final = iteration == ITERS - 2
+        out, remainder, solution_, step, *rest = call(
+            functools.partial(owner_kernel, sizes, start, final),
+            "owner_final" if final else "owner",
             [exchange(out), entry, precondition, remainder, direction, product] + ([] if start else [solution_]),
-            [messages, owned, owned, scalar],
+            [messages, owned, owned, scalar] + ([shape(3 * CP * sizes.own_rows, LANES)] if final else []),
             [owned_scratch] + factors(spread_rows(CP * PIECES, sizes.own_rows), LANES, entries),
         )
+        fields = rest[0] if final else None
     return call(
-        functools.partial(final_kernel, sizes),
+        functools.partial(final_kernel, sizes, masks),
         "final",
         [exchange(out), product, inverse, gradient, sums] + gathered,
         [shape(CP, CAM_OWN), shape(3, PT_DEV)],

time: 113 us -> 107 us (0.947)
  starting transfers between devices: 23 us -> 12.7 us
  waiting for transfers between devices: 15.2 us -> 19.3 us
    ppermute x7 -> x4, starting transfers between devices: 13.1 us -> 2.93 us  [flipped(): return lax.ppermute(value, 'pts', [(p, p ^ flip) for p in range(sizes.pts)])]
    ppermute x7 -> x4, waiting for transfers between devices: 0.28 us -> 4.35 us  [flipped(): return lax.ppermute(value, 'pts', [(p, p ^ flip) for p in range(sizes.pts)])]
  transfers between devices with their start and end apart: 9 -> 6, of which waited for: 3 -> 3; matrix products, arithmetic and copies ran while one was open for 0% -> 0% of each run, Pallas kernels for 3% -> 4%
where the time goes in v4:
time: 107 us
  blocking collectives  45.1 us (42%)
  Pallas kernels  29.2 us (27%)
  waiting for transfers between devices  19.3 us (18%)
  starting transfers between devices  12.7 us (12%)
    all_to_all x5, blocking collectives, exchange(): lax.all_to_all(flat, axes, split_axis=0, concat_axis=0, tiled=True)  45.1 us
    pallas_call x9, Pallas kernels, call(): pl.pallas_call(kernel, name=name, out_shape=outputs, in_specs=[smem] * le...  29.2 us
    all_to_all x2, waiting for transfers between devices, exchange(): lax.all_to_all(flat, axes, split_axis=0, concat_axis=0, tiled=True)  14.9 us
    all_to_all x2, starting transfers between devices, exchange(): lax.all_to_all(flat, axes, split_axis=0, concat_axis=0, tiled=True)  9.81 us
    ppermute x4, waiting for transfers between devices, flipped(): return lax.ppermute(value, 'pts', [(p, p ^ flip) for p in range(sizes.pts)])  4.35 us
    ppermute x4, starting transfers between devices, flipped(): return lax.ppermute(value, 'pts', [(p, p ^ flip) for p in range(sizes.pts)])  2.93 us
  transfers between devices with their start and end apart: 6, of which 3 were waited for; matrix products, arithmetic and copies ran while one was open for 0% of the time, Pallas kernels for 4%

profile of v4, /device:TPU:0, one launch (start us, length us, event | category | flops | bytes accessed | tf_op | source)
XLA Modules:
  0.0 107.1 jit_solution(18069770942575341248)
XLA Ops:
  0.6 10.9 %setup.1 = (f32[192,128]{1,0:T(8,128)}, f32[576,128]{1,0:T(8,128)S(1)}, f32[192,128]{1,0:T(8,128)S(1)}, f32[6,32,128]{2,1,0:T(8,128)S(1)}, f32[3,32,128]{2,1,0:T(8,128)S(1)}) custom-call(f32[18,4096]{1,0:T(8,128)} %refs_0_.1, f32[6,4096]{1,0:T(8,128)} %refs_1_.1, f32[2,4096]{1,0:T(2,128)} %refs_2_.1, s32[32,128]{1,0:T(8,128)} %bitcast.34, ...), custom_call_target="tpu_custom_call" | custom-call | tf_op jit(solution)/shard_map/setup/pallas_call | solution.py:483
  11.5 7.3 %all-to-all-start = ((f32[32,1,768]{2,1,0:T(1,128)}), f32[32,1,768]{2,1,0:T(1,128)S(1)}, u32[]{:S(2)}, u32[]{:S(2)}) async-start(f32[32,1,768]{2,1,0:T(1,128)} %bitcast.5), calls=%async_computation | async-start | bytes 196608 | tf_op jit(solution)/shard_map/all_to_all | solution.py:506
  18.8 7.8 %all-to-all-done = f32[32,1,768]{2,1,0:T(1,128)S(1)} async-done(((f32[32,1,768]{2,1,0:T(1,128)}), f32[32,1,768]{2,1,0:T(1,128)S(1)}, u32[]{:S(2)}, u32[]{:S(2)}) %all-to-all-start) | async-done | bytes 98336 | tf_op jit(solution)/shard_map/all_to_all | solution.py:506
  26.7 0.8 first_owner.1
  27.5 0.0 copy-start.1
  27.5 9.0 %all_to_all.35 = f32[32,1,384]{2,1,0:T(1,128)S(1)} all-to-all(f32[32,1,384]{2,1,0:T(1,128)S(1)} %bitcast.31), channel_id=1, replica_groups=mesh['pts'=8,'cams'=4] {'pts','cams'}, dimensions={0} | all-to-all | bytes 98304 | tf_op jit(solution)/shard_map/all_to_all | solution.py:506
  36.5 5.4 %schur.2 = (f32[96,128]{1,0:T(8,128)S(1)}, f32[8,128]{1,0:T(8,128)S(1)}, f32[9,8,128]{2,1,0:T(8,128)S(1)}, f32[9,8,128]{2,1,0:T(8,128)S(1)}, f32[3,32,128]{2,1,0:T(8,128)S(1)}) custom-call(f32[96,128]{1,0:T(8,128)S(1)} %bitcast.30, f32[576,128]{1,0:T(8,128)S(1)} %get-tuple-element.38.a_ref, f32[192,128]{1,0:T(8,128)S(1)} %get-tuple-element.39.b_ref, ...), custom_call_target="tpu_custom_call" | custom-call | flops 2000000000 | bytes 10000000 | tf_op jit(solution)/shard_map/schur/pallas_call | solution.py:483
  41.9 9.0 %all_to_all.36 = f32[32,1,384]{2,1,0:T(1,128)S(1)} all-to-all(f32[32,1,384]{2,1,0:T(1,128)S(1)} %bitcast.32), channel_id=1, replica_groups=mesh['pts'=8,'cams'=4] {'pts','cams'}, dimensions={0} | all-to-all | bytes 98304 | tf_op jit(solution)/shard_map/all_to_all | solution.py:506
  50.9 0.6 owner.1
  51.5 9.0 %all_to_all.37 = f32[32,1,384]{2,1,0:T(1,128)S(1)} all-to-all(f32[32,1,384]{2,1,0:T(1,128)S(1)} %bitcast.33), channel_id=1, replica_groups=mesh['pts'=8,'cams'=4] {'pts','cams'}, dimensions={0} | all-to-all | bytes 98304 | tf_op jit(solution)/shard_map/all_to_all | solution.py:506
  60.6 5.4 %schur.3 = (f32[96,128]{1,0:T(8,128)S(1)}, f32[8,128]{1,0:T(8,128)S(1)}, f32[9,8,128]{2,1,0:T(8,128)S(1)}, f32[9,8,128]{2,1,0:T(8,128)S(1)}, f32[3,32,128]{2,1,0:T(8,128)S(1)}, /*index=5*/f32[3,32,128]{2,1,0:T(8,128)S(1)}) custom-call(f32[96,128]{1,0:T(8,128)S(1)} %bitcast.27, f32[576,128]{1,0:T(8,128)S(1)} %get-tuple-element.38.a_ref, ...), custom_call_target="tpu_custom_call" | custom-call | flops 2000000000 | bytes 10000000 | tf_op jit(solution)/shard_map/schur/pallas_call | solution.py:483
  66.0 9.0 %all_to_all.38 = f32[32,1,384]{2,1,0:T(1,128)S(1)} all-to-all(f32[32,1,384]{2,1,0:T(1,128)S(1)} %bitcast.28), channel_id=1, replica_groups=mesh['pts'=8,'cams'=4] {'pts','cams'}, dimensions={0} | all-to-all | bytes 98304 | tf_op jit(solution)/shard_map/all_to_all | solution.py:506
  75.0 1.0 owner_final.1
  76.0 0.6 collective-permute-start
  76.6 9.0 %all_to_all.39 = f32[32,1,384]{2,1,0:T(1,128)S(1)} all-to-all(f32[32,1,384]{2,1,0:T(1,128)S(1)} %bitcast.29), channel_id=1, replica_groups=mesh['pts'=8,'cams'=4] {'pts','cams'}, dimensions={0} | all-to-all | bytes 98304 | tf_op jit(solution)/shard_map/all_to_all | solution.py:506
  85.7 0.1 tail.1.refs_0_
  85.8 0.7 collective-permute-start.1
  86.5 3.8 %schur_last.1 = (f32[32,128]{1,0:T(8,128)}, f32[8,128]{1,0:T(8,128)S(1)}, f32[9,8,128]{2,1,0:T(8,128)}, f32[9,8,128]{2,1,0:T(8,128)}, f32[3,32,128]{2,1,0:T(8,128)S(1)}, /*index=5*/f32[3,32,128]{2,1,0:T(8,128)S(1)}) custom-call(f32[96,128]{1,0:T(8,128)S(1)} %bitcast.23, f32[576,128]{1,0:T(8,128)S(1)} %get-tuple-element.38.a_ref, ...), custom_call_target="tpu_custom_call" | custom-call | flops 2000000000 | bytes 10000000 | tf_op jit(solution)/shard_map/schur_last/pallas_call | solution.py:483
  90.4 0.6 collective-permute-start.2
  91.0 4.3 %collective-permute-done.1.refs_1_ = f32[288,128]{1,0:T(8,128)S(1)} collective-permute-done((f32[288,128]{1,0:T(8,128)S(1)}, f32[288,128]{1,0:T(8,128)S(1)}, u32[]{:S(2)}, u32[]{:S(2)}) %collective-permute-start.1) | collective-permute-done | bytes 147488 | tf_op jit(solution)/shard_map/ppermute | solution.py:509
  95.3 1.0 collective-permute-start.3
  96.3 2.5 %all-to-all-start.6 = ((f32[32,1,128]{2,1,0:T(1,128)}), f32[32,1,128]{2,1,0:T(1,128)S(1)}, u32[]{:S(2)}, u32[]{:S(2)}) async-start(f32[32,1,128]{2,1,0:T(1,128)} %bitcast.18), calls=%async_computation.6 | async-start | bytes 32768 | tf_op jit(solution)/shard_map/all_to_all | solution.py:506
  98.9 7.1 %all-to-all-done.6 = f32[32,1,128]{2,1,0:T(1,128)S(1)} async-done(((f32[32,1,128]{2,1,0:T(1,128)}), f32[32,1,128]{2,1,0:T(1,128)S(1)}, u32[]{:S(2)}, u32[]{:S(2)}) %all-to-all-start.6) | async-done | bytes 16416 | tf_op jit(solution)/shard_map/all_to_all | solution.py:506
  106.0 1.1 %final.1 = (f32[9,8192]{1,0:T(8,128)}, f32[3,4096]{1,0:T(4,128)}) custom-call(s32[1]{0:T(128)} %bitcast.run_ref, f32[32,128]{1,0:T(8,128)S(1)} %bitcast.26, f32[8,128]{1,0:T(8,128)S(1)} %get-tuple-element.66.product_ref, f32[6,32,128]{2,1,0:T(8,128)S(1)} %get-tuple-element.40.inv_ref, f32[3,32,128]{2,1,0:T(8,128)S(1)} %get-tuple-element.67.grad_ref, ...), custom_call_target="tpu_custom_call" | custom-call | tf_op jit(solution)/shard_map/final/pallas_call | solution.py:483
  (6 shorter events, 0.0 us)
Async XLA Ops:
  11.5 15.1 %all-to-all-start = ((f32[32,1,768]{2,1,0:T(1,128)}), f32[32,1,768]{2,1,0:T(1,128)S(1)}, u32[]{:S(2)}, u32[]{:S(2)}) async-start(f32[32,1,768]{2,1,0:T(1,128)} %bitcast.5), calls=%async_computation | async-start | bytes 196608 | tf_op jit(solution)/shard_map/all_to_all | solution.py:506
  27.4 9.1 %copy-start = (s32[4096]{0:T(1024)S(1)}, s32[4096]{0:T(1024)}, u32[]{:S(2)}) copy-start(s32[4096]{0:T(1024)} %param.9) | copy-start | bytes 49156
  27.5 9.0 %copy-start.1 = (s32[4096]{0:T(1024)S(1)}, s32[4096]{0:T(1024)}, u32[]{:S(2)}) copy-start(s32[4096]{0:T(1024)} %param.10) | copy-start | bytes 49156
  76.0 9.6 %collective-permute-start = (f32[216,128]{1,0:T(8,128)S(1)}, f32[216,128]{1,0:T(8,128)S(1)}, u32[]{:S(2)}, u32[]{:S(2)}) collective-permute-start(f32[216,128]{1,0:T(8,128)S(1)} %get-tuple-element.58.own_ref), channel_id=1, source_target_pairs={{0,8},{4,12},{8,0},{12,4},{16,24},{20,28},{24,16},{28,20},{1,9},{5... | collective-permute-start | bytes 331784 | tf_op jit(solution)/shard_map/ppermute | solution.py:509
  85.8 9.5 %collective-permute-start.1 = (f32[288,128]{1,0:T(8,128)S(1)}, f32[288,128]{1,0:T(8,128)S(1)}, u32[]{:S(2)}, u32[]{:S(2)}) collective-permute-start(f32[288,128]{1,0:T(8,128)S(1)} %tail.1.refs_0_), channel_id=1, source_target_pairs={{0,16},{4,20},{8,24},{12,28},{16,0},{20,4},{24,8},{28,12},{1,17},{... | collective-permute-start | bytes 442376 | tf_op jit(solution)/shard_map/ppermute | solution.py:509
  90.4 8.5 %collective-permute-start.2 = (f32[288,128]{1,0:T(8,128)S(1)}, f32[288,128]{1,0:T(8,128)S(1)}, u32[]{:S(2)}, u32[]{:S(2)}) collective-permute-start(f32[288,128]{1,0:T(8,128)S(1)} %tail.1.refs_0_), channel_id=1, source_target_pairs={{0,4},{4,0},{8,12},{12,8},{16,20},{20,16},{24,28},{28,24},{1,5},{5... | collective-permute-start | bytes 442376 | tf_op jit(solution)/shard_map/ppermute | solution.py:509
  95.3 10.7 %collective-permute-start.3 = (f32[288,128]{1,0:T(8,128)S(1)}, f32[288,128]{1,0:T(8,128)S(1)}, u32[]{:S(2)}, u32[]{:S(2)}) collective-permute-start(f32[288,128]{1,0:T(8,128)S(1)} %collective-permute-done.1.refs_1_), channel_id=1, source_target_pairs={{0,4},{4,0},{8,12},{12,8},{16,20},{20,16},{24,28},{28,24},{1,5},{5... | collective-permute-start | bytes 442376 | tf_op jit(solution)/shard_map/ppermute | solution.py:509
  96.3 9.7 %all-to-all-start.6 = ((f32[32,1,128]{2,1,0:T(1,128)}), f32[32,1,128]{2,1,0:T(1,128)S(1)}, u32[]{:S(2)}, u32[]{:S(2)}) async-start(f32[32,1,128]{2,1,0:T(1,128)} %bitcast.18), calls=%async_computation.6 | async-start | bytes 32768 | tf_op jit(solution)/shard_map/all_to_all | solution.py:506

commit v5 on v4

--- a/solution.py
+++ b/solution.py
@@ -16,9 +16,10 @@
 PT_LO = 256
 PT_HI = PT_DEV // PT_LO
 PT_ROWS = PT_DEV // LANES
-PIECES = 3
+PIECES = 2
+FINE = 3
 NEAR = 2
-VMEM_LIMIT = 40 * 1024 * 1024
+VMEM_LIMIT = 24 * 1024 * 1024
 
 damping_camera = 1.0
 damping_point = 1.0
@@ -52,9 +53,9 @@
     return lax.broadcasted_iota(jnp.int32, (rows, LANES), 1)
 
 
-def cut(value):
+def cut(value, pieces=PIECES):
     parts = []
-    for _ in range(PIECES - 1):
+    for _ in range(pieces - 1):
         part = value.astype(bf16).astype(f32)
         parts.append(part)
         value = value - part
@@ -86,7 +87,7 @@
     return result
 
 
-def build(index, parts, high, low, high_count, low_count, spread_ref, place_ref):
+def spread_row(index, parts, high, high_count, spread_ref):
     columns = pl.ds(pl.multiple_of(index * LANES, LANES), LANES)
     mask = jnp.broadcast_to(high, (high_count, LANES)) == sub_iota(high_count)
     together = max(1, 16 // high_count)
@@ -99,8 +100,21 @@
             pieces.append(jnp.zeros((high_count, LANES), f32))
         tile = pieces[0] if together == 1 else jnp.concatenate(pieces, axis=0)
         spread_ref[start * high_count : start * high_count + tile.shape[0], columns] = tile.astype(bf16)
+
+
+def place_row(index, low, low_count, place_ref):
+    columns = pl.ds(pl.multiple_of(index * LANES, LANES), LANES)
     place = jnp.broadcast_to(low, (low_count, LANES)) == sub_iota(low_count)
     place_ref[:low_count, columns] = jnp.where(place, 1.0, 0.0).astype(bf16)
+
+
+def keep_parts(parts, parts_ref):
+    for k, part in enumerate(parts):
+        parts_ref[k * SUB : (k + 1) * SUB, :] = part
+
+
+def part_rows(count, s, parts_ref):
+    return [parts_ref[k * SUB + s : k * SUB + s + 1, :] for k in range(count)]
 
 
 def spread_rows(parts, high_count):
@@ -117,12 +131,17 @@
     )
 
 
-def joined(result, comp, high_count, pieces=PIECES):
-    first = comp * pieces * high_count
-    total = result[first + (pieces - 1) * high_count : first + pieces * high_count]
-    for piece in reversed(range(pieces - 1)):
-        total = total + result[first + piece * high_count : first + (piece + 1) * high_count]
-    return total
+def joined(result, count, high_count, pieces=None):
+    pieces = pieces or [PIECES] * count
+    values, first = [], 0
+    for number in pieces:
+        rows = [result[first + k * high_count : first + (k + 1) * high_count] for k in range(number)]
+        first += number * high_count
+        total = rows[-1]
+        for row in reversed(rows[:-1]):
+            total = total + row
+        values.append(total)
+    return values
 
 
 def point_rows(value):
@@ -130,8 +149,7 @@
 
 
 def point_place(point):
-    high = point >> 8
-    return high + ((point >> 7) & 1) * PT_HI, point & (LANES - 1), high, point & (PT_LO - 1)
+    return (point >> 8) + ((point >> 7) & 1) * PT_HI, point & (LANES - 1)
 
 
 def slot_place(slot, sizes):
@@ -190,12 +208,15 @@
 
 def setup_kernel(sizes, *refs):
     sources, refs = refs[:6], refs[6:]
-    out_ref, a_ref, b_ref, inv_ref, grad_ref = refs[:5]
-    r_ref, table_ref, spread_ref, place_ref = refs[5:9]
-    jac_ref, pjac_ref, res_ref, slot_ref, point_ref, list_ref = refs[9:15]
-    semaphores = refs[15]
+    out_ref, a_ref, b_ref, inv_ref, grad_ref, place_point_ref, place_slot_ref = refs[:7]
+    r_ref, table_ref, parts_ref, spread_ref, place_list_ref = refs[7:12]
+    jac_ref, pjac_ref, res_ref, slot_ref, point_ref, list_ref = refs[12:18]
+    semaphores = refs[18]
     rows = sizes.rows
-    copies = [pltpu.make_async_copy(source, target, semaphores.at[k]) for k, (source, target) in enumerate(zip(sources, refs[9:15]))]
+    copies = [
+        pltpu.make_async_copy(source, target, semaphores.at[k])
+        for k, (source, target) in enumerate(zip(sources, refs[12:18]))
+    ]
     for copy in copies:
         copy.start()
     for copy in copies:
@@ -211,22 +232,25 @@
     def at(ref, comp, group):
         return ref[pl.ds(pl.multiple_of(comp * rows + group * SUB, SUB), SUB), :]
 
+    normal_pieces = [FINE] * 6 + [PIECES] * 3
+
     def first(group, carry):
         b = [at(b_ref, k, group) for k in range(6)]
         r = [at(r_ref, k, group) for k in range(2)]
-        point = point_ref[pl.ds(pl.multiple_of(group * SUB, SUB), SUB), :]
-        _, _, high, low = point_place(point)
         values = [b[i] * b[j] + b[3 + i] * b[3 + j] for i, j in ((0, 0), (0, 1), (0, 2), (1, 1), (1, 2), (2, 2))]
         values += [b[i] * r[0] + b[3 + i] * r[1] for i in range(3)]
-        parts = [part for value in values for part in cut(value)]
+        parts = [part for value, pieces in zip(values, normal_pieces) for part in cut(value, pieces)]
+        keep_parts(parts, parts_ref)
         for s in range(SUB):
-            build(group * SUB + s, [part[s : s + 1] for part in parts], high[s : s + 1], low[s : s + 1],
-                  PT_HI, PT_LO, spread_ref, place_ref)
+            row = group * SUB + s
+            point = point_ref[pl.ds(row, 1), :]
+            spread_row(row, part_rows(len(parts), s, parts_ref), point >> 8, PT_HI, spread_ref)
+            place_row(row, point & (PT_LO - 1), PT_LO, place_point_ref)
         return carry
 
     lax.fori_loop(0, rows // SUB, first, 0)
-    result = scatter(9 * PIECES, sizes.obs, PT_HI, PT_LO, spread_ref, place_ref)
-    normal = [point_rows(joined(result, k, PT_HI)) for k in range(9)]
+    result = scatter(sum(normal_pieces), sizes.obs, PT_HI, PT_LO, spread_ref, place_point_ref)
+    normal = [point_rows(value) for value in joined(result, 9, PT_HI, normal_pieces)]
     top_left = normal[0] + damping_point
     top_mid = normal[1]
     top_right = normal[2]
@@ -253,7 +277,7 @@
 
     def second(group, carry):
         point = point_ref[pl.ds(pl.multiple_of(group * SUB, SUB), SUB), :]
-        high, low, _, _ = point_place(point)
+        high, low = point_place(point)
         at_point = gather_rows(lambda c, k: table_ref[c, k : k + 1, :], PT_ROWS, high, low, 3)
         b = [at(b_ref, k, group) for k in range(6)]
         errors = [at(r_ref, i, group) - sum(b[3 * i + k] * at_point[k] for k in range(3)) for i in range(2)]
@@ -261,15 +285,17 @@
         values = [a[k] * errors[0] + a[CP + k] * errors[1] for k in range(CP)]
         values += [a[k] * a[k] + a[CP + k] * a[CP + k] for k in range(CP)]
         parts = [part for value in values for part in cut(value)]
-        high, low = slot_place(slot_ref[pl.ds(pl.multiple_of(group * SUB, SUB), SUB), :], sizes)
+        keep_parts(parts, parts_ref)
         for s in range(SUB):
-            build(group * SUB + s, [part[s : s + 1] for part in parts], high[s : s + 1], low[s : s + 1],
-                  sizes.pts, LANES, spread_ref, place_ref)
+            row = group * SUB + s
+            high, low = slot_place(slot_ref[pl.ds(row, 1), :], sizes)
+            spread_row(row, part_rows(len(parts), s, parts_ref), high, sizes.pts, spread_ref)
+            place_row(row, low, LANES, place_slot_ref)
         return carry
 
     lax.fori_loop(0, rows // SUB, second, 0)
-    result = scatter(2 * CP * PIECES, sizes.obs, sizes.pts, LANES, spread_ref, place_ref)
-    fields = [joined(result, k, sizes.pts) for k in range(2 * CP)]
+    result = scatter(2 * CP * PIECES, sizes.obs, sizes.pts, LANES, spread_ref, place_slot_ref)
+    fields = joined(result, 2 * CP, sizes.pts)
 
     pieces = sizes.slot // LANES
     lane = lane_iota(1)
@@ -277,9 +303,10 @@
         for half in range(pieces):
             value = list_ref[c : c + 1, half * LANES : (half + 1) * LANES]
             low = c * sizes.block + half * (LANES // sizes.pts) + lane // sizes.pts
-            build(c * pieces + half, [(value >> 8).astype(f32), (value & 255).astype(f32)], lane % sizes.pts, low,
-                  sizes.pts, LANES, spread_ref, place_ref)
-    result = scatter(2, sizes.cams * sizes.slot, sizes.pts, LANES, spread_ref, place_ref)
+            parts = [(value >> 8).astype(f32), (value & 255).astype(f32)]
+            spread_row(c * pieces + half, parts, lane % sizes.pts, sizes.pts, spread_ref)
+            place_row(c * pieces + half, low, LANES, place_list_ref)
+    result = scatter(2, sizes.cams * sizes.slot, sizes.pts, LANES, spread_ref, place_list_ref)
     listed = result[: sizes.pts] * 256.0 + result[sizes.pts : 2 * sizes.pts]
     write_messages(fields, None, sizes.first_groups, sizes.first_message, out_ref, sizes, extra=listed)
 
@@ -288,10 +315,10 @@
     high, low = entry // LANES, entry % LANES
     parts = [part for value in fields for part in cut(value)]
     for p in range(sizes.pts):
-        build(p, [part[p : p + 1] for part in parts], high[p : p + 1], low[p : p + 1],
-              sizes.own_rows, LANES, spread_ref, place_ref)
+        spread_row(p, [part[p : p + 1] for part in parts], high[p : p + 1], sizes.own_rows, spread_ref)
+        place_row(p, low[p : p + 1], LANES, place_ref)
     result = scatter(len(parts), sizes.pts * LANES, sizes.own_rows, LANES, spread_ref, place_ref)
-    return [joined(result, k, sizes.own_rows) for k in range(len(fields))]
+    return joined(result, len(fields), sizes.own_rows)
 
 
 def send_owned(scaled, partial, entry, out_ref, table_ref, sizes):
@@ -353,7 +380,8 @@
     send_owned(scaled, dot_fields(remainder, scaled), entry, out_ref, table_ref, sizes)
 
 
-def schur_kernel(sizes, start, last, in_ref, a_ref, b_ref, inv_ref, slot_ref, point_ref, pre_ref, rem_ref, grad_ref, *refs):
+def schur_kernel(sizes, start, last, in_ref, a_ref, b_ref, inv_ref, slot_ref, point_ref,
+                 place_point_ref, place_slot_ref, pre_ref, rem_ref, grad_ref, *refs):
     refs = list(refs)
     if not start:
         product_ref, at_slot_ref, dir_ref, step_ref, sum_ref = refs[:5]
@@ -363,7 +391,7 @@
     refs = refs[5:]
     if not start:
         new_grad_ref = refs.pop(0)
-    q_ref, table_ref, spread_ref, place_ref = refs
+    q_ref, table_ref, parts_ref, spread_ref = refs
     rows = sizes.rows
 
     def at(ref, comp, group):
@@ -395,15 +423,15 @@
             q_ref[pl.ds(pl.multiple_of(i * rows + group * SUB, SUB), SUB), :] = q[i]
         values = [at(b_ref, k, group) * q[0] + at(b_ref, 3 + k, group) * q[1] for k in range(3)]
         parts = [part for value in values for part in cut(value)]
-        _, _, high, low = point_place(index(point_ref, group))
+        keep_parts(parts, parts_ref)
         for s in range(SUB):
-            build(group * SUB + s, [part[s : s + 1] for part in parts], high[s : s + 1], low[s : s + 1],
-                  PT_HI, PT_LO, spread_ref, place_ref)
+            row = group * SUB + s
+            spread_row(row, part_rows(len(parts), s, parts_ref), point_ref[pl.ds(row, 1), :] >> 8, PT_HI, spread_ref)
         return carry
 
     lax.fori_loop(0, rows // SUB, first, 0)
-    result = scatter(3 * PIECES, sizes.obs, PT_HI, PT_LO, spread_ref, place_ref)
-    sums = [point_rows(joined(result, k, PT_HI)) for k in range(3)]
+    result = scatter(3 * PIECES, sizes.obs, PT_HI, PT_LO, spread_ref, place_point_ref)
+    sums = [point_rows(value) for value in joined(result, 3, PT_HI)]
     folded = solve([inv_ref[k] for k in range(6)], sums)
     for k in range(3):
         table_ref[k] = folded[k]
@@ -412,7 +440,7 @@
             new_grad_ref[k] = grad_ref[k] + step_ref[:1, :] * sum_ref[k]
 
     def second(group, inner):
-        high, low, _, _ = point_place(index(point_ref, group))
+        high, low = point_place(index(point_ref, group))
         at_point = gather_rows(lambda c, k: table_ref[c, k : k + 1, :], PT_ROWS, high, low, 3)
         q = [at(q_ref, i, group) for i in range(2)]
         errors = [q[i] - sum(at(b_ref, 3 * i + k, group) * at_point[k] for k in range(3)) for i in range(2)]
@@ -420,10 +448,11 @@
         if not last:
             values = [at(a_ref, k, group) * errors[0] + at(a_ref, CP + k, group) * errors[1] for k in range(CP)]
             parts = [part for value in values for part in cut(value)]
-            high, low = slot_place(index(slot_ref, group), sizes)
+            keep_parts(parts, parts_ref)
             for s in range(SUB):
-                build(group * SUB + s, [part[s : s + 1] for part in parts], high[s : s + 1], low[s : s + 1],
-                      sizes.pts, LANES, spread_ref, place_ref)
+                row = group * SUB + s
+                high, _ = slot_place(slot_ref[pl.ds(row, 1), :], sizes)
+                spread_row(row, part_rows(len(parts), s, parts_ref), high, sizes.pts, spread_ref)
         return inner
 
     inner = lax.fori_loop(0, rows // SUB, second, jnp.zeros((SUB, LANES), f32))
@@ -431,8 +460,8 @@
     if last:
         out_ref[...] = jnp.broadcast_to(partial, (sizes.devices, LANES))
         return
-    result = scatter(CP * PIECES, sizes.obs, sizes.pts, LANES, spread_ref, place_ref)
-    fields = [joined(result, k, sizes.pts) for k in range(CP)]
+    result = scatter(CP * PIECES, sizes.obs, sizes.pts, LANES, spread_ref, place_slot_ref)
+    fields = joined(result, CP, sizes.pts)
     write_messages(fields, partial, sizes.groups, sizes.message, out_ref, sizes)
 
 
@@ -519,11 +548,15 @@
     point_scratch = pltpu.VMEM((3, PT_ROWS, LANES), f32)
     entries = sizes.pts * LANES
 
+    def parts_scratch(count):
+        return pltpu.VMEM((count * SUB, LANES), f32)
+
+
     given = [
         pltpu.with_memory_space_constraint(value, pltpu.HBM)
         for value in (camera_jacobian, point_jacobian, residual, slot, point, send_list[0])
     ]
-    first, a, b, inverse, gradient = call(
+    first, a, b, inverse, gradient, place_point, place_slot = call(
         functools.partial(setup_kernel, sizes),
         "setup",
         given,
@@ -533,9 +566,12 @@
             shape(6 * rows, LANES),
             shape(6, PT_ROWS, LANES),
             point_table,
+            shape(PT_LO, sizes.obs, dtype=bf16),
+            shape(LANES, sizes.obs, dtype=bf16),
         ],
-        [pltpu.VMEM((2 * rows, LANES), f32), point_scratch]
-        + factors(max(spread_rows(9 * PIECES, PT_HI), spread_rows(2 * CP * PIECES, sizes.pts)), PT_LO, sizes.obs)
+        [pltpu.VMEM((2 * rows, LANES), f32), point_scratch, parts_scratch(2 * CP * PIECES)]
+        + [pltpu.VMEM((max(spread_rows(6 * FINE + 3 * PIECES, PT_HI), spread_rows(2 * CP * PIECES, sizes.pts)), sizes.obs), bf16)]
+        + [pltpu.VMEM((LANES, sizes.cams * sizes.slot), bf16)]
         + [pltpu.VMEM(value.shape, value.dtype) for value in given]
         + [pltpu.SemaphoreType.DMA((len(given),))],
         inputs_at=pl.ANY,
@@ -548,9 +584,8 @@
         [owned_scratch] + factors(spread_rows(2 * CP * PIECES, sizes.own_rows), LANES, entries),
         scalars=[column],
     )
-    schur_scratch = [pltpu.VMEM((2 * rows, LANES), f32), point_scratch] + factors(
-        max(spread_rows(3 * PIECES, PT_HI), spread_rows(CP * PIECES, sizes.pts)), PT_LO, sizes.obs
-    )
+    schur_scratch = [pltpu.VMEM((2 * rows, LANES), f32), point_scratch, parts_scratch(CP * PIECES)]
+    schur_scratch += [pltpu.VMEM((max(spread_rows(3 * PIECES, PT_HI), spread_rows(CP * PIECES, sizes.pts)), sizes.obs), bf16)]
     at_slot = shape(CP, sizes.pts, LANES)
     product = slots = direction = step = sums = solution_ = None
     for iteration in range(ITERS):
@@ -573,7 +608,8 @@
         results = call(
             functools.partial(schur_kernel, sizes, start, last),
             "schur_last" if last else "schur",
-            [arrived, a, b, inverse, slot, point, precondition, remainder, gradient] + earlier,
+            [arrived, a, b, inverse, slot, point, place_point, place_slot, precondition, remainder, gradient]
+            + earlier,
             [shape(sizes.devices, LANES) if last else messages, scalar, at_slot, owned, point_table]
             + ([] if start else [point_table]),
             schur_scratch,

time: 107 us -> 106 us (level)
  Pallas kernels: 29.2 us -> 23.8 us
  local copies, waits for them, and re-layouts: 0.01 us -> 3.65 us
    pallas_call x9, Pallas kernels: 29.2 us -> 23.8 us  [call(): pl.pallas_call(kernel, name=name, out_shape=outputs, in_specs=[smem] * le...]
    unnamed x4 -> x12, local copies, waits for them, and re-layouts: 0.01 us -> 3.65 us
  transfers between devices with their start and end apart: 6 -> 6, of which waited for: 3 -> 3; matrix products, arithmetic and copies ran while one was open for 0% -> 0% of each run, Pallas kernels for 4% -> 3%
where the time goes in v5:
time: 106 us
  blocking collectives  45.1 us (43%)
  Pallas kernels  23.8 us (22%)
  waiting for transfers between devices  19.9 us (19%)
  starting transfers between devices  12.7 us (12%)
  local copies, waits for them, and re-layouts  3.65 us (3%)
    all_to_all x5, blocking collectives, exchange(): lax.all_to_all(flat, axes, split_axis=0, concat_axis=0, tiled=True)  45.1 us
    pallas_call x9, Pallas kernels, call(): pl.pallas_call(kernel, name=name, out_shape=outputs, in_specs=[smem] * le...  23.8 us
    all_to_all x2, waiting for transfers between devices, exchange(): lax.all_to_all(flat, axes, split_axis=0, concat_axis=0, tiled=True)  14.9 us
    all_to_all x2, starting transfers between devices, exchange(): lax.all_to_all(flat, axes, split_axis=0, concat_axis=0, tiled=True)  9.79 us
    ppermute x4, waiting for transfers between devices, flipped(): return lax.ppermute(value, 'pts', [(p, p ^ flip) for p in range(sizes.pts)])  4.99 us
    unnamed x12, local copies, waits for them, and re-layouts  3.65 us
    ppermute x4, starting transfers between devices, flipped(): return lax.ppermute(value, 'pts', [(p, p ^ flip) for p in range(sizes.pts)])  2.93 us
  transfers between devices with their start and end apart: 6, of which 3 were waited for; matrix products, arithmetic and copies ran while one was open for 0% of the time, Pallas kernels for 3%

profile of v5, /device:TPU:0, one launch (start us, length us, event | category | flops | bytes accessed | tf_op | source)
XLA Modules:
  0.0 106.0 jit_solution(4922367626231913227)
XLA Ops:
  0.6 9.2 %setup.1 = (f32[192,128]{1,0:T(8,128)}, f32[576,128]{1,0:T(8,128)S(1)}, f32[192,128]{1,0:T(8,128)S(1)}, f32[6,32,128]{2,1,0:T(8,128)S(1)}, f32[3,32,128]{2,1,0:T...) custom-call(f32[18,4096]{1,0:T(8,128)} %refs_0_.1, f32[6,4096]{1,0:T(8,128)} %refs_1_.1, ...), custom_call_target="tpu_custom_call" | custom-call | tf_op jit(solution)/shard_map/setup/pallas_call | solution.py:512
  9.9 1.0 copy-done.4
  10.9 7.3 %all-to-all-start = ((f32[32,1,768]{2,1,0:T(1,128)}), f32[32,1,768]{2,1,0:T(1,128)S(1)}, u32[]{:S(2)}, u32[]{:S(2)}) async-start(f32[32,1,768]{2,1,0:T(1,128)} %bitcast.5), calls=%async_computation | async-start | bytes 196608 | tf_op jit(solution)/shard_map/all_to_all | solution.py:535
  18.2 7.8 %all-to-all-done = f32[32,1,768]{2,1,0:T(1,128)S(1)} async-done(((f32[32,1,768]{2,1,0:T(1,128)}), f32[32,1,768]{2,1,0:T(1,128)S(1)}, u32[]{:S(2)}, u32[]{:S(2)}) %all-to-all-start) | async-done | bytes 98336 | tf_op jit(solution)/shard_map/all_to_all | solution.py:535
  26.0 0.7 first_owner.1
  26.7 9.0 %all_to_all.35 = f32[32,1,384]{2,1,0:T(1,128)S(1)} all-to-all(f32[32,1,384]{2,1,0:T(1,128)S(1)} %bitcast.31), channel_id=1, replica_groups=mesh['pts'=8,'cams'=4] {'pts','cams'}, dimensions={0} | all-to-all | bytes 98304 | tf_op jit(solution)/shard_map/all_to_all | solution.py:535
  35.7 0.7 copy-done
  36.4 0.7 copy-done.2
  37.1 1.2 %copy-done.5 = bf16[128,4096]{1,0:T(8,128)(2,1)S(1)} copy-done((bf16[128,4096]{1,0:T(8,128)(2,1)S(1)}, bf16[128,4096]{1,0:T(8,128)(2,1)}, u32[]{:S(2)}) %copy-start.5) | copy-done | bytes 1048600
  38.4 3.9 %schur.2 = (f32[96,128]{1,0:T(8,128)S(1)}, f32[8,128]{1,0:T(8,128)S(1)}, f32[9,8,128]{2,1,0:T(8,128)S(1)}, f32[9,8,128]{2,1,0:T(8,128)S(1)}, f32[3,32,128]{2,1,0:T(8,128)S(1)}) custom-call(f32[96,128]{1,0:T(8,128)S(1)} %bitcast.30, f32[576,128]{1,0:T(8,128)S(1)} %get-tuple-element.40.a_ref, f32[192,128]{1,0:T(8,128)S(1)} %get-tuple-element.41.b_ref, ...), custom_call_target="tpu_custom_call" | custom-call | flops 2000000000 | bytes 10000000 | tf_op jit(solution)/shard_map/schur/pallas_call | solution.py:512
  42.3 9.0 %all_to_all.36 = f32[32,1,384]{2,1,0:T(1,128)S(1)} all-to-all(f32[32,1,384]{2,1,0:T(1,128)S(1)} %bitcast.32), channel_id=1, replica_groups=mesh['pts'=8,'cams'=4] {'pts','cams'}, dimensions={0} | all-to-all | bytes 98304 | tf_op jit(solution)/shard_map/all_to_all | solution.py:535
  51.9 9.0 %all_to_all.37 = f32[32,1,384]{2,1,0:T(1,128)S(1)} all-to-all(f32[32,1,384]{2,1,0:T(1,128)S(1)} %bitcast.33), channel_id=1, replica_groups=mesh['pts'=8,'cams'=4] {'pts','cams'}, dimensions={0} | all-to-all | bytes 98304 | tf_op jit(solution)/shard_map/all_to_all | solution.py:535
  60.9 4.0 %schur.3 = (f32[96,128]{1,0:T(8,128)S(1)}, f32[8,128]{1,0:T(8,128)S(1)}, f32[9,8,128]{2,1,0:T(8,128)S(1)}, f32[9,8,128]{2,1,0:T(8,128)S(1)}, f32[3,32,128]{2,1,0:T(8,128)S(1)}, /*index=5*/f32[3,32,128]{2,1,0:T(8,128)S(1)}) custom-call(f32[96,128]{1,0:T(8,128)S(1)} %bitcast.27, f32[576,128]{1,0:T(8,128)S(1)} %get-tuple-element.40.a_ref, ...), custom_call_target="tpu_custom_call" | custom-call | flops 2000000000 | bytes 10000000 | tf_op jit(solution)/shard_map/schur/pallas_call | solution.py:512
  64.9 9.0 %all_to_all.38 = f32[32,1,384]{2,1,0:T(1,128)S(1)} all-to-all(f32[32,1,384]{2,1,0:T(1,128)S(1)} %bitcast.28), channel_id=1, replica_groups=mesh['pts'=8,'cams'=4] {'pts','cams'}, dimensions={0} | all-to-all | bytes 98304 | tf_op jit(solution)/shard_map/all_to_all | solution.py:535
  74.0 1.0 owner_final.1
  74.9 0.6 collective-permute-start
  75.5 9.0 %all_to_all.39 = f32[32,1,384]{2,1,0:T(1,128)S(1)} all-to-all(f32[32,1,384]{2,1,0:T(1,128)S(1)} %bitcast.29), channel_id=1, replica_groups=mesh['pts'=8,'cams'=4] {'pts','cams'}, dimensions={0} | all-to-all | bytes 98304 | tf_op jit(solution)/shard_map/all_to_all | solution.py:535
  84.7 0.7 collective-permute-start.1
  85.4 3.2 %schur_last.1 = (f32[32,128]{1,0:T(8,128)}, f32[8,128]{1,0:T(8,128)S(1)}, f32[9,8,128]{2,1,0:T(8,128)}, f32[9,8,128]{2,1,0:T(8,128)}, f32[3,32,128]{2,1,0:T(8,128)S(1)}, /*index=5*/f32[3,32,128]{2,1,0:T(8,128)S(1)}) custom-call(f32[96,128]{1,0:T(8,128)S(1)} %bitcast.23, f32[576,128]{1,0:T(8,128)S(1)} %get-tuple-element.40.a_ref, ...), custom_call_target="tpu_custom_call" | custom-call | flops 2000000000 | bytes 10000000 | tf_op jit(solution)/shard_map/schur_last/pallas_call | solution.py:512
  89.2 5.0 %collective-permute-done.1.refs_1_ = f32[288,128]{1,0:T(8,128)S(1)} collective-permute-done((f32[288,128]{1,0:T(8,128)S(1)}, f32[288,128]{1,0:T(8,128)S(1)}, u32[]{:S(2)}, u32[]{:S(2)}) %collective-permute-start.1) | collective-permute-done | bytes 147488 | tf_op jit(solution)/shard_map/ppermute | solution.py:538
  94.2 1.0 collective-permute-start.3
  95.2 2.5 %all-to-all-start.6 = ((f32[32,1,128]{2,1,0:T(1,128)}), f32[32,1,128]{2,1,0:T(1,128)S(1)}, u32[]{:S(2)}, u32[]{:S(2)}) async-start(f32[32,1,128]{2,1,0:T(1,128)} %bitcast.18), calls=%async_computation.6 | async-start | bytes 32768 | tf_op jit(solution)/shard_map/all_to_all | solution.py:535
  97.8 7.1 %all-to-all-done.6 = f32[32,1,128]{2,1,0:T(1,128)S(1)} async-done(((f32[32,1,128]{2,1,0:T(1,128)}), f32[32,1,128]{2,1,0:T(1,128)S(1)}, u32[]{:S(2)}, u32[]{:S(2)}) %all-to-all-start.6) | async-done | bytes 16416 | tf_op jit(solution)/shard_map/all_to_all | solution.py:535
  104.9 1.1 %final.1 = (f32[9,8192]{1,0:T(8,128)}, f32[3,4096]{1,0:T(4,128)}) custom-call(s32[1]{0:T(128)} %bitcast.run_ref, f32[32,128]{1,0:T(8,128)S(1)} %bitcast.26, f32[8,128]{1,0:T(8,128)S(1)} %get-tuple-element.70.product_ref, f32[6,32,128]{2,1,0:T(8,128)S(1)} %get-tuple-element.42.inv_ref, f32[3,32,128]{2,1,0:T(8,128)S(1)} %get-tuple-element.71.grad_ref, ...), custom_call_target="tpu_custom_call" | custom-call | tf_op jit(solution)/shard_map/final/pallas_call | solution.py:512
  (14 shorter events, 1.3 us)
Async XLA Ops:
  9.9 1.0 copy-start.4
  10.9 15.1 %all-to-all-start = ((f32[32,1,768]{2,1,0:T(1,128)}), f32[32,1,768]{2,1,0:T(1,128)S(1)}, u32[]{:S(2)}, u32[]{:S(2)}) async-start(f32[32,1,768]{2,1,0:T(1,128)} %bitcast.5), calls=%async_computation | async-start | bytes 196608 | tf_op jit(solution)/shard_map/all_to_all | solution.py:535
  35.7 0.7 copy-start
  36.4 0.7 copy-start.2
  37.1 1.2 %copy-start.5 = (bf16[128,4096]{1,0:T(8,128)(2,1)S(1)}, bf16[128,4096]{1,0:T(8,128)(2,1)}, u32[]{:S(2)}) copy-start(bf16[128,4096]{1,0:T(8,128)(2,1)} %copy-done.4) | copy-start | bytes 3145732
  38.4 22.6 %copy-start.1 = (s32[4096]{0:T(1024)S(1)}, s32[4096]{0:T(1024)}, u32[]{:S(2)}) copy-start(s32[4096]{0:T(1024)} %param.9) | copy-start | bytes 49156
  60.9 24.5 %copy-start.3 = (s32[4096]{0:T(1024)S(1)}, s32[4096]{0:T(1024)}, u32[]{:S(2)}) copy-start(s32[4096]{0:T(1024)} %param.10) | copy-start | bytes 49156
  74.9 9.6 %collective-permute-start = (f32[216,128]{1,0:T(8,128)S(1)}, f32[216,128]{1,0:T(8,128)S(1)}, u32[]{:S(2)}, u32[]{:S(2)}) collective-permute-start(f32[216,128]{1,0:T(8,128)S(1)} %get-tuple-element.62.own_ref), channel_id=1, source_target_pairs={{0,8},{4,12},{8,0},{12,4},{16,24},{20,28},{24,16},{28,20},{1,9},{5... | collective-permute-start | bytes 331784 | tf_op jit(solution)/shard_map/ppermute | solution.py:538
  84.7 9.5 %collective-permute-start.1 = (f32[288,128]{1,0:T(8,128)S(1)}, f32[288,128]{1,0:T(8,128)S(1)}, u32[]{:S(2)}, u32[]{:S(2)}) collective-permute-start(f32[288,128]{1,0:T(8,128)S(1)} %tail.1.refs_0_), channel_id=1, source_target_pairs={{0,16},{4,20},{8,24},{12,28},{16,0},{20,4},{24,8},{28,12},{1,17},{... | collective-permute-start | bytes 442376 | tf_op jit(solution)/shard_map/ppermute | solution.py:538
  88.6 9.1 %collective-permute-start.2 = (f32[288,128]{1,0:T(8,128)S(1)}, f32[288,128]{1,0:T(8,128)S(1)}, u32[]{:S(2)}, u32[]{:S(2)}) collective-permute-start(f32[288,128]{1,0:T(8,128)S(1)} %tail.1.refs_0_), channel_id=1, source_target_pairs={{0,4},{4,0},{8,12},{12,8},{16,20},{20,16},{24,28},{28,24},{1,5},{5... | collective-permute-start | bytes 442376 | tf_op jit(solution)/shard_map/ppermute | solution.py:538
  94.2 10.7 %collective-permute-start.3 = (f32[288,128]{1,0:T(8,128)S(1)}, f32[288,128]{1,0:T(8,128)S(1)}, u32[]{:S(2)}, u32[]{:S(2)}) collective-permute-start(f32[288,128]{1,0:T(8,128)S(1)} %collective-permute-done.1.refs_1_), channel_id=1, source_target_pairs={{0,4},{4,0},{8,12},{12,8},{16,20},{20,16},{24,28},{28,24},{1,5},{5... | collective-permute-start | bytes 442376 | tf_op jit(solution)/shard_map/ppermute | solution.py:538
  95.2 9.6 %all-to-all-start.6 = ((f32[32,1,128]{2,1,0:T(1,128)}), f32[32,1,128]{2,1,0:T(1,128)S(1)}, u32[]{:S(2)}, u32[]{:S(2)}) async-start(f32[32,1,128]{2,1,0:T(1,128)} %bitcast.18), calls=%async_computation.6 | async-start | bytes 32768 | tf_op jit(solution)/shard_map/all_to_all | solution.py:535

commit v6 on v5

--- a/solution.py
+++ b/solution.py
@@ -15,7 +15,6 @@
 SUB = 8
 PT_LO = 256
 PT_HI = PT_DEV // PT_LO
-PT_ROWS = PT_DEV // LANES
 PIECES = 2
 FINE = 3
 NEAR = 2
@@ -87,6 +86,26 @@
     return result
 
 
+def matmul_gather(group, tables, place_ref, high_of_row, high_count, picked_ref, found_ref):
+    pieces = [piece for table in tables for piece in cut(table)]
+    left = jnp.concatenate(pieces, axis=0).astype(bf16)
+    rows = len(pieces) * high_count
+    columns = pl.ds(pl.multiple_of(group * SUB * LANES, SUB * LANES), SUB * LANES)
+    picked = jnp.dot(left, place_ref[:, columns], preferred_element_type=f32)
+    for s in range(SUB):
+        mask = jnp.broadcast_to(high_of_row(group * SUB + s), (high_count, LANES)) == sub_iota(high_count)
+        mask = jnp.concatenate([mask.astype(f32)] * len(pieces), axis=0) > 0.5
+        lanes = slice(s * LANES, (s + 1) * LANES)
+        picked_ref[:rows, lanes] = jnp.where(mask, picked[:, lanes], 0.0).astype(bf16)
+    padded = -(-len(tables) // SUB) * SUB
+    owner = lax.broadcasted_iota(jnp.int32, (padded, rows), 1) // (PIECES * high_count)
+    chosen = (owner == lax.broadcasted_iota(jnp.int32, (padded, rows), 0)).astype(f32).astype(bf16)
+    total = jnp.dot(chosen, picked_ref[:rows, :], preferred_element_type=f32)
+    for s in range(SUB):
+        found_ref[s * padded : (s + 1) * padded, :] = total[:, s * LANES : (s + 1) * LANES]
+    return [found_ref[pl.ds(c, SUB, stride=padded), :] for c in range(len(tables))]
+
+
 def spread_row(index, parts, high, high_count, spread_ref):
     columns = pl.ds(pl.multiple_of(index * LANES, LANES), LANES)
     mask = jnp.broadcast_to(high, (high_count, LANES)) == sub_iota(high_count)
@@ -142,14 +161,6 @@
             total = total + row
         values.append(total)
     return values
-
-
-def point_rows(value):
-    return jnp.concatenate([value[:, :LANES], value[:, LANES:]], axis=0)
-
-
-def point_place(point):
-    return (point >> 8) + ((point >> 7) & 1) * PT_HI, point & (LANES - 1)
 
 
 def slot_place(slot, sizes):
@@ -209,18 +220,21 @@
 def setup_kernel(sizes, *refs):
     sources, refs = refs[:6], refs[6:]
     out_ref, a_ref, b_ref, inv_ref, grad_ref, place_point_ref, place_slot_ref = refs[:7]
-    r_ref, table_ref, parts_ref, spread_ref, place_list_ref = refs[7:12]
-    jac_ref, pjac_ref, res_ref, slot_ref, point_ref, list_ref = refs[12:18]
-    semaphores = refs[18]
+    new_slot_ref, new_point_ref = refs[7:9]
+    r_ref, table_ref, parts_ref, spread_ref, place_list_ref, picked_ref, found_ref = refs[9:16]
+    jac_ref, pjac_ref, res_ref, slot_ref, point_ref, list_ref = refs[16:22]
+    semaphores = refs[22]
     rows = sizes.rows
     copies = [
         pltpu.make_async_copy(source, target, semaphores.at[k])
-        for k, (source, target) in enumerate(zip(sources, refs[12:18]))
+        for k, (source, target) in enumerate(zip(sources, refs[16:22]))
     ]
     for copy in copies:
         copy.start()
     for copy in copies:
         copy.wait()
+    new_slot_ref[...] = slot_ref[...]
+    new_point_ref[...] = point_ref[...]
     for j in range(rows):
         columns = slice(j * LANES, (j + 1) * LANES)
         for start in range(0, 2 * CP, SUB):
@@ -250,7 +264,7 @@
 
     lax.fori_loop(0, rows // SUB, first, 0)
     result = scatter(sum(normal_pieces), sizes.obs, PT_HI, PT_LO, spread_ref, place_point_ref)
-    normal = [point_rows(value) for value in joined(result, 9, PT_HI, normal_pieces)]
+    normal = joined(result, 9, PT_HI, normal_pieces)
     top_left = normal[0] + damping_point
     top_mid = normal[1]
     top_right = normal[2]
@@ -276,9 +290,8 @@
         table_ref[k] = eliminated[k]
 
     def second(group, carry):
-        point = point_ref[pl.ds(pl.multiple_of(group * SUB, SUB), SUB), :]
-        high, low = point_place(point)
-        at_point = gather_rows(lambda c, k: table_ref[c, k : k + 1, :], PT_ROWS, high, low, 3)
+        at_point = matmul_gather(group, [table_ref[k] for k in range(3)], place_point_ref,
+                                 lambda row: point_ref[pl.ds(row, 1), :] >> 8, PT_HI, picked_ref, found_ref)
         b = [at(b_ref, k, group) for k in range(6)]
         errors = [at(r_ref, i, group) - sum(b[3 * i + k] * at_point[k] for k in range(3)) for i in range(2)]
         a = [at(a_ref, k, group) for k in range(2 * CP)]
@@ -391,14 +404,11 @@
     refs = refs[5:]
     if not start:
         new_grad_ref = refs.pop(0)
-    q_ref, table_ref, parts_ref, spread_ref = refs
+    q_ref, table_ref, parts_ref, spread_ref, picked_ref, found_ref = refs
     rows = sizes.rows
 
     def at(ref, comp, group):
         return ref[pl.ds(pl.multiple_of(comp * rows + group * SUB, SUB), SUB), :]
-
-    def index(ref, group):
-        return ref[pl.ds(pl.multiple_of(group * SUB, SUB), SUB), :]
 
     renewed = jnp.broadcast_to(read_scalar(in_ref, sizes.groups, sizes.message, sizes), (SUB, LANES))
     new_product_ref[...] = renewed
@@ -416,8 +426,9 @@
         squares = direction * direction if squares is None else squares + direction * direction
 
     def first(group, carry):
-        high, low = slot_place(index(slot_ref, group), sizes)
-        gathered = gather_rows(lambda c, k: new_at_slot_ref[c, k : k + 1, :], sizes.pts, high, low, CP)
+        gathered = matmul_gather(group, [new_at_slot_ref[k] for k in range(CP)], place_slot_ref,
+                                 lambda row: slot_place(slot_ref[pl.ds(row, 1), :], sizes)[0], sizes.pts,
+                                 picked_ref, found_ref)
         q = [sum(at(a_ref, i * CP + k, group) * gathered[k] for k in range(CP)) for i in range(2)]
         for i in range(2):
             q_ref[pl.ds(pl.multiple_of(i * rows + group * SUB, SUB), SUB), :] = q[i]
@@ -431,17 +442,17 @@
 
     lax.fori_loop(0, rows // SUB, first, 0)
     result = scatter(3 * PIECES, sizes.obs, PT_HI, PT_LO, spread_ref, place_point_ref)
-    sums = [point_rows(value) for value in joined(result, 3, PT_HI)]
+    sums = joined(result, 3, PT_HI)
     folded = solve([inv_ref[k] for k in range(6)], sums)
     for k in range(3):
         table_ref[k] = folded[k]
         new_sum_ref[k] = sums[k]
         if not start:
-            new_grad_ref[k] = grad_ref[k] + step_ref[:1, :] * sum_ref[k]
+            new_grad_ref[k] = grad_ref[k] + step_ref[:1, :1] * sum_ref[k]
 
     def second(group, inner):
-        high, low = point_place(index(point_ref, group))
-        at_point = gather_rows(lambda c, k: table_ref[c, k : k + 1, :], PT_ROWS, high, low, 3)
+        at_point = matmul_gather(group, [table_ref[k] for k in range(3)], place_point_ref,
+                                 lambda row: point_ref[pl.ds(row, 1), :] >> 8, PT_HI, picked_ref, found_ref)
         q = [at(q_ref, i, group) for i in range(2)]
         errors = [q[i] - sum(at(b_ref, 3 * i + k, group) * at_point[k] for k in range(3)) for i in range(2)]
         inner = inner + q[0] * errors[0] + q[1] * errors[1]
@@ -491,18 +502,21 @@
                     base = all_ref[pl.ds(first, size, stride=sizes.own_rows), :]
                     direction = all_ref[pl.ds(first + CP * sizes.own_rows, size, stride=sizes.own_rows), :]
                     cam_ref[start : start + size, columns] = base + step * direction
-    total = [grad_ref[k] + step * sum_ref[k] for k in range(3)]
+    total = [grad_ref[k] + step[:, :1] * sum_ref[k] for k in range(3)]
     solved = solve([inv_ref[k] for k in range(6)], total)
     for k in range(3):
-        table_ref[k * PT_ROWS : (k + 1) * PT_ROWS, :] = -solved[k]
-    for row in range(PT_ROWS):
-        half, high = row // PT_HI, row % PT_HI
-        chunk = high * (PT_LO // LANES) + half
-        pt_ref[:, chunk * LANES : (chunk + 1) * LANES] = table_ref[pl.ds(row, 3, stride=PT_ROWS), :]
+        table_ref[k * PT_HI : (k + 1) * PT_HI, :] = -solved[k]
+    for row in range(PT_HI):
+        for k in range(3):
+            pt_ref[k : k + 1, row * PT_LO : (row + 1) * PT_LO] = table_ref[k * PT_HI + row : k * PT_HI + row + 1, :]
 
 
 def shape(*dims, dtype=f32):
     return jax.ShapeDtypeStruct(dims, dtype)
+
+
+def kept(*dims, dtype=f32):
+    return pltpu.VMEM(dims, dtype)
 
 
 def call(kernel, name, inputs, outputs, scratch, scalars=(), inputs_at=pltpu.VMEM, cost=None):
@@ -540,13 +554,16 @@
     def factors(high_rows, low_rows, entries):
         return [pltpu.VMEM((high_rows, entries), bf16), pltpu.VMEM((low_rows, entries), bf16)]
 
-    point_table = shape(3, PT_ROWS, LANES)
-    owned = shape(CP, sizes.own_rows, LANES)
-    messages = shape(sizes.devices * sizes.message, LANES)
-    scalar = shape(SUB, LANES)
+    point_table = kept(3, PT_HI, PT_LO)
+    owned = kept(CP, sizes.own_rows, LANES)
+    messages = kept(sizes.devices * sizes.message, LANES)
+    scalar = kept(SUB, LANES)
     owned_scratch = pltpu.VMEM((CP, sizes.own_rows, LANES), f32)
-    point_scratch = pltpu.VMEM((3, PT_ROWS, LANES), f32)
+    point_scratch = pltpu.VMEM((3, PT_HI, PT_LO), f32)
     entries = sizes.pts * LANES
+
+    picked_rows = max(CP * PIECES * sizes.pts, 3 * PIECES * PT_HI)
+    gather_scratch = [pltpu.VMEM((picked_rows, SUB * LANES), bf16), pltpu.VMEM((2 * SUB * SUB, LANES), f32)]
 
     def parts_scratch(count):
         return pltpu.VMEM((count * SUB, LANES), f32)
@@ -556,22 +573,25 @@
         pltpu.with_memory_space_constraint(value, pltpu.HBM)
         for value in (camera_jacobian, point_jacobian, residual, slot, point, send_list[0])
     ]
-    first, a, b, inverse, gradient, place_point, place_slot = call(
+    first, a, b, inverse, gradient, place_point, place_slot, slot, point = call(
         functools.partial(setup_kernel, sizes),
         "setup",
         given,
         [
-            shape(sizes.devices * sizes.first_message, LANES),
-            shape(2 * CP * rows, LANES),
-            shape(6 * rows, LANES),
-            shape(6, PT_ROWS, LANES),
+            kept(sizes.devices * sizes.first_message, LANES),
+            kept(2 * CP * rows, LANES),
+            kept(6 * rows, LANES),
+            kept(6, PT_HI, PT_LO),
             point_table,
-            shape(PT_LO, sizes.obs, dtype=bf16),
-            shape(LANES, sizes.obs, dtype=bf16),
+            kept(PT_LO, sizes.obs, dtype=bf16),
+            kept(LANES, sizes.obs, dtype=bf16),
+            kept(rows, LANES, dtype=jnp.int32),
+            kept(rows, LANES, dtype=jnp.int32),
         ],
         [pltpu.VMEM((2 * rows, LANES), f32), point_scratch, parts_scratch(2 * CP * PIECES)]
         + [pltpu.VMEM((max(spread_rows(6 * FINE + 3 * PIECES, PT_HI), spread_rows(2 * CP * PIECES, sizes.pts)), sizes.obs), bf16)]
         + [pltpu.VMEM((LANES, sizes.cams * sizes.slot), bf16)]
+        + gather_scratch
         + [pltpu.VMEM(value.shape, value.dtype) for value in given]
         + [pltpu.SemaphoreType.DMA((len(given),))],
         inputs_at=pl.ANY,
@@ -580,13 +600,14 @@
         functools.partial(first_owner_kernel, sizes),
         "first_owner",
         [exchange(first)],
-        [messages, shape(sizes.pts, LANES, dtype=jnp.int32), owned, owned],
+        [messages, kept(sizes.pts, LANES, dtype=jnp.int32), owned, owned],
         [owned_scratch] + factors(spread_rows(2 * CP * PIECES, sizes.own_rows), LANES, entries),
         scalars=[column],
     )
     schur_scratch = [pltpu.VMEM((2 * rows, LANES), f32), point_scratch, parts_scratch(CP * PIECES)]
     schur_scratch += [pltpu.VMEM((max(spread_rows(3 * PIECES, PT_HI), spread_rows(CP * PIECES, sizes.pts)), sizes.obs), bf16)]
-    at_slot = shape(CP, sizes.pts, LANES)
+    schur_scratch += gather_scratch
+    at_slot = kept(CP, sizes.pts, LANES)
     product = slots = direction = step = sums = solution_ = None
     for iteration in range(ITERS):
         start, last = iteration == 0, iteration == ITERS - 1
@@ -599,7 +620,7 @@
                 functools.partial(tail_kernel, sizes),
                 "tail",
                 [arrived, product, fields, neighbour],
-                [shape(4 * CP * sizes.own_rows, LANES)],
+                [kept(4 * CP * sizes.own_rows, LANES)],
                 [],
             )
             flips = [1 << bit for bit in range(sizes.pts.bit_length() - 1) if 1 << bit != NEAR]
@@ -610,7 +631,7 @@
             "schur_last" if last else "schur",
             [arrived, a, b, inverse, slot, point, place_point, place_slot, precondition, remainder, gradient]
             + earlier,
-            [shape(sizes.devices, LANES) if last else messages, scalar, at_slot, owned, point_table]
+            [kept(sizes.devices, LANES) if last else messages, scalar, at_slot, owned, point_table]
             + ([] if start else [point_table]),
             schur_scratch,
             cost=pl.CostEstimate(flops=2_000_000_000, bytes_accessed=10_000_000, transcendentals=0),
@@ -630,7 +651,7 @@
             functools.partial(owner_kernel, sizes, start, final),
             "owner_final" if final else "owner",
             [exchange(out), entry, precondition, remainder, direction, product] + ([] if start else [solution_]),
-            [messages, owned, owned, scalar] + ([shape(3 * CP * sizes.own_rows, LANES)] if final else []),
+            [messages, owned, owned, scalar] + ([kept(3 * CP * sizes.own_rows, LANES)] if final else []),
             [owned_scratch] + factors(spread_rows(CP * PIECES, sizes.own_rows), LANES, entries),
         )
         fields = rest[0] if final else None
@@ -639,7 +660,7 @@
         "final",
         [exchange(out), product, inverse, gradient, sums] + gathered,
         [shape(CP, CAM_OWN), shape(3, PT_DEV)],
-        [pltpu.VMEM((3 * PT_ROWS, LANES), f32)],
+        [pltpu.VMEM((3 * PT_HI, PT_LO), f32)],
         scalars=[lax.axis_index("pts").astype(jnp.int32).reshape(1)],
     )
 

time: 106 us -> 106 us (level)
  Pallas kernels: 23.8 us -> 26.9 us
  waiting for transfers between devices: 19.9 us -> 18.3 us
  local copies, waits for them, and re-layouts: 3.65 us -> 2.19 us
    pallas_call x9, Pallas kernels: 23.8 us -> 26.9 us  [call(): pl.pallas_call(kernel, name=name, out_shape=outputs, in_specs=[smem] * le...]
    ppermute x4, waiting for transfers between devices: 4.99 us -> 3.37 us  [flipped(): return lax.ppermute(value, 'pts', [(p, p ^ flip) for p in range(sizes.pts)])]
    unnamed x12 -> x4, local copies, waits for them, and re-layouts: 3.65 us -> 2.19 us
  transfers between devices with their start and end apart: 6 -> 6, of which waited for: 3 -> 3; matrix products, arithmetic and copies ran while one was open for 0% -> 0% of each run, Pallas kernels for 3% -> 5%
where the time goes in v6:
time: 106 us
  blocking collectives  45.1 us (43%)
  Pallas kernels  26.9 us (25%)
  waiting for transfers between devices  18.3 us (17%)
  starting transfers between devices  12.7 us (12%)
  local copies, waits for them, and re-layouts  2.19 us (2%)
    all_to_all x5, blocking collectives, exchange(): lax.all_to_all(flat, axes, split_axis=0, concat_axis=0, tiled=True)  45.1 us
    pallas_call x9, Pallas kernels, call(): pl.pallas_call(kernel, name=name, out_shape=outputs, in_specs=[smem] * le...  26.9 us
    all_to_all x2, waiting for transfers between devices, exchange(): lax.all_to_all(flat, axes, split_axis=0, concat_axis=0, tiled=True)  14.9 us
    all_to_all x2, starting transfers between devices, exchange(): lax.all_to_all(flat, axes, split_axis=0, concat_axis=0, tiled=True)  9.8 us
    ppermute x4, waiting for transfers between devices, flipped(): return lax.ppermute(value, 'pts', [(p, p ^ flip) for p in range(sizes.pts)])  3.37 us
    ppermute x4, starting transfers between devices, flipped(): return lax.ppermute(value, 'pts', [(p, p ^ flip) for p in range(sizes.pts)])  2.93 us
    unnamed x4, local copies, waits for them, and re-layouts  2.19 us
  transfers between devices with their start and end apart: 6, of which 3 were waited for; matrix products, arithmetic and copies ran while one was open for 0% of the time, Pallas kernels for 5%

profile of v6, /device:TPU:0, one launch (start us, length us, event | category | flops | bytes accessed | tf_op | source)
XLA Modules:
  0.0 106.0 jit_solution(16540630772817220728)
XLA Ops:
  0.6 8.6 %setup.1 = (f32[192,128]{1,0:T(8,128)}, f32[576,128]{1,0:T(8,128)S(1)}, f32[192,128]{1,0:T(8,128)S(1)}, f32[6,16,256]{2,1,0:T(8,128)S(1)}, f32[3,16,256]{2,1,0:T...) custom-call(f32[18,4096]{1,0:T(8,128)} %refs_0_.1, ...), custom_call_target="tpu_custom_call" | custom-call | tf_op jit(solution)/shard_map/setup/pallas_call | solution.py:526
  9.3 1.0 copy-done
  10.3 7.3 %all-to-all-start = ((f32[32,1,768]{2,1,0:T(1,128)}), f32[32,1,768]{2,1,0:T(1,128)S(1)}, u32[]{:S(2)}, u32[]{:S(2)}) async-start(f32[32,1,768]{2,1,0:T(1,128)} %bitcast.5), calls=%async_computation | async-start | bytes 196608 | tf_op jit(solution)/shard_map/all_to_all | solution.py:549
  17.6 7.8 %all-to-all-done = f32[32,1,768]{2,1,0:T(1,128)S(1)} async-done(((f32[32,1,768]{2,1,0:T(1,128)}), f32[32,1,768]{2,1,0:T(1,128)S(1)}, u32[]{:S(2)}, u32[]{:S(2)}) %all-to-all-start) | async-done | bytes 98336 | tf_op jit(solution)/shard_map/all_to_all | solution.py:549
  25.4 0.7 first_owner.1
  26.1 9.0 %all_to_all.35 = f32[32,1,384]{2,1,0:T(1,128)S(1)} all-to-all(f32[32,1,384]{2,1,0:T(1,128)S(1)} %bitcast.31), channel_id=1, replica_groups=mesh['pts'=8,'cams'=4] {'pts','cams'}, dimensions={0} | all-to-all | bytes 98304 | tf_op jit(solution)/shard_map/all_to_all | solution.py:549
  35.1 1.2 %copy-done.1 = bf16[128,4096]{1,0:T(8,128)(2,1)S(1)} copy-done((bf16[128,4096]{1,0:T(8,128)(2,1)S(1)}, bf16[128,4096]{1,0:T(8,128)(2,1)}, u32[]{:S(2)}) %copy-start.1) | copy-done | bytes 1048600
  36.3 5.0 %schur.2 = (f32[96,128]{1,0:T(8,128)S(1)}, f32[8,128]{1,0:T(8,128)S(1)}, f32[9,8,128]{2,1,0:T(8,128)S(1)}, f32[9,8,128]{2,1,0:T(8,128)S(1)}, f32[3,16,256]{2,1,0:T(8,128)S(1)}) custom-call(f32[96,128]{1,0:T(8,128)S(1)} %bitcast.30, f32[576,128]{1,0:T(8,128)S(1)} %get-tuple-element.42.a_ref, f32[192,128]{1,0:T(8,128)S(1)} %get-tuple-element.43.b_ref, ...), custom_call_target="tpu_custom_call" | custom-call | flops 2000000000 | bytes 10000000 | tf_op jit(solution)/shard_map/schur/pallas_call | solution.py:526
  41.3 9.0 %all_to_all.36 = f32[32,1,384]{2,1,0:T(1,128)S(1)} all-to-all(f32[32,1,384]{2,1,0:T(1,128)S(1)} %bitcast.32), channel_id=1, replica_groups=mesh['pts'=8,'cams'=4] {'pts','cams'}, dimensions={0} | all-to-all | bytes 98304 | tf_op jit(solution)/shard_map/all_to_all | solution.py:549
  50.4 0.6 owner.1
  50.9 9.0 %all_to_all.37 = f32[32,1,384]{2,1,0:T(1,128)S(1)} all-to-all(f32[32,1,384]{2,1,0:T(1,128)S(1)} %bitcast.33), channel_id=1, replica_groups=mesh['pts'=8,'cams'=4] {'pts','cams'}, dimensions={0} | all-to-all | bytes 98304 | tf_op jit(solution)/shard_map/all_to_all | solution.py:549
  59.9 5.0 %schur.3 = (f32[96,128]{1,0:T(8,128)S(1)}, f32[8,128]{1,0:T(8,128)S(1)}, f32[9,8,128]{2,1,0:T(8,128)S(1)}, f32[9,8,128]{2,1,0:T(8,128)S(1)}, f32[3,16,256]{2,1,0:T(8,128)S(1)}, /*index=5*/f32[3,16,256]{2,1,0:T(8,128)S(1)}) custom-call(f32[96,128]{1,0:T(8,128)S(1)} %bitcast.27, f32[576,128]{1,0:T(8,128)S(1)} %get-tuple-element.42.a_ref, ...), custom_call_target="tpu_custom_call" | custom-call | flops 2000000000 | bytes 10000000 | tf_op jit(solution)/shard_map/schur/pallas_call | solution.py:526
  65.0 9.0 %all_to_all.38 = f32[32,1,384]{2,1,0:T(1,128)S(1)} all-to-all(f32[32,1,384]{2,1,0:T(1,128)S(1)} %bitcast.28), channel_id=1, replica_groups=mesh['pts'=8,'cams'=4] {'pts','cams'}, dimensions={0} | all-to-all | bytes 98304 | tf_op jit(solution)/shard_map/all_to_all | solution.py:549
  74.0 1.0 owner_final.1
  74.9 0.6 collective-permute-start
  75.5 9.0 %all_to_all.39 = f32[32,1,384]{2,1,0:T(1,128)S(1)} all-to-all(f32[32,1,384]{2,1,0:T(1,128)S(1)} %bitcast.29), channel_id=1, replica_groups=mesh['pts'=8,'cams'=4] {'pts','cams'}, dimensions={0} | all-to-all | bytes 98304 | tf_op jit(solution)/shard_map/all_to_all | solution.py:549
  84.7 0.7 collective-permute-start.1
  85.4 4.8 %schur_last.1 = (f32[32,128]{1,0:T(8,128)}, f32[8,128]{1,0:T(8,128)S(1)}, f32[9,8,128]{2,1,0:T(8,128)}, f32[9,8,128]{2,1,0:T(8,128)}, f32[3,16,256]{2,1,0:T(8,128)S(1)}, /*index=5*/f32[3,16,256]{2,1,0:T(8,128)S(1)}) custom-call(f32[96,128]{1,0:T(8,128)S(1)} %bitcast.23, f32[576,128]{1,0:T(8,128)S(1)} %get-tuple-element.42.a_ref, ...), custom_call_target="tpu_custom_call" | custom-call | flops 2000000000 | bytes 10000000 | tf_op jit(solution)/shard_map/schur_last/pallas_call | solution.py:526
  90.3 0.6 collective-permute-start.2
  90.8 3.4 %collective-permute-done.1.refs_1_ = f32[288,128]{1,0:T(8,128)S(1)} collective-permute-done((f32[288,128]{1,0:T(8,128)S(1)}, f32[288,128]{1,0:T(8,128)S(1)}, u32[]{:S(2)}, u32[]{:S(2)}) %collective-permute-start.1) | collective-permute-done | bytes 147488 | tf_op jit(solution)/shard_map/ppermute | solution.py:552
  94.2 1.0 collective-permute-start.3
  95.2 2.5 %all-to-all-start.6 = ((f32[32,1,128]{2,1,0:T(1,128)}), f32[32,1,128]{2,1,0:T(1,128)S(1)}, u32[]{:S(2)}, u32[]{:S(2)}) async-start(f32[32,1,128]{2,1,0:T(1,128)} %bitcast.18), calls=%async_computation.6 | async-start | bytes 32768 | tf_op jit(solution)/shard_map/all_to_all | solution.py:549
  97.8 7.1 %all-to-all-done.6 = f32[32,1,128]{2,1,0:T(1,128)S(1)} async-done(((f32[32,1,128]{2,1,0:T(1,128)}), f32[32,1,128]{2,1,0:T(1,128)S(1)}, u32[]{:S(2)}, u32[]{:S(2)}) %all-to-all-start.6) | async-done | bytes 16416 | tf_op jit(solution)/shard_map/all_to_all | solution.py:549
  104.9 1.1 %final.1 = (f32[9,8192]{1,0:T(8,128)}, f32[3,4096]{1,0:T(4,128)}) custom-call(s32[1]{0:T(128)} %bitcast.run_ref, f32[32,128]{1,0:T(8,128)S(1)} %bitcast.26, f32[8,128]{1,0:T(8,128)S(1)} %get-tuple-element.74.product_ref, f32[6,16,256]{2,1,0:T(8,128)S(1)} %get-tuple-element.44.inv_ref, f32[3,16,256]{2,1,0:T(8,128)S(1)} %get-tuple-element.75.grad_ref, ...), custom_call_target="tpu_custom_call" | custom-call | tf_op jit(solution)/shard_map/final/pallas_call | solution.py:526
  (6 shorter events, 0.1 us)
Async XLA Ops:
  9.3 1.0 copy-start
  10.3 15.1 %all-to-all-start = ((f32[32,1,768]{2,1,0:T(1,128)}), f32[32,1,768]{2,1,0:T(1,128)S(1)}, u32[]{:S(2)}, u32[]{:S(2)}) async-start(f32[32,1,768]{2,1,0:T(1,128)} %bitcast.5), calls=%async_computation | async-start | bytes 196608 | tf_op jit(solution)/shard_map/all_to_all | solution.py:549
  35.1 1.2 %copy-start.1 = (bf16[128,4096]{1,0:T(8,128)(2,1)S(1)}, bf16[128,4096]{1,0:T(8,128)(2,1)}, u32[]{:S(2)}) copy-start(bf16[128,4096]{1,0:T(8,128)(2,1)} %copy-done) | copy-start | bytes 3145732
  74.9 9.6 %collective-permute-start = (f32[216,128]{1,0:T(8,128)S(1)}, f32[216,128]{1,0:T(8,128)S(1)}, u32[]{:S(2)}, u32[]{:S(2)}) collective-permute-start(f32[216,128]{1,0:T(8,128)S(1)} %get-tuple-element.66.own_ref), channel_id=1, source_target_pairs={{0,8},{4,12},{8,0},{12,4},{16,24},{20,28},{24,16},{28,20},{1,9},{5... | collective-permute-start | bytes 331784 | tf_op jit(solution)/shard_map/ppermute | solution.py:552
  84.7 9.5 %collective-permute-start.1 = (f32[288,128]{1,0:T(8,128)S(1)}, f32[288,128]{1,0:T(8,128)S(1)}, u32[]{:S(2)}, u32[]{:S(2)}) collective-permute-start(f32[288,128]{1,0:T(8,128)S(1)} %tail.1.refs_0_), channel_id=1, source_target_pairs={{0,16},{4,20},{8,24},{12,28},{16,0},{20,4},{24,8},{28,12},{1,17},{... | collective-permute-start | bytes 442376 | tf_op jit(solution)/shard_map/ppermute | solution.py:552
  90.3 7.5 %collective-permute-start.2 = (f32[288,128]{1,0:T(8,128)S(1)}, f32[288,128]{1,0:T(8,128)S(1)}, u32[]{:S(2)}, u32[]{:S(2)}) collective-permute-start(f32[288,128]{1,0:T(8,128)S(1)} %tail.1.refs_0_), channel_id=1, source_target_pairs={{0,4},{4,0},{8,12},{12,8},{16,20},{20,16},{24,28},{28,24},{1,5},{5... | collective-permute-start | bytes 442376 | tf_op jit(solution)/shard_map/ppermute | solution.py:552
  94.2 10.7 %collective-permute-start.3 = (f32[288,128]{1,0:T(8,128)S(1)}, f32[288,128]{1,0:T(8,128)S(1)}, u32[]{:S(2)}, u32[]{:S(2)}) collective-permute-start(f32[288,128]{1,0:T(8,128)S(1)} %collective-permute-done.1.refs_1_), channel_id=1, source_target_pairs={{0,4},{4,0},{8,12},{12,8},{16,20},{20,16},{24,28},{28,24},{1,5},{5... | collective-permute-start | bytes 442376 | tf_op jit(solution)/shard_map/ppermute | solution.py:552
  95.2 9.7 %all-to-all-start.6 = ((f32[32,1,128]{2,1,0:T(1,128)}), f32[32,1,128]{2,1,0:T(1,128)S(1)}, u32[]{:S(2)}, u32[]{:S(2)}) async-start(f32[32,1,128]{2,1,0:T(1,128)} %bitcast.18), calls=%async_computation.6 | async-start | bytes 32768 | tf_op jit(solution)/shard_map/all_to_all | solution.py:549

commit v7 on v6

--- a/solution.py
+++ b/solution.py
@@ -86,28 +86,35 @@
     return result
 
 
-def matmul_gather(group, tables, place_ref, high_of_row, high_count, picked_ref, found_ref):
+def gather_factors(tables):
     pieces = [piece for table in tables for piece in cut(table)]
     left = jnp.concatenate(pieces, axis=0).astype(bf16)
-    rows = len(pieces) * high_count
-    columns = pl.ds(pl.multiple_of(group * SUB * LANES, SUB * LANES), SUB * LANES)
-    picked = jnp.dot(left, place_ref[:, columns], preferred_element_type=f32)
+    padded, rows = -(-len(tables) // SUB) * SUB, left.shape[0]
+    owner = lax.broadcasted_iota(jnp.int32, (padded, rows), 1) // (rows // len(tables))
+    chosen = (owner == lax.broadcasted_iota(jnp.int32, (padded, rows), 0)).astype(f32).astype(bf16)
+    return left, chosen
+
+
+def matmul_gather(group, factors, count, place_ref, high_of_row, high_count, picked_ref, found_ref):
+    left, chosen = factors
+    rows, padded = left.shape[0], chosen.shape[0]
+    width = SUB * LANES
+    picked = jnp.dot(left, place_ref[:, group * width : (group + 1) * width], preferred_element_type=f32)
     for s in range(SUB):
         mask = jnp.broadcast_to(high_of_row(group * SUB + s), (high_count, LANES)) == sub_iota(high_count)
-        mask = jnp.concatenate([mask.astype(f32)] * len(pieces), axis=0) > 0.5
-        lanes = slice(s * LANES, (s + 1) * LANES)
-        picked_ref[:rows, lanes] = jnp.where(mask, picked[:, lanes], 0.0).astype(bf16)
-    padded = -(-len(tables) // SUB) * SUB
-    owner = lax.broadcasted_iota(jnp.int32, (padded, rows), 1) // (PIECES * high_count)
-    chosen = (owner == lax.broadcasted_iota(jnp.int32, (padded, rows), 0)).astype(f32).astype(bf16)
-    total = jnp.dot(chosen, picked_ref[:rows, :], preferred_element_type=f32)
+        for first in range(0, rows, high_count):
+            block = picked[first : first + high_count, s * LANES : (s + 1) * LANES]
+            columns = slice(group * width + s * LANES, group * width + (s + 1) * LANES)
+            picked_ref[first : first + high_count, columns] = jnp.where(mask, block, 0.0).astype(bf16)
+    total = jnp.dot(chosen, picked_ref[:rows, group * width : (group + 1) * width], preferred_element_type=f32)
+    start = group * SUB * padded
     for s in range(SUB):
-        found_ref[s * padded : (s + 1) * padded, :] = total[:, s * LANES : (s + 1) * LANES]
-    return [found_ref[pl.ds(c, SUB, stride=padded), :] for c in range(len(tables))]
+        found_ref[start + s * padded : start + (s + 1) * padded, :] = total[:, s * LANES : (s + 1) * LANES]
+    return [found_ref[pl.ds(start + c, SUB, stride=padded), :] for c in range(count)]
 
 
 def spread_row(index, parts, high, high_count, spread_ref):
-    columns = pl.ds(pl.multiple_of(index * LANES, LANES), LANES)
+    columns = slice(index * LANES, (index + 1) * LANES)
     mask = jnp.broadcast_to(high, (high_count, LANES)) == sub_iota(high_count)
     together = max(1, 16 // high_count)
     for start in range(0, len(parts), together):
@@ -122,18 +129,18 @@
 
 
 def place_row(index, low, low_count, place_ref):
-    columns = pl.ds(pl.multiple_of(index * LANES, LANES), LANES)
+    columns = slice(index * LANES, (index + 1) * LANES)
     place = jnp.broadcast_to(low, (low_count, LANES)) == sub_iota(low_count)
     place_ref[:low_count, columns] = jnp.where(place, 1.0, 0.0).astype(bf16)
 
 
-def keep_parts(parts, parts_ref):
+def keep_parts(parts, group, parts_ref):
     for k, part in enumerate(parts):
-        parts_ref[k * SUB : (k + 1) * SUB, :] = part
-
-
-def part_rows(count, s, parts_ref):
-    return [parts_ref[k * SUB + s : k * SUB + s + 1, :] for k in range(count)]
+        parts_ref[group, k * SUB : (k + 1) * SUB, :] = part
+
+
+def part_rows(count, group, s, parts_ref):
+    return [parts_ref[group, k * SUB + s : k * SUB + s + 1, :] for k in range(count)]
 
 
 def spread_rows(parts, high_count):
@@ -219,15 +226,14 @@
 
 def setup_kernel(sizes, *refs):
     sources, refs = refs[:6], refs[6:]
-    out_ref, a_ref, b_ref, inv_ref, grad_ref, place_point_ref, place_slot_ref = refs[:7]
-    new_slot_ref, new_point_ref = refs[7:9]
-    r_ref, table_ref, parts_ref, spread_ref, place_list_ref, picked_ref, found_ref = refs[9:16]
-    jac_ref, pjac_ref, res_ref, slot_ref, point_ref, list_ref = refs[16:22]
-    semaphores = refs[22]
+    out_ref, a_ref, b_ref, inv_ref, grad_ref, place_point_ref, new_slot_ref, new_point_ref = refs[:8]
+    r_ref, parts_ref, spread_ref, picked_ref, found_ref, place_slot_ref, place_list_ref = refs[8:15]
+    jac_ref, pjac_ref, res_ref, slot_ref, point_ref, list_ref = refs[15:21]
+    semaphores = refs[21]
     rows = sizes.rows
     copies = [
         pltpu.make_async_copy(source, target, semaphores.at[k])
-        for k, (source, target) in enumerate(zip(sources, refs[16:22]))
+        for k, (source, target) in enumerate(zip(sources, refs[15:21]))
     ]
     for copy in copies:
         copy.start()
@@ -244,25 +250,22 @@
         r_ref[pl.ds(j, 2, stride=rows), :] = res_ref[:, columns]
 
     def at(ref, comp, group):
-        return ref[pl.ds(pl.multiple_of(comp * rows + group * SUB, SUB), SUB), :]
+        return ref[comp * rows + group * SUB : comp * rows + (group + 1) * SUB, :]
 
     normal_pieces = [FINE] * 6 + [PIECES] * 3
 
-    def first(group, carry):
+    for group in range(rows // SUB):
         b = [at(b_ref, k, group) for k in range(6)]
         r = [at(r_ref, k, group) for k in range(2)]
         values = [b[i] * b[j] + b[3 + i] * b[3 + j] for i, j in ((0, 0), (0, 1), (0, 2), (1, 1), (1, 2), (2, 2))]
         values += [b[i] * r[0] + b[3 + i] * r[1] for i in range(3)]
         parts = [part for value, pieces in zip(values, normal_pieces) for part in cut(value, pieces)]
-        keep_parts(parts, parts_ref)
+        keep_parts(parts, group, parts_ref)
         for s in range(SUB):
             row = group * SUB + s
-            point = point_ref[pl.ds(row, 1), :]
-            spread_row(row, part_rows(len(parts), s, parts_ref), point >> 8, PT_HI, spread_ref)
+            point = point_ref[row : row + 1, :]
+            spread_row(row, part_rows(len(parts), group, s, parts_ref), point >> 8, PT_HI, spread_ref)
             place_row(row, point & (PT_LO - 1), PT_LO, place_point_ref)
-        return carry
-
-    lax.fori_loop(0, rows // SUB, first, 0)
     result = scatter(sum(normal_pieces), sizes.obs, PT_HI, PT_LO, spread_ref, place_point_ref)
     normal = joined(result, 9, PT_HI, normal_pieces)
     top_left = normal[0] + damping_point
@@ -286,27 +289,22 @@
     for k in range(3):
         grad_ref[k] = normal[6 + k]
     eliminated = solve(inverse, normal[6:])
-    for k in range(3):
-        table_ref[k] = eliminated[k]
-
-    def second(group, carry):
-        at_point = matmul_gather(group, [table_ref[k] for k in range(3)], place_point_ref,
-                                 lambda row: point_ref[pl.ds(row, 1), :] >> 8, PT_HI, picked_ref, found_ref)
+    picking = gather_factors(eliminated)
+    for group in range(rows // SUB):
+        at_point = matmul_gather(group, picking, 3, place_point_ref,
+                                 lambda row: point_ref[row : row + 1, :] >> 8, PT_HI, picked_ref, found_ref)
         b = [at(b_ref, k, group) for k in range(6)]
         errors = [at(r_ref, i, group) - sum(b[3 * i + k] * at_point[k] for k in range(3)) for i in range(2)]
         a = [at(a_ref, k, group) for k in range(2 * CP)]
         values = [a[k] * errors[0] + a[CP + k] * errors[1] for k in range(CP)]
         values += [a[k] * a[k] + a[CP + k] * a[CP + k] for k in range(CP)]
         parts = [part for value in values for part in cut(value)]
-        keep_parts(parts, parts_ref)
+        keep_parts(parts, group, parts_ref)
         for s in range(SUB):
             row = group * SUB + s
-            high, low = slot_place(slot_ref[pl.ds(row, 1), :], sizes)
-            spread_row(row, part_rows(len(parts), s, parts_ref), high, sizes.pts, spread_ref)
+            high, low = slot_place(slot_ref[row : row + 1, :], sizes)
+            spread_row(row, part_rows(len(parts), group, s, parts_ref), high, sizes.pts, spread_ref)
             place_row(row, low, LANES, place_slot_ref)
-        return carry
-
-    lax.fori_loop(0, rows // SUB, second, 0)
     result = scatter(2 * CP * PIECES, sizes.obs, sizes.pts, LANES, spread_ref, place_slot_ref)
     fields = joined(result, 2 * CP, sizes.pts)
 
@@ -394,7 +392,7 @@
 
 
 def schur_kernel(sizes, start, last, in_ref, a_ref, b_ref, inv_ref, slot_ref, point_ref,
-                 place_point_ref, place_slot_ref, pre_ref, rem_ref, grad_ref, *refs):
+                 place_point_ref, pre_ref, rem_ref, grad_ref, *refs):
     refs = list(refs)
     if not start:
         product_ref, at_slot_ref, dir_ref, step_ref, sum_ref = refs[:5]
@@ -404,11 +402,11 @@
     refs = refs[5:]
     if not start:
         new_grad_ref = refs.pop(0)
-    q_ref, table_ref, parts_ref, spread_ref, picked_ref, found_ref = refs
+    q_ref, parts_ref, spread_ref, picked_ref, found_ref, place_slot_ref = refs
     rows = sizes.rows
 
     def at(ref, comp, group):
-        return ref[pl.ds(pl.multiple_of(comp * rows + group * SUB, SUB), SUB), :]
+        return ref[comp * rows + group * SUB : comp * rows + (group + 1) * SUB, :]
 
     renewed = jnp.broadcast_to(read_scalar(in_ref, sizes.groups, sizes.message, sizes), (SUB, LANES))
     new_product_ref[...] = renewed
@@ -425,48 +423,44 @@
         new_dir_ref[k] = direction
         squares = direction * direction if squares is None else squares + direction * direction
 
-    def first(group, carry):
-        gathered = matmul_gather(group, [new_at_slot_ref[k] for k in range(CP)], place_slot_ref,
-                                 lambda row: slot_place(slot_ref[pl.ds(row, 1), :], sizes)[0], sizes.pts,
-                                 picked_ref, found_ref)
+    for group in range(rows // SUB):
+        high, low = slot_place(slot_ref[group * SUB : (group + 1) * SUB, :], sizes)
+        gathered = gather_rows(lambda c, k: new_at_slot_ref[c, k : k + 1, :], sizes.pts, high, low, CP)
         q = [sum(at(a_ref, i * CP + k, group) * gathered[k] for k in range(CP)) for i in range(2)]
         for i in range(2):
-            q_ref[pl.ds(pl.multiple_of(i * rows + group * SUB, SUB), SUB), :] = q[i]
+            q_ref[i * rows + group * SUB : i * rows + (group + 1) * SUB, :] = q[i]
         values = [at(b_ref, k, group) * q[0] + at(b_ref, 3 + k, group) * q[1] for k in range(3)]
         parts = [part for value in values for part in cut(value)]
-        keep_parts(parts, parts_ref)
+        keep_parts(parts, group, parts_ref)
         for s in range(SUB):
             row = group * SUB + s
-            spread_row(row, part_rows(len(parts), s, parts_ref), point_ref[pl.ds(row, 1), :] >> 8, PT_HI, spread_ref)
-        return carry
-
-    lax.fori_loop(0, rows // SUB, first, 0)
+            spread_row(row, part_rows(len(parts), group, s, parts_ref), point_ref[row : row + 1, :] >> 8, PT_HI, spread_ref)
     result = scatter(3 * PIECES, sizes.obs, PT_HI, PT_LO, spread_ref, place_point_ref)
     sums = joined(result, 3, PT_HI)
     folded = solve([inv_ref[k] for k in range(6)], sums)
     for k in range(3):
-        table_ref[k] = folded[k]
         new_sum_ref[k] = sums[k]
         if not start:
             new_grad_ref[k] = grad_ref[k] + step_ref[:1, :1] * sum_ref[k]
 
-    def second(group, inner):
-        at_point = matmul_gather(group, [table_ref[k] for k in range(3)], place_point_ref,
-                                 lambda row: point_ref[pl.ds(row, 1), :] >> 8, PT_HI, picked_ref, found_ref)
+    inner = None
+    picking = gather_factors(folded)
+    for group in range(rows // SUB):
+        at_point = matmul_gather(group, picking, 3, place_point_ref,
+                                 lambda row: point_ref[row : row + 1, :] >> 8, PT_HI, picked_ref, found_ref)
         q = [at(q_ref, i, group) for i in range(2)]
         errors = [q[i] - sum(at(b_ref, 3 * i + k, group) * at_point[k] for k in range(3)) for i in range(2)]
-        inner = inner + q[0] * errors[0] + q[1] * errors[1]
+        here = q[0] * errors[0] + q[1] * errors[1]
+        inner = here if inner is None else inner + here
         if not last:
             values = [at(a_ref, k, group) * errors[0] + at(a_ref, CP + k, group) * errors[1] for k in range(CP)]
             parts = [part for value in values for part in cut(value)]
-            keep_parts(parts, parts_ref)
+            keep_parts(parts, group, parts_ref)
             for s in range(SUB):
                 row = group * SUB + s
-                high, _ = slot_place(slot_ref[pl.ds(row, 1), :], sizes)
-                spread_row(row, part_rows(len(parts), s, parts_ref), high, sizes.pts, spread_ref)
-        return inner
-
-    inner = lax.fori_loop(0, rows // SUB, second, jnp.zeros((SUB, LANES), f32))
+                high, low = slot_place(slot_ref[row : row + 1, :], sizes)
+                spread_row(row, part_rows(len(parts), group, s, parts_ref), high, sizes.pts, spread_ref)
+                place_row(row, low, LANES, place_slot_ref)
     partial = jnp.sum(inner, keepdims=True) + damping_camera * jnp.sum(squares, keepdims=True)
     if last:
         out_ref[...] = jnp.broadcast_to(partial, (sizes.devices, LANES))
@@ -559,21 +553,23 @@
     messages = kept(sizes.devices * sizes.message, LANES)
     scalar = kept(SUB, LANES)
     owned_scratch = pltpu.VMEM((CP, sizes.own_rows, LANES), f32)
-    point_scratch = pltpu.VMEM((3, PT_HI, PT_LO), f32)
     entries = sizes.pts * LANES
 
-    picked_rows = max(CP * PIECES * sizes.pts, 3 * PIECES * PT_HI)
-    gather_scratch = [pltpu.VMEM((picked_rows, SUB * LANES), bf16), pltpu.VMEM((2 * SUB * SUB, LANES), f32)]
+    gather_scratch = [
+        pltpu.VMEM((3 * PIECES * PT_HI, sizes.obs), bf16),
+        pltpu.VMEM((rows * SUB, LANES), f32),
+        pltpu.VMEM((LANES, sizes.obs), bf16),
+    ]
 
     def parts_scratch(count):
-        return pltpu.VMEM((count * SUB, LANES), f32)
+        return pltpu.VMEM((rows // SUB, count * SUB, LANES), f32)
 
 
     given = [
         pltpu.with_memory_space_constraint(value, pltpu.HBM)
         for value in (camera_jacobian, point_jacobian, residual, slot, point, send_list[0])
     ]
-    first, a, b, inverse, gradient, place_point, place_slot, slot, point = call(
+    first, a, b, inverse, gradient, place_point, slot, point = call(
         functools.partial(setup_kernel, sizes),
         "setup",
         given,
@@ -584,14 +580,13 @@
             kept(6, PT_HI, PT_LO),
             point_table,
             kept(PT_LO, sizes.obs, dtype=bf16),
-            kept(LANES, sizes.obs, dtype=bf16),
             kept(rows, LANES, dtype=jnp.int32),
             kept(rows, LANES, dtype=jnp.int32),
         ],
-        [pltpu.VMEM((2 * rows, LANES), f32), point_scratch, parts_scratch(2 * CP * PIECES)]
+        [pltpu.VMEM((2 * rows, LANES), f32), parts_scratch(2 * CP * PIECES)]
         + [pltpu.VMEM((max(spread_rows(6 * FINE + 3 * PIECES, PT_HI), spread_rows(2 * CP * PIECES, sizes.pts)), sizes.obs), bf16)]
+        + gather_scratch
         + [pltpu.VMEM((LANES, sizes.cams * sizes.slot), bf16)]
-        + gather_scratch
         + [pltpu.VMEM(value.shape, value.dtype) for value in given]
         + [pltpu.SemaphoreType.DMA((len(given),))],
         inputs_at=pl.ANY,
@@ -604,7 +599,7 @@
         [owned_scratch] + factors(spread_rows(2 * CP * PIECES, sizes.own_rows), LANES, entries),
         scalars=[column],
     )
-    schur_scratch = [pltpu.VMEM((2 * rows, LANES), f32), point_scratch, parts_scratch(CP * PIECES)]
+    schur_scratch = [pltpu.VMEM((2 * rows, LANES), f32), parts_scratch(CP * PIECES)]
     schur_scratch += [pltpu.VMEM((max(spread_rows(3 * PIECES, PT_HI), spread_rows(CP * PIECES, sizes.pts)), sizes.obs), bf16)]
     schur_scratch += gather_scratch
     at_slot = kept(CP, sizes.pts, LANES)
@@ -629,7 +624,7 @@
         results = call(
             functools.partial(schur_kernel, sizes, start, last),
             "schur_last" if last else "schur",
-            [arrived, a, b, inverse, slot, point, place_point, place_slot, precondition, remainder, gradient]
+            [arrived, a, b, inverse, slot, point, place_point, precondition, remainder, gradient]
             + earlier,
             [kept(sizes.devices, LANES) if last else messages, scalar, at_slot, owned, point_table]
             + ([] if start else [point_table]),

time: 106 us -> 100 us (0.943)
  Pallas kernels: 26.9 us -> 21.6 us
  local copies, waits for them, and re-layouts: 2.19 us -> 0 us
  waiting for transfers between devices: 18.3 us -> 19.7 us
    pallas_call x9, Pallas kernels: 26.9 us -> 21.6 us  [call(): pl.pallas_call(kernel, name=name, out_shape=outputs, in_specs=[smem] * le...]
    unnamed x4 -> x0, local copies, waits for them, and re-layouts: 2.19 us -> none
    ppermute x4, waiting for transfers between devices: 3.37 us -> 4.72 us  [flipped(): return lax.ppermute(value, 'pts', [(p, p ^ flip) for p in range(sizes.pts)])]
  transfers between devices with their start and end apart: 6 -> 6, of which waited for: 3 -> 3; matrix products, arithmetic and copies ran while one was open for 0% -> 0% of each run, Pallas kernels for 5% -> 3%
where the time goes in v7:
time: 100 us; the launch traced here: 99.8 us
  blocking collectives  45.1 us (45%)
  Pallas kernels  21.6 us (22%)
  waiting for transfers between devices  19.7 us (20%)
  starting transfers between devices  12.8 us (13%)
    all_to_all x5, blocking collectives, exchange(): lax.all_to_all(flat, axes, split_axis=0, concat_axis=0, tiled=True)  45.1 us
    pallas_call x9, Pallas kernels, call(): pl.pallas_call(kernel, name=name, out_shape=outputs, in_specs=[smem] * le...  21.6 us
    all_to_all x2, waiting for transfers between devices, exchange(): lax.all_to_all(flat, axes, split_axis=0, concat_axis=0, tiled=True)  14.9 us
    all_to_all x2, starting transfers between devices, exchange(): lax.all_to_all(flat, axes, split_axis=0, concat_axis=0, tiled=True)  9.83 us
    ppermute x4, waiting for transfers between devices, flipped(): return lax.ppermute(value, 'pts', [(p, p ^ flip) for p in range(sizes.pts)])  4.72 us
    ppermute x4, starting transfers between devices, flipped(): return lax.ppermute(value, 'pts', [(p, p ^ flip) for p in range(sizes.pts)])  2.93 us
  transfers between devices with their start and end apart: 6, of which 3 were waited for; matrix products, arithmetic and copies ran while one was open for 0% of the time, Pallas kernels for 3%

profile of v7, /device:TPU:0, one launch (start us, length us, event | category | flops | bytes accessed | tf_op | source)
XLA Modules:
  0.0 99.8 jit_solution(13119777405737400812)
XLA Ops:
  0.6 7.5 %setup.1 = (f32[192,128]{1,0:T(8,128)}, f32[576,128]{1,0:T(8,128)S(1)}, f32[192,128]{1,0:T(8,128)S(1)}, f32[6,16,256]{2,1,0:T(8,128)S(1)}, f32[3,16,256]{2,1,0:T...) custom-call(f32[18,4096]{1,0:T(8,128)} %refs_0_.1, f32[6,4096]{1,0:T(8,128)} %refs_1_.1, ...), custom_call_target="tpu_custom_call" | custom-call | tf_op jit(solution)/shard_map/setup/pallas_call | solution.py:520
  8.2 7.3 %all-to-all-start = ((f32[32,1,768]{2,1,0:T(1,128)}), f32[32,1,768]{2,1,0:T(1,128)S(1)}, u32[]{:S(2)}, u32[]{:S(2)}) async-start(f32[32,1,768]{2,1,0:T(1,128)} %bitcast.5), calls=%async_computation | async-start | bytes 196608 | tf_op jit(solution)/shard_map/all_to_all | solution.py:543
  15.5 7.8 %all-to-all-done = f32[32,1,768]{2,1,0:T(1,128)S(1)} async-done(((f32[32,1,768]{2,1,0:T(1,128)}), f32[32,1,768]{2,1,0:T(1,128)S(1)}, u32[]{:S(2)}, u32[]{:S(2)}) %all-to-all-start) | async-done | bytes 98336 | tf_op jit(solution)/shard_map/all_to_all | solution.py:543
  23.3 0.7 first_owner.1
  24.0 9.0 %all_to_all.35 = f32[32,1,384]{2,1,0:T(1,128)S(1)} all-to-all(f32[32,1,384]{2,1,0:T(1,128)S(1)} %bitcast.31), channel_id=1, replica_groups=mesh['pts'=8,'cams'=4] {'pts','cams'}, dimensions={0} | all-to-all | bytes 98304 | tf_op jit(solution)/shard_map/all_to_all | solution.py:543
  33.0 3.5 %schur.2 = (f32[96,128]{1,0:T(8,128)S(1)}, f32[8,128]{1,0:T(8,128)S(1)}, f32[9,8,128]{2,1,0:T(8,128)S(1)}, f32[9,8,128]{2,1,0:T(8,128)S(1)}, f32[3,16,256]{2,1,0:T(8,128)S(1)}) custom-call(f32[96,128]{1,0:T(8,128)S(1)} %bitcast.30, f32[576,128]{1,0:T(8,128)S(1)} %get-tuple-element.41.a_ref, f32[192,128]{1,0:T(8,128)S(1)} %get-tuple-element.42.b_ref, ...), custom_call_target="tpu_custom_call" | custom-call | flops 2000000000 | bytes 10000000 | tf_op jit(solution)/shard_map/schur/pallas_call | solution.py:520
  36.6 9.0 %all_to_all.36 = f32[32,1,384]{2,1,0:T(1,128)S(1)} all-to-all(f32[32,1,384]{2,1,0:T(1,128)S(1)} %bitcast.32), channel_id=1, replica_groups=mesh['pts'=8,'cams'=4] {'pts','cams'}, dimensions={0} | all-to-all | bytes 98304 | tf_op jit(solution)/shard_map/all_to_all | solution.py:543
  45.6 0.6 owner.1
  46.2 9.0 %all_to_all.37 = f32[32,1,384]{2,1,0:T(1,128)S(1)} all-to-all(f32[32,1,384]{2,1,0:T(1,128)S(1)} %bitcast.33), channel_id=1, replica_groups=mesh['pts'=8,'cams'=4] {'pts','cams'}, dimensions={0} | all-to-all | bytes 98304 | tf_op jit(solution)/shard_map/all_to_all | solution.py:543
  55.2 3.6 %schur.3 = (f32[96,128]{1,0:T(8,128)S(1)}, f32[8,128]{1,0:T(8,128)S(1)}, f32[9,8,128]{2,1,0:T(8,128)S(1)}, f32[9,8,128]{2,1,0:T(8,128)S(1)}, f32[3,16,256]{2,1,0:T(8,128)S(1)}, /*index=5*/f32[3,16,256]{2,1,0:T(8,128)S(1)}) custom-call(f32[96,128]{1,0:T(8,128)S(1)} %bitcast.27, f32[576,128]{1,0:T(8,128)S(1)} %get-tuple-element.41.a_ref, ...), custom_call_target="tpu_custom_call" | custom-call | flops 2000000000 | bytes 10000000 | tf_op jit(solution)/shard_map/schur/pallas_call | solution.py:520
  58.8 9.0 %all_to_all.38 = f32[32,1,384]{2,1,0:T(1,128)S(1)} all-to-all(f32[32,1,384]{2,1,0:T(1,128)S(1)} %bitcast.28), channel_id=1, replica_groups=mesh['pts'=8,'cams'=4] {'pts','cams'}, dimensions={0} | all-to-all | bytes 98304 | tf_op jit(solution)/shard_map/all_to_all | solution.py:543
  67.8 1.0 owner_final.1
  68.8 0.6 collective-permute-start
  69.4 9.0 %all_to_all.39 = f32[32,1,384]{2,1,0:T(1,128)S(1)} all-to-all(f32[32,1,384]{2,1,0:T(1,128)S(1)} %bitcast.29), channel_id=1, replica_groups=mesh['pts'=8,'cams'=4] {'pts','cams'}, dimensions={0} | all-to-all | bytes 98304 | tf_op jit(solution)/shard_map/all_to_all | solution.py:543
  78.4 0.0 collective-permute-done.other_ref
  78.4 0.1 tail.1.refs_0_
  78.5 0.7 collective-permute-start.1
  79.2 3.5 %schur_last.1 = (f32[32,128]{1,0:T(8,128)}, f32[8,128]{1,0:T(8,128)S(1)}, f32[9,8,128]{2,1,0:T(8,128)}, f32[9,8,128]{2,1,0:T(8,128)}, f32[3,16,256]{2,1,0:T(8,128)S(1)}, /*index=5*/f32[3,16,256]{2,1,0:T(8,128)S(1)}) custom-call(f32[96,128]{1,0:T(8,128)S(1)} %bitcast.23, f32[576,128]{1,0:T(8,128)S(1)} %get-tuple-element.41.a_ref, ...), custom_call_target="tpu_custom_call" | custom-call | flops 2000000000 | bytes 10000000 | tf_op jit(solution)/shard_map/schur_last/pallas_call | solution.py:520
  82.7 0.6 collective-permute-start.2
  83.3 4.7 %collective-permute-done.1.refs_1_ = f32[288,128]{1,0:T(8,128)S(1)} collective-permute-done((f32[288,128]{1,0:T(8,128)S(1)}, f32[288,128]{1,0:T(8,128)S(1)}, u32[]{:S(2)}, u32[]{:S(2)}) %collective-permute-start.1) | collective-permute-done | bytes 147488 | tf_op jit(solution)/shard_map/ppermute | solution.py:546
  88.0 1.0 %collective-permute-start.3 = (f32[288,128]{1,0:T(8,128)S(1)}, f32[288,128]{1,0:T(8,128)S(1)}, u32[]{:S(2)}, u32[]{:S(2)}) collective-permute-start(f32[288,128]{1,0:T(8,128)S(1)} %collective-permute-done.1.refs_1_), channel_id=1, source_target_pairs={{0,4},{4,0},{8,12},{12,8},{16,20},{20,16},{24,28},{28,24},{1,5},{5... | collective-permute-start | bytes 442376 | tf_op jit(solution)/shard_map/ppermute | solution.py:546
  89.1 2.5 %all-to-all-start.6 = ((f32[32,1,128]{2,1,0:T(1,128)}), f32[32,1,128]{2,1,0:T(1,128)S(1)}, u32[]{:S(2)}, u32[]{:S(2)}) async-start(f32[32,1,128]{2,1,0:T(1,128)} %bitcast.18), calls=%async_computation.6 | async-start | bytes 32768 | tf_op jit(solution)/shard_map/all_to_all | solution.py:543
  91.6 7.1 %all-to-all-done.6 = f32[32,1,128]{2,1,0:T(1,128)S(1)} async-done(((f32[32,1,128]{2,1,0:T(1,128)}), f32[32,1,128]{2,1,0:T(1,128)S(1)}, u32[]{:S(2)}, u32[]{:S(2)}) %all-to-all-start.6) | async-done | bytes 16416 | tf_op jit(solution)/shard_map/all_to_all | solution.py:543
  98.7 1.1 %final.1 = (f32[9,8192]{1,0:T(8,128)}, f32[3,4096]{1,0:T(4,128)}) custom-call(s32[1]{0:T(128)} %bitcast.run_ref, f32[32,128]{1,0:T(8,128)S(1)} %bitcast.26, f32[8,128]{1,0:T(8,128)S(1)} %get-tuple-element.72.product_ref, f32[6,16,256]{2,1,0:T(8,128)S(1)} %get-tuple-element.43.inv_ref, f32[3,16,256]{2,1,0:T(8,128)S(1)} %get-tuple-element.73.grad_ref, ...), custom_call_target="tpu_custom_call" | custom-call | tf_op jit(solution)/shard_map/final/pallas_call | solution.py:520
  (2 shorter events, 0.0 us)
Async XLA Ops:
  8.2 15.1 %all-to-all-start = ((f32[32,1,768]{2,1,0:T(1,128)}), f32[32,1,768]{2,1,0:T(1,128)S(1)}, u32[]{:S(2)}, u32[]{:S(2)}) async-start(f32[32,1,768]{2,1,0:T(1,128)} %bitcast.5), calls=%async_computation | async-start | bytes 196608 | tf_op jit(solution)/shard_map/all_to_all | solution.py:543
  68.8 9.6 %collective-permute-start = (f32[216,128]{1,0:T(8,128)S(1)}, f32[216,128]{1,0:T(8,128)S(1)}, u32[]{:S(2)}, u32[]{:S(2)}) collective-permute-start(f32[216,128]{1,0:T(8,128)S(1)} %get-tuple-element.64.own_ref), channel_id=1, source_target_pairs={{0,8},{4,12},{8,0},{12,4},{16,24},{20,28},{24,16},{28,20},{1,9},{5... | collective-permute-start | bytes 331784 | tf_op jit(solution)/shard_map/ppermute | solution.py:546
  78.5 9.5 %collective-permute-start.1 = (f32[288,128]{1,0:T(8,128)S(1)}, f32[288,128]{1,0:T(8,128)S(1)}, u32[]{:S(2)}, u32[]{:S(2)}) collective-permute-start(f32[288,128]{1,0:T(8,128)S(1)} %tail.1.refs_0_), channel_id=1, source_target_pairs={{0,16},{4,20},{8,24},{12,28},{16,0},{20,4},{24,8},{28,12},{1,17},{... | collective-permute-start | bytes 442376 | tf_op jit(solution)/shard_map/ppermute | solution.py:546
  82.7 8.9 %collective-permute-start.2 = (f32[288,128]{1,0:T(8,128)S(1)}, f32[288,128]{1,0:T(8,128)S(1)}, u32[]{:S(2)}, u32[]{:S(2)}) collective-permute-start(f32[288,128]{1,0:T(8,128)S(1)} %tail.1.refs_0_), channel_id=1, source_target_pairs={{0,4},{4,0},{8,12},{12,8},{16,20},{20,16},{24,28},{28,24},{1,5},{5... | collective-permute-start | bytes 442376 | tf_op jit(solution)/shard_map/ppermute | solution.py:546
  88.0 10.7 %collective-permute-start.3 = (f32[288,128]{1,0:T(8,128)S(1)}, f32[288,128]{1,0:T(8,128)S(1)}, u32[]{:S(2)}, u32[]{:S(2)}) collective-permute-start(f32[288,128]{1,0:T(8,128)S(1)} %collective-permute-done.1.refs_1_), channel_id=1, source_target_pairs={{0,4},{4,0},{8,12},{12,8},{16,20},{20,16},{24,28},{28,24},{1,5},{5... | collective-permute-start | bytes 442376 | tf_op jit(solution)/shard_map/ppermute | solution.py:546
  89.1 9.7 %all-to-all-start.6 = ((f32[32,1,128]{2,1,0:T(1,128)}), f32[32,1,128]{2,1,0:T(1,128)S(1)}, u32[]{:S(2)}, u32[]{:S(2)}) async-start(f32[32,1,128]{2,1,0:T(1,128)} %bitcast.18), calls=%async_computation.6 | async-start | bytes 32768 | tf_op jit(solution)/shard_map/all_to_all | solution.py:543

commit v8 on v7

--- a/solution.py
+++ b/solution.py
@@ -86,33 +86,6 @@
     return result
 
 
-def gather_factors(tables):
-    pieces = [piece for table in tables for piece in cut(table)]
-    left = jnp.concatenate(pieces, axis=0).astype(bf16)
-    padded, rows = -(-len(tables) // SUB) * SUB, left.shape[0]
-    owner = lax.broadcasted_iota(jnp.int32, (padded, rows), 1) // (rows // len(tables))
-    chosen = (owner == lax.broadcasted_iota(jnp.int32, (padded, rows), 0)).astype(f32).astype(bf16)
-    return left, chosen
-
-
-def matmul_gather(group, factors, count, place_ref, high_of_row, high_count, picked_ref, found_ref):
-    left, chosen = factors
-    rows, padded = left.shape[0], chosen.shape[0]
-    width = SUB * LANES
-    picked = jnp.dot(left, place_ref[:, group * width : (group + 1) * width], preferred_element_type=f32)
-    for s in range(SUB):
-        mask = jnp.broadcast_to(high_of_row(group * SUB + s), (high_count, LANES)) == sub_iota(high_count)
-        for first in range(0, rows, high_count):
-            block = picked[first : first + high_count, s * LANES : (s + 1) * LANES]
-            columns = slice(group * width + s * LANES, group * width + (s + 1) * LANES)
-            picked_ref[first : first + high_count, columns] = jnp.where(mask, block, 0.0).astype(bf16)
-    total = jnp.dot(chosen, picked_ref[:rows, group * width : (group + 1) * width], preferred_element_type=f32)
-    start = group * SUB * padded
-    for s in range(SUB):
-        found_ref[start + s * padded : start + (s + 1) * padded, :] = total[:, s * LANES : (s + 1) * LANES]
-    return [found_ref[pl.ds(start + c, SUB, stride=padded), :] for c in range(count)]
-
-
 def spread_row(index, parts, high, high_count, spread_ref):
     columns = slice(index * LANES, (index + 1) * LANES)
     mask = jnp.broadcast_to(high, (high_count, LANES)) == sub_iota(high_count)
@@ -170,6 +143,12 @@
     return values
 
 
+def point_gather(ref, point):
+    wide = PT_LO // LANES
+    row = lambda c, k: ref[c, k // wide : k // wide + 1, (k % wide) * LANES : (k % wide + 1) * LANES]
+    return gather_rows(row, PT_HI * wide, point // LANES, point % LANES, 3)
+
+
 def slot_place(slot, sizes):
     within = slot % sizes.slot
     return within % sizes.pts, (slot // sizes.slot) * sizes.block + within // sizes.pts
@@ -182,24 +161,39 @@
     return first, second, third
 
 
-def write_messages(fields, scalar, groups, message, out_ref, sizes, extra=None):
-    which = lane_iota(sizes.pts) // sizes.block
-    for g in range(groups):
-        rows = fields[g * sizes.cams : (g + 1) * sizes.cams]
-        moved = swap_partial(rows, sizes)
-        for c in range(sizes.cams):
-            value = moved[c]
+def write_messages(fields, scalar, groups, message, out_refs, column, sizes, extra=None):
+    last = lane_iota(sizes.pts) // sizes.block == sizes.cams - 1
+    for g in range(message):
+        if g < groups:
+            rows = swap_blocks(fields[g * sizes.cams : (g + 1) * sizes.cams], sizes.block, sizes.cams)
             if g == groups - 1 and scalar is not None:
-                value = jnp.where(which == sizes.cams - 1, scalar, value)
-            out_ref[pl.ds(c * message + g, sizes.pts, stride=sizes.cams * message), :] = value
-    for g in range(groups, message):
-        for c in range(sizes.cams):
-            value = extra if (extra is not None and g == groups) else jnp.zeros((sizes.pts, LANES), f32)
-            out_ref[pl.ds(c * message + g, sizes.pts, stride=sizes.cams * message), :] = value
-
-
-def swap_partial(rows, sizes):
-    return swap_blocks(rows, sizes.block, sizes.cams)
+                rows = [jnp.where(last, scalar, row) for row in rows]
+            bit = 1
+            while bit < sizes.cams:
+                odd = (column & bit) != 0
+                rows = [jnp.where(odd, rows[f ^ bit], rows[f]) for f in range(sizes.cams)]
+                bit *= 2
+        else:
+            rows = [extra] * sizes.cams
+        for row, out_ref in zip(rows, out_refs):
+            out_ref[pl.ds(g, sizes.pts, stride=message), :] = row
+
+
+def regroup_kernel(sizes, message, run_ref, *refs):
+    in_refs, out_refs = refs[: sizes.cams], refs[sizes.cams :]
+    for g, out_ref in enumerate(out_refs):
+        first = (run_ref[0] ^ g) * message
+        for f, in_ref in enumerate(in_refs):
+            for k in range(message):
+                out_ref[f * message + k : f * message + k + 1, :] = in_ref[pl.ds(first + k, 1), :]
+
+
+def sort_messages(in_refs, run, column, message, out_ref, sizes):
+    for g, in_ref in enumerate(in_refs):
+        for f in range(sizes.cams):
+            first = ((run ^ g) * sizes.cams + (column ^ f)) * message
+            for k in range(message):
+                out_ref[pl.ds(first + k, 1), :] = in_ref[f * message + k : f * message + k + 1, :]
 
 
 def read_row(in_ref, c, g, message, sizes):
@@ -224,16 +218,18 @@
     return jnp.sum(chosen, keepdims=True)
 
 
-def setup_kernel(sizes, *refs):
+def setup_kernel(sizes, column_ref, *refs):
     sources, refs = refs[:6], refs[6:]
-    out_ref, a_ref, b_ref, inv_ref, grad_ref, place_point_ref, new_slot_ref, new_point_ref = refs[:8]
-    r_ref, parts_ref, spread_ref, picked_ref, found_ref, place_slot_ref, place_list_ref = refs[8:15]
-    jac_ref, pjac_ref, res_ref, slot_ref, point_ref, list_ref = refs[15:21]
-    semaphores = refs[21]
+    out_refs, refs = refs[: sizes.cams], refs[sizes.cams :]
+    a_ref, b_ref, inv_ref, grad_ref, place_point_ref, new_slot_ref, new_point_ref = refs[:7]
+    refs = refs[7:]
+    r_ref, parts_ref, spread_ref, table_ref, place_slot_ref, place_list_ref = refs[:6]
+    jac_ref, pjac_ref, res_ref, slot_ref, point_ref, list_ref = refs[6:12]
+    semaphores = refs[12]
     rows = sizes.rows
     copies = [
         pltpu.make_async_copy(source, target, semaphores.at[k])
-        for k, (source, target) in enumerate(zip(sources, refs[15:21]))
+        for k, (source, target) in enumerate(zip(sources, refs[6:12]))
     ]
     for copy in copies:
         copy.start()
@@ -289,10 +285,10 @@
     for k in range(3):
         grad_ref[k] = normal[6 + k]
     eliminated = solve(inverse, normal[6:])
-    picking = gather_factors(eliminated)
+    for k in range(3):
+        table_ref[k] = eliminated[k]
     for group in range(rows // SUB):
-        at_point = matmul_gather(group, picking, 3, place_point_ref,
-                                 lambda row: point_ref[row : row + 1, :] >> 8, PT_HI, picked_ref, found_ref)
+        at_point = point_gather(table_ref, point_ref[group * SUB : (group + 1) * SUB, :])
         b = [at(b_ref, k, group) for k in range(6)]
         errors = [at(r_ref, i, group) - sum(b[3 * i + k] * at_point[k] for k in range(3)) for i in range(2)]
         a = [at(a_ref, k, group) for k in range(2 * CP)]
@@ -319,7 +315,7 @@
             place_row(c * pieces + half, low, LANES, place_list_ref)
     result = scatter(2, sizes.cams * sizes.slot, sizes.pts, LANES, spread_ref, place_list_ref)
     listed = result[: sizes.pts] * 256.0 + result[sizes.pts : 2 * sizes.pts]
-    write_messages(fields, None, sizes.first_groups, sizes.first_message, out_ref, sizes, extra=listed)
+    write_messages(fields, None, sizes.first_groups, sizes.first_message, out_refs, column_ref[0], sizes, extra=listed)
 
 
 def entries_scatter(fields, entry, sizes, spread_ref, place_ref):
@@ -332,19 +328,22 @@
     return joined(result, len(fields), sizes.own_rows)
 
 
-def send_owned(scaled, partial, entry, out_ref, table_ref, sizes):
+def send_owned(scaled, partial, entry, out_refs, column, table_ref, sizes):
     for k in range(CP):
         table_ref[k] = scaled[k]
     fields = gather_rows(lambda c, k: table_ref[c, k : k + 1, :], sizes.run_rows, entry // LANES, entry % LANES, CP)
-    write_messages(fields, partial, sizes.groups, sizes.message, out_ref, sizes)
+    write_messages(fields, partial, sizes.groups, sizes.message, out_refs, column, sizes)
 
 
 def dot_fields(left, right):
     return jnp.sum(sum(a * b for a, b in zip(left, right)), keepdims=True)
 
 
-def first_owner_kernel(sizes, column_ref, in_ref, out_ref, entry_ref, pre_ref, rem_ref,
-                       table_ref, spread_ref, place_ref):
+def first_owner_kernel(sizes, run_ref, column_ref, *refs):
+    in_refs, refs = refs[: sizes.pts], refs[sizes.pts :]
+    out_refs, refs = refs[: sizes.cams], refs[sizes.cams :]
+    entry_ref, pre_ref, rem_ref, table_ref, spread_ref, place_ref, in_ref = refs
+    sort_messages(in_refs, run_ref[0], column_ref[0], sizes.first_message, in_ref, sizes)
     listed = jnp.zeros((sizes.pts, LANES), f32)
     for c in range(sizes.cams):
         row = read_row(in_ref, c, sizes.first_groups, sizes.first_message, sizes)
@@ -359,15 +358,19 @@
     for k in range(CP):
         pre_ref[k] = precondition[k]
         rem_ref[k] = remainder[k]
-    send_owned(scaled, dot_fields(remainder, scaled), entry, out_ref, table_ref, sizes)
-
-
-def owner_kernel(sizes, start, final, in_ref, entry_ref, pre_ref, rem_ref, dir_ref, product_ref, *refs):
-    refs = list(refs)
+    send_owned(scaled, dot_fields(remainder, scaled), entry, out_refs, column_ref[0], table_ref, sizes)
+
+
+def owner_kernel(sizes, start, final, run_ref, column_ref, *refs):
+    in_refs, refs = refs[: sizes.pts], refs[sizes.pts :]
+    entry_ref, pre_ref, rem_ref, dir_ref, product_ref = refs[:5]
+    refs = list(refs[5:])
     sol_ref = None if start else refs.pop(0)
-    out_ref, new_rem_ref, new_sol_ref, step_ref = refs[:4]
-    fields_ref = refs[4] if final else None
-    table_ref, spread_ref, place_ref = refs[-3:]
+    out_refs, refs = refs[: sizes.cams], refs[sizes.cams :]
+    new_rem_ref, new_sol_ref, step_ref = refs[:3]
+    fields_ref = refs[3] if final else None
+    table_ref, spread_ref, place_ref, in_ref = refs[-4:]
+    sort_messages(in_refs, run_ref[0], column_ref[0], sizes.message, in_ref, sizes)
     entry = entry_ref[...]
     fields = read_messages(in_ref, CP, sizes.message, sizes)
     curvature = read_scalar(in_ref, sizes.groups, sizes.message, sizes)
@@ -388,22 +391,26 @@
             for j, field in enumerate((moved, direction, scaled[k])):
                 first = (j * CP + k) * sizes.own_rows
                 fields_ref[first : first + sizes.own_rows, :] = field
-    send_owned(scaled, dot_fields(remainder, scaled), entry, out_ref, table_ref, sizes)
-
-
-def schur_kernel(sizes, start, last, in_ref, a_ref, b_ref, inv_ref, slot_ref, point_ref,
-                 place_point_ref, pre_ref, rem_ref, grad_ref, *refs):
-    refs = list(refs)
+    send_owned(scaled, dot_fields(remainder, scaled), entry, out_refs, column_ref[0], table_ref, sizes)
+
+
+def schur_kernel(sizes, start, last, run_ref, column_ref, *refs):
+    in_refs, refs = refs[: sizes.pts], list(refs[sizes.pts :])
+    a_ref, b_ref, inv_ref, slot_ref, point_ref, place_point_ref, pre_ref, rem_ref, grad_ref = refs[:9]
+    refs = refs[9:]
     if not start:
         product_ref, at_slot_ref, dir_ref, step_ref, sum_ref = refs[:5]
         refs = refs[5:]
-    out_ref, new_product_ref, new_at_slot_ref, new_dir_ref, new_sum_ref = refs[:5]
+    out_count = 1 if last else sizes.cams
+    out_refs, refs = refs[:out_count], refs[out_count:]
+    new_product_ref, new_at_slot_ref, new_dir_ref, new_sum_ref = refs[:4]
     new_grad_ref = None
-    refs = refs[5:]
+    refs = refs[4:]
     if not start:
         new_grad_ref = refs.pop(0)
-    q_ref, parts_ref, spread_ref, picked_ref, found_ref, place_slot_ref = refs
+    q_ref, parts_ref, spread_ref, table_ref, place_slot_ref, in_ref = refs
     rows = sizes.rows
+    sort_messages(in_refs, run_ref[0], column_ref[0], sizes.message, in_ref, sizes)
 
     def at(ref, comp, group):
         return ref[comp * rows + group * SUB : comp * rows + (group + 1) * SUB, :]
@@ -444,10 +451,10 @@
             new_grad_ref[k] = grad_ref[k] + step_ref[:1, :1] * sum_ref[k]
 
     inner = None
-    picking = gather_factors(folded)
+    for k in range(3):
+        table_ref[k] = folded[k]
     for group in range(rows // SUB):
-        at_point = matmul_gather(group, picking, 3, place_point_ref,
-                                 lambda row: point_ref[row : row + 1, :] >> 8, PT_HI, picked_ref, found_ref)
+        at_point = point_gather(table_ref, point_ref[group * SUB : (group + 1) * SUB, :])
         q = [at(q_ref, i, group) for i in range(2)]
         errors = [q[i] - sum(at(b_ref, 3 * i + k, group) * at_point[k] for k in range(3)) for i in range(2)]
         here = q[0] * errors[0] + q[1] * errors[1]
@@ -463,14 +470,17 @@
                 place_row(row, low, LANES, place_slot_ref)
     partial = jnp.sum(inner, keepdims=True) + damping_camera * jnp.sum(squares, keepdims=True)
     if last:
-        out_ref[...] = jnp.broadcast_to(partial, (sizes.devices, LANES))
+        out_refs[0][...] = jnp.broadcast_to(partial, (SUB, LANES))
         return
     result = scatter(CP * PIECES, sizes.obs, sizes.pts, LANES, spread_ref, place_slot_ref)
     fields = joined(result, CP, sizes.pts)
-    write_messages(fields, partial, sizes.groups, sizes.message, out_ref, sizes)
-
-
-def tail_kernel(sizes, in_ref, product_ref, own_ref, other_ref, out_ref):
+    write_messages(fields, partial, sizes.groups, sizes.message, out_refs, column_ref[0], sizes)
+
+
+def tail_kernel(sizes, run_ref, column_ref, *refs):
+    in_refs, refs = refs[: sizes.pts], refs[sizes.pts :]
+    product_ref, own_ref, other_ref, out_ref, in_ref = refs
+    sort_messages(in_refs, run_ref[0], column_ref[0], sizes.message, in_ref, sizes)
     renewed = jnp.broadcast_to(read_scalar(in_ref, sizes.groups, sizes.message, sizes), (SUB, LANES))
     beta = (renewed / product_ref[...])[:1]
     field = CP * sizes.own_rows
@@ -483,8 +493,7 @@
 def final_kernel(sizes, masks, run_ref, in_ref, product_ref, inv_ref, grad_ref, sum_ref, *refs):
     all_refs = refs[: len(masks)]
     cam_ref, pt_ref, table_ref = refs[len(masks) :]
-    curvature = jnp.sum(jnp.where(lane_iota(sizes.devices) == 0, in_ref[...], 0.0), keepdims=True)
-    step = (product_ref[...] / jnp.broadcast_to(curvature, (SUB, LANES)))[:1]
+    step = (product_ref[...] / in_ref[...])[:1]
     for all_ref, pair in zip(all_refs, masks):
         for j, mask in enumerate(pair):
             base_column = (run_ref[0] ^ mask) * sizes.run
@@ -531,35 +540,40 @@
 
 def body(camera_jacobian, point_jacobian, residual, observed_slot, observed_point, send_list):
     sizes = Sizes(lax.axis_size("pts"), lax.axis_size("cams"), send_list.shape[2], camera_jacobian.shape[1])
-    axes = ("pts", "cams")
     rows = sizes.rows
     slot = observed_slot.reshape(rows, LANES)
     point = observed_point.reshape(rows, LANES)
     column = lax.axis_index("cams").astype(jnp.int32).reshape(1)
-
-    def exchange(messages):
-        width = messages.size // sizes.devices
-        flat = messages.reshape(sizes.devices, 1, width)
-        return lax.all_to_all(flat, axes, split_axis=0, concat_axis=0, tiled=True).reshape(messages.shape)
-
-    def flipped(value, flip):
-        return lax.ppermute(value, "pts", [(p, p ^ flip) for p in range(sizes.pts)])
+    run = lax.axis_index("pts").astype(jnp.int32).reshape(1)
+
+    def flipped(value, flip, axis="pts"):
+        return lax.ppermute(value, axis, [(p, p ^ flip) for p in range(lax.axis_size(axis))])
+
+    def exchange(blocks, message):
+        blocks = [flipped(block, f, "cams") if f else block for f, block in enumerate(blocks)]
+        blocks = call(
+            functools.partial(regroup_kernel, sizes, message),
+            "regroup",
+            blocks,
+            [kept(sizes.cams * message, LANES)] * sizes.pts,
+            [],
+            scalars=[run],
+        )
+        return [flipped(block, g) if g else block for g, block in enumerate(blocks)]
 
     def factors(high_rows, low_rows, entries):
         return [pltpu.VMEM((high_rows, entries), bf16), pltpu.VMEM((low_rows, entries), bf16)]
 
     point_table = kept(3, PT_HI, PT_LO)
     owned = kept(CP, sizes.own_rows, LANES)
-    messages = kept(sizes.devices * sizes.message, LANES)
+    messages = [kept(sizes.pts * sizes.message, LANES)] * sizes.cams
+    inbox = pltpu.VMEM((sizes.devices * sizes.message, LANES), f32)
+    place = [run, column]
     scalar = kept(SUB, LANES)
     owned_scratch = pltpu.VMEM((CP, sizes.own_rows, LANES), f32)
     entries = sizes.pts * LANES
 
-    gather_scratch = [
-        pltpu.VMEM((3 * PIECES * PT_HI, sizes.obs), bf16),
-        pltpu.VMEM((rows * SUB, LANES), f32),
-        pltpu.VMEM((LANES, sizes.obs), bf16),
-    ]
+    gather_scratch = [pltpu.VMEM((3, PT_HI, PT_LO), f32), pltpu.VMEM((LANES, sizes.obs), bf16)]
 
     def parts_scratch(count):
         return pltpu.VMEM((rows // SUB, count * SUB, LANES), f32)
@@ -569,12 +583,12 @@
         pltpu.with_memory_space_constraint(value, pltpu.HBM)
         for value in (camera_jacobian, point_jacobian, residual, slot, point, send_list[0])
     ]
-    first, a, b, inverse, gradient, place_point, slot, point = call(
+    *first, a, b, inverse, gradient, place_point, slot, point = call(
         functools.partial(setup_kernel, sizes),
         "setup",
         given,
-        [
-            kept(sizes.devices * sizes.first_message, LANES),
+        [kept(sizes.pts * sizes.first_message, LANES)] * sizes.cams
+        + [
             kept(2 * CP * rows, LANES),
             kept(6 * rows, LANES),
             kept(6, PT_HI, PT_LO),
@@ -589,19 +603,22 @@
         + [pltpu.VMEM((LANES, sizes.cams * sizes.slot), bf16)]
         + [pltpu.VMEM(value.shape, value.dtype) for value in given]
         + [pltpu.SemaphoreType.DMA((len(given),))],
+        scalars=[column],
         inputs_at=pl.ANY,
     )
-    out, entry, precondition, remainder = call(
+    *out, entry, precondition, remainder = call(
         functools.partial(first_owner_kernel, sizes),
         "first_owner",
-        [exchange(first)],
-        [messages, kept(sizes.pts, LANES, dtype=jnp.int32), owned, owned],
-        [owned_scratch] + factors(spread_rows(2 * CP * PIECES, sizes.own_rows), LANES, entries),
-        scalars=[column],
+        exchange(first, sizes.first_message),
+        messages + [kept(sizes.pts, LANES, dtype=jnp.int32), owned, owned],
+        [owned_scratch]
+        + factors(spread_rows(2 * CP * PIECES, sizes.own_rows), LANES, entries)
+        + [pltpu.VMEM((sizes.devices * sizes.first_message, LANES), f32)],
+        scalars=place,
     )
     schur_scratch = [pltpu.VMEM((2 * rows, LANES), f32), parts_scratch(CP * PIECES)]
     schur_scratch += [pltpu.VMEM((max(spread_rows(3 * PIECES, PT_HI), spread_rows(CP * PIECES, sizes.pts)), sizes.obs), bf16)]
-    schur_scratch += gather_scratch
+    schur_scratch += gather_scratch + [inbox]
     at_slot = kept(CP, sizes.pts, LANES)
     product = slots = direction = step = sums = solution_ = None
     for iteration in range(ITERS):
@@ -609,14 +626,15 @@
         earlier = [] if start else [product, slots, direction, step, sums]
         if last:
             neighbour = flipped(fields, NEAR)
-        arrived = exchange(out)
+        arrived = exchange(out, sizes.message)
         if last:
             (both,) = call(
                 functools.partial(tail_kernel, sizes),
                 "tail",
-                [arrived, product, fields, neighbour],
+                arrived + [product, fields, neighbour],
                 [kept(4 * CP * sizes.own_rows, LANES)],
-                [],
+                [inbox],
+                scalars=place,
             )
             flips = [1 << bit for bit in range(sizes.pts.bit_length() - 1) if 1 << bit != NEAR]
             flips = flips[1:] + flips[:1]
@@ -624,39 +642,50 @@
         results = call(
             functools.partial(schur_kernel, sizes, start, last),
             "schur_last" if last else "schur",
-            [arrived, a, b, inverse, slot, point, place_point, precondition, remainder, gradient]
-            + earlier,
-            [kept(sizes.devices, LANES) if last else messages, scalar, at_slot, owned, point_table]
+            arrived + [a, b, inverse, slot, point, place_point, precondition, remainder, gradient] + earlier,
+            ([scalar] if last else messages) + [scalar, at_slot, owned, point_table]
             + ([] if start else [point_table]),
             schur_scratch,
+            scalars=place,
             cost=pl.CostEstimate(flops=2_000_000_000, bytes_accessed=10_000_000, transcendentals=0),
         )
-        out, product, slots, direction, sums = results[:5]
+        count = 1 if last else sizes.cams
+        out, results = list(results[:count]), results[count:]
+        product, slots, direction, sums = results[:4]
         if not start:
-            gradient = results[5]
+            gradient = results[4]
         if last:
-            early[flips[0]], out = lax.optimization_barrier((early[flips[0]], out))
+            early[flips[0]], out[0] = lax.optimization_barrier((early[flips[0]], out[0]))
             gathered, masks = [both], [(0, NEAR)]
             for flip in flips:
                 gathered += [early[flip] if value is both and flip in early else flipped(value, flip) for value in gathered]
                 masks += [tuple(mask ^ flip for mask in pair) for pair in masks]
             break
         final = iteration == ITERS - 2
-        out, remainder, solution_, step, *rest = call(
+        results = call(
             functools.partial(owner_kernel, sizes, start, final),
             "owner_final" if final else "owner",
-            [exchange(out), entry, precondition, remainder, direction, product] + ([] if start else [solution_]),
-            [messages, owned, owned, scalar] + ([kept(3 * CP * sizes.own_rows, LANES)] if final else []),
-            [owned_scratch] + factors(spread_rows(CP * PIECES, sizes.own_rows), LANES, entries),
+            exchange(out, sizes.message)
+            + [entry, precondition, remainder, direction, product]
+            + ([] if start else [solution_]),
+            messages + [owned, owned, scalar] + ([kept(3 * CP * sizes.own_rows, LANES)] if final else []),
+            [owned_scratch] + factors(spread_rows(CP * PIECES, sizes.own_rows), LANES, entries) + [inbox],
+            scalars=place,
         )
+        out, (remainder, solution_, step, *rest) = results[: sizes.cams], results[sizes.cams :]
         fields = rest[0] if final else None
+    curvature = out[0]
+    for axis in ("cams", "pts"):
+        flips = [1 << bit for bit in range(lax.axis_size(axis).bit_length() - 1)]
+        for flip in reversed(flips):
+            curvature = curvature + flipped(curvature, flip, axis)
     return call(
         functools.partial(final_kernel, sizes, masks),
         "final",
-        [exchange(out), product, inverse, gradient, sums] + gathered,
+        [curvature, product, inverse, gradient, sums] + gathered,
         [shape(CP, CAM_OWN), shape(3, PT_DEV)],
         [pltpu.VMEM((3 * PT_HI, PT_LO), f32)],
-        scalars=[lax.axis_index("pts").astype(jnp.int32).reshape(1)],
+        scalars=[run],
     )
 
 

time: 100 us -> 161 us (1.61)
  starting transfers between devices: 12.8 us -> 85 us
  blocking collectives: 45.1 us -> 0 us
  waiting for transfers between devices: 19.7 us -> 58.3 us
  Pallas kernels: 21.6 us -> 17 us
    ppermute x4 -> x69, starting transfers between devices: 2.93 us -> 85 us  [flipped(): lax.ppermute(value, axis, [(p, p ^ flip) for p in range(lax.axis_size(axi...]
    ppermute x4 -> x69, waiting for transfers between devices: 4.72 us -> 58.3 us  [flipped(): lax.ppermute(value, axis, [(p, p ^ flip) for p in range(lax.axis_size(axi...]
    all_to_all x5 -> x0, blocking collectives: 45.1 us -> none  [exchange(): lax.all_to_all(flat, axes, split_axis=0, concat_axis=0, tiled=True)]
    all_to_all x2 -> x0, waiting for transfers between devices: 14.9 us -> none  [exchange(): lax.all_to_all(flat, axes, split_axis=0, concat_axis=0, tiled=True)]
    all_to_all x2 -> x0, starting transfers between devices: 9.83 us -> none  [exchange(): lax.all_to_all(flat, axes, split_axis=0, concat_axis=0, tiled=True)]
    pallas_call x9 -> x15, Pallas kernels: 21.6 us -> 17 us  [call(): pl.pallas_call(kernel, name=name, out_shape=outputs, in_specs=[smem] * le...]
  transfers between devices with their start and end apart: 6 -> 69, of which waited for: 3 -> 31; matrix products, arithmetic and copies ran while one was open for 0% -> 0% of each run, Pallas kernels for 3% -> 1%
where the time goes in v8:
time: 161 us
  starting transfers between devices  85 us (53%)
  waiting for transfers between devices  58.3 us (36%)
  Pallas kernels  17 us (11%)
    ppermute x69, starting transfers between devices, flipped(): lax.ppermute(value, axis, [(p, p ^ flip) for p in range(lax.axis_size(axi...  85 us
    ppermute x69, waiting for transfers between devices, flipped(): lax.ppermute(value, axis, [(p, p ^ flip) for p in range(lax.axis_size(axi...  58.3 us
    pallas_call x15, Pallas kernels, call(): pl.pallas_call(kernel, name=name, out_shape=outputs, in_specs=[smem] * le...  17 us
  transfers between devices with their start and end apart: 69, of which 31 were waited for; matrix products, arithmetic and copies ran while one was open for 0% of the time, Pallas kernels for 1%

profile of v8, /device:TPU:0, one launch (start us, length us, event | category | flops | bytes accessed | tf_op | source)
XLA Modules:
  0.0 161.1 jit_solution(16466398062886219333)
XLA Ops:
  0.6 5.8 %setup.1 = (f32[48,128]{1,0:T(8,128)S(1)}, f32[48,128]{1,0:T(8,128)S(1)}, f32[48,128]{1,0:T(8,128)S(1)}, f32[48,128]{1,0:T(8,128)S(1)}, f32[576,128]{1,0:T(8,128...) custom-call(s32[1]{0:T(128)} %bitcast.1.column_ref, ...), custom_call_target="tpu_custom_call" | custom-call | tf_op jit(solution)/shard_map/setup/pallas_call | solution.py:529
  7.0 2.6 %collective-permute-start.1 = (f32[48,128]{1,0:T(8,128)S(1)}, f32[48,128]{1,0:T(8,128)S(1)}, u32[]{:S(2)}, u32[]{:S(2)}) collective-permute-start(f32[48,128]{1,0:T(8,128)S(1)} %get-tuple-element.107), channel_id=1, source_target_pairs={{0,2},{1,3},{2,0},{3,1},{4,6},{5,7},{6,4},{7,5},{8,10},{9,11},{10,... | collective-permute-start | bytes 73736 | tf_op jit(solution)/shard_map/ppermute | solution.py:550
  16.4 2.6 %collective-permute-start.6 = (f32[24,128]{1,0:T(8,128)S(1)}, f32[24,128]{1,0:T(8,128)S(1)}, u32[]{:S(2)}, u32[]{:S(2)}) collective-permute-start(f32[24,128]{1,0:T(8,128)S(1)} %get-tuple-element.113), channel_id=1, source_target_pairs={{0,16},{4,20},{8,24},{12,28},{16,0},{20,4},{24,8},{28,12},{1,17},{... | collective-permute-start | bytes 36872 | tf_op jit(solution)/shard_map/ppermute | solution.py:550
  20.3 3.6 %collective-permute-start.8 = (f32[24,128]{1,0:T(8,128)S(1)}, f32[24,128]{1,0:T(8,128)S(1)}, u32[]{:S(2)}, u32[]{:S(2)}) collective-permute-start(f32[24,128]{1,0:T(8,128)S(1)} %get-tuple-element.115), channel_id=1, source_target_pairs={{0,24},{4,28},{8,16},{12,20},{16,8},{20,12},{24,0},{28,4},{1,25},{... | collective-permute-start | bytes 36872 | tf_op jit(solution)/shard_map/ppermute | solution.py:550
  25.8 4.5 %collective-permute-done.9.refs_7_ = f32[24,128]{1,0:T(8,128)S(1)} collective-permute-done((f32[24,128]{1,0:T(8,128)S(1)}, f32[24,128]{1,0:T(8,128)S(1)}, u32[]{:S(2)}, u32[]{:S(2)}) %collective-permute-start.9) | collective-permute-done | bytes 12320 | tf_op jit(solution)/shard_map/ppermute | solution.py:550
  35.7 2.9 %collective-permute-start.15 = (f32[12,128]{1,0:T(8,128)S(1)}, f32[12,128]{1,0:T(8,128)S(1)}, u32[]{:S(2)}, u32[]{:S(2)}) collective-permute-start(f32[12,128]{1,0:T(8,128)S(1)} %get-tuple-element.124), channel_id=1, source_target_pairs={{0,12},{4,8},{8,4},{12,0},{16,28},{20,24},{24,20},{28,16},{1,13},{... | collective-permute-start | bytes 18440 | tf_op jit(solution)/shard_map/ppermute | solution.py:550
  38.6 2.9 %collective-permute-start.17 = (f32[12,128]{1,0:T(8,128)S(1)}, f32[12,128]{1,0:T(8,128)S(1)}, u32[]{:S(2)}, u32[]{:S(2)}) collective-permute-start(f32[12,128]{1,0:T(8,128)S(1)} %get-tuple-element.126), channel_id=1, source_target_pairs={{0,20},{4,16},{8,28},{12,24},{16,4},{20,0},{24,12},{28,8},{1,21},{... | collective-permute-start | bytes 18440 | tf_op jit(solution)/shard_map/ppermute | solution.py:550
  41.7 4.6 %collective-permute-start.19 = (f32[12,128]{1,0:T(8,128)S(1)}, f32[12,128]{1,0:T(8,128)S(1)}, u32[]{:S(2)}, u32[]{:S(2)}) collective-permute-start(f32[12,128]{1,0:T(8,128)S(1)} %get-tuple-element.128), channel_id=1, source_target_pairs={{0,28},{4,24},{8,20},{12,16},{16,12},{20,8},{24,4},{28,0},{1,29},{... | collective-permute-start | bytes 18440 | tf_op jit(solution)/shard_map/ppermute | solution.py:550
  48.0 2.7 %schur.2 = (f32[24,128]{1,0:T(8,128)S(1)}, f32[24,128]{1,0:T(8,128)S(1)}, f32[24,128]{1,0:T(8,128)S(1)}, f32[24,128]{1,0:T(8,128)S(1)}, f32[8,128]{1,0:T(8,128)S...) custom-call(s32[1]{0:T(128)} %bitcast.run_ref, s32[1]{0:T(128)} %bitcast.1.column_ref, ...), custom_call_target="tpu_custom_call" | custom-call | flops 2000000000 | bytes 10000000 | tf_op jit(solution)/shard_map/schur/pallas_call | solution.py:529
  62.8 3.6 %collective-permute-start.28 = (f32[12,128]{1,0:T(8,128)S(1)}, f32[12,128]{1,0:T(8,128)S(1)}, u32[]{:S(2)}, u32[]{:S(2)}) collective-permute-start(f32[12,128]{1,0:T(8,128)S(1)} %get-tuple-element.148), channel_id=1, source_target_pairs={{0,24},{4,28},{8,16},{12,20},{16,8},{20,12},{24,0},{28,4},{1,25},{... | collective-permute-start | bytes 18440 | tf_op jit(solution)/shard_map/ppermute | solution.py:550
  68.3 4.5 %collective-permute-done.29.refs_7_ = f32[12,128]{1,0:T(8,128)S(1)} collective-permute-done((f32[12,128]{1,0:T(8,128)S(1)}, f32[12,128]{1,0:T(8,128)S(1)}, u32[]{:S(2)}, u32[]{:S(2)}) %collective-permute-start.29) | collective-permute-done | bytes 6176 | tf_op jit(solution)/shard_map/ppermute | solution.py:550
  78.0 2.9 %collective-permute-start.35 = (f32[12,128]{1,0:T(8,128)S(1)}, f32[12,128]{1,0:T(8,128)S(1)}, u32[]{:S(2)}, u32[]{:S(2)}) collective-permute-start(f32[12,128]{1,0:T(8,128)S(1)} %get-tuple-element.160), channel_id=1, source_target_pairs={{0,12},{4,8},{8,4},{12,0},{16,28},{20,24},{24,20},{28,16},{1,13},{... | collective-permute-start | bytes 18440 | tf_op jit(solution)/shard_map/ppermute | solution.py:550
  81.0 2.9 %collective-permute-start.37 = (f32[12,128]{1,0:T(8,128)S(1)}, f32[12,128]{1,0:T(8,128)S(1)}, u32[]{:S(2)}, u32[]{:S(2)}) collective-permute-start(f32[12,128]{1,0:T(8,128)S(1)} %get-tuple-element.162), channel_id=1, source_target_pairs={{0,20},{4,16},{8,28},{12,24},{16,4},{20,0},{24,12},{28,8},{1,21},{... | collective-permute-start | bytes 18440 | tf_op jit(solution)/shard_map/ppermute | solution.py:550
  84.0 4.6 %collective-permute-start.39 = (f32[12,128]{1,0:T(8,128)S(1)}, f32[12,128]{1,0:T(8,128)S(1)}, u32[]{:S(2)}, u32[]{:S(2)}) collective-permute-start(f32[12,128]{1,0:T(8,128)S(1)} %get-tuple-element.164), channel_id=1, source_target_pairs={{0,28},{4,24},{8,20},{12,16},{16,12},{20,8},{24,4},{28,0},{1,29},{... | collective-permute-start | bytes 18440 | tf_op jit(solution)/shard_map/ppermute | solution.py:550
  90.4 2.8 %schur.3 = (f32[24,128]{1,0:T(8,128)S(1)}, f32[24,128]{1,0:T(8,128)S(1)}, f32[24,128]{1,0:T(8,128)S(1)}, f32[24,128]{1,0:T(8,128)S(1)}, f32[8,128]{1,0:T(8,128)S...) custom-call(s32[1]{0:T(128)} %bitcast.run_ref, ...), custom_call_target="tpu_custom_call" | custom-call | flops 2000000000 | bytes 10000000 | tf_op jit(solution)/shard_map/schur/pallas_call | solution.py:529
  105.2 3.6 %collective-permute-start.48 = (f32[12,128]{1,0:T(8,128)S(1)}, f32[12,128]{1,0:T(8,128)S(1)}, u32[]{:S(2)}, u32[]{:S(2)}) collective-permute-start(f32[12,128]{1,0:T(8,128)S(1)} %get-tuple-element.179), channel_id=1, source_target_pairs={{0,24},{4,28},{8,16},{12,20},{16,8},{20,12},{24,0},{28,4},{1,25},{... | collective-permute-start | bytes 18440 | tf_op jit(solution)/shard_map/ppermute | solution.py:550
  110.7 4.6 %collective-permute-done.49.refs_7_ = f32[12,128]{1,0:T(8,128)S(1)} collective-permute-done((f32[12,128]{1,0:T(8,128)S(1)}, f32[12,128]{1,0:T(8,128)S(1)}, u32[]{:S(2)}, u32[]{:S(2)}) %collective-permute-start.49) | collective-permute-done | bytes 6176 | tf_op jit(solution)/shard_map/ppermute | solution.py:550
  128.3 3.2 %collective-permute-start.59 = (f32[12,128]{1,0:T(8,128)S(1)}, f32[12,128]{1,0:T(8,128)S(1)}, u32[]{:S(2)}, u32[]{:S(2)}) collective-permute-start(f32[12,128]{1,0:T(8,128)S(1)} %get-tuple-element.195), channel_id=1, source_target_pairs={{0,28},{4,24},{8,20},{12,16},{16,12},{20,8},{24,4},{28,0},{1,29},{... | collective-permute-start | bytes 18440 | tf_op jit(solution)/shard_map/ppermute | solution.py:550
  132.3 2.4 %collective-permute-done.59.refs_7_ = f32[12,128]{1,0:T(8,128)S(1)} collective-permute-done((f32[12,128]{1,0:T(8,128)S(1)}, f32[12,128]{1,0:T(8,128)S(1)}, u32[]{:S(2)}, u32[]{:S(2)}) %collective-permute-start.59) | collective-permute-done | bytes 6176 | tf_op jit(solution)/shard_map/ppermute | solution.py:550
  138.5 3.6 %collective-permute-done.61.refs_1_ = f32[288,128]{1,0:T(8,128)S(1)} collective-permute-done((f32[288,128]{1,0:T(8,128)S(1)}, f32[288,128]{1,0:T(8,128)S(1)}, u32[]{:S(2)}, u32[]{:S(2)}) %collective-permute-start.61) | collective-permute-done | bytes 147488 | tf_op jit(solution)/shard_map/ppermute | solution.py:550
  144.8 2.4 %collective-permute-done.62 = f32[8,128]{1,0:T(8,128)S(1)} collective-permute-done((f32[8,128]{1,0:T(8,128)S(1)}, f32[8,128]{1,0:T(8,128)S(1)}, u32[]{:S(2)}, u32[]{:S(2)}) %collective-permute-start.62) | collective-permute-done | bytes 4128 | tf_op jit(solution)/shard_map/ppermute | solution.py:550
  148.3 4.5 %collective-permute-done.64 = f32[8,128]{1,0:T(8,128)S(1)} collective-permute-done((f32[8,128]{1,0:T(8,128)S(1)}, f32[8,128]{1,0:T(8,128)S(1)}, u32[]{:S(2)}, u32[]{:S(2)}) %collective-permute-start.64) | collective-permute-done | bytes 4128 | tf_op jit(solution)/shard_map/ppermute | solution.py:550
  152.9 3.6 %collective-permute-done.65 = f32[8,128]{1,0:T(8,128)S(1)} collective-permute-done((f32[8,128]{1,0:T(8,128)S(1)}, f32[8,128]{1,0:T(8,128)S(1)}, u32[]{:S(2)}, u32[]{:S(2)}) %collective-permute-start.65) | collective-permute-done | bytes 4128 | tf_op jit(solution)/shard_map/ppermute | solution.py:550
  157.0 3.0 %collective-permute-done.66 = f32[8,128]{1,0:T(8,128)S(1)} collective-permute-done((f32[8,128]{1,0:T(8,128)S(1)}, f32[8,128]{1,0:T(8,128)S(1)}, u32[]{:S(2)}, u32[]{:S(2)}) %collective-permute-start.66) | collective-permute-done | bytes 4128 | tf_op jit(solution)/shard_map/ppermute | solution.py:550
  (134 shorter events, 75.7 us)
Async XLA Ops:
  12.8 7.4 %collective-permute-start.3 = (f32[24,128]{1,0:T(8,128)S(1)}, f32[24,128]{1,0:T(8,128)S(1)}, u32[]{:S(2)}, u32[]{:S(2)}) collective-permute-start(f32[24,128]{1,0:T(8,128)S(1)} %get-tuple-element.110), channel_id=1, source_target_pairs={{0,4},{4,0},{8,12},{12,8},{16,20},{20,16},{24,28},{28,24},{1,5},{5... | collective-permute-start | bytes 36872 | tf_op jit(solution)/shard_map/ppermute | solution.py:550
  14.4 9.5 %collective-permute-start.4 = (f32[24,128]{1,0:T(8,128)S(1)}, f32[24,128]{1,0:T(8,128)S(1)}, u32[]{:S(2)}, u32[]{:S(2)}) collective-permute-start(f32[24,128]{1,0:T(8,128)S(1)} %get-tuple-element.111), channel_id=1, source_target_pairs={{0,8},{4,12},{8,0},{12,4},{16,24},{20,28},{24,16},{28,20},{1,9},{5... | collective-permute-start | bytes 36872 | tf_op jit(solution)/shard_map/ppermute | solution.py:550
  16.0 8.1 %collective-permute-start.5 = (f32[24,128]{1,0:T(8,128)S(1)}, f32[24,128]{1,0:T(8,128)S(1)}, u32[]{:S(2)}, u32[]{:S(2)}) collective-permute-start(f32[24,128]{1,0:T(8,128)S(1)} %get-tuple-element.112), channel_id=1, source_target_pairs={{0,12},{4,8},{8,4},{12,0},{16,28},{20,24},{24,20},{28,16},{1,13},{... | collective-permute-start | bytes 36872 | tf_op jit(solution)/shard_map/ppermute | solution.py:550
  16.4 7.7 %collective-permute-start.6 = (f32[24,128]{1,0:T(8,128)S(1)}, f32[24,128]{1,0:T(8,128)S(1)}, u32[]{:S(2)}, u32[]{:S(2)}) collective-permute-start(f32[24,128]{1,0:T(8,128)S(1)} %get-tuple-element.113), channel_id=1, source_target_pairs={{0,16},{4,20},{8,24},{12,28},{16,0},{20,4},{24,8},{28,12},{1,17},{... | collective-permute-start | bytes 36872 | tf_op jit(solution)/shard_map/ppermute | solution.py:550
  35.7 10.6 %collective-permute-start.15 = (f32[12,128]{1,0:T(8,128)S(1)}, f32[12,128]{1,0:T(8,128)S(1)}, u32[]{:S(2)}, u32[]{:S(2)}) collective-permute-start(f32[12,128]{1,0:T(8,128)S(1)} %get-tuple-element.124), channel_id=1, source_target_pairs={{0,12},{4,8},{8,4},{12,0},{16,28},{20,24},{24,20},{28,16},{1,13},{... | collective-permute-start | bytes 18440 | tf_op jit(solution)/shard_map/ppermute | solution.py:550
  38.6 7.7 %collective-permute-start.16 = (f32[12,128]{1,0:T(8,128)S(1)}, f32[12,128]{1,0:T(8,128)S(1)}, u32[]{:S(2)}, u32[]{:S(2)}) collective-permute-start(f32[12,128]{1,0:T(8,128)S(1)} %get-tuple-element.125), channel_id=1, source_target_pairs={{0,16},{4,20},{8,24},{12,28},{16,0},{20,4},{24,8},{28,12},{1,17},{... | collective-permute-start | bytes 18440 | tf_op jit(solution)/shard_map/ppermute | solution.py:550
  38.6 7.7 %collective-permute-start.17 = (f32[12,128]{1,0:T(8,128)S(1)}, f32[12,128]{1,0:T(8,128)S(1)}, u32[]{:S(2)}, u32[]{:S(2)}) collective-permute-start(f32[12,128]{1,0:T(8,128)S(1)} %get-tuple-element.126), channel_id=1, source_target_pairs={{0,20},{4,16},{8,28},{12,24},{16,4},{20,0},{24,12},{28,8},{1,21},{... | collective-permute-start | bytes 18440 | tf_op jit(solution)/shard_map/ppermute | solution.py:550
  55.4 7.4 %collective-permute-start.23 = (f32[12,128]{1,0:T(8,128)S(1)}, f32[12,128]{1,0:T(8,128)S(1)}, u32[]{:S(2)}, u32[]{:S(2)}) collective-permute-start(f32[12,128]{1,0:T(8,128)S(1)} %get-tuple-element.143), channel_id=1, source_target_pairs={{0,4},{4,0},{8,12},{12,8},{16,20},{20,16},{24,28},{28,24},{1,5},{5... | collective-permute-start | bytes 18440 | tf_op jit(solution)/shard_map/ppermute | solution.py:550
  57.0 9.5 %collective-permute-start.24 = (f32[12,128]{1,0:T(8,128)S(1)}, f32[12,128]{1,0:T(8,128)S(1)}, u32[]{:S(2)}, u32[]{:S(2)}) collective-permute-start(f32[12,128]{1,0:T(8,128)S(1)} %get-tuple-element.144), channel_id=1, source_target_pairs={{0,8},{4,12},{8,0},{12,4},{16,24},{20,28},{24,16},{28,20},{1,9},{5... | collective-permute-start | bytes 18440 | tf_op jit(solution)/shard_map/ppermute | solution.py:550
  57.0 9.7 %collective-permute-start.25 = (f32[12,128]{1,0:T(8,128)S(1)}, f32[12,128]{1,0:T(8,128)S(1)}, u32[]{:S(2)}, u32[]{:S(2)}) collective-permute-start(f32[12,128]{1,0:T(8,128)S(1)} %get-tuple-element.145), channel_id=1, source_target_pairs={{0,12},{4,8},{8,4},{12,0},{16,28},{20,24},{24,20},{28,16},{1,13},{... | collective-permute-start | bytes 18440 | tf_op jit(solution)/shard_map/ppermute | solution.py:550
  59.0 7.7 %collective-permute-start.26 = (f32[12,128]{1,0:T(8,128)S(1)}, f32[12,128]{1,0:T(8,128)S(1)}, u32[]{:S(2)}, u32[]{:S(2)}) collective-permute-start(f32[12,128]{1,0:T(8,128)S(1)} %get-tuple-element.146), channel_id=1, source_target_pairs={{0,16},{4,20},{8,24},{12,28},{16,0},{20,4},{24,8},{28,12},{1,17},{... | collective-permute-start | bytes 18440 | tf_op jit(solution)/shard_map/ppermute | solution.py:550
  78.0 10.6 %collective-permute-start.35 = (f32[12,128]{1,0:T(8,128)S(1)}, f32[12,128]{1,0:T(8,128)S(1)}, u32[]{:S(2)}, u32[]{:S(2)}) collective-permute-start(f32[12,128]{1,0:T(8,128)S(1)} %get-tuple-element.160), channel_id=1, source_target_pairs={{0,12},{4,8},{8,4},{12,0},{16,28},{20,24},{24,20},{28,16},{1,13},{... | collective-permute-start | bytes 18440 | tf_op jit(solution)/shard_map/ppermute | solution.py:550
  81.0 7.7 %collective-permute-start.36 = (f32[12,128]{1,0:T(8,128)S(1)}, f32[12,128]{1,0:T(8,128)S(1)}, u32[]{:S(2)}, u32[]{:S(2)}) collective-permute-start(f32[12,128]{1,0:T(8,128)S(1)} %get-tuple-element.161), channel_id=1, source_target_pairs={{0,16},{4,20},{8,24},{12,28},{16,0},{20,4},{24,8},{28,12},{1,17},{... | collective-permute-start | bytes 18440 | tf_op jit(solution)/shard_map/ppermute | solution.py:550
  81.0 7.7 %collective-permute-start.37 = (f32[12,128]{1,0:T(8,128)S(1)}, f32[12,128]{1,0:T(8,128)S(1)}, u32[]{:S(2)}, u32[]{:S(2)}) collective-permute-start(f32[12,128]{1,0:T(8,128)S(1)} %get-tuple-element.162), channel_id=1, source_target_pairs={{0,20},{4,16},{8,28},{12,24},{16,4},{20,0},{24,12},{28,8},{1,21},{... | collective-permute-start | bytes 18440 | tf_op jit(solution)/shard_map/ppermute | solution.py:550
  97.8 7.4 %collective-permute-start.43 = (f32[12,128]{1,0:T(8,128)S(1)}, f32[12,128]{1,0:T(8,128)S(1)}, u32[]{:S(2)}, u32[]{:S(2)}) collective-permute-start(f32[12,128]{1,0:T(8,128)S(1)} %get-tuple-element.174), channel_id=1, source_target_pairs={{0,4},{4,0},{8,12},{12,8},{16,20},{20,16},{24,28},{28,24},{1,5},{5... | collective-permute-start | bytes 18440 | tf_op jit(solution)/shard_map/ppermute | solution.py:550
  99.4 9.5 %collective-permute-start.44 = (f32[12,128]{1,0:T(8,128)S(1)}, f32[12,128]{1,0:T(8,128)S(1)}, u32[]{:S(2)}, u32[]{:S(2)}) collective-permute-start(f32[12,128]{1,0:T(8,128)S(1)} %get-tuple-element.175), channel_id=1, source_target_pairs={{0,8},{4,12},{8,0},{12,4},{16,24},{20,28},{24,16},{28,20},{1,9},{5... | collective-permute-start | bytes 18440 | tf_op jit(solution)/shard_map/ppermute | solution.py:550
  99.4 9.7 %collective-permute-start.45 = (f32[12,128]{1,0:T(8,128)S(1)}, f32[12,128]{1,0:T(8,128)S(1)}, u32[]{:S(2)}, u32[]{:S(2)}) collective-permute-start(f32[12,128]{1,0:T(8,128)S(1)} %get-tuple-element.176), channel_id=1, source_target_pairs={{0,12},{4,8},{8,4},{12,0},{16,28},{20,24},{24,20},{28,16},{1,13},{... | collective-permute-start | bytes 18440 | tf_op jit(solution)/shard_map/ppermute | solution.py:550
  101.4 7.7 %collective-permute-start.46 = (f32[12,128]{1,0:T(8,128)S(1)}, f32[12,128]{1,0:T(8,128)S(1)}, u32[]{:S(2)}, u32[]{:S(2)}) collective-permute-start(f32[12,128]{1,0:T(8,128)S(1)} %get-tuple-element.177), channel_id=1, source_target_pairs={{0,16},{4,20},{8,24},{12,28},{16,0},{20,4},{24,8},{28,12},{1,17},{... | collective-permute-start | bytes 18440 | tf_op jit(solution)/shard_map/ppermute | solution.py:550
  116.4 18.3 %collective-permute-start.60 = (f32[216,128]{1,0:T(8,128)S(1)}, f32[216,128]{1,0:T(8,128)S(1)}, u32[]{:S(2)}, u32[]{:S(2)}) collective-permute-start(f32[216,128]{1,0:T(8,128)S(1)} %get-tuple-element.196.refs_9_), channel_id=1, source_target_pairs={{0,8},{4,12},{8,0},{12,4},{16,24},{20,28},{24,16},{28,20},{1,9},{5... | collective-permute-start | bytes 331784 | tf_op jit(solution)/shard_map/ppermute | solution.py:550
  123.9 7.7 %collective-permute-start.56 = (f32[12,128]{1,0:T(8,128)S(1)}, f32[12,128]{1,0:T(8,128)S(1)}, u32[]{:S(2)}, u32[]{:S(2)}) collective-permute-start(f32[12,128]{1,0:T(8,128)S(1)} %get-tuple-element.192), channel_id=1, source_target_pairs={{0,16},{4,20},{8,24},{12,28},{16,0},{20,4},{24,8},{28,12},{1,17},{... | collective-permute-start | bytes 18440 | tf_op jit(solution)/shard_map/ppermute | solution.py:550
  124.6 7.0 %collective-permute-start.57 = (f32[12,128]{1,0:T(8,128)S(1)}, f32[12,128]{1,0:T(8,128)S(1)}, u32[]{:S(2)}, u32[]{:S(2)}) collective-permute-start(f32[12,128]{1,0:T(8,128)S(1)} %get-tuple-element.193), channel_id=1, source_target_pairs={{0,20},{4,16},{8,28},{12,24},{16,4},{20,0},{24,12},{28,8},{1,21},{... | collective-permute-start | bytes 18440 | tf_op jit(solution)/shard_map/ppermute | solution.py:550
  134.9 7.2 %collective-permute-start.61 = (f32[288,128]{1,0:T(8,128)S(1)}, f32[288,128]{1,0:T(8,128)S(1)}, u32[]{:S(2)}, u32[]{:S(2)}) collective-permute-start(f32[288,128]{1,0:T(8,128)S(1)} %tail.1.refs_0_), channel_id=1, source_target_pairs={{0,16},{4,20},{8,24},{12,28},{16,0},{20,4},{24,8},{28,12},{1,17},{... | collective-permute-start | bytes 442376 | tf_op jit(solution)/shard_map/ppermute | solution.py:550
  136.8 23.2 %collective-permute-start.67 = (f32[288,128]{1,0:T(8,128)S(1)}, f32[288,128]{1,0:T(8,128)S(1)}, u32[]{:S(2)}, u32[]{:S(2)}) collective-permute-start(f32[288,128]{1,0:T(8,128)S(1)} %tail.1.refs_0_), channel_id=1, source_target_pairs={{0,4},{4,0},{8,12},{12,8},{16,20},{20,16},{24,28},{28,24},{1,5},{5... | collective-permute-start | bytes 442376 | tf_op jit(solution)/shard_map/ppermute | solution.py:550
  142.1 18.0 %collective-permute-start.68 = (f32[288,128]{1,0:T(8,128)S(1)}, f32[288,128]{1,0:T(8,128)S(1)}, u32[]{:S(2)}, u32[]{:S(2)}) collective-permute-start(f32[288,128]{1,0:T(8,128)S(1)} %collective-permute-done.61.refs_1_), channel_id=1, source_target_pairs={{0,4},{4,0},{8,12},{12,8},{16,20},{20,16},{24,28},{28,24},{1,5},{5... | collective-permute-start | bytes 442376 | tf_op jit(solution)/shard_map/ppermute | solution.py:550
  (45 other events, 199.4 us)

commit v9 on v7

--- a/solution.py
+++ b/solution.py
@@ -17,7 +17,6 @@
 PT_HI = PT_DEV // PT_LO
 PIECES = 2
 FINE = 3
-NEAR = 2
 VMEM_LIMIT = 24 * 1024 * 1024
 
 damping_camera = 1.0
@@ -86,33 +85,6 @@
     return result
 
 
-def gather_factors(tables):
-    pieces = [piece for table in tables for piece in cut(table)]
-    left = jnp.concatenate(pieces, axis=0).astype(bf16)
-    padded, rows = -(-len(tables) // SUB) * SUB, left.shape[0]
-    owner = lax.broadcasted_iota(jnp.int32, (padded, rows), 1) // (rows // len(tables))
-    chosen = (owner == lax.broadcasted_iota(jnp.int32, (padded, rows), 0)).astype(f32).astype(bf16)
-    return left, chosen
-
-
-def matmul_gather(group, factors, count, place_ref, high_of_row, high_count, picked_ref, found_ref):
-    left, chosen = factors
-    rows, padded = left.shape[0], chosen.shape[0]
-    width = SUB * LANES
-    picked = jnp.dot(left, place_ref[:, group * width : (group + 1) * width], preferred_element_type=f32)
-    for s in range(SUB):
-        mask = jnp.broadcast_to(high_of_row(group * SUB + s), (high_count, LANES)) == sub_iota(high_count)
-        for first in range(0, rows, high_count):
-            block = picked[first : first + high_count, s * LANES : (s + 1) * LANES]
-            columns = slice(group * width + s * LANES, group * width + (s + 1) * LANES)
-            picked_ref[first : first + high_count, columns] = jnp.where(mask, block, 0.0).astype(bf16)
-    total = jnp.dot(chosen, picked_ref[:rows, group * width : (group + 1) * width], preferred_element_type=f32)
-    start = group * SUB * padded
-    for s in range(SUB):
-        found_ref[start + s * padded : start + (s + 1) * padded, :] = total[:, s * LANES : (s + 1) * LANES]
-    return [found_ref[pl.ds(start + c, SUB, stride=padded), :] for c in range(count)]
-
-
 def spread_row(index, parts, high, high_count, spread_ref):
     columns = slice(index * LANES, (index + 1) * LANES)
     mask = jnp.broadcast_to(high, (high_count, LANES)) == sub_iota(high_count)
@@ -168,6 +140,12 @@
             total = total + row
         values.append(total)
     return values
+
+
+def point_gather(ref, point):
+    wide = PT_LO // LANES
+    row = lambda c, k: ref[c, k // wide : k // wide + 1, (k % wide) * LANES : (k % wide + 1) * LANES]
+    return gather_rows(row, PT_HI * wide, point // LANES, point % LANES, 3)
 
 
 def slot_place(slot, sizes):
@@ -227,13 +205,14 @@
 def setup_kernel(sizes, *refs):
     sources, refs = refs[:6], refs[6:]
     out_ref, a_ref, b_ref, inv_ref, grad_ref, place_point_ref, new_slot_ref, new_point_ref = refs[:8]
-    r_ref, parts_ref, spread_ref, picked_ref, found_ref, place_slot_ref, place_list_ref = refs[8:15]
-    jac_ref, pjac_ref, res_ref, slot_ref, point_ref, list_ref = refs[15:21]
-    semaphores = refs[21]
+    refs = refs[8:]
+    r_ref, parts_ref, spread_ref, table_ref, place_slot_ref, place_list_ref = refs[:6]
+    jac_ref, pjac_ref, res_ref, slot_ref, point_ref, list_ref = refs[6:12]
+    semaphores = refs[12]
     rows = sizes.rows
     copies = [
         pltpu.make_async_copy(source, target, semaphores.at[k])
-        for k, (source, target) in enumerate(zip(sources, refs[15:21]))
+        for k, (source, target) in enumerate(zip(sources, refs[6:12]))
     ]
     for copy in copies:
         copy.start()
@@ -289,10 +268,10 @@
     for k in range(3):
         grad_ref[k] = normal[6 + k]
     eliminated = solve(inverse, normal[6:])
-    picking = gather_factors(eliminated)
+    for k in range(3):
+        table_ref[k] = eliminated[k]
     for group in range(rows // SUB):
-        at_point = matmul_gather(group, picking, 3, place_point_ref,
-                                 lambda row: point_ref[row : row + 1, :] >> 8, PT_HI, picked_ref, found_ref)
+        at_point = point_gather(table_ref, point_ref[group * SUB : (group + 1) * SUB, :])
         b = [at(b_ref, k, group) for k in range(6)]
         errors = [at(r_ref, i, group) - sum(b[3 * i + k] * at_point[k] for k in range(3)) for i in range(2)]
         a = [at(a_ref, k, group) for k in range(2 * CP)]
@@ -343,7 +322,7 @@
     return jnp.sum(sum(a * b for a, b in zip(left, right)), keepdims=True)
 
 
-def first_owner_kernel(sizes, column_ref, in_ref, out_ref, entry_ref, pre_ref, rem_ref,
+def first_owner_kernel(sizes, column_ref, in_ref, out_ref, entry_ref, pre_ref, rem_ref, scaled_ref,
                        table_ref, spread_ref, place_ref):
     listed = jnp.zeros((sizes.pts, LANES), f32)
     for c in range(sizes.cams):
@@ -359,15 +338,12 @@
     for k in range(CP):
         pre_ref[k] = precondition[k]
         rem_ref[k] = remainder[k]
+        scaled_ref[k] = scaled[k]
     send_owned(scaled, dot_fields(remainder, scaled), entry, out_ref, table_ref, sizes)
 
 
-def owner_kernel(sizes, start, final, in_ref, entry_ref, pre_ref, rem_ref, dir_ref, product_ref, *refs):
-    refs = list(refs)
-    sol_ref = None if start else refs.pop(0)
-    out_ref, new_rem_ref, new_sol_ref, step_ref = refs[:4]
-    fields_ref = refs[4] if final else None
-    table_ref, spread_ref, place_ref = refs[-3:]
+def owner_kernel(sizes, in_ref, entry_ref, pre_ref, rem_ref, dir_ref, product_ref,
+                 out_ref, new_rem_ref, scaled_ref, step_ref, table_ref, spread_ref, place_ref):
     entry = entry_ref[...]
     fields = read_messages(in_ref, CP, sizes.message, sizes)
     curvature = read_scalar(in_ref, sizes.groups, sizes.message, sizes)
@@ -376,23 +352,16 @@
     sums = entries_scatter(fields, entry, sizes, spread_ref, place_ref)
     remainder, scaled = [], []
     for k in range(CP):
-        direction = dir_ref[k]
-        moved = step[:1] * direction
-        moved = moved if start else sol_ref[k] + moved
-        new_sol_ref[k] = moved
-        value = rem_ref[k] - step[:1] * (sums[k] + damping_camera * direction)
+        value = rem_ref[k] - step[:1] * (sums[k] + damping_camera * dir_ref[k])
         new_rem_ref[k] = value
         remainder.append(value)
         scaled.append(pre_ref[k] * value)
-        if final:
-            for j, field in enumerate((moved, direction, scaled[k])):
-                first = (j * CP + k) * sizes.own_rows
-                fields_ref[first : first + sizes.own_rows, :] = field
+        scaled_ref[k] = scaled[k]
     send_owned(scaled, dot_fields(remainder, scaled), entry, out_ref, table_ref, sizes)
 
 
 def schur_kernel(sizes, start, last, in_ref, a_ref, b_ref, inv_ref, slot_ref, point_ref,
-                 place_point_ref, pre_ref, rem_ref, grad_ref, *refs):
+                 place_point_ref, scaled_ref, grad_ref, *refs):
     refs = list(refs)
     if not start:
         product_ref, at_slot_ref, dir_ref, step_ref, sum_ref = refs[:5]
@@ -402,7 +371,7 @@
     refs = refs[5:]
     if not start:
         new_grad_ref = refs.pop(0)
-    q_ref, parts_ref, spread_ref, picked_ref, found_ref, place_slot_ref = refs
+    q_ref, parts_ref, spread_ref, table_ref, place_slot_ref = refs
     rows = sizes.rows
 
     def at(ref, comp, group):
@@ -414,7 +383,7 @@
     beta = None if start else (renewed / product_ref[...])[:1]
     squares = None
     for k in range(CP):
-        direction = pre_ref[k] * rem_ref[k]
+        direction = scaled_ref[k]
         if start:
             new_at_slot_ref[k] = fields[k]
         else:
@@ -444,10 +413,10 @@
             new_grad_ref[k] = grad_ref[k] + step_ref[:1, :1] * sum_ref[k]
 
     inner = None
-    picking = gather_factors(folded)
+    for k in range(3):
+        table_ref[k] = folded[k]
     for group in range(rows // SUB):
-        at_point = matmul_gather(group, picking, 3, place_point_ref,
-                                 lambda row: point_ref[row : row + 1, :] >> 8, PT_HI, picked_ref, found_ref)
+        at_point = point_gather(table_ref, point_ref[group * SUB : (group + 1) * SUB, :])
         q = [at(q_ref, i, group) for i in range(2)]
         errors = [q[i] - sum(at(b_ref, 3 * i + k, group) * at_point[k] for k in range(3)) for i in range(2)]
         here = q[0] * errors[0] + q[1] * errors[1]
@@ -470,32 +439,28 @@
     write_messages(fields, partial, sizes.groups, sizes.message, out_ref, sizes)
 
 
-def tail_kernel(sizes, in_ref, product_ref, own_ref, other_ref, out_ref):
-    renewed = jnp.broadcast_to(read_scalar(in_ref, sizes.groups, sizes.message, sizes), (SUB, LANES))
-    beta = (renewed / product_ref[...])[:1]
-    field = CP * sizes.own_rows
-    for j, ref in enumerate((own_ref, other_ref)):
-        first = j * 2 * field
-        out_ref[first : first + field, :] = ref[:field, :]
-        out_ref[first + field : first + 2 * field, :] = ref[2 * field :, :] + beta * ref[field : 2 * field, :]
-
-
-def final_kernel(sizes, masks, run_ref, in_ref, product_ref, inv_ref, grad_ref, sum_ref, *refs):
-    all_refs = refs[: len(masks)]
-    cam_ref, pt_ref, table_ref = refs[len(masks) :]
+def final_kernel(sizes, in_ref, inv_ref, grad_ref, sum_ref, early_ref, late_ref, *refs):
+    products, steps = [ref[...] for ref in refs[:ITERS]], [ref[...] for ref in refs[ITERS : 2 * ITERS - 1]]
+    cam_ref, pt_ref, table_ref = refs[2 * ITERS - 1 :]
     curvature = jnp.sum(jnp.where(lane_iota(sizes.devices) == 0, in_ref[...], 0.0), keepdims=True)
-    step = (product_ref[...] / jnp.broadcast_to(curvature, (SUB, LANES)))[:1]
-    for all_ref, pair in zip(all_refs, masks):
-        for j, mask in enumerate(pair):
-            base_column = (run_ref[0] ^ mask) * sizes.run
-            for h in range(sizes.run_rows):
-                columns = pl.ds(pl.multiple_of(base_column + h * LANES, LANES), LANES)
-                for start in range(0, CP, SUB):
-                    size = min(SUB, CP - start)
-                    first = (j * 2 * CP + start) * sizes.own_rows + h
-                    base = all_ref[pl.ds(first, size, stride=sizes.own_rows), :]
-                    direction = all_ref[pl.ds(first + CP * sizes.own_rows, size, stride=sizes.own_rows), :]
-                    cam_ref[start : start + size, columns] = base + step * direction
+    steps.append(products[-1] / jnp.broadcast_to(curvature, (SUB, LANES)))
+    factors = [steps[-1]]
+    for k in reversed(range(ITERS - 1)):
+        factors.insert(0, steps[k] + factors[0] * (products[k + 1] / products[k]))
+    factors = [factor[:1] for factor in factors]
+    step = steps[-1][:1]
+    for r in range(sizes.pts):
+        for h in range(sizes.run_rows):
+            columns = slice((r * sizes.run_rows + h) * LANES, (r * sizes.run_rows + h + 1) * LANES)
+            for start in range(0, CP, SUB):
+                size = min(SUB, CP - start)
+                total = None
+                for k, factor in enumerate(factors):
+                    ref, held, place = (late_ref, 1, 0) if k == ITERS - 1 else (early_ref, ITERS - 1, k)
+                    first = ((r * held + place) * CP + start) * sizes.own_rows + h
+                    term = factor * ref[pl.ds(first, size, stride=sizes.own_rows), :]
+                    total = term if total is None else total + term
+                cam_ref[start : start + size, columns] = total
     total = [grad_ref[k] + step[:, :1] * sum_ref[k] for k in range(3)]
     solved = solve([inv_ref[k] for k in range(6)], total)
     for k in range(3):
@@ -542,9 +507,6 @@
         flat = messages.reshape(sizes.devices, 1, width)
         return lax.all_to_all(flat, axes, split_axis=0, concat_axis=0, tiled=True).reshape(messages.shape)
 
-    def flipped(value, flip):
-        return lax.ppermute(value, "pts", [(p, p ^ flip) for p in range(sizes.pts)])
-
     def factors(high_rows, low_rows, entries):
         return [pltpu.VMEM((high_rows, entries), bf16), pltpu.VMEM((low_rows, entries), bf16)]
 
@@ -555,11 +517,7 @@
     owned_scratch = pltpu.VMEM((CP, sizes.own_rows, LANES), f32)
     entries = sizes.pts * LANES
 
-    gather_scratch = [
-        pltpu.VMEM((3 * PIECES * PT_HI, sizes.obs), bf16),
-        pltpu.VMEM((rows * SUB, LANES), f32),
-        pltpu.VMEM((LANES, sizes.obs), bf16),
-    ]
+    gather_scratch = [pltpu.VMEM((3, PT_HI, PT_LO), f32), pltpu.VMEM((LANES, sizes.obs), bf16)]
 
     def parts_scratch(count):
         return pltpu.VMEM((rows // SUB, count * SUB, LANES), f32)
@@ -591,11 +549,11 @@
         + [pltpu.SemaphoreType.DMA((len(given),))],
         inputs_at=pl.ANY,
     )
-    out, entry, precondition, remainder = call(
+    out, entry, precondition, remainder, scaled = call(
         functools.partial(first_owner_kernel, sizes),
         "first_owner",
         [exchange(first)],
-        [messages, kept(sizes.pts, LANES, dtype=jnp.int32), owned, owned],
+        [messages, kept(sizes.pts, LANES, dtype=jnp.int32), owned, owned, owned],
         [owned_scratch] + factors(spread_rows(2 * CP * PIECES, sizes.own_rows), LANES, entries),
         scalars=[column],
     )
@@ -603,60 +561,46 @@
     schur_scratch += [pltpu.VMEM((max(spread_rows(3 * PIECES, PT_HI), spread_rows(CP * PIECES, sizes.pts)), sizes.obs), bf16)]
     schur_scratch += gather_scratch
     at_slot = kept(CP, sizes.pts, LANES)
-    product = slots = direction = step = sums = solution_ = None
+    product = slots = direction = step = sums = None
+    products, steps, everything = [], [], [scaled]
+
+    def over_pts(values):
+        rows = jnp.concatenate(values).reshape(-1, LANES)
+        return lax.all_gather(rows, "pts", axis=0, tiled=True)
+
     for iteration in range(ITERS):
         start, last = iteration == 0, iteration == ITERS - 1
         earlier = [] if start else [product, slots, direction, step, sums]
-        if last:
-            neighbour = flipped(fields, NEAR)
-        arrived = exchange(out)
-        if last:
-            (both,) = call(
-                functools.partial(tail_kernel, sizes),
-                "tail",
-                [arrived, product, fields, neighbour],
-                [kept(4 * CP * sizes.own_rows, LANES)],
-                [],
-            )
-            flips = [1 << bit for bit in range(sizes.pts.bit_length() - 1) if 1 << bit != NEAR]
-            flips = flips[1:] + flips[:1]
-            early = {flip: flipped(both, flip) for flip in (flips[0], flips[-1])}
         results = call(
             functools.partial(schur_kernel, sizes, start, last),
             "schur_last" if last else "schur",
-            [arrived, a, b, inverse, slot, point, place_point, precondition, remainder, gradient]
-            + earlier,
+            [exchange(out), a, b, inverse, slot, point, place_point, scaled, gradient] + earlier,
             [kept(sizes.devices, LANES) if last else messages, scalar, at_slot, owned, point_table]
             + ([] if start else [point_table]),
             schur_scratch,
             cost=pl.CostEstimate(flops=2_000_000_000, bytes_accessed=10_000_000, transcendentals=0),
         )
         out, product, slots, direction, sums = results[:5]
+        products.append(product)
         if not start:
             gradient = results[5]
         if last:
-            early[flips[0]], out = lax.optimization_barrier((early[flips[0]], out))
-            gathered, masks = [both], [(0, NEAR)]
-            for flip in flips:
-                gathered += [early[flip] if value is both and flip in early else flipped(value, flip) for value in gathered]
-                masks += [tuple(mask ^ flip for mask in pair) for pair in masks]
             break
-        final = iteration == ITERS - 2
-        out, remainder, solution_, step, *rest = call(
-            functools.partial(owner_kernel, sizes, start, final),
-            "owner_final" if final else "owner",
-            [exchange(out), entry, precondition, remainder, direction, product] + ([] if start else [solution_]),
-            [messages, owned, owned, scalar] + ([kept(3 * CP * sizes.own_rows, LANES)] if final else []),
+        out, remainder, scaled, step = call(
+            functools.partial(owner_kernel, sizes),
+            "owner",
+            [exchange(out), entry, precondition, remainder, direction, product],
+            [messages, owned, owned, scalar],
             [owned_scratch] + factors(spread_rows(CP * PIECES, sizes.own_rows), LANES, entries),
         )
-        fields = rest[0] if final else None
+        steps.append(step)
+        everything.append(scaled)
     return call(
-        functools.partial(final_kernel, sizes, masks),
+        functools.partial(final_kernel, sizes),
         "final",
-        [exchange(out), product, inverse, gradient, sums] + gathered,
+        [exchange(out), inverse, gradient, sums, over_pts(everything[:-1]), over_pts(everything[-1:])] + products + steps,
         [shape(CP, CAM_OWN), shape(3, PT_DEV)],
         [pltpu.VMEM((3 * PT_HI, PT_LO), f32)],
-        scalars=[lax.axis_index("pts").astype(jnp.int32).reshape(1)],
     )
 
 

time: 100 us -> 147 us (1.47)
  blocking collectives: 45.1 us -> 90.4 us
  waiting for transfers between devices: 19.7 us -> 14.5 us
  starting transfers between devices: 12.8 us -> 17.9 us
  local copies, waits for them, and re-layouts: 0 us -> 3.58 us
  Pallas kernels: 21.6 us -> 18.3 us
    all_gather x0 -> x2, blocking collectives: none -> 63.3 us  [over_pts(): return lax.all_gather(rows, 'pts', axis=0, tiled=True)]
    all_to_all x5 -> x3, blocking collectives: 45.1 us -> 27.1 us  [exchange(): lax.all_to_all(flat, axes, split_axis=0, concat_axis=0, tiled=True)]
    all_to_all x2 -> x4, starting transfers between devices: 9.83 us -> 17.9 us  [exchange(): lax.all_to_all(flat, axes, split_axis=0, concat_axis=0, tiled=True)]
    ppermute x4 -> x0, waiting for transfers between devices: 4.72 us -> none  [flipped(): return lax.ppermute(value, 'pts', [(p, p ^ flip) for p in range(sizes.pts)])]
    unnamed x0 -> x12, local copies, waits for them, and re-layouts: none -> 3.58 us
    pallas_call x9 -> x8, Pallas kernels: 21.6 us -> 18.3 us  [call(): pl.pallas_call(kernel, name=name, out_shape=outputs, in_specs=[smem] * le...]
    ppermute x4 -> x0, starting transfers between devices: 2.93 us -> none  [flipped(): return lax.ppermute(value, 'pts', [(p, p ^ flip) for p in range(sizes.pts)])]
    all_to_all x2 -> x4, waiting for transfers between devices: 14.9 us -> 14.5 us  [exchange(): lax.all_to_all(flat, axes, split_axis=0, concat_axis=0, tiled=True)]
  transfers between devices with their start and end apart: 6 -> 4, of which waited for: 3 -> 2; matrix products, arithmetic and copies ran while one was open for 0% -> 0% of each run, Pallas kernels for 3% -> 0%
where the time goes in v9:
time: 147 us; the launch traced here: 146 us
  blocking collectives  90.4 us (61%)
  Pallas kernels  18.3 us (12%)
  starting transfers between devices  17.9 us (12%)
  waiting for transfers between devices  14.5 us (10%)
  local copies, waits for them, and re-layouts  3.58 us (2%)
    all_gather x2, blocking collectives, over_pts(): return lax.all_gather(rows, 'pts', axis=0, tiled=True)  63.3 us
    all_to_all x3, blocking collectives, exchange(): lax.all_to_all(flat, axes, split_axis=0, concat_axis=0, tiled=True)  27.1 us
    pallas_call x8, Pallas kernels, call(): pl.pallas_call(kernel, name=name, out_shape=outputs, in_specs=[smem] * le...  18.3 us
    all_to_all x4, starting transfers between devices, exchange(): lax.all_to_all(flat, axes, split_axis=0, concat_axis=0, tiled=True)  17.9 us
    all_to_all x4, waiting for transfers between devices, exchange(): lax.all_to_all(flat, axes, split_axis=0, concat_axis=0, tiled=True)  14.5 us
    unnamed x12, local copies, waits for them, and re-layouts  3.58 us
  transfers between devices with their start and end apart: 4, of which 2 were waited for; matrix products, arithmetic and copies ran while one was open for 0% of the time, Pallas kernels for 0%

profile of v9, /device:TPU:0, one launch (start us, length us, event | category | flops | bytes accessed | tf_op | source)
XLA Modules:
  0.0 146.0 jit_solution(14301398841363438602)
XLA Ops:
  0.6 6.4 %setup.1 = (f32[192,128]{1,0:T(8,128)}, f32[576,128]{1,0:T(8,128)S(1)}, f32[192,128]{1,0:T(8,128)S(1)}, f32[6,16,256]{2,1,0:T(8,128)S(1)}, f32[3,16,256]{2,1,0:T...) custom-call(f32[18,4096]{1,0:T(8,128)} %refs_0_.1, f32[6,4096]{1,0:T(8,128)} %refs_1_.1, ...), custom_call_target="tpu_custom_call" | custom-call | tf_op jit(solution)/shard_map/setup/pallas_call | solution.py:485
  7.1 7.3 %all-to-all-start = ((f32[32,1,768]{2,1,0:T(1,128)}), f32[32,1,768]{2,1,0:T(1,128)S(1)}, u32[]{:S(2)}, u32[]{:S(2)}) async-start(f32[32,1,768]{2,1,0:T(1,128)} %bitcast.4), calls=%async_computation | async-start | bytes 196608 | tf_op jit(solution)/shard_map/all_to_all | solution.py:508
  14.4 7.8 %all-to-all-done = f32[32,1,768]{2,1,0:T(1,128)S(1)} async-done(((f32[32,1,768]{2,1,0:T(1,128)}), f32[32,1,768]{2,1,0:T(1,128)S(1)}, u32[]{:S(2)}, u32[]{:S(2)}) %all-to-all-start) | async-done | bytes 98336 | tf_op jit(solution)/shard_map/all_to_all | solution.py:508
  22.2 0.7 first_owner.1
  22.9 9.0 %all_to_all.35 = f32[32,1,384]{2,1,0:T(1,128)S(1)} all-to-all(f32[32,1,384]{2,1,0:T(1,128)S(1)} %bitcast.29), channel_id=1, replica_groups=mesh['pts'=8,'cams'=4] {'pts','cams'}, dimensions={0} | all-to-all | bytes 98304 | tf_op jit(solution)/shard_map/all_to_all | solution.py:508
  31.9 2.7 %schur.2 = (f32[96,128]{1,0:T(8,128)S(1)}, f32[8,128]{1,0:T(8,128)S(1)}, f32[9,8,128]{2,1,0:T(8,128)S(1)}, f32[9,8,128]{2,1,0:T(8,128)S(1)}, f32[3,16,256]{2,1,0:T(8,128)S(1)}) custom-call(f32[96,128]{1,0:T(8,128)S(1)} %bitcast.30, f32[576,128]{1,0:T(8,128)S(1)} %get-tuple-element.39.a_ref, f32[192,128]{1,0:T(8,128)S(1)} %get-tuple-element.40.b_ref, ...), custom_call_target="tpu_custom_call" | custom-call | flops 2000000000 | bytes 10000000 | tf_op jit(solution)/shard_map/schur/pallas_call | solution.py:485
  34.6 9.0 %all_to_all.36 = f32[32,1,384]{2,1,0:T(1,128)S(1)} all-to-all(f32[32,1,384]{2,1,0:T(1,128)S(1)} %bitcast.31), channel_id=1, replica_groups=mesh['pts'=8,'cams'=4] {'pts','cams'}, dimensions={0} | all-to-all | bytes 98304 | tf_op jit(solution)/shard_map/all_to_all | solution.py:508
  44.2 9.0 %all_to_all.37 = f32[32,1,384]{2,1,0:T(1,128)S(1)} all-to-all(f32[32,1,384]{2,1,0:T(1,128)S(1)} %bitcast.32), channel_id=1, replica_groups=mesh['pts'=8,'cams'=4] {'pts','cams'}, dimensions={0} | all-to-all | bytes 98304 | tf_op jit(solution)/shard_map/all_to_all | solution.py:508
  53.2 3.3 %schur.3 = (f32[96,128]{1,0:T(8,128)}, f32[8,128]{1,0:T(8,128)S(1)}, f32[9,8,128]{2,1,0:T(8,128)S(1)}, f32[9,8,128]{2,1,0:T(8,128)S(1)}, f32[3,16,256]{2,1,0:T(8,128)S(1)}, /*index=5*/f32[3,16,256]{2,1,0:T(8,128)S(1)}) custom-call(f32[96,128]{1,0:T(8,128)S(1)} %bitcast.28, f32[576,128]{1,0:T(8,128)S(1)} %get-tuple-element.39.a_ref, ...), custom_call_target="tpu_custom_call" | custom-call | flops 2000000000 | bytes 10000000 | tf_op jit(solution)/shard_map/schur/pallas_call | solution.py:485
  56.6 0.6 copy-done
  57.2 0.6 copy-done.4
  57.8 2.6 %all-to-all-start.4 = ((f32[32,1,384]{2,1,0:T(1,128)}), f32[32,1,384]{2,1,0:T(1,128)S(1)}, u32[]{:S(2)}, u32[]{:S(2)}) async-start(f32[32,1,384]{2,1,0:T(1,128)} %bitcast.12), calls=%async_computation.4 | async-start | bytes 98304 | tf_op jit(solution)/shard_map/all_to_all | solution.py:508
  60.4 0.6 maximum_bitcast_fusion
  61.0 6.7 %all-to-all-done.4 = f32[32,1,384]{2,1,0:T(1,128)S(1)} async-done(((f32[32,1,384]{2,1,0:T(1,128)}), f32[32,1,384]{2,1,0:T(1,128)S(1)}, u32[]{:S(2)}, u32[]{:S(2)}) %all-to-all-start.4) | async-done | bytes 49184 | tf_op jit(solution)/shard_map/all_to_all | solution.py:508
  67.7 1.2 owner.3
  68.9 2.6 %all-to-all-start.5 = ((f32[32,1,384]{2,1,0:T(1,128)}), f32[32,1,384]{2,1,0:T(1,128)S(1)}, u32[]{:S(2)}, u32[]{:S(2)}) async-start(f32[32,1,384]{2,1,0:T(1,128)} %bitcast.14), calls=%async_computation.5 | async-start | bytes 98304 | tf_op jit(solution)/shard_map/all_to_all | solution.py:508
  71.4 32.1 %all_gather.6.early_ref = f32[1152,128]{1,0:T(8,128)S(1)} all-gather(f32[144,128]{1,0:T(8,128)} %maximum_bitcast_fusion), channel_id=1, replica_groups=mesh['pts'=8,'cams'=4] {'pts'}, dimensions={0}, use_global_device_ids=true | all-gather | bytes 663552 | tf_op jit(solution)/shard_map/all_gather | solution.py:569
  103.6 0.8 copy-done.1
  104.4 0.8 copy-done.3
  105.2 0.8 copy-done.5
  106.0 2.4 %schur_last.1 = (f32[32,128]{1,0:T(8,128)}, f32[8,128]{1,0:T(8,128)S(1)}, f32[9,8,128]{2,1,0:T(8,128)}, f32[9,8,128]{2,1,0:T(8,128)}, f32[3,16,256]{2,1,0:T(8,128)S(1)}, /*index=5*/f32[3,16,256]{2,1,0:T(8,128)S(1)}) custom-call(f32[96,128]{1,0:T(8,128)S(1)} %bitcast.27, f32[576,128]{1,0:T(8,128)S(1)} %get-tuple-element.39.a_ref, ...), custom_call_target="tpu_custom_call" | custom-call | flops 2000000000 | bytes 10000000 | tf_op jit(solution)/shard_map/schur_last/pallas_call | solution.py:485
  108.3 5.5 %all-to-all-start.6 = ((f32[32,1,128]{2,1,0:T(1,128)}), f32[32,1,128]{2,1,0:T(1,128)S(1)}, u32[]{:S(2)}, u32[]{:S(2)}) async-start(f32[32,1,128]{2,1,0:T(1,128)} %bitcast.17), calls=%async_computation.6 | async-start | bytes 32768 | tf_op jit(solution)/shard_map/all_to_all | solution.py:508
  113.8 31.2 %all_gather.7.late_ref = f32[576,128]{1,0:T(8,128)S(1)} all-gather(f32[72,128]{1,0:T(8,128)S(1)} %bitcast.33), channel_id=1, replica_groups=mesh['pts'=8,'cams'=4] {'pts'}, dimensions={0}, use_global_device_ids=true | all-gather | bytes 331776 | tf_op jit(solution)/shard_map/all_gather | solution.py:569
  144.9 1.1 final.1
  (10 shorter events, 0.6 us)
Async XLA Ops:
  7.1 15.1 %all-to-all-start = ((f32[32,1,768]{2,1,0:T(1,128)}), f32[32,1,768]{2,1,0:T(1,128)S(1)}, u32[]{:S(2)}, u32[]{:S(2)}) async-start(f32[32,1,768]{2,1,0:T(1,128)} %bitcast.4), calls=%async_computation | async-start | bytes 196608 | tf_op jit(solution)/shard_map/all_to_all | solution.py:508
  56.6 0.6 copy-start
  57.2 0.6 copy-start.4
  57.8 45.8 %copy-start.2 = (f32[3,16,256]{2,1,0:T(8,128)}, f32[3,16,256]{2,1,0:T(8,128)S(1)}, u32[]{:S(2)}) copy-start(f32[3,16,256]{2,1,0:T(8,128)S(1)} %get-tuple-element.64.grad_ref) | copy-start | bytes 147460
  57.8 9.9 %all-to-all-start.4 = ((f32[32,1,384]{2,1,0:T(1,128)}), f32[32,1,384]{2,1,0:T(1,128)S(1)}, u32[]{:S(2)}, u32[]{:S(2)}) async-start(f32[32,1,384]{2,1,0:T(1,128)} %bitcast.12), calls=%async_computation.4 | async-start | bytes 98304 | tf_op jit(solution)/shard_map/all_to_all | solution.py:508
  68.9 34.7 %all-to-all-start.5 = ((f32[32,1,384]{2,1,0:T(1,128)}), f32[32,1,384]{2,1,0:T(1,128)S(1)}, u32[]{:S(2)}, u32[]{:S(2)}) async-start(f32[32,1,384]{2,1,0:T(1,128)} %bitcast.14), calls=%async_computation.5 | async-start | bytes 98304 | tf_op jit(solution)/shard_map/all_to_all | solution.py:508
  103.6 0.8 copy-start.1
  104.4 0.8 copy-start.3
  105.2 0.8 copy-start.5
  108.3 36.6 %all-to-all-start.6 = ((f32[32,1,128]{2,1,0:T(1,128)}), f32[32,1,128]{2,1,0:T(1,128)S(1)}, u32[]{:S(2)}, u32[]{:S(2)}) async-start(f32[32,1,128]{2,1,0:T(1,128)} %bitcast.17), calls=%async_computation.6 | async-start | bytes 32768 | tf_op jit(solution)/shard_map/all_to_all | solution.py:508

commit v10 on v7

--- a/solution.py
+++ b/solution.py
@@ -17,7 +17,7 @@
 PT_HI = PT_DEV // PT_LO
 PIECES = 2
 FINE = 3
-NEAR = 2
+FIRST = 4
 VMEM_LIMIT = 24 * 1024 * 1024
 
 damping_camera = 1.0
@@ -86,33 +86,6 @@
     return result
 
 
-def gather_factors(tables):
-    pieces = [piece for table in tables for piece in cut(table)]
-    left = jnp.concatenate(pieces, axis=0).astype(bf16)
-    padded, rows = -(-len(tables) // SUB) * SUB, left.shape[0]
-    owner = lax.broadcasted_iota(jnp.int32, (padded, rows), 1) // (rows // len(tables))
-    chosen = (owner == lax.broadcasted_iota(jnp.int32, (padded, rows), 0)).astype(f32).astype(bf16)
-    return left, chosen
-
-
-def matmul_gather(group, factors, count, place_ref, high_of_row, high_count, picked_ref, found_ref):
-    left, chosen = factors
-    rows, padded = left.shape[0], chosen.shape[0]
-    width = SUB * LANES
-    picked = jnp.dot(left, place_ref[:, group * width : (group + 1) * width], preferred_element_type=f32)
-    for s in range(SUB):
-        mask = jnp.broadcast_to(high_of_row(group * SUB + s), (high_count, LANES)) == sub_iota(high_count)
-        for first in range(0, rows, high_count):
-            block = picked[first : first + high_count, s * LANES : (s + 1) * LANES]
-            columns = slice(group * width + s * LANES, group * width + (s + 1) * LANES)
-            picked_ref[first : first + high_count, columns] = jnp.where(mask, block, 0.0).astype(bf16)
-    total = jnp.dot(chosen, picked_ref[:rows, group * width : (group + 1) * width], preferred_element_type=f32)
-    start = group * SUB * padded
-    for s in range(SUB):
-        found_ref[start + s * padded : start + (s + 1) * padded, :] = total[:, s * LANES : (s + 1) * LANES]
-    return [found_ref[pl.ds(start + c, SUB, stride=padded), :] for c in range(count)]
-
-
 def spread_row(index, parts, high, high_count, spread_ref):
     columns = slice(index * LANES, (index + 1) * LANES)
     mask = jnp.broadcast_to(high, (high_count, LANES)) == sub_iota(high_count)
@@ -168,6 +141,12 @@
             total = total + row
         values.append(total)
     return values
+
+
+def point_gather(ref, point):
+    wide = PT_LO // LANES
+    row = lambda c, k: ref[c, k // wide : k // wide + 1, (k % wide) * LANES : (k % wide + 1) * LANES]
+    return gather_rows(row, PT_HI * wide, point // LANES, point % LANES, 3)
 
 
 def slot_place(slot, sizes):
@@ -227,13 +206,14 @@
 def setup_kernel(sizes, *refs):
     sources, refs = refs[:6], refs[6:]
     out_ref, a_ref, b_ref, inv_ref, grad_ref, place_point_ref, new_slot_ref, new_point_ref = refs[:8]
-    r_ref, parts_ref, spread_ref, picked_ref, found_ref, place_slot_ref, place_list_ref = refs[8:15]
-    jac_ref, pjac_ref, res_ref, slot_ref, point_ref, list_ref = refs[15:21]
-    semaphores = refs[21]
+    refs = refs[8:]
+    r_ref, parts_ref, spread_ref, table_ref, place_slot_ref, place_list_ref = refs[:6]
+    jac_ref, pjac_ref, res_ref, slot_ref, point_ref, list_ref = refs[6:12]
+    semaphores = refs[12]
     rows = sizes.rows
     copies = [
         pltpu.make_async_copy(source, target, semaphores.at[k])
-        for k, (source, target) in enumerate(zip(sources, refs[15:21]))
+        for k, (source, target) in enumerate(zip(sources, refs[6:12]))
     ]
     for copy in copies:
         copy.start()
@@ -289,10 +269,10 @@
     for k in range(3):
         grad_ref[k] = normal[6 + k]
     eliminated = solve(inverse, normal[6:])
-    picking = gather_factors(eliminated)
+    for k in range(3):
+        table_ref[k] = eliminated[k]
     for group in range(rows // SUB):
-        at_point = matmul_gather(group, picking, 3, place_point_ref,
-                                 lambda row: point_ref[row : row + 1, :] >> 8, PT_HI, picked_ref, found_ref)
+        at_point = point_gather(table_ref, point_ref[group * SUB : (group + 1) * SUB, :])
         b = [at(b_ref, k, group) for k in range(6)]
         errors = [at(r_ref, i, group) - sum(b[3 * i + k] * at_point[k] for k in range(3)) for i in range(2)]
         a = [at(a_ref, k, group) for k in range(2 * CP)]
@@ -402,7 +382,7 @@
     refs = refs[5:]
     if not start:
         new_grad_ref = refs.pop(0)
-    q_ref, parts_ref, spread_ref, picked_ref, found_ref, place_slot_ref = refs
+    q_ref, parts_ref, spread_ref, table_ref, place_slot_ref = refs
     rows = sizes.rows
 
     def at(ref, comp, group):
@@ -444,10 +424,10 @@
             new_grad_ref[k] = grad_ref[k] + step_ref[:1, :1] * sum_ref[k]
 
     inner = None
-    picking = gather_factors(folded)
+    for k in range(3):
+        table_ref[k] = folded[k]
     for group in range(rows // SUB):
-        at_point = matmul_gather(group, picking, 3, place_point_ref,
-                                 lambda row: point_ref[row : row + 1, :] >> 8, PT_HI, picked_ref, found_ref)
+        at_point = point_gather(table_ref, point_ref[group * SUB : (group + 1) * SUB, :])
         q = [at(q_ref, i, group) for i in range(2)]
         errors = [q[i] - sum(at(b_ref, 3 * i + k, group) * at_point[k] for k in range(3)) for i in range(2)]
         here = q[0] * errors[0] + q[1] * errors[1]
@@ -555,11 +535,7 @@
     owned_scratch = pltpu.VMEM((CP, sizes.own_rows, LANES), f32)
     entries = sizes.pts * LANES
 
-    gather_scratch = [
-        pltpu.VMEM((3 * PIECES * PT_HI, sizes.obs), bf16),
-        pltpu.VMEM((rows * SUB, LANES), f32),
-        pltpu.VMEM((LANES, sizes.obs), bf16),
-    ]
+    gather_scratch = [pltpu.VMEM((3, PT_HI, PT_LO), f32), pltpu.VMEM((LANES, sizes.obs), bf16)]
 
     def parts_scratch(count):
         return pltpu.VMEM((rows // SUB, count * SUB, LANES), f32)
@@ -608,7 +584,7 @@
         start, last = iteration == 0, iteration == ITERS - 1
         earlier = [] if start else [product, slots, direction, step, sums]
         if last:
-            neighbour = flipped(fields, NEAR)
+            neighbour = flipped(fields, FIRST)
         arrived = exchange(out)
         if last:
             (both,) = call(
@@ -618,7 +594,7 @@
                 [kept(4 * CP * sizes.own_rows, LANES)],
                 [],
             )
-            flips = [1 << bit for bit in range(sizes.pts.bit_length() - 1) if 1 << bit != NEAR]
+            flips = [1 << bit for bit in range(sizes.pts.bit_length() - 1) if 1 << bit != FIRST]
             flips = flips[1:] + flips[:1]
             early = {flip: flipped(both, flip) for flip in (flips[0], flips[-1])}
         results = call(
@@ -636,7 +612,7 @@
             gradient = results[5]
         if last:
             early[flips[0]], out = lax.optimization_barrier((early[flips[0]], out))
-            gathered, masks = [both], [(0, NEAR)]
+            gathered, masks = [both], [(0, FIRST)]
             for flip in flips:
                 gathered += [early[flip] if value is both and flip in early else flipped(value, flip) for value in gathered]
                 masks += [tuple(mask ^ flip for mask in pair) for pair in masks]

time: 100 us -> 94.3 us (0.943)
  Pallas kernels: 21.6 us -> 17.7 us
  waiting for transfers between devices: 19.7 us -> 17.2 us
    pallas_call x9, Pallas kernels: 21.6 us -> 17.7 us  [call(): pl.pallas_call(kernel, name=name, out_shape=outputs, in_specs=[smem] * le...]
    ppermute x4, waiting for transfers between devices: 4.72 us -> 2.28 us  [flipped(): return lax.ppermute(value, 'pts', [(p, p ^ flip) for p in range(sizes.pts)])]
where the time goes in v10:
time: 94.3 us; the launch traced here: 94 us
  blocking collectives  46 us (49%)
  Pallas kernels  17.7 us (19%)
  waiting for transfers between devices  17.2 us (18%)
  starting transfers between devices  12.3 us (13%)
    all_to_all x5, blocking collectives, exchange(): lax.all_to_all(flat, axes, split_axis=0, concat_axis=0, tiled=True)  46 us
    pallas_call x9, Pallas kernels, call(): pl.pallas_call(kernel, name=name, out_shape=outputs, in_specs=[smem] * le...  17.7 us
    all_to_all x2, waiting for transfers between devices, exchange(): lax.all_to_all(flat, axes, split_axis=0, concat_axis=0, tiled=True)  14.9 us
    all_to_all x2, starting transfers between devices, exchange(): lax.all_to_all(flat, axes, split_axis=0, concat_axis=0, tiled=True)  9.83 us
    ppermute x4, starting transfers between devices, flipped(): return lax.ppermute(value, 'pts', [(p, p ^ flip) for p in range(sizes.pts)])  2.44 us
    ppermute x4, waiting for transfers between devices, flipped(): return lax.ppermute(value, 'pts', [(p, p ^ flip) for p in range(sizes.pts)])  2.28 us
  transfers between devices with their start and end apart: 6, of which 3 were waited for; matrix products, arithmetic and copies ran while one was open for 0% of the time, Pallas kernels for 3%

profile of v10, /device:TPU:0, one launch (start us, length us, event | category | flops | bytes accessed | tf_op | source)
XLA Modules:
  0.0 94.0 jit_solution(9911456811612356441)
XLA Ops:
  0.6 6.5 %setup.1 = (f32[192,128]{1,0:T(8,128)}, f32[576,128]{1,0:T(8,128)S(1)}, f32[192,128]{1,0:T(8,128)S(1)}, f32[6,16,256]{2,1,0:T(8,128)S(1)}, f32[3,16,256]{2,1,0:T...) custom-call(f32[18,4096]{1,0:T(8,128)} %refs_0_.1, f32[6,4096]{1,0:T(8,128)} %refs_1_.1, ...), custom_call_target="tpu_custom_call" | custom-call | tf_op jit(solution)/shard_map/setup/pallas_call | solution.py:500
  7.1 7.3 %all-to-all-start = ((f32[32,1,768]{2,1,0:T(1,128)}), f32[32,1,768]{2,1,0:T(1,128)S(1)}, u32[]{:S(2)}, u32[]{:S(2)}) async-start(f32[32,1,768]{2,1,0:T(1,128)} %bitcast.5), calls=%async_computation | async-start | bytes 196608 | tf_op jit(solution)/shard_map/all_to_all | solution.py:523
  14.4 7.8 %all-to-all-done = f32[32,1,768]{2,1,0:T(1,128)S(1)} async-done(((f32[32,1,768]{2,1,0:T(1,128)}), f32[32,1,768]{2,1,0:T(1,128)S(1)}, u32[]{:S(2)}, u32[]{:S(2)}) %all-to-all-start) | async-done | bytes 98336 | tf_op jit(solution)/shard_map/all_to_all | solution.py:523
  22.2 0.7 first_owner.1
  22.9 9.0 %all_to_all.35 = f32[32,1,384]{2,1,0:T(1,128)S(1)} all-to-all(f32[32,1,384]{2,1,0:T(1,128)S(1)} %bitcast.31), channel_id=1, replica_groups=mesh['pts'=8,'cams'=4] {'pts','cams'}, dimensions={0} | all-to-all | bytes 98304 | tf_op jit(solution)/shard_map/all_to_all | solution.py:523
  32.0 2.7 %schur.2 = (f32[96,128]{1,0:T(8,128)S(1)}, f32[8,128]{1,0:T(8,128)S(1)}, f32[9,8,128]{2,1,0:T(8,128)S(1)}, f32[9,8,128]{2,1,0:T(8,128)S(1)}, f32[3,16,256]{2,1,0:T(8,128)S(1)}) custom-call(f32[96,128]{1,0:T(8,128)S(1)} %bitcast.30, f32[576,128]{1,0:T(8,128)S(1)} %get-tuple-element.41.a_ref, f32[192,128]{1,0:T(8,128)S(1)} %get-tuple-element.42.b_ref, ...), custom_call_target="tpu_custom_call" | custom-call | flops 2000000000 | bytes 10000000 | tf_op jit(solution)/shard_map/schur/pallas_call | solution.py:500
  34.7 9.0 %all_to_all.36 = f32[32,1,384]{2,1,0:T(1,128)S(1)} all-to-all(f32[32,1,384]{2,1,0:T(1,128)S(1)} %bitcast.32), channel_id=1, replica_groups=mesh['pts'=8,'cams'=4] {'pts','cams'}, dimensions={0} | all-to-all | bytes 98304 | tf_op jit(solution)/shard_map/all_to_all | solution.py:523
  43.7 0.6 owner.1
  44.3 9.0 %all_to_all.37 = f32[32,1,384]{2,1,0:T(1,128)S(1)} all-to-all(f32[32,1,384]{2,1,0:T(1,128)S(1)} %bitcast.33), channel_id=1, replica_groups=mesh['pts'=8,'cams'=4] {'pts','cams'}, dimensions={0} | all-to-all | bytes 98304 | tf_op jit(solution)/shard_map/all_to_all | solution.py:523
  53.3 2.7 %schur.3 = (f32[96,128]{1,0:T(8,128)S(1)}, f32[8,128]{1,0:T(8,128)S(1)}, f32[9,8,128]{2,1,0:T(8,128)S(1)}, f32[9,8,128]{2,1,0:T(8,128)S(1)}, f32[3,16,256]{2,1,0:T(8,128)S(1)}, /*index=5*/f32[3,16,256]{2,1,0:T(8,128)S(1)}) custom-call(f32[96,128]{1,0:T(8,128)S(1)} %bitcast.27, f32[576,128]{1,0:T(8,128)S(1)} %get-tuple-element.41.a_ref, ...), custom_call_target="tpu_custom_call" | custom-call | flops 2000000000 | bytes 10000000 | tf_op jit(solution)/shard_map/schur/pallas_call | solution.py:500
  56.0 9.0 %all_to_all.38 = f32[32,1,384]{2,1,0:T(1,128)S(1)} all-to-all(f32[32,1,384]{2,1,0:T(1,128)S(1)} %bitcast.28), channel_id=1, replica_groups=mesh['pts'=8,'cams'=4] {'pts','cams'}, dimensions={0} | all-to-all | bytes 98304 | tf_op jit(solution)/shard_map/all_to_all | solution.py:523
  65.0 1.0 %owner_final.1 = (f32[96,128]{1,0:T(8,128)S(1)}, f32[9,8,128]{2,1,0:T(8,128)S(1)}, f32[9,8,128]{2,1,0:T(8,128)}, f32[8,128]{1,0:T(8,128)S(1)}, f32[216,128]{1,0:T(8,128)S(1)}) custom-call(f32[96,128]{1,0:T(8,128)S(1)} %bitcast.24, s32[8,128]{1,0:T(8,128)S(1)} %get-tuple-element.51.entry_ref, f32[9,8,128]{2,1,0:T(8,128)S(1)} %get-tuple-element.47.pre_ref, ...), custom_call_target="tpu_custom_call" | custom-call | tf_op jit(solution)/shard_map/owner_final/pallas_call | solution.py:500
  66.0 0.6 collective-permute-start
  66.7 9.9 %all_to_all.39 = f32[32,1,384]{2,1,0:T(1,128)S(1)} all-to-all(f32[32,1,384]{2,1,0:T(1,128)S(1)} %bitcast.29), channel_id=1, replica_groups=mesh['pts'=8,'cams'=4] {'pts','cams'}, dimensions={0} | all-to-all | bytes 98304 | tf_op jit(solution)/shard_map/all_to_all | solution.py:523
  76.6 0.0 collective-permute-done.other_ref
  76.6 0.1 tail.1.refs_0_
  76.7 0.7 collective-permute-start.1
  77.4 2.4 %schur_last.1 = (f32[32,128]{1,0:T(8,128)}, f32[8,128]{1,0:T(8,128)S(1)}, f32[9,8,128]{2,1,0:T(8,128)}, f32[9,8,128]{2,1,0:T(8,128)}, f32[3,16,256]{2,1,0:T(8,128)S(1)}, /*index=5*/f32[3,16,256]{2,1,0:T(8,128)S(1)}) custom-call(f32[96,128]{1,0:T(8,128)S(1)} %bitcast.23, f32[576,128]{1,0:T(8,128)S(1)} %get-tuple-element.41.a_ref, ...), custom_call_target="tpu_custom_call" | custom-call | flops 2000000000 | bytes 10000000 | tf_op jit(solution)/shard_map/schur_last/pallas_call | solution.py:500
  79.8 0.6 collective-permute-start.2
  80.4 2.3 %collective-permute-done.1.refs_1_ = f32[288,128]{1,0:T(8,128)S(1)} collective-permute-done((f32[288,128]{1,0:T(8,128)S(1)}, f32[288,128]{1,0:T(8,128)S(1)}, u32[]{:S(2)}, u32[]{:S(2)}) %collective-permute-start.1) | collective-permute-done | bytes 147488 | tf_op jit(solution)/shard_map/ppermute | solution.py:526
  82.7 0.5 collective-permute-start.3
  83.2 2.5 %all-to-all-start.6 = ((f32[32,1,128]{2,1,0:T(1,128)}), f32[32,1,128]{2,1,0:T(1,128)S(1)}, u32[]{:S(2)}, u32[]{:S(2)}) async-start(f32[32,1,128]{2,1,0:T(1,128)} %bitcast.18), calls=%async_computation.6 | async-start | bytes 32768 | tf_op jit(solution)/shard_map/all_to_all | solution.py:523
  85.7 7.1 %all-to-all-done.6 = f32[32,1,128]{2,1,0:T(1,128)S(1)} async-done(((f32[32,1,128]{2,1,0:T(1,128)}), f32[32,1,128]{2,1,0:T(1,128)S(1)}, u32[]{:S(2)}, u32[]{:S(2)}) %all-to-all-start.6) | async-done | bytes 16416 | tf_op jit(solution)/shard_map/all_to_all | solution.py:523
  92.9 1.1 %final.1 = (f32[9,8192]{1,0:T(8,128)}, f32[3,4096]{1,0:T(4,128)}) custom-call(s32[1]{0:T(128)} %bitcast.run_ref, f32[32,128]{1,0:T(8,128)S(1)} %bitcast.26, f32[8,128]{1,0:T(8,128)S(1)} %get-tuple-element.72.product_ref, f32[6,16,256]{2,1,0:T(8,128)S(1)} %get-tuple-element.43.inv_ref, f32[3,16,256]{2,1,0:T(8,128)S(1)} %get-tuple-element.73.grad_ref, ...), custom_call_target="tpu_custom_call" | custom-call | tf_op jit(solution)/shard_map/final/pallas_call | solution.py:500
  (2 shorter events, 0.0 us)
Async XLA Ops:
  7.1 15.1 %all-to-all-start = ((f32[32,1,768]{2,1,0:T(1,128)}), f32[32,1,768]{2,1,0:T(1,128)S(1)}, u32[]{:S(2)}, u32[]{:S(2)}) async-start(f32[32,1,768]{2,1,0:T(1,128)} %bitcast.5), calls=%async_computation | async-start | bytes 196608 | tf_op jit(solution)/shard_map/all_to_all | solution.py:523
  66.0 10.6 %collective-permute-start = (f32[216,128]{1,0:T(8,128)S(1)}, f32[216,128]{1,0:T(8,128)S(1)}, u32[]{:S(2)}, u32[]{:S(2)}) collective-permute-start(f32[216,128]{1,0:T(8,128)S(1)} %get-tuple-element.64.own_ref), channel_id=1, source_target_pairs={{0,16},{4,20},{8,24},{12,28},{16,0},{20,4},{24,8},{28,12},{1,17},{... | collective-permute-start | bytes 331784 | tf_op jit(solution)/shard_map/ppermute | solution.py:526
  76.7 5.9 %collective-permute-start.1 = (f32[288,128]{1,0:T(8,128)S(1)}, f32[288,128]{1,0:T(8,128)S(1)}, u32[]{:S(2)}, u32[]{:S(2)}) collective-permute-start(f32[288,128]{1,0:T(8,128)S(1)} %tail.1.refs_0_), channel_id=1, source_target_pairs={{0,8},{4,12},{8,0},{12,4},{16,24},{20,28},{24,16},{28,20},{1,9},{5... | collective-permute-start | bytes 442376 | tf_op jit(solution)/shard_map/ppermute | solution.py:526
  79.8 5.9 %collective-permute-start.2 = (f32[288,128]{1,0:T(8,128)S(1)}, f32[288,128]{1,0:T(8,128)S(1)}, u32[]{:S(2)}, u32[]{:S(2)}) collective-permute-start(f32[288,128]{1,0:T(8,128)S(1)} %tail.1.refs_0_), channel_id=1, source_target_pairs={{0,4},{4,0},{8,12},{12,8},{16,20},{20,16},{24,28},{28,24},{1,5},{5... | collective-permute-start | bytes 442376 | tf_op jit(solution)/shard_map/ppermute | solution.py:526
  82.7 10.2 %collective-permute-start.3 = (f32[288,128]{1,0:T(8,128)S(1)}, f32[288,128]{1,0:T(8,128)S(1)}, u32[]{:S(2)}, u32[]{:S(2)}) collective-permute-start(f32[288,128]{1,0:T(8,128)S(1)} %collective-permute-done.1.refs_1_), channel_id=1, source_target_pairs={{0,4},{4,0},{8,12},{12,8},{16,20},{20,16},{24,28},{28,24},{1,5},{5... | collective-permute-start | bytes 442376 | tf_op jit(solution)/shard_map/ppermute | solution.py:526
  83.2 9.7 %all-to-all-start.6 = ((f32[32,1,128]{2,1,0:T(1,128)}), f32[32,1,128]{2,1,0:T(1,128)S(1)}, u32[]{:S(2)}, u32[]{:S(2)}) async-start(f32[32,1,128]{2,1,0:T(1,128)} %bitcast.18), calls=%async_computation.6 | async-start | bytes 32768 | tf_op jit(solution)/shard_map/all_to_all | solution.py:523

commit v11 on v10

--- a/solution.py
+++ b/solution.py
@@ -161,7 +161,7 @@
     return first, second, third
 
 
-def write_messages(fields, scalar, groups, message, out_ref, sizes, extra=None):
+def write_messages(fields, scalar, groups, message, out_ref, sizes, extra=None, column=None):
     which = lane_iota(sizes.pts) // sizes.block
     for g in range(groups):
         rows = fields[g * sizes.cams : (g + 1) * sizes.cams]
@@ -173,7 +173,7 @@
             out_ref[pl.ds(c * message + g, sizes.pts, stride=sizes.cams * message), :] = value
     for g in range(groups, message):
         for c in range(sizes.cams):
-            value = extra if (extra is not None and g == groups) else jnp.zeros((sizes.pts, LANES), f32)
+            value = jnp.where(column == c, extra, 0.0)
             out_ref[pl.ds(c * message + g, sizes.pts, stride=sizes.cams * message), :] = value
 
 
@@ -203,7 +203,7 @@
     return jnp.sum(chosen, keepdims=True)
 
 
-def setup_kernel(sizes, *refs):
+def setup_kernel(sizes, column_ref, *refs):
     sources, refs = refs[:6], refs[6:]
     out_ref, a_ref, b_ref, inv_ref, grad_ref, place_point_ref, new_slot_ref, new_point_ref = refs[:8]
     refs = refs[8:]
@@ -217,22 +217,18 @@
     ]
     for copy in copies:
         copy.start()
-    for copy in copies:
-        copy.wait()
-    new_slot_ref[...] = slot_ref[...]
+    for k in (1, 2, 4):
+        copies[k].wait()
     new_point_ref[...] = point_ref[...]
     for j in range(rows):
         columns = slice(j * LANES, (j + 1) * LANES)
-        for start in range(0, 2 * CP, SUB):
-            size = min(SUB, 2 * CP - start)
-            a_ref[pl.ds(start * rows + j, size, stride=rows), :] = jac_ref[start : start + size, columns]
         b_ref[pl.ds(j, 6, stride=rows), :] = pjac_ref[:, columns]
         r_ref[pl.ds(j, 2, stride=rows), :] = res_ref[:, columns]
 
     def at(ref, comp, group):
         return ref[comp * rows + group * SUB : comp * rows + (group + 1) * SUB, :]
 
-    normal_pieces = [FINE] * 6 + [PIECES] * 3
+    normal_pieces = [FINE] * 9
 
     for group in range(rows // SUB):
         b = [at(b_ref, k, group) for k in range(6)]
@@ -271,6 +267,16 @@
     eliminated = solve(inverse, normal[6:])
     for k in range(3):
         table_ref[k] = eliminated[k]
+    for k in (0, 3, 5):
+        copies[k].wait()
+    new_slot_ref[...] = slot_ref[...]
+    for j in range(rows):
+        for start in range(0, 2 * CP, SUB):
+            size = min(SUB, 2 * CP - start)
+            a_ref[pl.ds(start * rows + j, size, stride=rows), :] = jac_ref[
+                start : start + size, j * LANES : (j + 1) * LANES
+            ]
+
     for group in range(rows // SUB):
         at_point = point_gather(table_ref, point_ref[group * SUB : (group + 1) * SUB, :])
         b = [at(b_ref, k, group) for k in range(6)]
@@ -299,7 +305,7 @@
             place_row(c * pieces + half, low, LANES, place_list_ref)
     result = scatter(2, sizes.cams * sizes.slot, sizes.pts, LANES, spread_ref, place_list_ref)
     listed = result[: sizes.pts] * 256.0 + result[sizes.pts : 2 * sizes.pts]
-    write_messages(fields, None, sizes.first_groups, sizes.first_message, out_ref, sizes, extra=listed)
+    write_messages(fields, None, sizes.first_groups, sizes.first_message, out_ref, sizes, extra=listed, column=column_ref[0])
 
 
 def entries_scatter(fields, entry, sizes, spread_ref, place_ref):
@@ -323,12 +329,11 @@
     return jnp.sum(sum(a * b for a, b in zip(left, right)), keepdims=True)
 
 
-def first_owner_kernel(sizes, column_ref, in_ref, out_ref, entry_ref, pre_ref, rem_ref,
+def first_owner_kernel(sizes, in_ref, out_ref, entry_ref, pre_ref, rem_ref,
                        table_ref, spread_ref, place_ref):
     listed = jnp.zeros((sizes.pts, LANES), f32)
     for c in range(sizes.cams):
-        row = read_row(in_ref, c, sizes.first_groups, sizes.first_message, sizes)
-        listed = jnp.where(column_ref[0] == c, row, listed)
+        listed = listed + read_row(in_ref, c, sizes.first_groups, sizes.first_message, sizes)
     entry = listed.astype(jnp.int32) % sizes.run
     entry_ref[...] = entry
     fields = read_messages(in_ref, 2 * CP, sizes.first_message, sizes)
@@ -377,12 +382,11 @@
     if not start:
         product_ref, at_slot_ref, dir_ref, step_ref, sum_ref = refs[:5]
         refs = refs[5:]
-    out_ref, new_product_ref, new_at_slot_ref, new_dir_ref, new_sum_ref = refs[:5]
-    new_grad_ref = None
-    refs = refs[5:]
-    if not start:
-        new_grad_ref = refs.pop(0)
-    q_ref, parts_ref, spread_ref, table_ref, place_slot_ref = refs
+    out_ref, new_product_ref, new_sum_ref = refs[:3]
+    refs = refs[3:]
+    new_grad_ref = None if start else refs.pop(0)
+    q_ref, parts_ref, spread_ref, table_ref, place_slot_ref = refs[-5:]
+    new_at_slot_ref, new_dir_ref = (refs[0], None) if last else refs[:2]
     rows = sizes.rows
 
     def at(ref, comp, group):
@@ -400,7 +404,8 @@
         else:
             new_at_slot_ref[k] = fields[k] + beta * at_slot_ref[k]
             direction = direction + beta * dir_ref[k]
-        new_dir_ref[k] = direction
+        if not last:
+            new_dir_ref[k] = direction
         squares = direction * direction if squares is None else squares + direction * direction
 
     for group in range(rows // SUB):
@@ -410,13 +415,13 @@
         for i in range(2):
             q_ref[i * rows + group * SUB : i * rows + (group + 1) * SUB, :] = q[i]
         values = [at(b_ref, k, group) * q[0] + at(b_ref, 3 + k, group) * q[1] for k in range(3)]
-        parts = [part for value in values for part in cut(value)]
+        parts = [part for value in values for part in cut(value, FINE)]
         keep_parts(parts, group, parts_ref)
         for s in range(SUB):
             row = group * SUB + s
             spread_row(row, part_rows(len(parts), group, s, parts_ref), point_ref[row : row + 1, :] >> 8, PT_HI, spread_ref)
-    result = scatter(3 * PIECES, sizes.obs, PT_HI, PT_LO, spread_ref, place_point_ref)
-    sums = joined(result, 3, PT_HI)
+    result = scatter(3 * FINE, sizes.obs, PT_HI, PT_LO, spread_ref, place_point_ref)
+    sums = joined(result, 3, PT_HI, [FINE] * 3)
     folded = solve([inv_ref[k] for k in range(6)], sums)
     for k in range(3):
         new_sum_ref[k] = sums[k]
@@ -443,7 +448,7 @@
                 place_row(row, low, LANES, place_slot_ref)
     partial = jnp.sum(inner, keepdims=True) + damping_camera * jnp.sum(squares, keepdims=True)
     if last:
-        out_ref[...] = jnp.broadcast_to(partial, (sizes.devices, LANES))
+        out_ref[...] = jnp.broadcast_to(partial, (SUB, LANES))
         return
     result = scatter(CP * PIECES, sizes.obs, sizes.pts, LANES, spread_ref, place_slot_ref)
     fields = joined(result, CP, sizes.pts)
@@ -463,8 +468,7 @@
 def final_kernel(sizes, masks, run_ref, in_ref, product_ref, inv_ref, grad_ref, sum_ref, *refs):
     all_refs = refs[: len(masks)]
     cam_ref, pt_ref, table_ref = refs[len(masks) :]
-    curvature = jnp.sum(jnp.where(lane_iota(sizes.devices) == 0, in_ref[...], 0.0), keepdims=True)
-    step = (product_ref[...] / jnp.broadcast_to(curvature, (SUB, LANES)))[:1]
+    step = (product_ref[...] / in_ref[...])[:1]
     for all_ref, pair in zip(all_refs, masks):
         for j, mask in enumerate(pair):
             base_column = (run_ref[0] ^ mask) * sizes.run
@@ -560,11 +564,12 @@
             kept(rows, LANES, dtype=jnp.int32),
         ],
         [pltpu.VMEM((2 * rows, LANES), f32), parts_scratch(2 * CP * PIECES)]
-        + [pltpu.VMEM((max(spread_rows(6 * FINE + 3 * PIECES, PT_HI), spread_rows(2 * CP * PIECES, sizes.pts)), sizes.obs), bf16)]
+        + [pltpu.VMEM((max(spread_rows(9 * FINE, PT_HI), spread_rows(2 * CP * PIECES, sizes.pts)), sizes.obs), bf16)]
         + gather_scratch
         + [pltpu.VMEM((LANES, sizes.cams * sizes.slot), bf16)]
         + [pltpu.VMEM(value.shape, value.dtype) for value in given]
         + [pltpu.SemaphoreType.DMA((len(given),))],
+        scalars=[column],
         inputs_at=pl.ANY,
     )
     out, entry, precondition, remainder = call(
@@ -573,10 +578,9 @@
         [exchange(first)],
         [messages, kept(sizes.pts, LANES, dtype=jnp.int32), owned, owned],
         [owned_scratch] + factors(spread_rows(2 * CP * PIECES, sizes.own_rows), LANES, entries),
-        scalars=[column],
     )
     schur_scratch = [pltpu.VMEM((2 * rows, LANES), f32), parts_scratch(CP * PIECES)]
-    schur_scratch += [pltpu.VMEM((max(spread_rows(3 * PIECES, PT_HI), spread_rows(CP * PIECES, sizes.pts)), sizes.obs), bf16)]
+    schur_scratch += [pltpu.VMEM((max(spread_rows(3 * FINE, PT_HI), spread_rows(CP * PIECES, sizes.pts)), sizes.obs), bf16)]
     schur_scratch += gather_scratch
     at_slot = kept(CP, sizes.pts, LANES)
     product = slots = direction = step = sums = solution_ = None
@@ -602,14 +606,17 @@
             "schur_last" if last else "schur",
             [arrived, a, b, inverse, slot, point, place_point, precondition, remainder, gradient]
             + earlier,
-            [kept(sizes.devices, LANES) if last else messages, scalar, at_slot, owned, point_table]
-            + ([] if start else [point_table]),
-            schur_scratch,
+            [scalar if last else messages, scalar, point_table]
+            + ([] if start else [point_table])
+            + ([] if last else [at_slot, owned]),
+            ([pltpu.VMEM((CP, sizes.pts, LANES), f32)] if last else []) + schur_scratch,
             cost=pl.CostEstimate(flops=2_000_000_000, bytes_accessed=10_000_000, transcendentals=0),
         )
-        out, product, slots, direction, sums = results[:5]
+        out, product, sums, *results = results
         if not start:
-            gradient = results[5]
+            gradient, *results = results
+        if not last:
+            slots, direction = results
         if last:
             early[flips[0]], out = lax.optimization_barrier((early[flips[0]], out))
             gathered, masks = [both], [(0, FIRST)]
@@ -629,7 +636,7 @@
     return call(
         functools.partial(final_kernel, sizes, masks),
         "final",
-        [exchange(out), product, inverse, gradient, sums] + gathered,
+        [lax.psum(out, ("pts", "cams")), product, inverse, gradient, sums] + gathered,
         [shape(CP, CAM_OWN), shape(3, PT_DEV)],
         [pltpu.VMEM((3 * PT_HI, PT_LO), f32)],
         scalars=[lax.axis_index("pts").astype(jnp.int32).reshape(1)],

time: 94.3 us -> 122 us (1.29)
  blocking collectives: 46 us -> 99.2 us
  waiting for transfers between devices: 17.2 us -> 2.78 us
  starting transfers between devices: 12.3 us -> 2.5 us
    psum x0 -> x1, blocking collectives: none -> 38.3 us  [body(): lax.psum(out, ('pts', 'cams'))]
    all_to_all x2 -> x0, waiting for transfers between devices: 14.9 us -> none  [exchange(): lax.all_to_all(flat, axes, split_axis=0, concat_axis=0, tiled=True)]
    all_to_all x5 -> x6, blocking collectives: 46 us -> 61 us  [exchange(): lax.all_to_all(flat, axes, split_axis=0, concat_axis=0, tiled=True)]
    all_to_all x2 -> x0, starting transfers between devices: 9.83 us -> none  [exchange(): lax.all_to_all(flat, axes, split_axis=0, concat_axis=0, tiled=True)]
    pallas_call x9, Pallas kernels: 17.7 us -> 16.5 us  [call(): pl.pallas_call(kernel, name=name, out_shape=outputs, in_specs=[smem] * le...]
  transfers between devices with their start and end apart: 6 -> 4, of which waited for: 3 -> 1; matrix products, arithmetic and copies ran while one was open for 0% -> 0% of each run, Pallas kernels for 3% -> 2%
where the time goes in v11:
time: 122 us
  blocking collectives  99.2 us (81%)
  Pallas kernels  16.5 us (14%)
  waiting for transfers between devices  2.78 us (2%)
  starting transfers between devices  2.5 us (2%)
    all_to_all x6, blocking collectives, exchange(): lax.all_to_all(flat, axes, split_axis=0, concat_axis=0, tiled=True)  61 us
    psum x1, blocking collectives, body(): lax.psum(out, ('pts', 'cams'))  38.3 us
    pallas_call x9, Pallas kernels, call(): pl.pallas_call(kernel, name=name, out_shape=outputs, in_specs=[smem] * le...  16.5 us
    ppermute x4, waiting for transfers between devices, flipped(): return lax.ppermute(value, 'pts', [(p, p ^ flip) for p in range(sizes.pts)])  2.78 us
    ppermute x4, starting transfers between devices, flipped(): return lax.ppermute(value, 'pts', [(p, p ^ flip) for p in range(sizes.pts)])  2.5 us
  transfers between devices with their start and end apart: 4, of which 1 were waited for; matrix products, arithmetic and copies ran while one was open for 0% of the time, Pallas kernels for 2%

profile of v11, /device:TPU:0, one launch (start us, length us, event | category | flops | bytes accessed | tf_op | source)
XLA Modules:
  0.0 121.7 jit_solution(15095151242590490483)
XLA Ops:
  0.6 5.9 %setup.1 = (f32[192,128]{1,0:T(8,128)S(1)}, f32[576,128]{1,0:T(8,128)S(1)}, f32[192,128]{1,0:T(8,128)S(1)}, f32[6,16,256]{2,1,0:T(8,128)S(1)}, f32[3,16,256]{2,1...) custom-call(s32[1]{0:T(128)} %bitcast.1.column_ref, ...), custom_call_target="tpu_custom_call" | custom-call | tf_op jit(solution)/shard_map/setup/pallas_call | solution.py:504
  6.5 14.9 %all_to_all.30 = f32[32,1,768]{2,1,0:T(1,128)S(1)} all-to-all(f32[32,1,768]{2,1,0:T(1,128)S(1)} %bitcast.22), channel_id=1, replica_groups=mesh['pts'=8,'cams'=4] {'pts','cams'}, dimensions={0} | all-to-all | bytes 196608 | tf_op jit(solution)/shard_map/all_to_all | solution.py:527
  21.5 0.7 first_owner.1
  22.2 9.0 %all_to_all.31 = f32[32,1,384]{2,1,0:T(1,128)S(1)} all-to-all(f32[32,1,384]{2,1,0:T(1,128)S(1)} %bitcast.29), channel_id=1, replica_groups=mesh['pts'=8,'cams'=4] {'pts','cams'}, dimensions={0} | all-to-all | bytes 98304 | tf_op jit(solution)/shard_map/all_to_all | solution.py:527
  31.2 2.7 %schur.2 = (f32[96,128]{1,0:T(8,128)S(1)}, f32[8,128]{1,0:T(8,128)S(1)}, f32[3,16,256]{2,1,0:T(8,128)S(1)}, f32[9,8,128]{2,1,0:T(8,128)S(1)}, f32[9,8,128]{2,1,0:T(8,128)S(1)}) custom-call(f32[96,128]{1,0:T(8,128)S(1)} %bitcast.26, f32[576,128]{1,0:T(8,128)S(1)} %get-tuple-element.41.a_ref, f32[192,128]{1,0:T(8,128)S(1)} %get-tuple-element.42.b_ref, ...), custom_call_target="tpu_custom_call" | custom-call | flops 2000000000 | bytes 10000000 | tf_op jit(solution)/shard_map/schur/pallas_call | solution.py:504
  33.9 9.0 %all_to_all.32 = f32[32,1,384]{2,1,0:T(1,128)S(1)} all-to-all(f32[32,1,384]{2,1,0:T(1,128)S(1)} %bitcast.27), channel_id=1, replica_groups=mesh['pts'=8,'cams'=4] {'pts','cams'}, dimensions={0} | all-to-all | bytes 98304 | tf_op jit(solution)/shard_map/all_to_all | solution.py:527
  42.9 0.6 owner.1
  43.5 9.0 %all_to_all.33 = f32[32,1,384]{2,1,0:T(1,128)S(1)} all-to-all(f32[32,1,384]{2,1,0:T(1,128)S(1)} %bitcast.28), channel_id=1, replica_groups=mesh['pts'=8,'cams'=4] {'pts','cams'}, dimensions={0} | all-to-all | bytes 98304 | tf_op jit(solution)/shard_map/all_to_all | solution.py:527
  52.5 2.7 %schur.3 = (f32[96,128]{1,0:T(8,128)S(1)}, f32[8,128]{1,0:T(8,128)S(1)}, f32[3,16,256]{2,1,0:T(8,128)S(1)}, f32[3,16,256]{2,1,0:T(8,128)S(1)}, f32[9,8,128]{2,1,0:T(8,128)S(1)}, /*index=5*/f32[9,8,128]{2,1,0:T(8,128)S(1)}) custom-call(f32[96,128]{1,0:T(8,128)S(1)} %bitcast.23, f32[576,128]{1,0:T(8,128)S(1)} %get-tuple-element.41.a_ref, ...), custom_call_target="tpu_custom_call" | custom-call | flops 2000000000 | bytes 10000000 | tf_op jit(solution)/shard_map/schur/pallas_call | solution.py:504
  55.2 9.0 %all_to_all.34 = f32[32,1,384]{2,1,0:T(1,128)S(1)} all-to-all(f32[32,1,384]{2,1,0:T(1,128)S(1)} %bitcast.24), channel_id=1, replica_groups=mesh['pts'=8,'cams'=4] {'pts','cams'}, dimensions={0} | all-to-all | bytes 98304 | tf_op jit(solution)/shard_map/all_to_all | solution.py:527
  64.2 1.0 owner_final.1
  65.2 0.6 collective-permute-start
  65.8 9.9 %all_to_all.35 = f32[32,1,384]{2,1,0:T(1,128)S(1)} all-to-all(f32[32,1,384]{2,1,0:T(1,128)S(1)} %bitcast.25), channel_id=1, replica_groups=mesh['pts'=8,'cams'=4] {'pts','cams'}, dimensions={0} | all-to-all | bytes 98304 | tf_op jit(solution)/shard_map/all_to_all | solution.py:527
  75.8 0.0 collective-permute-done.other_ref
  75.8 0.1 tail.1.refs_0_
  75.9 0.7 collective-permute-start.1
  76.6 1.8 %schur_last.1 = (f32[8,128]{1,0:T(8,128)S(1)}, f32[8,128]{1,0:T(8,128)S(1)}, f32[3,16,256]{2,1,0:T(8,128)S(1)}, f32[3,16,256]{2,1,0:T(8,128)S(1)}) custom-call(f32[96,128]{1,0:T(8,128)S(1)} %bitcast.19, f32[576,128]{1,0:T(8,128)S(1)} %get-tuple-element.41.a_ref, f32[192,128]{1,0:T(8,128)S(1)} %get-tuple-element.42.b_ref, ...), custom_call_target="tpu_custom_call" | custom-call | flops 2000000000 | bytes 10000000 | tf_op jit(solution)/shard_map/schur_last/pallas_call | solution.py:504
  78.4 0.7 collective-permute-start.2
  79.1 2.8 %collective-permute-done.1.refs_1_ = f32[288,128]{1,0:T(8,128)S(1)} collective-permute-done((f32[288,128]{1,0:T(8,128)S(1)}, f32[288,128]{1,0:T(8,128)S(1)}, u32[]{:S(2)}, u32[]{:S(2)}) %collective-permute-start.1) | collective-permute-done | bytes 147488 | tf_op jit(solution)/shard_map/ppermute | solution.py:530
  81.9 0.5 collective-permute-start.3
  82.4 38.3 %psum.7.in_ref = f32[8,128]{1,0:T(8,128)S(1)} all-reduce(f32[8,128]{1,0:T(8,128)S(1)} %get-tuple-element.71), channel_id=1, replica_groups=mesh['pts'=8,'cams'=4] {'pts','cams'}, use_global_device_ids=true, to_apply=%region_0.0 | all-reduce | flops 1024 | bytes 8192 | tf_op jit(solution)/shard_map/psum | solution.py:639
  120.7 0.0 collective-permute-done.2.refs_2_
  120.7 0.0 collective-permute-done.3.refs_3_
  120.7 1.0 final.1
Async XLA Ops:
  65.2 10.6 %collective-permute-start = (f32[216,128]{1,0:T(8,128)S(1)}, f32[216,128]{1,0:T(8,128)S(1)}, u32[]{:S(2)}, u32[]{:S(2)}) collective-permute-start(f32[216,128]{1,0:T(8,128)S(1)} %get-tuple-element.64.own_ref), channel_id=1, source_target_pairs={{0,16},{4,20},{8,24},{12,28},{16,0},{20,4},{24,8},{28,12},{1,17},{... | collective-permute-start | bytes 331784 | tf_op jit(solution)/shard_map/ppermute | solution.py:530
  75.9 5.9 %collective-permute-start.1 = (f32[288,128]{1,0:T(8,128)S(1)}, f32[288,128]{1,0:T(8,128)S(1)}, u32[]{:S(2)}, u32[]{:S(2)}) collective-permute-start(f32[288,128]{1,0:T(8,128)S(1)} %tail.1.refs_0_), channel_id=1, source_target_pairs={{0,8},{4,12},{8,0},{12,4},{16,24},{20,28},{24,16},{28,20},{1,9},{5... | collective-permute-start | bytes 442376 | tf_op jit(solution)/shard_map/ppermute | solution.py:530
  78.4 42.3 %collective-permute-start.2 = (f32[288,128]{1,0:T(8,128)S(1)}, f32[288,128]{1,0:T(8,128)S(1)}, u32[]{:S(2)}, u32[]{:S(2)}) collective-permute-start(f32[288,128]{1,0:T(8,128)S(1)} %tail.1.refs_0_), channel_id=1, source_target_pairs={{0,4},{4,0},{8,12},{12,8},{16,20},{20,16},{24,28},{28,24},{1,5},{5... | collective-permute-start | bytes 442376 | tf_op jit(solution)/shard_map/ppermute | solution.py:530
  81.9 38.8 %collective-permute-start.3 = (f32[288,128]{1,0:T(8,128)S(1)}, f32[288,128]{1,0:T(8,128)S(1)}, u32[]{:S(2)}, u32[]{:S(2)}) collective-permute-start(f32[288,128]{1,0:T(8,128)S(1)} %collective-permute-done.1.refs_1_), channel_id=1, source_target_pairs={{0,4},{4,0},{8,12},{12,8},{16,20},{20,16},{24,28},{28,24},{1,5},{5... | collective-permute-start | bytes 442376 | tf_op jit(solution)/shard_map/ppermute | solution.py:530

commit v12 on v11

--- a/solution.py
+++ b/solution.py
@@ -448,7 +448,7 @@
                 place_row(row, low, LANES, place_slot_ref)
     partial = jnp.sum(inner, keepdims=True) + damping_camera * jnp.sum(squares, keepdims=True)
     if last:
-        out_ref[...] = jnp.broadcast_to(partial, (SUB, LANES))
+        out_ref[...] = jnp.broadcast_to(partial, (sizes.devices, LANES))
         return
     result = scatter(CP * PIECES, sizes.obs, sizes.pts, LANES, spread_ref, place_slot_ref)
     fields = joined(result, CP, sizes.pts)
@@ -468,7 +468,8 @@
 def final_kernel(sizes, masks, run_ref, in_ref, product_ref, inv_ref, grad_ref, sum_ref, *refs):
     all_refs = refs[: len(masks)]
     cam_ref, pt_ref, table_ref = refs[len(masks) :]
-    step = (product_ref[...] / in_ref[...])[:1]
+    curvature = jnp.sum(jnp.where(lane_iota(sizes.devices) == 0, in_ref[...], 0.0), keepdims=True)
+    step = (product_ref[...] / jnp.broadcast_to(curvature, (SUB, LANES)))[:1]
     for all_ref, pair in zip(all_refs, masks):
         for j, mask in enumerate(pair):
             base_column = (run_ref[0] ^ mask) * sizes.run
@@ -606,7 +607,7 @@
             "schur_last" if last else "schur",
             [arrived, a, b, inverse, slot, point, place_point, precondition, remainder, gradient]
             + earlier,
-            [scalar if last else messages, scalar, point_table]
+            [kept(sizes.devices, LANES) if last else messages, scalar, point_table]
             + ([] if start else [point_table])
             + ([] if last else [at_slot, owned]),
             ([pltpu.VMEM((CP, sizes.pts, LANES), f32)] if last else []) + schur_scratch,
@@ -636,7 +637,7 @@
     return call(
         functools.partial(final_kernel, sizes, masks),
         "final",
-        [lax.psum(out, ("pts", "cams")), product, inverse, gradient, sums] + gathered,
+        [exchange(out), product, inverse, gradient, sums] + gathered,
         [shape(CP, CAM_OWN), shape(3, PT_DEV)],
         [pltpu.VMEM((3 * PT_HI, PT_LO), f32)],
         scalars=[lax.axis_index("pts").astype(jnp.int32).reshape(1)],

time: 122 us -> 93.4 us (0.77)
  blocking collectives: 99.2 us -> 61 us
  waiting for transfers between devices: 2.78 us -> 9.31 us
  starting transfers between devices: 2.5 us -> 4.98 us
    psum x1 -> x0, blocking collectives: 38.3 us -> none  [body(): lax.psum(out, ('pts', 'cams'))]
    all_to_all x0 -> x1, waiting for transfers between devices: none -> 7.06 us  [exchange(): lax.all_to_all(flat, axes, split_axis=0, concat_axis=0, tiled=True)]
    all_to_all x0 -> x1, starting transfers between devices: none -> 2.54 us  [exchange(): lax.all_to_all(flat, axes, split_axis=0, concat_axis=0, tiled=True)]
  transfers between devices with their start and end apart: 4 -> 5, of which waited for: 1 -> 2; matrix products, arithmetic and copies ran while one was open for 0% -> 0% of each run, Pallas kernels for 2% -> 3%
where the time goes in v12:
time: 93.4 us; the launch traced here: 93.1 us
  blocking collectives  61 us (65%)
  Pallas kernels  17.1 us (18%)
  waiting for transfers between devices  9.31 us (10%)
  starting transfers between devices  4.98 us (5%)
    all_to_all x6, blocking collectives, exchange(): lax.all_to_all(flat, axes, split_axis=0, concat_axis=0, tiled=True)  61 us
    pallas_call x9, Pallas kernels, call(): pl.pallas_call(kernel, name=name, out_shape=outputs, in_specs=[smem] * le...  17.1 us
    all_to_all x1, waiting for transfers between devices, exchange(): lax.all_to_all(flat, axes, split_axis=0, concat_axis=0, tiled=True)  7.06 us
    all_to_all x1, starting transfers between devices, exchange(): lax.all_to_all(flat, axes, split_axis=0, concat_axis=0, tiled=True)  2.54 us
    ppermute x4, starting transfers between devices, flipped(): return lax.ppermute(value, 'pts', [(p, p ^ flip) for p in range(sizes.pts)])  2.44 us
    ppermute x4, waiting for transfers between devices, flipped(): return lax.ppermute(value, 'pts', [(p, p ^ flip) for p in range(sizes.pts)])  2.25 us
  transfers between devices with their start and end apart: 5, of which 2 were waited for; matrix products, arithmetic and copies ran while one was open for 0% of the time, Pallas kernels for 3%

profile of v12, /device:TPU:0, one launch (start us, length us, event | category | flops | bytes accessed | tf_op | source)
XLA Modules:
  0.0 93.1 jit_solution(14974594948072959967)
XLA Ops:
  0.6 5.9 %setup.1 = (f32[192,128]{1,0:T(8,128)S(1)}, f32[576,128]{1,0:T(8,128)S(1)}, f32[192,128]{1,0:T(8,128)S(1)}, f32[6,16,256]{2,1,0:T(8,128)S(1)}, f32[3,16,256]{2,1...) custom-call(s32[1]{0:T(128)} %bitcast.1.column_ref, ...), custom_call_target="tpu_custom_call" | custom-call | tf_op jit(solution)/shard_map/setup/pallas_call | solution.py:505
  6.5 14.9 %all_to_all.35 = f32[32,1,768]{2,1,0:T(1,128)S(1)} all-to-all(f32[32,1,768]{2,1,0:T(1,128)S(1)} %bitcast.26), channel_id=1, replica_groups=mesh['pts'=8,'cams'=4] {'pts','cams'}, dimensions={0} | all-to-all | bytes 196608 | tf_op jit(solution)/shard_map/all_to_all | solution.py:528
  21.5 0.7 first_owner.1
  22.2 9.0 %all_to_all.36 = f32[32,1,384]{2,1,0:T(1,128)S(1)} all-to-all(f32[32,1,384]{2,1,0:T(1,128)S(1)} %bitcast.34), channel_id=1, replica_groups=mesh['pts'=8,'cams'=4] {'pts','cams'}, dimensions={0} | all-to-all | bytes 98304 | tf_op jit(solution)/shard_map/all_to_all | solution.py:528
  31.2 2.7 %schur.2 = (f32[96,128]{1,0:T(8,128)S(1)}, f32[8,128]{1,0:T(8,128)S(1)}, f32[3,16,256]{2,1,0:T(8,128)S(1)}, f32[9,8,128]{2,1,0:T(8,128)S(1)}, f32[9,8,128]{2,1,0:T(8,128)S(1)}) custom-call(f32[96,128]{1,0:T(8,128)S(1)} %bitcast.31, f32[576,128]{1,0:T(8,128)S(1)} %get-tuple-element.41.a_ref, f32[192,128]{1,0:T(8,128)S(1)} %get-tuple-element.42.b_ref, ...), custom_call_target="tpu_custom_call" | custom-call | flops 2000000000 | bytes 10000000 | tf_op jit(solution)/shard_map/schur/pallas_call | solution.py:505
  33.9 9.0 %all_to_all.37 = f32[32,1,384]{2,1,0:T(1,128)S(1)} all-to-all(f32[32,1,384]{2,1,0:T(1,128)S(1)} %bitcast.32), channel_id=1, replica_groups=mesh['pts'=8,'cams'=4] {'pts','cams'}, dimensions={0} | all-to-all | bytes 98304 | tf_op jit(solution)/shard_map/all_to_all | solution.py:528
  42.9 0.6 owner.1
  43.5 9.0 %all_to_all.38 = f32[32,1,384]{2,1,0:T(1,128)S(1)} all-to-all(f32[32,1,384]{2,1,0:T(1,128)S(1)} %bitcast.33), channel_id=1, replica_groups=mesh['pts'=8,'cams'=4] {'pts','cams'}, dimensions={0} | all-to-all | bytes 98304 | tf_op jit(solution)/shard_map/all_to_all | solution.py:528
  52.5 2.7 %schur.3 = (f32[96,128]{1,0:T(8,128)S(1)}, f32[8,128]{1,0:T(8,128)S(1)}, f32[3,16,256]{2,1,0:T(8,128)S(1)}, f32[3,16,256]{2,1,0:T(8,128)S(1)}, f32[9,8,128]{2,1,0:T(8,128)S(1)}, /*index=5*/f32[9,8,128]{2,1,0:T(8,128)S(1)}) custom-call(f32[96,128]{1,0:T(8,128)S(1)} %bitcast.28, f32[576,128]{1,0:T(8,128)S(1)} %get-tuple-element.41.a_ref, ...), custom_call_target="tpu_custom_call" | custom-call | flops 2000000000 | bytes 10000000 | tf_op jit(solution)/shard_map/schur/pallas_call | solution.py:505
  55.2 9.0 %all_to_all.39 = f32[32,1,384]{2,1,0:T(1,128)S(1)} all-to-all(f32[32,1,384]{2,1,0:T(1,128)S(1)} %bitcast.29), channel_id=1, replica_groups=mesh['pts'=8,'cams'=4] {'pts','cams'}, dimensions={0} | all-to-all | bytes 98304 | tf_op jit(solution)/shard_map/all_to_all | solution.py:528
  64.2 1.0 %owner_final.1 = (f32[96,128]{1,0:T(8,128)S(1)}, f32[9,8,128]{2,1,0:T(8,128)S(1)}, f32[9,8,128]{2,1,0:T(8,128)}, f32[8,128]{1,0:T(8,128)S(1)}, f32[216,128]{1,0:T(8,128)S(1)}) custom-call(f32[96,128]{1,0:T(8,128)S(1)} %bitcast.24, s32[8,128]{1,0:T(8,128)S(1)} %get-tuple-element.51.entry_ref, f32[9,8,128]{2,1,0:T(8,128)S(1)} %get-tuple-element.47.pre_ref, ...), custom_call_target="tpu_custom_call" | custom-call | tf_op jit(solution)/shard_map/owner_final/pallas_call | solution.py:505
  65.2 0.6 collective-permute-start
  65.8 9.9 %all_to_all.40 = f32[32,1,384]{2,1,0:T(1,128)S(1)} all-to-all(f32[32,1,384]{2,1,0:T(1,128)S(1)} %bitcast.30), channel_id=1, replica_groups=mesh['pts'=8,'cams'=4] {'pts','cams'}, dimensions={0} | all-to-all | bytes 98304 | tf_op jit(solution)/shard_map/all_to_all | solution.py:528
  75.8 0.0 collective-permute-done.other_ref
  75.8 0.1 tail.1.refs_0_
  75.9 0.7 collective-permute-start.1
  76.6 2.4 %schur_last.1 = (f32[32,128]{1,0:T(8,128)}, f32[8,128]{1,0:T(8,128)S(1)}, f32[3,16,256]{2,1,0:T(8,128)S(1)}, f32[3,16,256]{2,1,0:T(8,128)S(1)}) custom-call(f32[96,128]{1,0:T(8,128)S(1)} %bitcast.23, f32[576,128]{1,0:T(8,128)S(1)} %get-tuple-element.41.a_ref, f32[192,128]{1,0:T(8,128)S(1)} %get-tuple-element.42.b_ref, ...), custom_call_target="tpu_custom_call" | custom-call | flops 2000000000 | bytes 10000000 | tf_op jit(solution)/shard_map/schur_last/pallas_call | solution.py:505
  79.0 0.6 collective-permute-start.2
  79.6 2.2 %collective-permute-done.1.refs_1_ = f32[288,128]{1,0:T(8,128)S(1)} collective-permute-done((f32[288,128]{1,0:T(8,128)S(1)}, f32[288,128]{1,0:T(8,128)S(1)}, u32[]{:S(2)}, u32[]{:S(2)}) %collective-permute-start.1) | collective-permute-done | bytes 147488 | tf_op jit(solution)/shard_map/ppermute | solution.py:531
  81.9 0.5 collective-permute-start.3
  82.4 2.5 %all-to-all-start.6 = ((f32[32,1,128]{2,1,0:T(1,128)}), f32[32,1,128]{2,1,0:T(1,128)S(1)}, u32[]{:S(2)}, u32[]{:S(2)}) async-start(f32[32,1,128]{2,1,0:T(1,128)} %bitcast.18), calls=%async_computation.6 | async-start | bytes 32768 | tf_op jit(solution)/shard_map/all_to_all | solution.py:528
  84.9 0.0 collective-permute-done.2.refs_2_
  85.0 7.1 %all-to-all-done.6 = f32[32,1,128]{2,1,0:T(1,128)S(1)} async-done(((f32[32,1,128]{2,1,0:T(1,128)}), f32[32,1,128]{2,1,0:T(1,128)S(1)}, u32[]{:S(2)}, u32[]{:S(2)}) %all-to-all-start.6) | async-done | bytes 16416 | tf_op jit(solution)/shard_map/all_to_all | solution.py:528
  92.0 1.1 %final.1 = (f32[9,8192]{1,0:T(8,128)}, f32[3,4096]{1,0:T(4,128)}) custom-call(s32[1]{0:T(128)} %bitcast.run_ref, f32[32,128]{1,0:T(8,128)S(1)} %bitcast.27, f32[8,128]{1,0:T(8,128)S(1)} %get-tuple-element.72.product_ref, f32[6,16,256]{2,1,0:T(8,128)S(1)} %get-tuple-element.43.inv_ref, f32[3,16,256]{2,1,0:T(8,128)S(1)} %get-tuple-element.73.grad_ref, ...), custom_call_target="tpu_custom_call" | custom-call | tf_op jit(solution)/shard_map/final/pallas_call | solution.py:505
  (1 shorter events, 0.0 us)
Async XLA Ops:
  65.2 10.6 %collective-permute-start = (f32[216,128]{1,0:T(8,128)S(1)}, f32[216,128]{1,0:T(8,128)S(1)}, u32[]{:S(2)}, u32[]{:S(2)}) collective-permute-start(f32[216,128]{1,0:T(8,128)S(1)} %get-tuple-element.64.own_ref), channel_id=1, source_target_pairs={{0,16},{4,20},{8,24},{12,28},{16,0},{20,4},{24,8},{28,12},{1,17},{... | collective-permute-start | bytes 331784 | tf_op jit(solution)/shard_map/ppermute | solution.py:531
  75.9 5.9 %collective-permute-start.1 = (f32[288,128]{1,0:T(8,128)S(1)}, f32[288,128]{1,0:T(8,128)S(1)}, u32[]{:S(2)}, u32[]{:S(2)}) collective-permute-start(f32[288,128]{1,0:T(8,128)S(1)} %tail.1.refs_0_), channel_id=1, source_target_pairs={{0,8},{4,12},{8,0},{12,4},{16,24},{20,28},{24,16},{28,20},{1,9},{5... | collective-permute-start | bytes 442376 | tf_op jit(solution)/shard_map/ppermute | solution.py:531
  79.0 5.9 %collective-permute-start.2 = (f32[288,128]{1,0:T(8,128)S(1)}, f32[288,128]{1,0:T(8,128)S(1)}, u32[]{:S(2)}, u32[]{:S(2)}) collective-permute-start(f32[288,128]{1,0:T(8,128)S(1)} %tail.1.refs_0_), channel_id=1, source_target_pairs={{0,4},{4,0},{8,12},{12,8},{16,20},{20,16},{24,28},{28,24},{1,5},{5... | collective-permute-start | bytes 442376 | tf_op jit(solution)/shard_map/ppermute | solution.py:531
  81.9 10.2 %collective-permute-start.3 = (f32[288,128]{1,0:T(8,128)S(1)}, f32[288,128]{1,0:T(8,128)S(1)}, u32[]{:S(2)}, u32[]{:S(2)}) collective-permute-start(f32[288,128]{1,0:T(8,128)S(1)} %collective-permute-done.1.refs_1_), channel_id=1, source_target_pairs={{0,4},{4,0},{8,12},{12,8},{16,20},{20,16},{24,28},{28,24},{1,5},{5... | collective-permute-start | bytes 442376 | tf_op jit(solution)/shard_map/ppermute | solution.py:531
  82.4 9.6 %all-to-all-start.6 = ((f32[32,1,128]{2,1,0:T(1,128)}), f32[32,1,128]{2,1,0:T(1,128)S(1)}, u32[]{:S(2)}, u32[]{:S(2)}) async-start(f32[32,1,128]{2,1,0:T(1,128)} %bitcast.18), calls=%async_computation.6 | async-start | bytes 32768 | tf_op jit(solution)/shard_map/all_to_all | solution.py:528

commit v13 on v12

--- a/solution.py
+++ b/solution.py
@@ -13,6 +13,7 @@
 ITERS = 3
 LANES = 128
 SUB = 8
+PT_ROWS = PT_DEV // LANES
 PT_LO = 256
 PT_HI = PT_DEV // PT_LO
 PIECES = 2
@@ -144,9 +145,13 @@
 
 
 def point_gather(ref, point):
-    wide = PT_LO // LANES
-    row = lambda c, k: ref[c, k // wide : k // wide + 1, (k % wide) * LANES : (k % wide + 1) * LANES]
-    return gather_rows(row, PT_HI * wide, point // LANES, point % LANES, 3)
+    return gather_rows(lambda c, k: ref[c, k : k + 1, :], PT_ROWS, point // LANES, point % LANES, 3)
+
+
+def narrow(ref, k, value):
+    parts = PT_LO // LANES
+    for part in range(parts):
+        ref[k, pl.ds(part, PT_HI, stride=parts), :] = value[:, part * LANES : (part + 1) * LANES]
 
 
 def slot_place(slot, sizes):
@@ -205,9 +210,9 @@
 
 def setup_kernel(sizes, column_ref, *refs):
     sources, refs = refs[:6], refs[6:]
-    out_ref, a_ref, b_ref, inv_ref, grad_ref, place_point_ref, new_slot_ref, new_point_ref = refs[:8]
-    refs = refs[8:]
-    r_ref, parts_ref, spread_ref, table_ref, place_slot_ref, place_list_ref = refs[:6]
+    out_ref, a_ref, b_ref, inv_ref, grad_ref, place_point_ref, place_slot_ref, new_slot_ref, new_point_ref = refs[:9]
+    refs = refs[9:]
+    r_ref, parts_ref, spread_ref, table_ref, place_wide_ref, place_list_ref = refs[:6]
     jac_ref, pjac_ref, res_ref, slot_ref, point_ref, list_ref = refs[6:12]
     semaphores = refs[12]
     rows = sizes.rows
@@ -241,8 +246,8 @@
             row = group * SUB + s
             point = point_ref[row : row + 1, :]
             spread_row(row, part_rows(len(parts), group, s, parts_ref), point >> 8, PT_HI, spread_ref)
-            place_row(row, point & (PT_LO - 1), PT_LO, place_point_ref)
-    result = scatter(sum(normal_pieces), sizes.obs, PT_HI, PT_LO, spread_ref, place_point_ref)
+            place_row(row, point & (PT_LO - 1), PT_LO, place_wide_ref)
+    result = scatter(sum(normal_pieces), sizes.obs, PT_HI, PT_LO, spread_ref, place_wide_ref)
     normal = joined(result, 9, PT_HI, normal_pieces)
     top_left = normal[0] + damping_point
     top_mid = normal[1]
@@ -261,12 +266,13 @@
     determinant = top_left * adjugate[0] + top_mid * adjugate[1] + top_right * adjugate[2]
     inverse = [value / determinant for value in adjugate]
     for k in range(6):
-        inv_ref[k] = inverse[k]
+        narrow(inv_ref, k, inverse[k])
     for k in range(3):
-        grad_ref[k] = normal[6 + k]
+        narrow(grad_ref, k, normal[6 + k])
     eliminated = solve(inverse, normal[6:])
     for k in range(3):
-        table_ref[k] = eliminated[k]
+        narrow(table_ref, k, eliminated[k])
+    place_point_ref[...] = place_wide_ref[:LANES, :] + place_wide_ref[LANES:, :]
     for k in (0, 3, 5):
         copies[k].wait()
     new_slot_ref[...] = slot_ref[...]
@@ -377,7 +383,7 @@
 
 
 def schur_kernel(sizes, start, last, in_ref, a_ref, b_ref, inv_ref, slot_ref, point_ref,
-                 place_point_ref, pre_ref, rem_ref, grad_ref, *refs):
+                 place_point_ref, place_slot_ref, pre_ref, rem_ref, grad_ref, *refs):
     refs = list(refs)
     if not start:
         product_ref, at_slot_ref, dir_ref, step_ref, sum_ref = refs[:5]
@@ -385,7 +391,7 @@
     out_ref, new_product_ref, new_sum_ref = refs[:3]
     refs = refs[3:]
     new_grad_ref = None if start else refs.pop(0)
-    q_ref, parts_ref, spread_ref, table_ref, place_slot_ref = refs[-5:]
+    q_ref, parts_ref, spread_ref, table_ref = refs[-4:]
     new_at_slot_ref, new_dir_ref = (refs[0], None) if last else refs[:2]
     rows = sizes.rows
 
@@ -419,9 +425,9 @@
         keep_parts(parts, group, parts_ref)
         for s in range(SUB):
             row = group * SUB + s
-            spread_row(row, part_rows(len(parts), group, s, parts_ref), point_ref[row : row + 1, :] >> 8, PT_HI, spread_ref)
-    result = scatter(3 * FINE, sizes.obs, PT_HI, PT_LO, spread_ref, place_point_ref)
-    sums = joined(result, 3, PT_HI, [FINE] * 3)
+            spread_row(row, part_rows(len(parts), group, s, parts_ref), point_ref[row : row + 1, :] // LANES, PT_ROWS, spread_ref)
+    result = scatter(3 * FINE, sizes.obs, PT_ROWS, LANES, spread_ref, place_point_ref)
+    sums = joined(result, 3, PT_ROWS, [FINE] * 3)
     folded = solve([inv_ref[k] for k in range(6)], sums)
     for k in range(3):
         new_sum_ref[k] = sums[k]
@@ -443,9 +449,8 @@
             keep_parts(parts, group, parts_ref)
             for s in range(SUB):
                 row = group * SUB + s
-                high, low = slot_place(slot_ref[row : row + 1, :], sizes)
+                high, _ = slot_place(slot_ref[row : row + 1, :], sizes)
                 spread_row(row, part_rows(len(parts), group, s, parts_ref), high, sizes.pts, spread_ref)
-                place_row(row, low, LANES, place_slot_ref)
     partial = jnp.sum(inner, keepdims=True) + damping_camera * jnp.sum(squares, keepdims=True)
     if last:
         out_ref[...] = jnp.broadcast_to(partial, (sizes.devices, LANES))
@@ -484,10 +489,9 @@
     total = [grad_ref[k] + step[:, :1] * sum_ref[k] for k in range(3)]
     solved = solve([inv_ref[k] for k in range(6)], total)
     for k in range(3):
-        table_ref[k * PT_HI : (k + 1) * PT_HI, :] = -solved[k]
-    for row in range(PT_HI):
-        for k in range(3):
-            pt_ref[k : k + 1, row * PT_LO : (row + 1) * PT_LO] = table_ref[k * PT_HI + row : k * PT_HI + row + 1, :]
+        table_ref[k * PT_ROWS : (k + 1) * PT_ROWS, :] = -solved[k]
+    for row in range(PT_ROWS):
+        pt_ref[:, row * LANES : (row + 1) * LANES] = table_ref[pl.ds(row, 3, stride=PT_ROWS), :]
 
 
 def shape(*dims, dtype=f32):
@@ -533,14 +537,14 @@
     def factors(high_rows, low_rows, entries):
         return [pltpu.VMEM((high_rows, entries), bf16), pltpu.VMEM((low_rows, entries), bf16)]
 
-    point_table = kept(3, PT_HI, PT_LO)
+    point_table = kept(3, PT_ROWS, LANES)
     owned = kept(CP, sizes.own_rows, LANES)
     messages = kept(sizes.devices * sizes.message, LANES)
     scalar = kept(SUB, LANES)
     owned_scratch = pltpu.VMEM((CP, sizes.own_rows, LANES), f32)
     entries = sizes.pts * LANES
 
-    gather_scratch = [pltpu.VMEM((3, PT_HI, PT_LO), f32), pltpu.VMEM((LANES, sizes.obs), bf16)]
+    point_scratch = pltpu.VMEM((3, PT_ROWS, LANES), f32)
 
     def parts_scratch(count):
         return pltpu.VMEM((rows // SUB, count * SUB, LANES), f32)
@@ -550,7 +554,7 @@
         pltpu.with_memory_space_constraint(value, pltpu.HBM)
         for value in (camera_jacobian, point_jacobian, residual, slot, point, send_list[0])
     ]
-    first, a, b, inverse, gradient, place_point, slot, point = call(
+    first, a, b, inverse, gradient, place_point, place_slot, slot, point = call(
         functools.partial(setup_kernel, sizes),
         "setup",
         given,
@@ -558,16 +562,16 @@
             kept(sizes.devices * sizes.first_message, LANES),
             kept(2 * CP * rows, LANES),
             kept(6 * rows, LANES),
-            kept(6, PT_HI, PT_LO),
+            kept(6, PT_ROWS, LANES),
             point_table,
-            kept(PT_LO, sizes.obs, dtype=bf16),
+            kept(LANES, sizes.obs, dtype=bf16),
+            kept(LANES, sizes.obs, dtype=bf16),
             kept(rows, LANES, dtype=jnp.int32),
             kept(rows, LANES, dtype=jnp.int32),
         ],
         [pltpu.VMEM((2 * rows, LANES), f32), parts_scratch(2 * CP * PIECES)]
         + [pltpu.VMEM((max(spread_rows(9 * FINE, PT_HI), spread_rows(2 * CP * PIECES, sizes.pts)), sizes.obs), bf16)]
-        + gather_scratch
-        + [pltpu.VMEM((LANES, sizes.cams * sizes.slot), bf16)]
+        + [point_scratch, pltpu.VMEM((PT_LO, sizes.obs), bf16), pltpu.VMEM((LANES, sizes.cams * sizes.slot), bf16)]
         + [pltpu.VMEM(value.shape, value.dtype) for value in given]
         + [pltpu.SemaphoreType.DMA((len(given),))],
         scalars=[column],
@@ -581,8 +585,8 @@
         [owned_scratch] + factors(spread_rows(2 * CP * PIECES, sizes.own_rows), LANES, entries),
     )
     schur_scratch = [pltpu.VMEM((2 * rows, LANES), f32), parts_scratch(CP * PIECES)]
-    schur_scratch += [pltpu.VMEM((max(spread_rows(3 * FINE, PT_HI), spread_rows(CP * PIECES, sizes.pts)), sizes.obs), bf16)]
-    schur_scratch += gather_scratch
+    schur_scratch += [pltpu.VMEM((max(spread_rows(3 * FINE, PT_ROWS), spread_rows(CP * PIECES, sizes.pts)), sizes.obs), bf16)]
+    schur_scratch += [point_scratch]
     at_slot = kept(CP, sizes.pts, LANES)
     product = slots = direction = step = sums = solution_ = None
     for iteration in range(ITERS):
@@ -605,7 +609,7 @@
         results = call(
             functools.partial(schur_kernel, sizes, start, last),
             "schur_last" if last else "schur",
-            [arrived, a, b, inverse, slot, point, place_point, precondition, remainder, gradient]
+            [arrived, a, b, inverse, slot, point, place_point, place_slot, precondition, remainder, gradient]
             + earlier,
             [kept(sizes.devices, LANES) if last else messages, scalar, point_table]
             + ([] if start else [point_table])
@@ -619,7 +623,7 @@
         if not last:
             slots, direction = results
         if last:
-            early[flips[0]], out = lax.optimization_barrier((early[flips[0]], out))
+            early, out = lax.optimization_barrier((early, out))
             gathered, masks = [both], [(0, FIRST)]
             for flip in flips:
                 gathered += [early[flip] if value is both and flip in early else flipped(value, flip) for value in gathered]
@@ -639,7 +643,7 @@
         "final",
         [exchange(out), product, inverse, gradient, sums] + gathered,
         [shape(CP, CAM_OWN), shape(3, PT_DEV)],
-        [pltpu.VMEM((3 * PT_HI, PT_LO), f32)],
+        [pltpu.VMEM((3 * PT_ROWS, LANES), f32)],
         scalars=[lax.axis_index("pts").astype(jnp.int32).reshape(1)],
     )
 

time: 93.4 us -> 93.5 us (level)
  transfers between devices with their start and end apart: 5 -> 5, of which waited for: 2 -> 3; matrix products, arithmetic and copies ran while one was open for 0% -> 0% of each run, Pallas kernels for 3% -> 3%
where the time goes in v13:
time: 93.5 us; the launch traced here: 93.2 us
  blocking collectives  61 us (65%)
  Pallas kernels  16.9 us (18%)
  waiting for transfers between devices  9.27 us (10%)
  starting transfers between devices  5.4 us (6%)
    all_to_all x6, blocking collectives, exchange(): lax.all_to_all(flat, axes, split_axis=0, concat_axis=0, tiled=True)  61 us
    pallas_call x9, Pallas kernels, call(): pl.pallas_call(kernel, name=name, out_shape=outputs, in_specs=[smem] * le...  16.9 us
    all_to_all x1, waiting for transfers between devices, exchange(): lax.all_to_all(flat, axes, split_axis=0, concat_axis=0, tiled=True)  7.07 us
    all_to_all x1, starting transfers between devices, exchange(): lax.all_to_all(flat, axes, split_axis=0, concat_axis=0, tiled=True)  2.71 us
    ppermute x4, starting transfers between devices, flipped(): return lax.ppermute(value, 'pts', [(p, p ^ flip) for p in range(sizes.pts)])  2.69 us
    ppermute x4, waiting for transfers between devices, flipped(): return lax.ppermute(value, 'pts', [(p, p ^ flip) for p in range(sizes.pts)])  2.2 us
  transfers between devices with their start and end apart: 5, of which 3 were waited for; matrix products, arithmetic and copies ran while one was open for 0% of the time, Pallas kernels for 3%

profile of v13, /device:TPU:0, one launch (start us, length us, event | category | flops | bytes accessed | tf_op | source)
XLA Modules:
  0.0 93.2 jit_solution(222331721072770277)
XLA Ops:
  0.6 5.9 %setup.1 = (f32[192,128]{1,0:T(8,128)S(1)}, f32[576,128]{1,0:T(8,128)S(1)}, f32[192,128]{1,0:T(8,128)S(1)}, f32[6,32,128]{2,1,0:T(8,128)S(1)}, f32[3,32,128]{2,1...) custom-call(s32[1]{0:T(128)} %bitcast.1.column_ref, ...), custom_call_target="tpu_custom_call" | custom-call | tf_op jit(solution)/shard_map/setup/pallas_call | solution.py:509
  6.6 14.9 %all_to_all.35 = f32[32,1,768]{2,1,0:T(1,128)S(1)} all-to-all(f32[32,1,768]{2,1,0:T(1,128)S(1)} %bitcast.26), channel_id=1, replica_groups=mesh['pts'=8,'cams'=4] {'pts','cams'}, dimensions={0} | all-to-all | bytes 196608 | tf_op jit(solution)/shard_map/all_to_all | solution.py:532
  21.5 0.7 first_owner.1
  22.2 9.0 %all_to_all.36 = f32[32,1,384]{2,1,0:T(1,128)S(1)} all-to-all(f32[32,1,384]{2,1,0:T(1,128)S(1)} %bitcast.34), channel_id=1, replica_groups=mesh['pts'=8,'cams'=4] {'pts','cams'}, dimensions={0} | all-to-all | bytes 98304 | tf_op jit(solution)/shard_map/all_to_all | solution.py:532
  31.2 2.5 %schur.2 = (f32[96,128]{1,0:T(8,128)S(1)}, f32[8,128]{1,0:T(8,128)S(1)}, f32[3,32,128]{2,1,0:T(8,128)S(1)}, f32[9,8,128]{2,1,0:T(8,128)S(1)}, f32[9,8,128]{2,1,0:T(8,128)S(1)}) custom-call(f32[96,128]{1,0:T(8,128)S(1)} %bitcast.31, f32[576,128]{1,0:T(8,128)S(1)} %get-tuple-element.43.a_ref, f32[192,128]{1,0:T(8,128)S(1)} %get-tuple-element.44.b_ref, ...), custom_call_target="tpu_custom_call" | custom-call | flops 2000000000 | bytes 10000000 | tf_op jit(solution)/shard_map/schur/pallas_call | solution.py:509
  33.7 9.0 %all_to_all.37 = f32[32,1,384]{2,1,0:T(1,128)S(1)} all-to-all(f32[32,1,384]{2,1,0:T(1,128)S(1)} %bitcast.32), channel_id=1, replica_groups=mesh['pts'=8,'cams'=4] {'pts','cams'}, dimensions={0} | all-to-all | bytes 98304 | tf_op jit(solution)/shard_map/all_to_all | solution.py:532
  42.7 0.6 owner.1
  43.3 9.0 %all_to_all.38 = f32[32,1,384]{2,1,0:T(1,128)S(1)} all-to-all(f32[32,1,384]{2,1,0:T(1,128)S(1)} %bitcast.33), channel_id=1, replica_groups=mesh['pts'=8,'cams'=4] {'pts','cams'}, dimensions={0} | all-to-all | bytes 98304 | tf_op jit(solution)/shard_map/all_to_all | solution.py:532
  52.3 2.5 %schur.3 = (f32[96,128]{1,0:T(8,128)S(1)}, f32[8,128]{1,0:T(8,128)S(1)}, f32[3,32,128]{2,1,0:T(8,128)S(1)}, f32[3,32,128]{2,1,0:T(8,128)S(1)}, f32[9,8,128]{2,1,0:T(8,128)S(1)}, /*index=5*/f32[9,8,128]{2,1,0:T(8,128)S(1)}) custom-call(f32[96,128]{1,0:T(8,128)S(1)} %bitcast.28, f32[576,128]{1,0:T(8,128)S(1)} %get-tuple-element.43.a_ref, ...), custom_call_target="tpu_custom_call" | custom-call | flops 2000000000 | bytes 10000000 | tf_op jit(solution)/shard_map/schur/pallas_call | solution.py:509
  54.8 9.0 %all_to_all.39 = f32[32,1,384]{2,1,0:T(1,128)S(1)} all-to-all(f32[32,1,384]{2,1,0:T(1,128)S(1)} %bitcast.29), channel_id=1, replica_groups=mesh['pts'=8,'cams'=4] {'pts','cams'}, dimensions={0} | all-to-all | bytes 98304 | tf_op jit(solution)/shard_map/all_to_all | solution.py:532
  63.9 1.0 %owner_final.1 = (f32[96,128]{1,0:T(8,128)S(1)}, f32[9,8,128]{2,1,0:T(8,128)S(1)}, f32[9,8,128]{2,1,0:T(8,128)}, f32[8,128]{1,0:T(8,128)S(1)}, f32[216,128]{1,0:T(8,128)S(1)}) custom-call(f32[96,128]{1,0:T(8,128)S(1)} %bitcast.24, s32[8,128]{1,0:T(8,128)S(1)} %get-tuple-element.54.entry_ref, f32[9,8,128]{2,1,0:T(8,128)S(1)} %get-tuple-element.50.pre_ref, ...), custom_call_target="tpu_custom_call" | custom-call | tf_op jit(solution)/shard_map/owner_final/pallas_call | solution.py:509
  64.8 0.6 collective-permute-start
  65.5 9.9 %all_to_all.40 = f32[32,1,384]{2,1,0:T(1,128)S(1)} all-to-all(f32[32,1,384]{2,1,0:T(1,128)S(1)} %bitcast.30), channel_id=1, replica_groups=mesh['pts'=8,'cams'=4] {'pts','cams'}, dimensions={0} | all-to-all | bytes 98304 | tf_op jit(solution)/shard_map/all_to_all | solution.py:532
  75.4 0.0 collective-permute-done.other_ref
  75.4 0.1 tail.1.refs_0_
  75.5 0.7 collective-permute-start.2
  76.2 0.6 collective-permute-start.1
  76.8 2.6 %schur_last.1 = (f32[32,128]{1,0:T(8,128)}, f32[8,128]{1,0:T(8,128)S(1)}, f32[3,32,128]{2,1,0:T(8,128)S(1)}, f32[3,32,128]{2,1,0:T(8,128)S(1)}) custom-call(f32[96,128]{1,0:T(8,128)S(1)} %bitcast.23, f32[576,128]{1,0:T(8,128)S(1)} %get-tuple-element.43.a_ref, f32[192,128]{1,0:T(8,128)S(1)} %get-tuple-element.44.b_ref, ...), custom_call_target="tpu_custom_call" | custom-call | flops 2000000000 | bytes 10000000 | tf_op jit(solution)/shard_map/schur_last/pallas_call | solution.py:509
  79.4 2.1 %collective-permute-done.2.refs_1_ = f32[288,128]{1,0:T(8,128)S(1)} collective-permute-done((f32[288,128]{1,0:T(8,128)S(1)}, f32[288,128]{1,0:T(8,128)S(1)}, u32[]{:S(2)}, u32[]{:S(2)}) %collective-permute-start.2) | collective-permute-done | bytes 147488 | tf_op jit(solution)/shard_map/ppermute | solution.py:535
  81.5 0.1 collective-permute-done.1.refs_2_
  81.6 0.8 collective-permute-start.3
  82.3 2.7 %all-to-all-start.6 = ((f32[32,1,128]{2,1,0:T(1,128)}), f32[32,1,128]{2,1,0:T(1,128)S(1)}, u32[]{:S(2)}, u32[]{:S(2)}) async-start(f32[32,1,128]{2,1,0:T(1,128)} %bitcast.18), calls=%async_computation.6 | async-start | bytes 32768 | tf_op jit(solution)/shard_map/all_to_all | solution.py:532
  85.1 7.1 %all-to-all-done.6 = f32[32,1,128]{2,1,0:T(1,128)S(1)} async-done(((f32[32,1,128]{2,1,0:T(1,128)}), f32[32,1,128]{2,1,0:T(1,128)S(1)}, u32[]{:S(2)}, u32[]{:S(2)}) %all-to-all-start.6) | async-done | bytes 16416 | tf_op jit(solution)/shard_map/all_to_all | solution.py:532
  92.1 1.1 %final.1 = (f32[9,8192]{1,0:T(8,128)}, f32[3,4096]{1,0:T(4,128)}) custom-call(s32[1]{0:T(128)} %bitcast.run_ref, f32[32,128]{1,0:T(8,128)S(1)} %bitcast.27, f32[8,128]{1,0:T(8,128)S(1)} %get-tuple-element.75.product_ref, f32[6,32,128]{2,1,0:T(8,128)S(1)} %get-tuple-element.45.inv_ref, f32[3,32,128]{2,1,0:T(8,128)S(1)} %get-tuple-element.76.grad_ref, ...), custom_call_target="tpu_custom_call" | custom-call | tf_op jit(solution)/shard_map/final/pallas_call | solution.py:509
  (1 shorter events, 0.0 us)
Async XLA Ops:
  64.8 10.6 %collective-permute-start = (f32[216,128]{1,0:T(8,128)S(1)}, f32[216,128]{1,0:T(8,128)S(1)}, u32[]{:S(2)}, u32[]{:S(2)}) collective-permute-start(f32[216,128]{1,0:T(8,128)S(1)} %get-tuple-element.67.own_ref), channel_id=1, source_target_pairs={{0,16},{4,20},{8,24},{12,28},{16,0},{20,4},{24,8},{28,12},{1,17},{... | collective-permute-start | bytes 331784 | tf_op jit(solution)/shard_map/ppermute | solution.py:535
  75.5 5.9 %collective-permute-start.2 = (f32[288,128]{1,0:T(8,128)S(1)}, f32[288,128]{1,0:T(8,128)S(1)}, u32[]{:S(2)}, u32[]{:S(2)}) collective-permute-start(f32[288,128]{1,0:T(8,128)S(1)} %tail.1.refs_0_), channel_id=1, source_target_pairs={{0,8},{4,12},{8,0},{12,4},{16,24},{20,28},{24,16},{28,20},{1,9},{5... | collective-permute-start | bytes 442376 | tf_op jit(solution)/shard_map/ppermute | solution.py:535
  76.2 5.3 %collective-permute-start.1 = (f32[288,128]{1,0:T(8,128)S(1)}, f32[288,128]{1,0:T(8,128)S(1)}, u32[]{:S(2)}, u32[]{:S(2)}) collective-permute-start(f32[288,128]{1,0:T(8,128)S(1)} %tail.1.refs_0_), channel_id=1, source_target_pairs={{0,4},{4,0},{8,12},{12,8},{16,20},{20,16},{24,28},{28,24},{1,5},{5... | collective-permute-start | bytes 442376 | tf_op jit(solution)/shard_map/ppermute | solution.py:535
  81.6 10.6 %collective-permute-start.3 = (f32[288,128]{1,0:T(8,128)S(1)}, f32[288,128]{1,0:T(8,128)S(1)}, u32[]{:S(2)}, u32[]{:S(2)}) collective-permute-start(f32[288,128]{1,0:T(8,128)S(1)} %collective-permute-done.2.refs_1_), channel_id=1, source_target_pairs={{0,4},{4,0},{8,12},{12,8},{16,20},{20,16},{24,28},{28,24},{1,5},{5... | collective-permute-start | bytes 442376 | tf_op jit(solution)/shard_map/ppermute | solution.py:535
  82.3 9.8 %all-to-all-start.6 = ((f32[32,1,128]{2,1,0:T(1,128)}), f32[32,1,128]{2,1,0:T(1,128)S(1)}, u32[]{:S(2)}, u32[]{:S(2)}) async-start(f32[32,1,128]{2,1,0:T(1,128)} %bitcast.18), calls=%async_computation.6 | async-start | bytes 32768 | tf_op jit(solution)/shard_map/all_to_all | solution.py:532

commit v14 on v13

--- a/solution.py
+++ b/solution.py
@@ -208,7 +208,8 @@
     return jnp.sum(chosen, keepdims=True)
 
 
-def setup_kernel(sizes, column_ref, *refs):
+def setup_kernel(sizes, run_ref, column_ref, *refs):
+    del run_ref
     sources, refs = refs[:6], refs[6:]
     out_ref, a_ref, b_ref, inv_ref, grad_ref, place_point_ref, place_slot_ref, new_slot_ref, new_point_ref = refs[:9]
     refs = refs[9:]
@@ -356,8 +357,7 @@
 def owner_kernel(sizes, start, final, in_ref, entry_ref, pre_ref, rem_ref, dir_ref, product_ref, *refs):
     refs = list(refs)
     sol_ref = None if start else refs.pop(0)
-    out_ref, new_rem_ref, new_sol_ref, step_ref = refs[:4]
-    fields_ref = refs[4] if final else None
+    out_ref, new_rem_ref, step_ref, new_sol_ref = refs[:4]
     table_ref, spread_ref, place_ref = refs[-3:]
     entry = entry_ref[...]
     fields = read_messages(in_ref, CP, sizes.message, sizes)
@@ -370,7 +370,8 @@
         direction = dir_ref[k]
         moved = step[:1] * direction
         moved = moved if start else sol_ref[k] + moved
-        new_sol_ref[k] = moved
+        if not final:
+            new_sol_ref[k] = moved
         value = rem_ref[k] - step[:1] * (sums[k] + damping_camera * direction)
         new_rem_ref[k] = value
         remainder.append(value)
@@ -378,7 +379,7 @@
         if final:
             for j, field in enumerate((moved, direction, scaled[k])):
                 first = (j * CP + k) * sizes.own_rows
-                fields_ref[first : first + sizes.own_rows, :] = field
+                new_sol_ref[first : first + sizes.own_rows, :] = field
     send_owned(scaled, dot_fields(remainder, scaled), entry, out_ref, table_ref, sizes)
 
 
@@ -525,6 +526,7 @@
     slot = observed_slot.reshape(rows, LANES)
     point = observed_point.reshape(rows, LANES)
     column = lax.axis_index("cams").astype(jnp.int32).reshape(1)
+    run = lax.axis_index("pts").astype(jnp.int32).reshape(1)
 
     def exchange(messages):
         width = messages.size // sizes.devices
@@ -574,7 +576,7 @@
         + [point_scratch, pltpu.VMEM((PT_LO, sizes.obs), bf16), pltpu.VMEM((LANES, sizes.cams * sizes.slot), bf16)]
         + [pltpu.VMEM(value.shape, value.dtype) for value in given]
         + [pltpu.SemaphoreType.DMA((len(given),))],
-        scalars=[column],
+        scalars=[run, column],
         inputs_at=pl.ANY,
     )
     out, entry, precondition, remainder = call(
@@ -630,21 +632,21 @@
                 masks += [tuple(mask ^ flip for mask in pair) for pair in masks]
             break
         final = iteration == ITERS - 2
-        out, remainder, solution_, step, *rest = call(
+        out, remainder, step, solution_ = call(
             functools.partial(owner_kernel, sizes, start, final),
             "owner_final" if final else "owner",
             [exchange(out), entry, precondition, remainder, direction, product] + ([] if start else [solution_]),
-            [messages, owned, owned, scalar] + ([kept(3 * CP * sizes.own_rows, LANES)] if final else []),
+            [messages, owned, scalar, kept(3 * CP * sizes.own_rows, LANES) if final else owned],
             [owned_scratch] + factors(spread_rows(CP * PIECES, sizes.own_rows), LANES, entries),
         )
-        fields = rest[0] if final else None
+        fields = solution_
     return call(
         functools.partial(final_kernel, sizes, masks),
         "final",
         [exchange(out), product, inverse, gradient, sums] + gathered,
         [shape(CP, CAM_OWN), shape(3, PT_DEV)],
         [pltpu.VMEM((3 * PT_ROWS, LANES), f32)],
-        scalars=[lax.axis_index("pts").astype(jnp.int32).reshape(1)],
+        scalars=[run],
     )
 
 

time: 93.5 us -> 92.9 us (level)
  blocking collectives: 61 us -> 70.6 us
  waiting for transfers between devices: 9.27 us -> 2.82 us
  starting transfers between devices: 5.4 us -> 2.76 us
  Pallas kernels: 16.9 us -> 15.8 us
    all_to_all x6 -> x7, blocking collectives: 61 us -> 70.6 us  [exchange(): lax.all_to_all(flat, axes, split_axis=0, concat_axis=0, tiled=True)]
    all_to_all x1 -> x0, waiting for transfers between devices: 7.07 us -> none  [exchange(): lax.all_to_all(flat, axes, split_axis=0, concat_axis=0, tiled=True)]
    all_to_all x1 -> x0, starting transfers between devices: 2.71 us -> none  [exchange(): lax.all_to_all(flat, axes, split_axis=0, concat_axis=0, tiled=True)]
    pallas_call x9, Pallas kernels: 16.9 us -> 15.8 us  [call(): pl.pallas_call(kernel, name=name, out_shape=outputs, in_specs=[smem] * le...]
  transfers between devices with their start and end apart: 5 -> 4, of which waited for: 3 -> 2; matrix products, arithmetic and copies ran while one was open for 0% -> 0% of each run, Pallas kernels for 3% -> 2%
where the time goes in v14:
time: 92.9 us; the launch traced here: 92.7 us
  blocking collectives  70.6 us (76%)
  Pallas kernels  15.8 us (17%)
  waiting for transfers between devices  2.82 us (3%)
  starting transfers between devices  2.76 us (3%)
    all_to_all x7, blocking collectives, exchange(): lax.all_to_all(flat, axes, split_axis=0, concat_axis=0, tiled=True)  70.6 us
    pallas_call x9, Pallas kernels, call(): pl.pallas_call(kernel, name=name, out_shape=outputs, in_specs=[smem] * le...  15.8 us
    ppermute x4, waiting for transfers between devices, flipped(): return lax.ppermute(value, 'pts', [(p, p ^ flip) for p in range(sizes.pts)])  2.82 us
    ppermute x4, starting transfers between devices, flipped(): return lax.ppermute(value, 'pts', [(p, p ^ flip) for p in range(sizes.pts)])  2.76 us
  transfers between devices with their start and end apart: 4, of which 2 were waited for; matrix products, arithmetic and copies ran while one was open for 0% of the time, Pallas kernels for 2%

profile of v14, /device:TPU:0, one launch (start us, length us, event | category | flops | bytes accessed | tf_op | source)
XLA Modules:
  0.0 92.7 jit_solution(10796259625740837685)
XLA Ops:
  0.6 5.9 %setup.1 = (f32[192,128]{1,0:T(8,128)S(1)}, f32[576,128]{1,0:T(8,128)S(1)}, f32[192,128]{1,0:T(8,128)S(1)}, f32[6,32,128]{2,1,0:T(8,128)S(1)}, f32[3,32,128]{2,1...) custom-call(s32[1]{0:T(128)} %bitcast.run_ref, ...), custom_call_target="tpu_custom_call" | custom-call | tf_op jit(solution)/shard_map/setup/pallas_call | solution.py:510
  6.6 14.9 %all_to_all.35 = f32[32,1,768]{2,1,0:T(1,128)S(1)} all-to-all(f32[32,1,768]{2,1,0:T(1,128)S(1)} %bitcast.26), channel_id=1, replica_groups=mesh['pts'=8,'cams'=4] {'pts','cams'}, dimensions={0} | all-to-all | bytes 196608 | tf_op jit(solution)/shard_map/all_to_all | solution.py:534
  21.5 0.7 first_owner.1
  22.2 9.0 %all_to_all.36 = f32[32,1,384]{2,1,0:T(1,128)S(1)} all-to-all(f32[32,1,384]{2,1,0:T(1,128)S(1)} %bitcast.34), channel_id=1, replica_groups=mesh['pts'=8,'cams'=4] {'pts','cams'}, dimensions={0} | all-to-all | bytes 98304 | tf_op jit(solution)/shard_map/all_to_all | solution.py:534
  31.2 2.4 %schur.2 = (f32[96,128]{1,0:T(8,128)S(1)}, f32[8,128]{1,0:T(8,128)S(1)}, f32[3,32,128]{2,1,0:T(8,128)S(1)}, f32[9,8,128]{2,1,0:T(8,128)S(1)}, f32[9,8,128]{2,1,0:T(8,128)S(1)}) custom-call(f32[96,128]{1,0:T(8,128)S(1)} %bitcast.31, f32[576,128]{1,0:T(8,128)S(1)} %get-tuple-element.43.a_ref, f32[192,128]{1,0:T(8,128)S(1)} %get-tuple-element.44.b_ref, ...), custom_call_target="tpu_custom_call" | custom-call | flops 2000000000 | bytes 10000000 | tf_op jit(solution)/shard_map/schur/pallas_call | solution.py:510
  33.6 9.0 %all_to_all.37 = f32[32,1,384]{2,1,0:T(1,128)S(1)} all-to-all(f32[32,1,384]{2,1,0:T(1,128)S(1)} %bitcast.32), channel_id=1, replica_groups=mesh['pts'=8,'cams'=4] {'pts','cams'}, dimensions={0} | all-to-all | bytes 98304 | tf_op jit(solution)/shard_map/all_to_all | solution.py:534
  42.7 0.6 owner.1
  43.2 9.0 %all_to_all.38 = f32[32,1,384]{2,1,0:T(1,128)S(1)} all-to-all(f32[32,1,384]{2,1,0:T(1,128)S(1)} %bitcast.33), channel_id=1, replica_groups=mesh['pts'=8,'cams'=4] {'pts','cams'}, dimensions={0} | all-to-all | bytes 98304 | tf_op jit(solution)/shard_map/all_to_all | solution.py:534
  52.3 2.5 %schur.3 = (f32[96,128]{1,0:T(8,128)S(1)}, f32[8,128]{1,0:T(8,128)S(1)}, f32[3,32,128]{2,1,0:T(8,128)S(1)}, f32[3,32,128]{2,1,0:T(8,128)S(1)}, f32[9,8,128]{2,1,0:T(8,128)S(1)}, /*index=5*/f32[9,8,128]{2,1,0:T(8,128)S(1)}) custom-call(f32[96,128]{1,0:T(8,128)S(1)} %bitcast.28, f32[576,128]{1,0:T(8,128)S(1)} %get-tuple-element.43.a_ref, ...), custom_call_target="tpu_custom_call" | custom-call | flops 2000000000 | bytes 10000000 | tf_op jit(solution)/shard_map/schur/pallas_call | solution.py:510
  54.7 9.0 %all_to_all.39 = f32[32,1,384]{2,1,0:T(1,128)S(1)} all-to-all(f32[32,1,384]{2,1,0:T(1,128)S(1)} %bitcast.29), channel_id=1, replica_groups=mesh['pts'=8,'cams'=4] {'pts','cams'}, dimensions={0} | all-to-all | bytes 98304 | tf_op jit(solution)/shard_map/all_to_all | solution.py:534
  63.8 0.6 owner_final.1
  64.3 0.7 collective-permute-start
  65.0 9.9 %all_to_all.40 = f32[32,1,384]{2,1,0:T(1,128)S(1)} all-to-all(f32[32,1,384]{2,1,0:T(1,128)S(1)} %bitcast.30), channel_id=1, replica_groups=mesh['pts'=8,'cams'=4] {'pts','cams'}, dimensions={0} | all-to-all | bytes 98304 | tf_op jit(solution)/shard_map/all_to_all | solution.py:534
  75.0 0.0 collective-permute-done.other_ref
  75.0 0.1 tail.1.refs_0_
  75.1 0.7 collective-permute-start.2
  75.8 0.6 collective-permute-start.1
  76.4 1.9 %schur_last.1 = (f32[32,128]{1,0:T(8,128)S(1)}, f32[8,128]{1,0:T(8,128)S(1)}, f32[3,32,128]{2,1,0:T(8,128)S(1)}, f32[3,32,128]{2,1,0:T(8,128)S(1)}) custom-call(f32[96,128]{1,0:T(8,128)S(1)} %bitcast.23, f32[576,128]{1,0:T(8,128)S(1)} %get-tuple-element.43.a_ref, f32[192,128]{1,0:T(8,128)S(1)} %get-tuple-element.44.b_ref, ...), custom_call_target="tpu_custom_call" | custom-call | flops 2000000000 | bytes 10000000 | tf_op jit(solution)/shard_map/schur_last/pallas_call | solution.py:510
  78.3 2.7 %collective-permute-done.2.refs_1_ = f32[288,128]{1,0:T(8,128)S(1)} collective-permute-done((f32[288,128]{1,0:T(8,128)S(1)}, f32[288,128]{1,0:T(8,128)S(1)}, u32[]{:S(2)}, u32[]{:S(2)}) %collective-permute-start.2) | collective-permute-done | bytes 147488 | tf_op jit(solution)/shard_map/ppermute | solution.py:537
  81.0 0.1 collective-permute-done.1.refs_2_
  81.1 0.8 collective-permute-start.3
  81.9 9.7 %all_to_all.41 = f32[32,1,128]{2,1,0:T(1,128)S(1)} all-to-all(f32[32,1,128]{2,1,0:T(1,128)S(1)} %bitcast.35), channel_id=1, replica_groups=mesh['pts'=8,'cams'=4] {'pts','cams'}, dimensions={0} | all-to-all | bytes 32768 | tf_op jit(solution)/shard_map/all_to_all | solution.py:534
  91.6 0.0 collective-permute-done.3.refs_3_
  91.6 1.1 %final.1 = (f32[9,8192]{1,0:T(8,128)}, f32[3,4096]{1,0:T(4,128)}) custom-call(s32[1]{0:T(128)} %bitcast.run_ref, f32[32,128]{1,0:T(8,128)S(1)} %bitcast.27, f32[8,128]{1,0:T(8,128)S(1)} %get-tuple-element.75.product_ref, f32[6,32,128]{2,1,0:T(8,128)S(1)} %get-tuple-element.45.inv_ref, f32[3,32,128]{2,1,0:T(8,128)S(1)} %get-tuple-element.76.grad_ref, ...), custom_call_target="tpu_custom_call" | custom-call | tf_op jit(solution)/shard_map/final/pallas_call | solution.py:510
Async XLA Ops:
  64.3 10.7 %collective-permute-start = (f32[216,128]{1,0:T(8,128)S(1)}, f32[216,128]{1,0:T(8,128)S(1)}, u32[]{:S(2)}, u32[]{:S(2)}) collective-permute-start(f32[216,128]{1,0:T(8,128)S(1)} %get-tuple-element.67.own_ref), channel_id=1, source_target_pairs={{0,16},{4,20},{8,24},{12,28},{16,0},{20,4},{24,8},{28,12},{1,17},{... | collective-permute-start | bytes 331784 | tf_op jit(solution)/shard_map/ppermute | solution.py:537
  75.1 5.9 %collective-permute-start.2 = (f32[288,128]{1,0:T(8,128)S(1)}, f32[288,128]{1,0:T(8,128)S(1)}, u32[]{:S(2)}, u32[]{:S(2)}) collective-permute-start(f32[288,128]{1,0:T(8,128)S(1)} %tail.1.refs_0_), channel_id=1, source_target_pairs={{0,8},{4,12},{8,0},{12,4},{16,24},{20,28},{24,16},{28,20},{1,9},{5... | collective-permute-start | bytes 442376 | tf_op jit(solution)/shard_map/ppermute | solution.py:537
  75.8 5.3 %collective-permute-start.1 = (f32[288,128]{1,0:T(8,128)S(1)}, f32[288,128]{1,0:T(8,128)S(1)}, u32[]{:S(2)}, u32[]{:S(2)}) collective-permute-start(f32[288,128]{1,0:T(8,128)S(1)} %tail.1.refs_0_), channel_id=1, source_target_pairs={{0,4},{4,0},{8,12},{12,8},{16,20},{20,16},{24,28},{28,24},{1,5},{5... | collective-permute-start | bytes 442376 | tf_op jit(solution)/shard_map/ppermute | solution.py:537
  81.1 10.4 %collective-permute-start.3 = (f32[288,128]{1,0:T(8,128)S(1)}, f32[288,128]{1,0:T(8,128)S(1)}, u32[]{:S(2)}, u32[]{:S(2)}) collective-permute-start(f32[288,128]{1,0:T(8,128)S(1)} %collective-permute-done.2.refs_1_), channel_id=1, source_target_pairs={{0,4},{4,0},{8,12},{12,8},{16,20},{20,16},{24,28},{28,24},{1,5},{5... | collective-permute-start | bytes 442376 | tf_op jit(solution)/shard_map/ppermute | solution.py:537

commit v15 on v14

--- a/solution.py
+++ b/solution.py
@@ -18,7 +18,7 @@
 PT_HI = PT_DEV // PT_LO
 PIECES = 2
 FINE = 3
-FIRST = 4
+FAR, NEAR = 4, 2
 VMEM_LIMIT = 24 * 1024 * 1024
 
 damping_camera = 1.0
@@ -208,6 +208,20 @@
     return jnp.sum(chosen, keepdims=True)
 
 
+def own_lists(sizes, list_ref, spread_ref, place_ref):
+    pieces = sizes.slot // LANES
+    lane = lane_iota(1)
+    for c in range(sizes.cams):
+        for half in range(pieces):
+            value = list_ref[c : c + 1, half * LANES : (half + 1) * LANES]
+            low = c * sizes.block + half * (LANES // sizes.pts) + lane // sizes.pts
+            parts = [(value >> 8).astype(f32), (value & 255).astype(f32)]
+            spread_row(c * pieces + half, parts, lane % sizes.pts, sizes.pts, spread_ref)
+            place_row(c * pieces + half, low, LANES, place_ref)
+    result = scatter(2, sizes.cams * sizes.slot, sizes.pts, LANES, spread_ref, place_ref)
+    return result[: sizes.pts] * 256.0 + result[sizes.pts : 2 * sizes.pts]
+
+
 def setup_kernel(sizes, run_ref, column_ref, *refs):
     del run_ref
     sources, refs = refs[:6], refs[6:]
@@ -223,9 +237,17 @@
     ]
     for copy in copies:
         copy.start()
-    for k in (1, 2, 4):
+    for k in (3, 4, 5):
         copies[k].wait()
+    new_slot_ref[...] = slot_ref[...]
     new_point_ref[...] = point_ref[...]
+    for row in range(rows):
+        place_row(row, point_ref[row : row + 1, :] & (PT_LO - 1), PT_LO, place_wide_ref)
+        place_row(row, slot_place(slot_ref[row : row + 1, :], sizes)[1], LANES, place_slot_ref)
+    place_point_ref[...] = place_wide_ref[:LANES, :] + place_wide_ref[LANES:, :]
+    listed = own_lists(sizes, list_ref, spread_ref, place_list_ref)
+    for k in (1, 2):
+        copies[k].wait()
     for j in range(rows):
         columns = slice(j * LANES, (j + 1) * LANES)
         b_ref[pl.ds(j, 6, stride=rows), :] = pjac_ref[:, columns]
@@ -245,9 +267,8 @@
         keep_parts(parts, group, parts_ref)
         for s in range(SUB):
             row = group * SUB + s
-            point = point_ref[row : row + 1, :]
-            spread_row(row, part_rows(len(parts), group, s, parts_ref), point >> 8, PT_HI, spread_ref)
-            place_row(row, point & (PT_LO - 1), PT_LO, place_wide_ref)
+            high = point_ref[row : row + 1, :] // PT_LO
+            spread_row(row, part_rows(len(parts), group, s, parts_ref), high, PT_HI, spread_ref)
     result = scatter(sum(normal_pieces), sizes.obs, PT_HI, PT_LO, spread_ref, place_wide_ref)
     normal = joined(result, 9, PT_HI, normal_pieces)
     top_left = normal[0] + damping_point
@@ -273,10 +294,7 @@
     eliminated = solve(inverse, normal[6:])
     for k in range(3):
         narrow(table_ref, k, eliminated[k])
-    place_point_ref[...] = place_wide_ref[:LANES, :] + place_wide_ref[LANES:, :]
-    for k in (0, 3, 5):
-        copies[k].wait()
-    new_slot_ref[...] = slot_ref[...]
+    copies[0].wait()
     for j in range(rows):
         for start in range(0, 2 * CP, SUB):
             size = min(SUB, 2 * CP - start)
@@ -295,23 +313,11 @@
         keep_parts(parts, group, parts_ref)
         for s in range(SUB):
             row = group * SUB + s
-            high, low = slot_place(slot_ref[row : row + 1, :], sizes)
+            high, _ = slot_place(slot_ref[row : row + 1, :], sizes)
             spread_row(row, part_rows(len(parts), group, s, parts_ref), high, sizes.pts, spread_ref)
-            place_row(row, low, LANES, place_slot_ref)
     result = scatter(2 * CP * PIECES, sizes.obs, sizes.pts, LANES, spread_ref, place_slot_ref)
     fields = joined(result, 2 * CP, sizes.pts)
 
-    pieces = sizes.slot // LANES
-    lane = lane_iota(1)
-    for c in range(sizes.cams):
-        for half in range(pieces):
-            value = list_ref[c : c + 1, half * LANES : (half + 1) * LANES]
-            low = c * sizes.block + half * (LANES // sizes.pts) + lane // sizes.pts
-            parts = [(value >> 8).astype(f32), (value & 255).astype(f32)]
-            spread_row(c * pieces + half, parts, lane % sizes.pts, sizes.pts, spread_ref)
-            place_row(c * pieces + half, low, LANES, place_list_ref)
-    result = scatter(2, sizes.cams * sizes.slot, sizes.pts, LANES, spread_ref, place_list_ref)
-    listed = result[: sizes.pts] * 256.0 + result[sizes.pts : 2 * sizes.pts]
     write_messages(fields, None, sizes.first_groups, sizes.first_message, out_ref, sizes, extra=listed, column=column_ref[0])
 
 
@@ -461,38 +467,46 @@
     write_messages(fields, partial, sizes.groups, sizes.message, out_ref, sizes)
 
 
-def tail_kernel(sizes, in_ref, product_ref, own_ref, other_ref, out_ref):
+def tail_kernel(sizes, in_ref, product_ref, own_ref, far_ref, near_ref, out_ref, far_out_ref):
     renewed = jnp.broadcast_to(read_scalar(in_ref, sizes.groups, sizes.message, sizes), (SUB, LANES))
     beta = (renewed / product_ref[...])[:1]
     field = CP * sizes.own_rows
-    for j, ref in enumerate((own_ref, other_ref)):
-        first = j * 2 * field
-        out_ref[first : first + field, :] = ref[:field, :]
-        out_ref[first + field : first + 2 * field, :] = ref[2 * field :, :] + beta * ref[field : 2 * field, :]
+    for j, ref in enumerate((own_ref, far_ref, near_ref)):
+        base = ref[:field, :]
+        direction = ref[2 * field :, :] + beta * ref[field : 2 * field, :]
+        for target, first in [(out_ref, j * 2 * field)] + ([(far_out_ref, 0)] if ref is far_ref else []):
+            target[first : first + field, :] = base
+            target[first + field : first + 2 * field, :] = direction
 
 
 def final_kernel(sizes, masks, run_ref, in_ref, product_ref, inv_ref, grad_ref, sum_ref, *refs):
     all_refs = refs[: len(masks)]
-    cam_ref, pt_ref, table_ref = refs[len(masks) :]
+    cam_ref, pt_ref, table_ref, run_out_ref, semaphores = refs[len(masks) :]
     curvature = jnp.sum(jnp.where(lane_iota(sizes.devices) == 0, in_ref[...], 0.0), keepdims=True)
     step = (product_ref[...] / jnp.broadcast_to(curvature, (SUB, LANES)))[:1]
-    for all_ref, pair in zip(all_refs, masks):
-        for j, mask in enumerate(pair):
-            base_column = (run_ref[0] ^ mask) * sizes.run
+    copies = []
+    for all_ref, group in zip(all_refs, masks):
+        for j, mask in enumerate(group):
+            slot = len(copies)
             for h in range(sizes.run_rows):
-                columns = pl.ds(pl.multiple_of(base_column + h * LANES, LANES), LANES)
+                columns = slice(h * LANES, (h + 1) * LANES)
                 for start in range(0, CP, SUB):
                     size = min(SUB, CP - start)
                     first = (j * 2 * CP + start) * sizes.own_rows + h
                     base = all_ref[pl.ds(first, size, stride=sizes.own_rows), :]
                     direction = all_ref[pl.ds(first + CP * sizes.own_rows, size, stride=sizes.own_rows), :]
-                    cam_ref[start : start + size, columns] = base + step * direction
+                    run_out_ref[slot, start : start + size, columns] = base + step * direction
+            columns = pl.ds(pl.multiple_of((run_ref[0] ^ mask) * sizes.run, LANES), sizes.run)
+            copies.append(pltpu.make_async_copy(run_out_ref.at[slot], cam_ref.at[:, columns], semaphores.at[slot]))
+            copies[-1].start()
     total = [grad_ref[k] + step[:, :1] * sum_ref[k] for k in range(3)]
     solved = solve([inv_ref[k] for k in range(6)], total)
     for k in range(3):
         table_ref[k * PT_ROWS : (k + 1) * PT_ROWS, :] = -solved[k]
     for row in range(PT_ROWS):
         pt_ref[:, row * LANES : (row + 1) * LANES] = table_ref[pl.ds(row, 3, stride=PT_ROWS), :]
+    for copy in copies:
+        copy.wait()
 
 
 def shape(*dims, dtype=f32):
@@ -503,8 +517,7 @@
     return pltpu.VMEM(dims, dtype)
 
 
-def call(kernel, name, inputs, outputs, scratch, scalars=(), inputs_at=pltpu.VMEM, cost=None):
-    vmem = pl.BlockSpec(memory_space=pltpu.VMEM)
+def call(kernel, name, inputs, outputs, scratch, scalars=(), inputs_at=pltpu.VMEM, outputs_at=None, cost=None):
     given = pl.BlockSpec(memory_space=inputs_at)
     smem = pl.BlockSpec(memory_space=pltpu.SMEM)
     return pl.pallas_call(
@@ -512,7 +525,7 @@
         name=name,
         out_shape=outputs,
         in_specs=[smem] * len(scalars) + [given] * len(inputs),
-        out_specs=[vmem] * len(outputs),
+        out_specs=[pl.BlockSpec(memory_space=space) for space in outputs_at or [pltpu.VMEM] * len(outputs)],
         scratch_shapes=scratch,
         cost_estimate=cost,
         compiler_params=pltpu.CompilerParams(vmem_limit_bytes=VMEM_LIMIT),
@@ -595,19 +608,18 @@
         start, last = iteration == 0, iteration == ITERS - 1
         earlier = [] if start else [product, slots, direction, step, sums]
         if last:
-            neighbour = flipped(fields, FIRST)
+            neighbours = [flipped(fields, FAR), flipped(fields, NEAR)]
         arrived = exchange(out)
         if last:
-            (both,) = call(
+            near_side, far_block = call(
                 functools.partial(tail_kernel, sizes),
                 "tail",
-                [arrived, product, fields, neighbour],
-                [kept(4 * CP * sizes.own_rows, LANES)],
+                [arrived, product, fields] + neighbours,
+                [kept(6 * CP * sizes.own_rows, LANES), kept(2 * CP * sizes.own_rows, LANES)],
                 [],
             )
-            flips = [1 << bit for bit in range(sizes.pts.bit_length() - 1) if 1 << bit != FIRST]
-            flips = flips[1:] + flips[:1]
-            early = {flip: flipped(both, flip) for flip in (flips[0], flips[-1])}
+            flips = [1 << bit for bit in reversed(range(sizes.pts.bit_length() - 1)) if 1 << bit not in (FAR, NEAR)]
+            early = [flipped(far_block, NEAR), flipped(near_side, flips[0])]
         results = call(
             functools.partial(schur_kernel, sizes, start, last),
             "schur_last" if last else "schur",
@@ -625,11 +637,13 @@
         if not last:
             slots, direction = results
         if last:
-            early, out = lax.optimization_barrier((early, out))
-            gathered, masks = [both], [(0, FIRST)]
+            early[0], out = lax.optimization_barrier((early[0], out))
+            gathered, masks = [near_side, early[0]], [(0, FAR, NEAR), (FAR ^ NEAR,)]
             for flip in flips:
-                gathered += [early[flip] if value is both and flip in early else flipped(value, flip) for value in gathered]
-                masks += [tuple(mask ^ flip for mask in pair) for pair in masks]
+                gathered += [
+                    early[1] if value is near_side and flip == flips[0] else flipped(value, flip) for value in gathered
+                ]
+                masks += [tuple(mask ^ flip for mask in group) for group in masks]
             break
         final = iteration == ITERS - 2
         out, remainder, step, solution_ = call(
@@ -645,7 +659,12 @@
         "final",
         [exchange(out), product, inverse, gradient, sums] + gathered,
         [shape(CP, CAM_OWN), shape(3, PT_DEV)],
-        [pltpu.VMEM((3 * PT_ROWS, LANES), f32)],
+        [
+            pltpu.VMEM((3 * PT_ROWS, LANES), f32),
+            pltpu.VMEM((sizes.pts, CP, sizes.run), f32),
+            pltpu.SemaphoreType.DMA((sizes.pts,)),
+        ],
+        outputs_at=[pl.ANY, pltpu.VMEM],
         scalars=[run],
     )
 

time: 92.9 us -> 93.9 us (1.011)
  Pallas kernels: 15.8 us -> 17.9 us
  waiting for transfers between devices: 2.82 us -> 1.21 us
    pallas_call x9, Pallas kernels: 15.8 us -> 17.9 us  [call(): pl.pallas_call(kernel, name=name, out_shape=outputs, in_specs=[smem] * le...]
    ppermute x4 -> x5, waiting for transfers between devices: 2.82 us -> 1.21 us  [flipped(): return lax.ppermute(value, 'pts', [(p, p ^ flip) for p in range(sizes.pts)])]
    ppermute x4 -> x5, starting transfers between devices: 2.76 us -> 3.07 us  [flipped(): return lax.ppermute(value, 'pts', [(p, p ^ flip) for p in range(sizes.pts)])]
  transfers between devices with their start and end apart: 4 -> 5, of which waited for: 2 -> 1; matrix products, arithmetic and copies ran while one was open for 0% -> 0% of each run, Pallas kernels for 2% -> 2%
where the time goes in v15:
time: 93.9 us; the launch traced here: 93.6 us
  blocking collectives  70.7 us (75%)
  Pallas kernels  17.9 us (19%)
  starting transfers between devices  3.07 us (3%)
  waiting for transfers between devices  1.21 us (1%)
    all_to_all x7, blocking collectives, exchange(): lax.all_to_all(flat, axes, split_axis=0, concat_axis=0, tiled=True)  70.7 us
    pallas_call x9, Pallas kernels, call(): pl.pallas_call(kernel, name=name, out_shape=outputs, in_specs=[smem] * le...  17.9 us
    ppermute x5, starting transfers between devices, flipped(): return lax.ppermute(value, 'pts', [(p, p ^ flip) for p in range(sizes.pts)])  3.07 us
  transfers between devices with their start and end apart: 5, of which 1 were waited for; matrix products, arithmetic and copies ran while one was open for 0% of the time, Pallas kernels for 2%

profile of v15, /device:TPU:0, one launch (start us, length us, event | category | flops | bytes accessed | tf_op | source)
XLA Modules:
  0.0 93.6 jit_solution(11741910062413129903)
XLA Ops:
  0.6 7.3 %setup.1 = (f32[192,128]{1,0:T(8,128)S(1)}, f32[576,128]{1,0:T(8,128)S(1)}, f32[192,128]{1,0:T(8,128)S(1)}, f32[6,32,128]{2,1,0:T(8,128)S(1)}, f32[3,32,128]{2,1...) custom-call(s32[1]{0:T(128)} %bitcast.run_ref, ...), custom_call_target="tpu_custom_call" | custom-call | tf_op jit(solution)/shard_map/setup/pallas_call | solution.py:523
  8.0 14.9 %all_to_all.35 = f32[32,1,768]{2,1,0:T(1,128)S(1)} all-to-all(f32[32,1,768]{2,1,0:T(1,128)S(1)} %bitcast.26), channel_id=1, replica_groups=mesh['pts'=8,'cams'=4] {'pts','cams'}, dimensions={0} | all-to-all | bytes 196608 | tf_op jit(solution)/shard_map/all_to_all | solution.py:547
  22.9 0.7 first_owner.1
  23.6 9.0 %all_to_all.36 = f32[32,1,384]{2,1,0:T(1,128)S(1)} all-to-all(f32[32,1,384]{2,1,0:T(1,128)S(1)} %bitcast.34), channel_id=1, replica_groups=mesh['pts'=8,'cams'=4] {'pts','cams'}, dimensions={0} | all-to-all | bytes 98304 | tf_op jit(solution)/shard_map/all_to_all | solution.py:547
  32.6 2.5 %schur.2 = (f32[96,128]{1,0:T(8,128)S(1)}, f32[8,128]{1,0:T(8,128)S(1)}, f32[3,32,128]{2,1,0:T(8,128)S(1)}, f32[9,8,128]{2,1,0:T(8,128)S(1)}, f32[9,8,128]{2,1,0:T(8,128)S(1)}) custom-call(f32[96,128]{1,0:T(8,128)S(1)} %bitcast.31, f32[576,128]{1,0:T(8,128)S(1)} %get-tuple-element.44.a_ref, f32[192,128]{1,0:T(8,128)S(1)} %get-tuple-element.45.b_ref, ...), custom_call_target="tpu_custom_call" | custom-call | flops 2000000000 | bytes 10000000 | tf_op jit(solution)/shard_map/schur/pallas_call | solution.py:523
  35.1 9.0 %all_to_all.37 = f32[32,1,384]{2,1,0:T(1,128)S(1)} all-to-all(f32[32,1,384]{2,1,0:T(1,128)S(1)} %bitcast.32), channel_id=1, replica_groups=mesh['pts'=8,'cams'=4] {'pts','cams'}, dimensions={0} | all-to-all | bytes 98304 | tf_op jit(solution)/shard_map/all_to_all | solution.py:547
  44.2 0.6 owner.1
  44.7 9.0 %all_to_all.38 = f32[32,1,384]{2,1,0:T(1,128)S(1)} all-to-all(f32[32,1,384]{2,1,0:T(1,128)S(1)} %bitcast.33), channel_id=1, replica_groups=mesh['pts'=8,'cams'=4] {'pts','cams'}, dimensions={0} | all-to-all | bytes 98304 | tf_op jit(solution)/shard_map/all_to_all | solution.py:547
  53.8 2.6 %schur.3 = (f32[96,128]{1,0:T(8,128)S(1)}, f32[8,128]{1,0:T(8,128)S(1)}, f32[3,32,128]{2,1,0:T(8,128)S(1)}, f32[3,32,128]{2,1,0:T(8,128)S(1)}, f32[9,8,128]{2,1,0:T(8,128)S(1)}, /*index=5*/f32[9,8,128]{2,1,0:T(8,128)S(1)}) custom-call(f32[96,128]{1,0:T(8,128)S(1)} %bitcast.29, f32[576,128]{1,0:T(8,128)S(1)} %get-tuple-element.44.a_ref, ...), custom_call_target="tpu_custom_call" | custom-call | flops 2000000000 | bytes 10000000 | tf_op jit(solution)/shard_map/schur/pallas_call | solution.py:523
  56.3 9.0 %all_to_all.39 = f32[32,1,384]{2,1,0:T(1,128)S(1)} all-to-all(f32[32,1,384]{2,1,0:T(1,128)S(1)} %bitcast.30), channel_id=1, replica_groups=mesh['pts'=8,'cams'=4] {'pts','cams'}, dimensions={0} | all-to-all | bytes 98304 | tf_op jit(solution)/shard_map/all_to_all | solution.py:547
  65.4 0.6 owner_final.1
  65.9 0.7 collective-permute-start.1
  66.6 0.6 collective-permute-start
  67.1 10.8 %all_to_all.40 = f32[32,1,384]{2,1,0:T(1,128)S(1)} all-to-all(f32[32,1,384]{2,1,0:T(1,128)S(1)} %bitcast.28), channel_id=1, replica_groups=mesh['pts'=8,'cams'=4] {'pts','cams'}, dimensions={0} | all-to-all | bytes 98304 | tf_op jit(solution)/shard_map/all_to_all | solution.py:547
  78.0 0.0 collective-permute-done.1.near_ref
  78.0 0.0 collective-permute-done.far_ref
  78.0 0.1 tail.1
  78.1 0.7 collective-permute-start.2
  78.8 0.6 collective-permute-start.3
  79.4 2.0 %schur_last.1 = (f32[32,128]{1,0:T(8,128)S(1)}, f32[8,128]{1,0:T(8,128)S(1)}, f32[3,32,128]{2,1,0:T(8,128)S(1)}, f32[3,32,128]{2,1,0:T(8,128)S(1)}) custom-call(f32[96,128]{1,0:T(8,128)S(1)} %bitcast.23, f32[576,128]{1,0:T(8,128)S(1)} %get-tuple-element.44.a_ref, f32[192,128]{1,0:T(8,128)S(1)} %get-tuple-element.45.b_ref, ...), custom_call_target="tpu_custom_call" | custom-call | flops 2000000000 | bytes 10000000 | tf_op jit(solution)/shard_map/schur_last/pallas_call | solution.py:523
  81.4 1.2 %collective-permute-done.2.refs_1_ = f32[144,128]{1,0:T(8,128)S(1)} collective-permute-done((f32[144,128]{1,0:T(8,128)S(1)}, f32[144,128]{1,0:T(8,128)S(1)}, u32[]{:S(2)}, u32[]{:S(2)}) %collective-permute-start.2) | collective-permute-done | bytes 73760 | tf_op jit(solution)/shard_map/ppermute | solution.py:550
  82.5 0.6 collective-permute-start.4
  83.1 8.9 %all_to_all.41 = f32[32,1,128]{2,1,0:T(1,128)S(1)} all-to-all(f32[32,1,128]{2,1,0:T(1,128)S(1)} %bitcast.35), channel_id=1, replica_groups=mesh['pts'=8,'cams'=4] {'pts','cams'}, dimensions={0} | all-to-all | bytes 32768 | tf_op jit(solution)/shard_map/all_to_all | solution.py:547
  92.0 1.6 %final.1 = (f32[9,8192]{1,0:T(8,128)}, f32[3,4096]{1,0:T(4,128)}) custom-call(s32[1]{0:T(128)} %bitcast.run_ref, f32[32,128]{1,0:T(8,128)S(1)} %bitcast.27, f32[8,128]{1,0:T(8,128)S(1)} %get-tuple-element.77.product_ref, f32[6,32,128]{2,1,0:T(8,128)S(1)} %get-tuple-element.46.inv_ref, f32[3,32,128]{2,1,0:T(8,128)S(1)} %get-tuple-element.78.grad_ref, ...), custom_call_target="tpu_custom_call" | custom-call | tf_op jit(solution)/shard_map/final/pallas_call | solution.py:523
  (2 shorter events, 0.0 us)
Async XLA Ops:
  65.9 12.1 %collective-permute-start.1 = (f32[216,128]{1,0:T(8,128)S(1)}, f32[216,128]{1,0:T(8,128)S(1)}, u32[]{:S(2)}, u32[]{:S(2)}) collective-permute-start(f32[216,128]{1,0:T(8,128)S(1)} %get-tuple-element.68.own_ref), channel_id=1, source_target_pairs={{0,8},{4,12},{8,0},{12,4},{16,24},{20,28},{24,16},{28,20},{1,9},{5... | collective-permute-start | bytes 331784 | tf_op jit(solution)/shard_map/ppermute | solution.py:550
  66.6 11.4 %collective-permute-start = (f32[216,128]{1,0:T(8,128)S(1)}, f32[216,128]{1,0:T(8,128)S(1)}, u32[]{:S(2)}, u32[]{:S(2)}) collective-permute-start(f32[216,128]{1,0:T(8,128)S(1)} %get-tuple-element.68.own_ref), channel_id=1, source_target_pairs={{0,16},{4,20},{8,24},{12,28},{16,0},{20,4},{24,8},{28,12},{1,17},{... | collective-permute-start | bytes 331784 | tf_op jit(solution)/shard_map/ppermute | solution.py:550
  78.1 4.4 %collective-permute-start.2 = (f32[144,128]{1,0:T(8,128)S(1)}, f32[144,128]{1,0:T(8,128)S(1)}, u32[]{:S(2)}, u32[]{:S(2)}) collective-permute-start(f32[144,128]{1,0:T(8,128)S(1)} %get-tuple-element.69), channel_id=1, source_target_pairs={{0,8},{4,12},{8,0},{12,4},{16,24},{20,28},{24,16},{28,20},{1,9},{5... | collective-permute-start | bytes 221192 | tf_op jit(solution)/shard_map/ppermute | solution.py:550
  78.8 13.2 %collective-permute-start.3 = (f32[432,128]{1,0:T(8,128)S(1)}, f32[432,128]{1,0:T(8,128)S(1)}, u32[]{:S(2)}, u32[]{:S(2)}) collective-permute-start(f32[432,128]{1,0:T(8,128)S(1)} %get-tuple-element.80.refs_0_), channel_id=1, source_target_pairs={{0,4},{4,0},{8,12},{12,8},{16,20},{20,16},{24,28},{28,24},{1,5},{5... | collective-permute-start | bytes 663560 | tf_op jit(solution)/shard_map/ppermute | solution.py:550
  82.5 9.5 %collective-permute-start.4 = (f32[144,128]{1,0:T(8,128)S(1)}, f32[144,128]{1,0:T(8,128)S(1)}, u32[]{:S(2)}, u32[]{:S(2)}) collective-permute-start(f32[144,128]{1,0:T(8,128)S(1)} %collective-permute-done.2.refs_1_), channel_id=1, source_target_pairs={{0,4},{4,0},{8,12},{12,8},{16,20},{20,16},{24,28},{28,24},{1,5},{5... | collective-permute-start | bytes 221192 | tf_op jit(solution)/shard_map/ppermute | solution.py:550

commit v16 on v14

--- a/solution.py
+++ b/solution.py
@@ -18,7 +18,7 @@
 PT_HI = PT_DEV // PT_LO
 PIECES = 2
 FINE = 3
-FIRST = 4
+FAR, NEAR = 4, 2
 VMEM_LIMIT = 24 * 1024 * 1024
 
 damping_camera = 1.0
@@ -87,7 +87,7 @@
     return result
 
 
-def spread_row(index, parts, high, high_count, spread_ref):
+def spread_row(index, parts, high, high_count, spread_ref, base=0):
     columns = slice(index * LANES, (index + 1) * LANES)
     mask = jnp.broadcast_to(high, (high_count, LANES)) == sub_iota(high_count)
     together = max(1, 16 // high_count)
@@ -99,7 +99,8 @@
         while len(pieces) < together:
             pieces.append(jnp.zeros((high_count, LANES), f32))
         tile = pieces[0] if together == 1 else jnp.concatenate(pieces, axis=0)
-        spread_ref[start * high_count : start * high_count + tile.shape[0], columns] = tile.astype(bf16)
+        first = base + start * high_count
+        spread_ref[first : first + tile.shape[0], columns] = tile.astype(bf16)
 
 
 def place_row(index, low, low_count, place_ref):
@@ -108,13 +109,13 @@
     place_ref[:low_count, columns] = jnp.where(place, 1.0, 0.0).astype(bf16)
 
 
-def keep_parts(parts, group, parts_ref):
-    for k, part in enumerate(parts):
+def keep_parts(parts, group, parts_ref, base=0):
+    for k, part in enumerate(parts, base):
         parts_ref[group, k * SUB : (k + 1) * SUB, :] = part
 
 
-def part_rows(count, group, s, parts_ref):
-    return [parts_ref[group, k * SUB + s : k * SUB + s + 1, :] for k in range(count)]
+def part_rows(count, group, s, parts_ref, base=0):
+    return [parts_ref[group, k * SUB + s : k * SUB + s + 1, :] for k in range(base, base + count)]
 
 
 def spread_rows(parts, high_count):
@@ -213,13 +214,13 @@
     sources, refs = refs[:6], refs[6:]
     out_ref, a_ref, b_ref, inv_ref, grad_ref, place_point_ref, place_slot_ref, new_slot_ref, new_point_ref = refs[:9]
     refs = refs[9:]
-    r_ref, parts_ref, spread_ref, table_ref, place_wide_ref, place_list_ref = refs[:6]
-    jac_ref, pjac_ref, res_ref, slot_ref, point_ref, list_ref = refs[6:12]
-    semaphores = refs[12]
+    r_ref, parts_ref, spread_ref, table_ref, place_wide_ref, place_list_ref, slot_parts_ref, spread_slot_ref, spread_list_ref = refs[:9]
+    jac_ref, pjac_ref, res_ref, slot_ref, point_ref, list_ref = refs[9:15]
+    semaphores = refs[15]
     rows = sizes.rows
     copies = [
         pltpu.make_async_copy(source, target, semaphores.at[k])
-        for k, (source, target) in enumerate(zip(sources, refs[6:12]))
+        for k, (source, target) in enumerate(zip(sources, refs[9:15]))
     ]
     for copy in copies:
         copy.start()
@@ -248,6 +249,39 @@
             point = point_ref[row : row + 1, :]
             spread_row(row, part_rows(len(parts), group, s, parts_ref), point >> 8, PT_HI, spread_ref)
             place_row(row, point & (PT_LO - 1), PT_LO, place_wide_ref)
+    for k in (0, 3, 5):
+        copies[k].wait()
+    new_slot_ref[...] = slot_ref[...]
+    for j in range(rows):
+        for start in range(0, 2 * CP, SUB):
+            size = min(SUB, 2 * CP - start)
+            a_ref[pl.ds(start * rows + j, size, stride=rows), :] = jac_ref[
+                start : start + size, j * LANES : (j + 1) * LANES
+            ]
+
+    count = CP * PIECES
+    for group in range(rows // SUB):
+        a = [at(a_ref, k, group) for k in range(2 * CP)]
+        values = [a[k] * a[k] + a[CP + k] * a[CP + k] for k in range(CP)]
+        keep_parts([part for value in values for part in cut(value)], group, slot_parts_ref, count)
+        for s in range(SUB):
+            row = group * SUB + s
+            high, low = slot_place(slot_ref[row : row + 1, :], sizes)
+            parts = part_rows(count, group, s, slot_parts_ref, count)
+            spread_row(row, parts, high, sizes.pts, spread_slot_ref, count * sizes.pts)
+            place_row(row, low, LANES, place_slot_ref)
+
+    pieces = sizes.slot // LANES
+    lane = lane_iota(1)
+    for c in range(sizes.cams):
+        for half in range(pieces):
+            value = list_ref[c : c + 1, half * LANES : (half + 1) * LANES]
+            low = c * sizes.block + half * (LANES // sizes.pts) + lane // sizes.pts
+            parts = [(value >> 8).astype(f32), (value & 255).astype(f32)]
+            spread_row(c * pieces + half, parts, lane % sizes.pts, sizes.pts, spread_list_ref)
+            place_row(c * pieces + half, low, LANES, place_list_ref)
+    result = scatter(2, sizes.cams * sizes.slot, sizes.pts, LANES, spread_list_ref, place_list_ref)
+    listed = result[: sizes.pts] * 256.0 + result[sizes.pts : 2 * sizes.pts]
     result = scatter(sum(normal_pieces), sizes.obs, PT_HI, PT_LO, spread_ref, place_wide_ref)
     normal = joined(result, 9, PT_HI, normal_pieces)
     top_left = normal[0] + damping_point
@@ -274,44 +308,20 @@
     for k in range(3):
         narrow(table_ref, k, eliminated[k])
     place_point_ref[...] = place_wide_ref[:LANES, :] + place_wide_ref[LANES:, :]
-    for k in (0, 3, 5):
-        copies[k].wait()
-    new_slot_ref[...] = slot_ref[...]
-    for j in range(rows):
-        for start in range(0, 2 * CP, SUB):
-            size = min(SUB, 2 * CP - start)
-            a_ref[pl.ds(start * rows + j, size, stride=rows), :] = jac_ref[
-                start : start + size, j * LANES : (j + 1) * LANES
-            ]
-
     for group in range(rows // SUB):
         at_point = point_gather(table_ref, point_ref[group * SUB : (group + 1) * SUB, :])
         b = [at(b_ref, k, group) for k in range(6)]
         errors = [at(r_ref, i, group) - sum(b[3 * i + k] * at_point[k] for k in range(3)) for i in range(2)]
         a = [at(a_ref, k, group) for k in range(2 * CP)]
         values = [a[k] * errors[0] + a[CP + k] * errors[1] for k in range(CP)]
-        values += [a[k] * a[k] + a[CP + k] * a[CP + k] for k in range(CP)]
-        parts = [part for value in values for part in cut(value)]
-        keep_parts(parts, group, parts_ref)
+        keep_parts([part for value in values for part in cut(value)], group, slot_parts_ref)
         for s in range(SUB):
             row = group * SUB + s
-            high, low = slot_place(slot_ref[row : row + 1, :], sizes)
-            spread_row(row, part_rows(len(parts), group, s, parts_ref), high, sizes.pts, spread_ref)
-            place_row(row, low, LANES, place_slot_ref)
-    result = scatter(2 * CP * PIECES, sizes.obs, sizes.pts, LANES, spread_ref, place_slot_ref)
+            high, _ = slot_place(slot_ref[row : row + 1, :], sizes)
+            spread_row(row, part_rows(count, group, s, slot_parts_ref), high, sizes.pts, spread_slot_ref)
+    result = scatter(2 * count, sizes.obs, sizes.pts, LANES, spread_slot_ref, place_slot_ref)
     fields = joined(result, 2 * CP, sizes.pts)
 
-    pieces = sizes.slot // LANES
-    lane = lane_iota(1)
-    for c in range(sizes.cams):
-        for half in range(pieces):
-            value = list_ref[c : c + 1, half * LANES : (half + 1) * LANES]
-            low = c * sizes.block + half * (LANES // sizes.pts) + lane // sizes.pts
-            parts = [(value >> 8).astype(f32), (value & 255).astype(f32)]
-            spread_row(c * pieces + half, parts, lane % sizes.pts, sizes.pts, spread_ref)
-            place_row(c * pieces + half, low, LANES, place_list_ref)
-    result = scatter(2, sizes.cams * sizes.slot, sizes.pts, LANES, spread_ref, place_list_ref)
-    listed = result[: sizes.pts] * 256.0 + result[sizes.pts : 2 * sizes.pts]
     write_messages(fields, None, sizes.first_groups, sizes.first_message, out_ref, sizes, extra=listed, column=column_ref[0])
 
 
@@ -461,14 +471,16 @@
     write_messages(fields, partial, sizes.groups, sizes.message, out_ref, sizes)
 
 
-def tail_kernel(sizes, in_ref, product_ref, own_ref, other_ref, out_ref):
+def tail_kernel(sizes, in_ref, product_ref, own_ref, far_ref, near_ref, out_ref, far_out_ref):
     renewed = jnp.broadcast_to(read_scalar(in_ref, sizes.groups, sizes.message, sizes), (SUB, LANES))
     beta = (renewed / product_ref[...])[:1]
     field = CP * sizes.own_rows
-    for j, ref in enumerate((own_ref, other_ref)):
-        first = j * 2 * field
-        out_ref[first : first + field, :] = ref[:field, :]
-        out_ref[first + field : first + 2 * field, :] = ref[2 * field :, :] + beta * ref[field : 2 * field, :]
+    for j, ref in enumerate((own_ref, far_ref, near_ref)):
+        base = ref[:field, :]
+        direction = ref[2 * field :, :] + beta * ref[field : 2 * field, :]
+        for target, first in [(out_ref, j * 2 * field)] + ([(far_out_ref, 0)] if ref is far_ref else []):
+            target[first : first + field, :] = base
+            target[first + field : first + 2 * field, :] = direction
 
 
 def final_kernel(sizes, masks, run_ref, in_ref, product_ref, inv_ref, grad_ref, sum_ref, *refs):
@@ -571,9 +583,11 @@
             kept(rows, LANES, dtype=jnp.int32),
             kept(rows, LANES, dtype=jnp.int32),
         ],
-        [pltpu.VMEM((2 * rows, LANES), f32), parts_scratch(2 * CP * PIECES)]
-        + [pltpu.VMEM((max(spread_rows(9 * FINE, PT_HI), spread_rows(2 * CP * PIECES, sizes.pts)), sizes.obs), bf16)]
+        [pltpu.VMEM((2 * rows, LANES), f32), parts_scratch(9 * FINE)]
+        + [pltpu.VMEM((spread_rows(9 * FINE, PT_HI), sizes.obs), bf16)]
         + [point_scratch, pltpu.VMEM((PT_LO, sizes.obs), bf16), pltpu.VMEM((LANES, sizes.cams * sizes.slot), bf16)]
+        + [parts_scratch(2 * CP * PIECES), pltpu.VMEM((spread_rows(2 * CP * PIECES, sizes.pts), sizes.obs), bf16)]
+        + [pltpu.VMEM((spread_rows(2, sizes.pts), sizes.cams * sizes.slot), bf16)]
         + [pltpu.VMEM(value.shape, value.dtype) for value in given]
         + [pltpu.SemaphoreType.DMA((len(given),))],
         scalars=[run, column],
@@ -595,19 +609,18 @@
         start, last = iteration == 0, iteration == ITERS - 1
         earlier = [] if start else [product, slots, direction, step, sums]
         if last:
-            neighbour = flipped(fields, FIRST)
+            neighbours = [flipped(fields, FAR), flipped(fields, NEAR)]
         arrived = exchange(out)
         if last:
-            (both,) = call(
+            near_side, far_block = call(
                 functools.partial(tail_kernel, sizes),
                 "tail",
-                [arrived, product, fields, neighbour],
-                [kept(4 * CP * sizes.own_rows, LANES)],
+                [arrived, product, fields] + neighbours,
+                [kept(6 * CP * sizes.own_rows, LANES), kept(2 * CP * sizes.own_rows, LANES)],
                 [],
             )
-            flips = [1 << bit for bit in range(sizes.pts.bit_length() - 1) if 1 << bit != FIRST]
-            flips = flips[1:] + flips[:1]
-            early = {flip: flipped(both, flip) for flip in (flips[0], flips[-1])}
+            flips = [1 << bit for bit in reversed(range(sizes.pts.bit_length() - 1)) if 1 << bit not in (FAR, NEAR)]
+            early = [flipped(far_block, NEAR), flipped(near_side, flips[0])]
         results = call(
             functools.partial(schur_kernel, sizes, start, last),
             "schur_last" if last else "schur",
@@ -625,11 +638,13 @@
         if not last:
             slots, direction = results
         if last:
-            early, out = lax.optimization_barrier((early, out))
-            gathered, masks = [both], [(0, FIRST)]
+            early[0], out = lax.optimization_barrier((early[0], out))
+            gathered, masks = [near_side, early[0]], [(0, FAR, NEAR), (FAR ^ NEAR,)]
             for flip in flips:
-                gathered += [early[flip] if value is both and flip in early else flipped(value, flip) for value in gathered]
-                masks += [tuple(mask ^ flip for mask in pair) for pair in masks]
+                gathered += [
+                    early[1] if value is near_side and flip == flips[0] else flipped(value, flip) for value in gathered
+                ]
+                masks += [tuple(mask ^ flip for mask in group) for group in masks]
             break
         final = iteration == ITERS - 2
         out, remainder, step, solution_ = call(

time: 92.9 us -> 93.8 us (level)
  Pallas kernels: 15.8 us -> 17.8 us
  waiting for transfers between devices: 2.82 us -> 1.21 us
    pallas_call x9, Pallas kernels: 15.8 us -> 17.8 us  [call(): pl.pallas_call(kernel, name=name, out_shape=outputs, in_specs=[smem] * le...]
    ppermute x4 -> x5, waiting for transfers between devices: 2.82 us -> 1.21 us  [flipped(): return lax.ppermute(value, 'pts', [(p, p ^ flip) for p in range(sizes.pts)])]
    ppermute x4 -> x5, starting transfers between devices: 2.76 us -> 3.07 us  [flipped(): return lax.ppermute(value, 'pts', [(p, p ^ flip) for p in range(sizes.pts)])]
  transfers between devices with their start and end apart: 4 -> 5, of which waited for: 2 -> 1; matrix products, arithmetic and copies ran while one was open for 0% -> 0% of each run, Pallas kernels for 2% -> 2%
where the time goes in v16:
time: 93.8 us; the launch traced here: 93.5 us
  blocking collectives  70.7 us (75%)
  Pallas kernels  17.8 us (19%)
  starting transfers between devices  3.07 us (3%)
  waiting for transfers between devices  1.21 us (1%)
    all_to_all x7, blocking collectives, exchange(): lax.all_to_all(flat, axes, split_axis=0, concat_axis=0, tiled=True)  70.7 us
    pallas_call x9, Pallas kernels, call(): pl.pallas_call(kernel, name=name, out_shape=outputs, in_specs=[smem] * le...  17.8 us
    ppermute x5, starting transfers between devices, flipped(): return lax.ppermute(value, 'pts', [(p, p ^ flip) for p in range(sizes.pts)])  3.07 us
  transfers between devices with their start and end apart: 5, of which 1 were waited for; matrix products, arithmetic and copies ran while one was open for 0% of the time, Pallas kernels for 2%

profile of v16, /device:TPU:0, one launch (start us, length us, event | category | flops | bytes accessed | tf_op | source)
XLA Modules:
  0.0 93.5 jit_solution(13494791462199655268)
XLA Ops:
  0.6 7.8 %setup.1 = (f32[192,128]{1,0:T(8,128)S(1)}, f32[576,128]{1,0:T(8,128)S(1)}, f32[192,128]{1,0:T(8,128)S(1)}, f32[6,32,128]{2,1,0:T(8,128)S(1)}, f32[3,32,128]{2,1...) custom-call(s32[1]{0:T(128)} %bitcast.run_ref, ...), custom_call_target="tpu_custom_call" | custom-call | tf_op jit(solution)/shard_map/setup/pallas_call | solution.py:522
  8.4 14.9 %all_to_all.35 = f32[32,1,768]{2,1,0:T(1,128)S(1)} all-to-all(f32[32,1,768]{2,1,0:T(1,128)S(1)} %bitcast.26), channel_id=1, replica_groups=mesh['pts'=8,'cams'=4] {'pts','cams'}, dimensions={0} | all-to-all | bytes 196608 | tf_op jit(solution)/shard_map/all_to_all | solution.py:546
  23.3 0.7 first_owner.1
  24.0 9.0 %all_to_all.36 = f32[32,1,384]{2,1,0:T(1,128)S(1)} all-to-all(f32[32,1,384]{2,1,0:T(1,128)S(1)} %bitcast.34), channel_id=1, replica_groups=mesh['pts'=8,'cams'=4] {'pts','cams'}, dimensions={0} | all-to-all | bytes 98304 | tf_op jit(solution)/shard_map/all_to_all | solution.py:546
  33.0 2.5 %schur.2 = (f32[96,128]{1,0:T(8,128)S(1)}, f32[8,128]{1,0:T(8,128)S(1)}, f32[3,32,128]{2,1,0:T(8,128)S(1)}, f32[9,8,128]{2,1,0:T(8,128)S(1)}, f32[9,8,128]{2,1,0:T(8,128)S(1)}) custom-call(f32[96,128]{1,0:T(8,128)S(1)} %bitcast.31, f32[576,128]{1,0:T(8,128)S(1)} %get-tuple-element.44.a_ref, f32[192,128]{1,0:T(8,128)S(1)} %get-tuple-element.45.b_ref, ...), custom_call_target="tpu_custom_call" | custom-call | flops 2000000000 | bytes 10000000 | tf_op jit(solution)/shard_map/schur/pallas_call | solution.py:522
  35.6 9.0 %all_to_all.37 = f32[32,1,384]{2,1,0:T(1,128)S(1)} all-to-all(f32[32,1,384]{2,1,0:T(1,128)S(1)} %bitcast.32), channel_id=1, replica_groups=mesh['pts'=8,'cams'=4] {'pts','cams'}, dimensions={0} | all-to-all | bytes 98304 | tf_op jit(solution)/shard_map/all_to_all | solution.py:546
  44.6 0.6 owner.1
  45.1 9.0 %all_to_all.38 = f32[32,1,384]{2,1,0:T(1,128)S(1)} all-to-all(f32[32,1,384]{2,1,0:T(1,128)S(1)} %bitcast.33), channel_id=1, replica_groups=mesh['pts'=8,'cams'=4] {'pts','cams'}, dimensions={0} | all-to-all | bytes 98304 | tf_op jit(solution)/shard_map/all_to_all | solution.py:546
  54.2 2.6 %schur.3 = (f32[96,128]{1,0:T(8,128)S(1)}, f32[8,128]{1,0:T(8,128)S(1)}, f32[3,32,128]{2,1,0:T(8,128)S(1)}, f32[3,32,128]{2,1,0:T(8,128)S(1)}, f32[9,8,128]{2,1,0:T(8,128)S(1)}, /*index=5*/f32[9,8,128]{2,1,0:T(8,128)S(1)}) custom-call(f32[96,128]{1,0:T(8,128)S(1)} %bitcast.29, f32[576,128]{1,0:T(8,128)S(1)} %get-tuple-element.44.a_ref, ...), custom_call_target="tpu_custom_call" | custom-call | flops 2000000000 | bytes 10000000 | tf_op jit(solution)/shard_map/schur/pallas_call | solution.py:522
  56.7 9.0 %all_to_all.39 = f32[32,1,384]{2,1,0:T(1,128)S(1)} all-to-all(f32[32,1,384]{2,1,0:T(1,128)S(1)} %bitcast.30), channel_id=1, replica_groups=mesh['pts'=8,'cams'=4] {'pts','cams'}, dimensions={0} | all-to-all | bytes 98304 | tf_op jit(solution)/shard_map/all_to_all | solution.py:546
  65.8 0.6 owner_final.1
  66.3 0.7 collective-permute-start.1
  67.0 0.6 collective-permute-start
  67.5 10.8 %all_to_all.40 = f32[32,1,384]{2,1,0:T(1,128)S(1)} all-to-all(f32[32,1,384]{2,1,0:T(1,128)S(1)} %bitcast.28), channel_id=1, replica_groups=mesh['pts'=8,'cams'=4] {'pts','cams'}, dimensions={0} | all-to-all | bytes 98304 | tf_op jit(solution)/shard_map/all_to_all | solution.py:546
  78.4 0.0 collective-permute-done.1.near_ref
  78.4 0.0 collective-permute-done.far_ref
  78.4 0.1 tail.1
  78.5 0.7 collective-permute-start.2
  79.2 0.6 collective-permute-start.3
  79.8 2.0 %schur_last.1 = (f32[32,128]{1,0:T(8,128)S(1)}, f32[8,128]{1,0:T(8,128)S(1)}, f32[3,32,128]{2,1,0:T(8,128)S(1)}, f32[3,32,128]{2,1,0:T(8,128)S(1)}) custom-call(f32[96,128]{1,0:T(8,128)S(1)} %bitcast.23, f32[576,128]{1,0:T(8,128)S(1)} %get-tuple-element.44.a_ref, f32[192,128]{1,0:T(8,128)S(1)} %get-tuple-element.45.b_ref, ...), custom_call_target="tpu_custom_call" | custom-call | flops 2000000000 | bytes 10000000 | tf_op jit(solution)/shard_map/schur_last/pallas_call | solution.py:522
  81.8 1.2 %collective-permute-done.2.refs_1_ = f32[144,128]{1,0:T(8,128)S(1)} collective-permute-done((f32[144,128]{1,0:T(8,128)S(1)}, f32[144,128]{1,0:T(8,128)S(1)}, u32[]{:S(2)}, u32[]{:S(2)}) %collective-permute-start.2) | collective-permute-done | bytes 73760 | tf_op jit(solution)/shard_map/ppermute | solution.py:549
  83.0 0.6 collective-permute-start.4
  83.6 8.9 %all_to_all.41 = f32[32,1,128]{2,1,0:T(1,128)S(1)} all-to-all(f32[32,1,128]{2,1,0:T(1,128)S(1)} %bitcast.35), channel_id=1, replica_groups=mesh['pts'=8,'cams'=4] {'pts','cams'}, dimensions={0} | all-to-all | bytes 32768 | tf_op jit(solution)/shard_map/all_to_all | solution.py:546
  92.4 1.1 %final.1 = (f32[9,8192]{1,0:T(8,128)}, f32[3,4096]{1,0:T(4,128)}) custom-call(s32[1]{0:T(128)} %bitcast.run_ref, f32[32,128]{1,0:T(8,128)S(1)} %bitcast.27, f32[8,128]{1,0:T(8,128)S(1)} %get-tuple-element.77.product_ref, f32[6,32,128]{2,1,0:T(8,128)S(1)} %get-tuple-element.46.inv_ref, f32[3,32,128]{2,1,0:T(8,128)S(1)} %get-tuple-element.78.grad_ref, ...), custom_call_target="tpu_custom_call" | custom-call | tf_op jit(solution)/shard_map/final/pallas_call | solution.py:522
  (2 shorter events, 0.0 us)
Async XLA Ops:
  66.3 12.1 %collective-permute-start.1 = (f32[216,128]{1,0:T(8,128)S(1)}, f32[216,128]{1,0:T(8,128)S(1)}, u32[]{:S(2)}, u32[]{:S(2)}) collective-permute-start(f32[216,128]{1,0:T(8,128)S(1)} %get-tuple-element.68.own_ref), channel_id=1, source_target_pairs={{0,8},{4,12},{8,0},{12,4},{16,24},{20,28},{24,16},{28,20},{1,9},{5... | collective-permute-start | bytes 331784 | tf_op jit(solution)/shard_map/ppermute | solution.py:549
  67.0 11.4 %collective-permute-start = (f32[216,128]{1,0:T(8,128)S(1)}, f32[216,128]{1,0:T(8,128)S(1)}, u32[]{:S(2)}, u32[]{:S(2)}) collective-permute-start(f32[216,128]{1,0:T(8,128)S(1)} %get-tuple-element.68.own_ref), channel_id=1, source_target_pairs={{0,16},{4,20},{8,24},{12,28},{16,0},{20,4},{24,8},{28,12},{1,17},{... | collective-permute-start | bytes 331784 | tf_op jit(solution)/shard_map/ppermute | solution.py:549
  78.5 4.4 %collective-permute-start.2 = (f32[144,128]{1,0:T(8,128)S(1)}, f32[144,128]{1,0:T(8,128)S(1)}, u32[]{:S(2)}, u32[]{:S(2)}) collective-permute-start(f32[144,128]{1,0:T(8,128)S(1)} %get-tuple-element.69), channel_id=1, source_target_pairs={{0,8},{4,12},{8,0},{12,4},{16,24},{20,28},{24,16},{28,20},{1,9},{5... | collective-permute-start | bytes 221192 | tf_op jit(solution)/shard_map/ppermute | solution.py:549
  79.2 13.2 %collective-permute-start.3 = (f32[432,128]{1,0:T(8,128)S(1)}, f32[432,128]{1,0:T(8,128)S(1)}, u32[]{:S(2)}, u32[]{:S(2)}) collective-permute-start(f32[432,128]{1,0:T(8,128)S(1)} %get-tuple-element.80.refs_0_), channel_id=1, source_target_pairs={{0,4},{4,0},{8,12},{12,8},{16,20},{20,16},{24,28},{28,24},{1,5},{5... | collective-permute-start | bytes 663560 | tf_op jit(solution)/shard_map/ppermute | solution.py:549
  83.0 9.5 %collective-permute-start.4 = (f32[144,128]{1,0:T(8,128)S(1)}, f32[144,128]{1,0:T(8,128)S(1)}, u32[]{:S(2)}, u32[]{:S(2)}) collective-permute-start(f32[144,128]{1,0:T(8,128)S(1)} %collective-permute-done.2.refs_1_), channel_id=1, source_target_pairs={{0,4},{4,0},{8,12},{12,8},{16,20},{20,16},{24,28},{28,24},{1,5},{5... | collective-permute-start | bytes 221192 | tf_op jit(solution)/shard_map/ppermute | solution.py:549

commit v17 on v14

--- a/solution.py
+++ b/solution.py
@@ -18,7 +18,7 @@
 PT_HI = PT_DEV // PT_LO
 PIECES = 2
 FINE = 3
-FIRST = 4
+FAR, NEAR = 4, 2
 VMEM_LIMIT = 24 * 1024 * 1024
 
 damping_camera = 1.0
@@ -213,13 +213,13 @@
     sources, refs = refs[:6], refs[6:]
     out_ref, a_ref, b_ref, inv_ref, grad_ref, place_point_ref, place_slot_ref, new_slot_ref, new_point_ref = refs[:9]
     refs = refs[9:]
-    r_ref, parts_ref, spread_ref, table_ref, place_wide_ref, place_list_ref = refs[:6]
-    jac_ref, pjac_ref, res_ref, slot_ref, point_ref, list_ref = refs[6:12]
-    semaphores = refs[12]
+    r_ref, parts_ref, spread_ref, table_ref, place_wide_ref, place_list_ref, spread_list_ref = refs[:7]
+    jac_ref, pjac_ref, res_ref, slot_ref, point_ref, list_ref = refs[7:13]
+    semaphores = refs[13]
     rows = sizes.rows
     copies = [
         pltpu.make_async_copy(source, target, semaphores.at[k])
-        for k, (source, target) in enumerate(zip(sources, refs[6:12]))
+        for k, (source, target) in enumerate(zip(sources, refs[7:13]))
     ]
     for copy in copies:
         copy.start()
@@ -308,9 +308,9 @@
             value = list_ref[c : c + 1, half * LANES : (half + 1) * LANES]
             low = c * sizes.block + half * (LANES // sizes.pts) + lane // sizes.pts
             parts = [(value >> 8).astype(f32), (value & 255).astype(f32)]
-            spread_row(c * pieces + half, parts, lane % sizes.pts, sizes.pts, spread_ref)
+            spread_row(c * pieces + half, parts, lane % sizes.pts, sizes.pts, spread_list_ref)
             place_row(c * pieces + half, low, LANES, place_list_ref)
-    result = scatter(2, sizes.cams * sizes.slot, sizes.pts, LANES, spread_ref, place_list_ref)
+    result = scatter(2, sizes.cams * sizes.slot, sizes.pts, LANES, spread_list_ref, place_list_ref)
     listed = result[: sizes.pts] * 256.0 + result[sizes.pts : 2 * sizes.pts]
     write_messages(fields, None, sizes.first_groups, sizes.first_message, out_ref, sizes, extra=listed, column=column_ref[0])
 
@@ -461,14 +461,16 @@
     write_messages(fields, partial, sizes.groups, sizes.message, out_ref, sizes)
 
 
-def tail_kernel(sizes, in_ref, product_ref, own_ref, other_ref, out_ref):
+def tail_kernel(sizes, in_ref, product_ref, own_ref, far_ref, near_ref, out_ref, far_out_ref):
     renewed = jnp.broadcast_to(read_scalar(in_ref, sizes.groups, sizes.message, sizes), (SUB, LANES))
     beta = (renewed / product_ref[...])[:1]
     field = CP * sizes.own_rows
-    for j, ref in enumerate((own_ref, other_ref)):
-        first = j * 2 * field
-        out_ref[first : first + field, :] = ref[:field, :]
-        out_ref[first + field : first + 2 * field, :] = ref[2 * field :, :] + beta * ref[field : 2 * field, :]
+    for j, ref in enumerate((own_ref, far_ref, near_ref)):
+        base = ref[:field, :]
+        direction = ref[2 * field :, :] + beta * ref[field : 2 * field, :]
+        for target, first in [(out_ref, j * 2 * field)] + ([(far_out_ref, 0)] if ref is far_ref else []):
+            target[first : first + field, :] = base
+            target[first + field : first + 2 * field, :] = direction
 
 
 def final_kernel(sizes, masks, run_ref, in_ref, product_ref, inv_ref, grad_ref, sum_ref, *refs):
@@ -574,6 +576,7 @@
         [pltpu.VMEM((2 * rows, LANES), f32), parts_scratch(2 * CP * PIECES)]
         + [pltpu.VMEM((max(spread_rows(9 * FINE, PT_HI), spread_rows(2 * CP * PIECES, sizes.pts)), sizes.obs), bf16)]
         + [point_scratch, pltpu.VMEM((PT_LO, sizes.obs), bf16), pltpu.VMEM((LANES, sizes.cams * sizes.slot), bf16)]
+        + [pltpu.VMEM((spread_rows(2, sizes.pts), sizes.cams * sizes.slot), bf16)]
         + [pltpu.VMEM(value.shape, value.dtype) for value in given]
         + [pltpu.SemaphoreType.DMA((len(given),))],
         scalars=[run, column],
@@ -595,19 +598,18 @@
         start, last = iteration == 0, iteration == ITERS - 1
         earlier = [] if start else [product, slots, direction, step, sums]
         if last:
-            neighbour = flipped(fields, FIRST)
+            neighbours = [flipped(fields, FAR), flipped(fields, NEAR)]
         arrived = exchange(out)
         if last:
-            (both,) = call(
+            near_side, far_block = call(
                 functools.partial(tail_kernel, sizes),
                 "tail",
-                [arrived, product, fields, neighbour],
-                [kept(4 * CP * sizes.own_rows, LANES)],
+                [arrived, product, fields] + neighbours,
+                [kept(6 * CP * sizes.own_rows, LANES), kept(2 * CP * sizes.own_rows, LANES)],
                 [],
             )
-            flips = [1 << bit for bit in range(sizes.pts.bit_length() - 1) if 1 << bit != FIRST]
-            flips = flips[1:] + flips[:1]
-            early = {flip: flipped(both, flip) for flip in (flips[0], flips[-1])}
+            flips = [1 << bit for bit in reversed(range(sizes.pts.bit_length() - 1)) if 1 << bit not in (FAR, NEAR)]
+            early = [flipped(far_block, NEAR), flipped(near_side, flips[0])]
         results = call(
             functools.partial(schur_kernel, sizes, start, last),
             "schur_last" if last else "schur",
@@ -625,11 +627,13 @@
         if not last:
             slots, direction = results
         if last:
-            early, out = lax.optimization_barrier((early, out))
-            gathered, masks = [both], [(0, FIRST)]
+            early[0], out = lax.optimization_barrier((early[0], out))
+            gathered, masks = [near_side, early[0]], [(0, FAR, NEAR), (FAR ^ NEAR,)]
             for flip in flips:
-                gathered += [early[flip] if value is both and flip in early else flipped(value, flip) for value in gathered]
-                masks += [tuple(mask ^ flip for mask in pair) for pair in masks]
+                gathered += [
+                    early[1] if value is near_side and flip == flips[0] else flipped(value, flip) for value in gathered
+                ]
+                masks += [tuple(mask ^ flip for mask in group) for group in masks]
             break
         final = iteration == ITERS - 2
         out, remainder, step, solution_ = call(

time: 92.9 us -> 92 us (level)
  waiting for transfers between devices: 2.82 us -> 1.21 us
    ppermute x4 -> x5, waiting for transfers between devices: 2.82 us -> 1.21 us  [flipped(): return lax.ppermute(value, 'pts', [(p, p ^ flip) for p in range(sizes.pts)])]
    ppermute x4 -> x5, starting transfers between devices: 2.76 us -> 3.07 us  [flipped(): return lax.ppermute(value, 'pts', [(p, p ^ flip) for p in range(sizes.pts)])]
  transfers between devices with their start and end apart: 4 -> 5, of which waited for: 2 -> 1; matrix products, arithmetic and copies ran while one was open for 0% -> 0% of each run, Pallas kernels for 2% -> 2%
where the time goes in v17:
time: 92 us; the launch traced here: 91.7 us
  blocking collectives  70.7 us (77%)
  Pallas kernels  16 us (17%)
  starting transfers between devices  3.07 us (3%)
  waiting for transfers between devices  1.21 us (1%)
    all_to_all x7, blocking collectives, exchange(): lax.all_to_all(flat, axes, split_axis=0, concat_axis=0, tiled=True)  70.7 us
    pallas_call x9, Pallas kernels, call(): pl.pallas_call(kernel, name=name, out_shape=outputs, in_specs=[smem] * le...  16 us
    ppermute x5, starting transfers between devices, flipped(): return lax.ppermute(value, 'pts', [(p, p ^ flip) for p in range(sizes.pts)])  3.07 us
  transfers between devices with their start and end apart: 5, of which 1 were waited for; matrix products, arithmetic and copies ran while one was open for 0% of the time, Pallas kernels for 2%

profile of v17, /device:TPU:0, one launch (start us, length us, event | category | flops | bytes accessed | tf_op | source)
XLA Modules:
  0.0 91.7 jit_solution(11281196825100153014)
XLA Ops:
  0.6 6.0 %setup.1 = (f32[192,128]{1,0:T(8,128)S(1)}, f32[576,128]{1,0:T(8,128)S(1)}, f32[192,128]{1,0:T(8,128)S(1)}, f32[6,32,128]{2,1,0:T(8,128)S(1)}, f32[3,32,128]{2,1...) custom-call(s32[1]{0:T(128)} %bitcast.run_ref, ...), custom_call_target="tpu_custom_call" | custom-call | tf_op jit(solution)/shard_map/setup/pallas_call | solution.py:512
  6.6 14.9 %all_to_all.35 = f32[32,1,768]{2,1,0:T(1,128)S(1)} all-to-all(f32[32,1,768]{2,1,0:T(1,128)S(1)} %bitcast.26), channel_id=1, replica_groups=mesh['pts'=8,'cams'=4] {'pts','cams'}, dimensions={0} | all-to-all | bytes 196608 | tf_op jit(solution)/shard_map/all_to_all | solution.py:536
  21.5 0.7 first_owner.1
  22.2 9.0 %all_to_all.36 = f32[32,1,384]{2,1,0:T(1,128)S(1)} all-to-all(f32[32,1,384]{2,1,0:T(1,128)S(1)} %bitcast.34), channel_id=1, replica_groups=mesh['pts'=8,'cams'=4] {'pts','cams'}, dimensions={0} | all-to-all | bytes 98304 | tf_op jit(solution)/shard_map/all_to_all | solution.py:536
  31.3 2.5 %schur.2 = (f32[96,128]{1,0:T(8,128)S(1)}, f32[8,128]{1,0:T(8,128)S(1)}, f32[3,32,128]{2,1,0:T(8,128)S(1)}, f32[9,8,128]{2,1,0:T(8,128)S(1)}, f32[9,8,128]{2,1,0:T(8,128)S(1)}) custom-call(f32[96,128]{1,0:T(8,128)S(1)} %bitcast.31, f32[576,128]{1,0:T(8,128)S(1)} %get-tuple-element.44.a_ref, f32[192,128]{1,0:T(8,128)S(1)} %get-tuple-element.45.b_ref, ...), custom_call_target="tpu_custom_call" | custom-call | flops 2000000000 | bytes 10000000 | tf_op jit(solution)/shard_map/schur/pallas_call | solution.py:512
  33.8 9.0 %all_to_all.37 = f32[32,1,384]{2,1,0:T(1,128)S(1)} all-to-all(f32[32,1,384]{2,1,0:T(1,128)S(1)} %bitcast.32), channel_id=1, replica_groups=mesh['pts'=8,'cams'=4] {'pts','cams'}, dimensions={0} | all-to-all | bytes 98304 | tf_op jit(solution)/shard_map/all_to_all | solution.py:536
  42.8 0.6 owner.1
  43.4 9.0 %all_to_all.38 = f32[32,1,384]{2,1,0:T(1,128)S(1)} all-to-all(f32[32,1,384]{2,1,0:T(1,128)S(1)} %bitcast.33), channel_id=1, replica_groups=mesh['pts'=8,'cams'=4] {'pts','cams'}, dimensions={0} | all-to-all | bytes 98304 | tf_op jit(solution)/shard_map/all_to_all | solution.py:536
  52.4 2.6 %schur.3 = (f32[96,128]{1,0:T(8,128)S(1)}, f32[8,128]{1,0:T(8,128)S(1)}, f32[3,32,128]{2,1,0:T(8,128)S(1)}, f32[3,32,128]{2,1,0:T(8,128)S(1)}, f32[9,8,128]{2,1,0:T(8,128)S(1)}, /*index=5*/f32[9,8,128]{2,1,0:T(8,128)S(1)}) custom-call(f32[96,128]{1,0:T(8,128)S(1)} %bitcast.29, f32[576,128]{1,0:T(8,128)S(1)} %get-tuple-element.44.a_ref, ...), custom_call_target="tpu_custom_call" | custom-call | flops 2000000000 | bytes 10000000 | tf_op jit(solution)/shard_map/schur/pallas_call | solution.py:512
  55.0 9.0 %all_to_all.39 = f32[32,1,384]{2,1,0:T(1,128)S(1)} all-to-all(f32[32,1,384]{2,1,0:T(1,128)S(1)} %bitcast.30), channel_id=1, replica_groups=mesh['pts'=8,'cams'=4] {'pts','cams'}, dimensions={0} | all-to-all | bytes 98304 | tf_op jit(solution)/shard_map/all_to_all | solution.py:536
  64.0 0.6 owner_final.1
  64.5 0.7 collective-permute-start.1
  65.2 0.6 collective-permute-start
  65.8 10.8 %all_to_all.40 = f32[32,1,384]{2,1,0:T(1,128)S(1)} all-to-all(f32[32,1,384]{2,1,0:T(1,128)S(1)} %bitcast.28), channel_id=1, replica_groups=mesh['pts'=8,'cams'=4] {'pts','cams'}, dimensions={0} | all-to-all | bytes 98304 | tf_op jit(solution)/shard_map/all_to_all | solution.py:536
  76.6 0.0 collective-permute-done.1.near_ref
  76.6 0.0 collective-permute-done.far_ref
  76.6 0.1 tail.1
  76.8 0.7 collective-permute-start.2
  77.4 0.6 collective-permute-start.3
  78.0 2.0 %schur_last.1 = (f32[32,128]{1,0:T(8,128)S(1)}, f32[8,128]{1,0:T(8,128)S(1)}, f32[3,32,128]{2,1,0:T(8,128)S(1)}, f32[3,32,128]{2,1,0:T(8,128)S(1)}) custom-call(f32[96,128]{1,0:T(8,128)S(1)} %bitcast.23, f32[576,128]{1,0:T(8,128)S(1)} %get-tuple-element.44.a_ref, f32[192,128]{1,0:T(8,128)S(1)} %get-tuple-element.45.b_ref, ...), custom_call_target="tpu_custom_call" | custom-call | flops 2000000000 | bytes 10000000 | tf_op jit(solution)/shard_map/schur_last/pallas_call | solution.py:512
  80.0 1.2 %collective-permute-done.2.refs_1_ = f32[144,128]{1,0:T(8,128)S(1)} collective-permute-done((f32[144,128]{1,0:T(8,128)S(1)}, f32[144,128]{1,0:T(8,128)S(1)}, u32[]{:S(2)}, u32[]{:S(2)}) %collective-permute-start.2) | collective-permute-done | bytes 73760 | tf_op jit(solution)/shard_map/ppermute | solution.py:539
  81.2 0.6 collective-permute-start.4
  81.8 8.9 %all_to_all.41 = f32[32,1,128]{2,1,0:T(1,128)S(1)} all-to-all(f32[32,1,128]{2,1,0:T(1,128)S(1)} %bitcast.35), channel_id=1, replica_groups=mesh['pts'=8,'cams'=4] {'pts','cams'}, dimensions={0} | all-to-all | bytes 32768 | tf_op jit(solution)/shard_map/all_to_all | solution.py:536
  90.6 1.1 %final.1 = (f32[9,8192]{1,0:T(8,128)}, f32[3,4096]{1,0:T(4,128)}) custom-call(s32[1]{0:T(128)} %bitcast.run_ref, f32[32,128]{1,0:T(8,128)S(1)} %bitcast.27, f32[8,128]{1,0:T(8,128)S(1)} %get-tuple-element.77.product_ref, f32[6,32,128]{2,1,0:T(8,128)S(1)} %get-tuple-element.46.inv_ref, f32[3,32,128]{2,1,0:T(8,128)S(1)} %get-tuple-element.78.grad_ref, ...), custom_call_target="tpu_custom_call" | custom-call | tf_op jit(solution)/shard_map/final/pallas_call | solution.py:512
  (2 shorter events, 0.0 us)
Async XLA Ops:
  64.5 12.1 %collective-permute-start.1 = (f32[216,128]{1,0:T(8,128)S(1)}, f32[216,128]{1,0:T(8,128)S(1)}, u32[]{:S(2)}, u32[]{:S(2)}) collective-permute-start(f32[216,128]{1,0:T(8,128)S(1)} %get-tuple-element.68.own_ref), channel_id=1, source_target_pairs={{0,8},{4,12},{8,0},{12,4},{16,24},{20,28},{24,16},{28,20},{1,9},{5... | collective-permute-start | bytes 331784 | tf_op jit(solution)/shard_map/ppermute | solution.py:539
  65.2 11.4 %collective-permute-start = (f32[216,128]{1,0:T(8,128)S(1)}, f32[216,128]{1,0:T(8,128)S(1)}, u32[]{:S(2)}, u32[]{:S(2)}) collective-permute-start(f32[216,128]{1,0:T(8,128)S(1)} %get-tuple-element.68.own_ref), channel_id=1, source_target_pairs={{0,16},{4,20},{8,24},{12,28},{16,0},{20,4},{24,8},{28,12},{1,17},{... | collective-permute-start | bytes 331784 | tf_op jit(solution)/shard_map/ppermute | solution.py:539
  76.8 4.4 %collective-permute-start.2 = (f32[144,128]{1,0:T(8,128)S(1)}, f32[144,128]{1,0:T(8,128)S(1)}, u32[]{:S(2)}, u32[]{:S(2)}) collective-permute-start(f32[144,128]{1,0:T(8,128)S(1)} %get-tuple-element.69), channel_id=1, source_target_pairs={{0,8},{4,12},{8,0},{12,4},{16,24},{20,28},{24,16},{28,20},{1,9},{5... | collective-permute-start | bytes 221192 | tf_op jit(solution)/shard_map/ppermute | solution.py:539
  77.4 13.2 %collective-permute-start.3 = (f32[432,128]{1,0:T(8,128)S(1)}, f32[432,128]{1,0:T(8,128)S(1)}, u32[]{:S(2)}, u32[]{:S(2)}) collective-permute-start(f32[432,128]{1,0:T(8,128)S(1)} %get-tuple-element.80.refs_0_), channel_id=1, source_target_pairs={{0,4},{4,0},{8,12},{12,8},{16,20},{20,16},{24,28},{28,24},{1,5},{5... | collective-permute-start | bytes 663560 | tf_op jit(solution)/shard_map/ppermute | solution.py:539
  81.2 9.5 %collective-permute-start.4 = (f32[144,128]{1,0:T(8,128)S(1)}, f32[144,128]{1,0:T(8,128)S(1)}, u32[]{:S(2)}, u32[]{:S(2)}) collective-permute-start(f32[144,128]{1,0:T(8,128)S(1)} %collective-permute-done.2.refs_1_), channel_id=1, source_target_pairs={{0,4},{4,0},{8,12},{12,8},{16,20},{20,16},{24,28},{28,24},{1,5},{5... | collective-permute-start | bytes 221192 | tf_op jit(solution)/shard_map/ppermute | solution.py:539

commit v18 on v17

--- a/solution.py
+++ b/solution.py
@@ -14,8 +14,6 @@
 LANES = 128
 SUB = 8
 PT_ROWS = PT_DEV // LANES
-PT_LO = 256
-PT_HI = PT_DEV // PT_LO
 PIECES = 2
 FINE = 3
 FAR, NEAR = 4, 2
@@ -148,12 +146,6 @@
     return gather_rows(lambda c, k: ref[c, k : k + 1, :], PT_ROWS, point // LANES, point % LANES, 3)
 
 
-def narrow(ref, k, value):
-    parts = PT_LO // LANES
-    for part in range(parts):
-        ref[k, pl.ds(part, PT_HI, stride=parts), :] = value[:, part * LANES : (part + 1) * LANES]
-
-
 def slot_place(slot, sizes):
     within = slot % sizes.slot
     return within % sizes.pts, (slot // sizes.slot) * sizes.block + within // sizes.pts
@@ -213,13 +205,13 @@
     sources, refs = refs[:6], refs[6:]
     out_ref, a_ref, b_ref, inv_ref, grad_ref, place_point_ref, place_slot_ref, new_slot_ref, new_point_ref = refs[:9]
     refs = refs[9:]
-    r_ref, parts_ref, spread_ref, table_ref, place_wide_ref, place_list_ref, spread_list_ref = refs[:7]
-    jac_ref, pjac_ref, res_ref, slot_ref, point_ref, list_ref = refs[7:13]
-    semaphores = refs[13]
+    r_ref, parts_ref, spread_ref, table_ref, place_list_ref, spread_list_ref = refs[:6]
+    jac_ref, pjac_ref, res_ref, slot_ref, point_ref, list_ref = refs[6:12]
+    semaphores = refs[12]
     rows = sizes.rows
     copies = [
         pltpu.make_async_copy(source, target, semaphores.at[k])
-        for k, (source, target) in enumerate(zip(sources, refs[7:13]))
+        for k, (source, target) in enumerate(zip(sources, refs[6:12]))
     ]
     for copy in copies:
         copy.start()
@@ -246,10 +238,10 @@
         for s in range(SUB):
             row = group * SUB + s
             point = point_ref[row : row + 1, :]
-            spread_row(row, part_rows(len(parts), group, s, parts_ref), point >> 8, PT_HI, spread_ref)
-            place_row(row, point & (PT_LO - 1), PT_LO, place_wide_ref)
-    result = scatter(sum(normal_pieces), sizes.obs, PT_HI, PT_LO, spread_ref, place_wide_ref)
-    normal = joined(result, 9, PT_HI, normal_pieces)
+            spread_row(row, part_rows(len(parts), group, s, parts_ref), point // LANES, PT_ROWS, spread_ref)
+            place_row(row, point % LANES, LANES, place_point_ref)
+    result = scatter(sum(normal_pieces), sizes.obs, PT_ROWS, LANES, spread_ref, place_point_ref)
+    normal = joined(result, 9, PT_ROWS, normal_pieces)
     top_left = normal[0] + damping_point
     top_mid = normal[1]
     top_right = normal[2]
@@ -267,13 +259,12 @@
     determinant = top_left * adjugate[0] + top_mid * adjugate[1] + top_right * adjugate[2]
     inverse = [value / determinant for value in adjugate]
     for k in range(6):
-        narrow(inv_ref, k, inverse[k])
+        inv_ref[k] = inverse[k]
     for k in range(3):
-        narrow(grad_ref, k, normal[6 + k])
+        grad_ref[k] = normal[6 + k]
     eliminated = solve(inverse, normal[6:])
     for k in range(3):
-        narrow(table_ref, k, eliminated[k])
-    place_point_ref[...] = place_wide_ref[:LANES, :] + place_wide_ref[LANES:, :]
+        table_ref[k] = eliminated[k]
     for k in (0, 3, 5):
         copies[k].wait()
     new_slot_ref[...] = slot_ref[...]
@@ -574,8 +565,8 @@
             kept(rows, LANES, dtype=jnp.int32),
         ],
         [pltpu.VMEM((2 * rows, LANES), f32), parts_scratch(2 * CP * PIECES)]
-        + [pltpu.VMEM((max(spread_rows(9 * FINE, PT_HI), spread_rows(2 * CP * PIECES, sizes.pts)), sizes.obs), bf16)]
-        + [point_scratch, pltpu.VMEM((PT_LO, sizes.obs), bf16), pltpu.VMEM((LANES, sizes.cams * sizes.slot), bf16)]
+        + [pltpu.VMEM((max(spread_rows(9 * FINE, PT_ROWS), spread_rows(2 * CP * PIECES, sizes.pts)), sizes.obs), bf16)]
+        + [point_scratch, pltpu.VMEM((LANES, sizes.cams * sizes.slot), bf16)]
         + [pltpu.VMEM((spread_rows(2, sizes.pts), sizes.cams * sizes.slot), bf16)]
         + [pltpu.VMEM(value.shape, value.dtype) for value in given]
         + [pltpu.SemaphoreType.DMA((len(given),))],

time: 92 us -> 92.3 us (level)
  no operation moved by 1% of the time
where the time goes in v18:
time: 92.3 us; the launch traced here: 92.1 us
  blocking collectives  70.7 us (77%)
  Pallas kernels  16.4 us (18%)
  starting transfers between devices  3.07 us (3%)
  waiting for transfers between devices  1.21 us (1%)
    all_to_all x7, blocking collectives, exchange(): lax.all_to_all(flat, axes, split_axis=0, concat_axis=0, tiled=True)  70.7 us
    pallas_call x9, Pallas kernels, call(): pl.pallas_call(kernel, name=name, out_shape=outputs, in_specs=[smem] * le...  16.4 us
    ppermute x5, starting transfers between devices, flipped(): return lax.ppermute(value, 'pts', [(p, p ^ flip) for p in range(sizes.pts)])  3.07 us
  transfers between devices with their start and end apart: 5, of which 1 were waited for; matrix products, arithmetic and copies ran while one was open for 0% of the time, Pallas kernels for 2%

profile of v18, /device:TPU:0, one launch (start us, length us, event | category | flops | bytes accessed | tf_op | source)
XLA Modules:
  0.0 92.1 jit_solution(14573730374279158554)
XLA Ops:
  0.6 6.3 %setup.1 = (f32[192,128]{1,0:T(8,128)S(1)}, f32[576,128]{1,0:T(8,128)S(1)}, f32[192,128]{1,0:T(8,128)S(1)}, f32[6,32,128]{2,1,0:T(8,128)S(1)}, f32[3,32,128]{2,1...) custom-call(s32[1]{0:T(128)} %bitcast.run_ref, ...), custom_call_target="tpu_custom_call" | custom-call | tf_op jit(solution)/shard_map/setup/pallas_call | solution.py:503
  7.0 14.9 %all_to_all.35 = f32[32,1,768]{2,1,0:T(1,128)S(1)} all-to-all(f32[32,1,768]{2,1,0:T(1,128)S(1)} %bitcast.26), channel_id=1, replica_groups=mesh['pts'=8,'cams'=4] {'pts','cams'}, dimensions={0} | all-to-all | bytes 196608 | tf_op jit(solution)/shard_map/all_to_all | solution.py:527
  21.9 0.7 first_owner.1
  22.6 9.0 %all_to_all.36 = f32[32,1,384]{2,1,0:T(1,128)S(1)} all-to-all(f32[32,1,384]{2,1,0:T(1,128)S(1)} %bitcast.34), channel_id=1, replica_groups=mesh['pts'=8,'cams'=4] {'pts','cams'}, dimensions={0} | all-to-all | bytes 98304 | tf_op jit(solution)/shard_map/all_to_all | solution.py:527
  31.6 2.5 %schur.2 = (f32[96,128]{1,0:T(8,128)S(1)}, f32[8,128]{1,0:T(8,128)S(1)}, f32[3,32,128]{2,1,0:T(8,128)S(1)}, f32[9,8,128]{2,1,0:T(8,128)S(1)}, f32[9,8,128]{2,1,0:T(8,128)S(1)}) custom-call(f32[96,128]{1,0:T(8,128)S(1)} %bitcast.31, f32[576,128]{1,0:T(8,128)S(1)} %get-tuple-element.44.a_ref, f32[192,128]{1,0:T(8,128)S(1)} %get-tuple-element.45.b_ref, ...), custom_call_target="tpu_custom_call" | custom-call | flops 2000000000 | bytes 10000000 | tf_op jit(solution)/shard_map/schur/pallas_call | solution.py:503
  34.1 9.0 %all_to_all.37 = f32[32,1,384]{2,1,0:T(1,128)S(1)} all-to-all(f32[32,1,384]{2,1,0:T(1,128)S(1)} %bitcast.32), channel_id=1, replica_groups=mesh['pts'=8,'cams'=4] {'pts','cams'}, dimensions={0} | all-to-all | bytes 98304 | tf_op jit(solution)/shard_map/all_to_all | solution.py:527
  43.1 0.6 owner.1
  43.7 9.0 %all_to_all.38 = f32[32,1,384]{2,1,0:T(1,128)S(1)} all-to-all(f32[32,1,384]{2,1,0:T(1,128)S(1)} %bitcast.33), channel_id=1, replica_groups=mesh['pts'=8,'cams'=4] {'pts','cams'}, dimensions={0} | all-to-all | bytes 98304 | tf_op jit(solution)/shard_map/all_to_all | solution.py:527
  52.7 2.6 %schur.3 = (f32[96,128]{1,0:T(8,128)S(1)}, f32[8,128]{1,0:T(8,128)S(1)}, f32[3,32,128]{2,1,0:T(8,128)S(1)}, f32[3,32,128]{2,1,0:T(8,128)S(1)}, f32[9,8,128]{2,1,0:T(8,128)S(1)}, /*index=5*/f32[9,8,128]{2,1,0:T(8,128)S(1)}) custom-call(f32[96,128]{1,0:T(8,128)S(1)} %bitcast.29, f32[576,128]{1,0:T(8,128)S(1)} %get-tuple-element.44.a_ref, ...), custom_call_target="tpu_custom_call" | custom-call | flops 2000000000 | bytes 10000000 | tf_op jit(solution)/shard_map/schur/pallas_call | solution.py:503
  55.3 9.0 %all_to_all.39 = f32[32,1,384]{2,1,0:T(1,128)S(1)} all-to-all(f32[32,1,384]{2,1,0:T(1,128)S(1)} %bitcast.30), channel_id=1, replica_groups=mesh['pts'=8,'cams'=4] {'pts','cams'}, dimensions={0} | all-to-all | bytes 98304 | tf_op jit(solution)/shard_map/all_to_all | solution.py:527
  64.3 0.6 owner_final.1
  64.9 0.7 collective-permute-start.1
  65.6 0.6 collective-permute-start
  66.1 10.8 %all_to_all.40 = f32[32,1,384]{2,1,0:T(1,128)S(1)} all-to-all(f32[32,1,384]{2,1,0:T(1,128)S(1)} %bitcast.28), channel_id=1, replica_groups=mesh['pts'=8,'cams'=4] {'pts','cams'}, dimensions={0} | all-to-all | bytes 98304 | tf_op jit(solution)/shard_map/all_to_all | solution.py:527
  77.0 0.0 collective-permute-done.1.near_ref
  77.0 0.0 collective-permute-done.far_ref
  77.0 0.1 tail.1
  77.1 0.7 collective-permute-start.2
  77.8 0.6 collective-permute-start.3
  78.4 2.0 %schur_last.1 = (f32[32,128]{1,0:T(8,128)S(1)}, f32[8,128]{1,0:T(8,128)S(1)}, f32[3,32,128]{2,1,0:T(8,128)S(1)}, f32[3,32,128]{2,1,0:T(8,128)S(1)}) custom-call(f32[96,128]{1,0:T(8,128)S(1)} %bitcast.23, f32[576,128]{1,0:T(8,128)S(1)} %get-tuple-element.44.a_ref, f32[192,128]{1,0:T(8,128)S(1)} %get-tuple-element.45.b_ref, ...), custom_call_target="tpu_custom_call" | custom-call | flops 2000000000 | bytes 10000000 | tf_op jit(solution)/shard_map/schur_last/pallas_call | solution.py:503
  80.3 1.2 %collective-permute-done.2.refs_1_ = f32[144,128]{1,0:T(8,128)S(1)} collective-permute-done((f32[144,128]{1,0:T(8,128)S(1)}, f32[144,128]{1,0:T(8,128)S(1)}, u32[]{:S(2)}, u32[]{:S(2)}) %collective-permute-start.2) | collective-permute-done | bytes 73760 | tf_op jit(solution)/shard_map/ppermute | solution.py:530
  81.5 0.6 collective-permute-start.4
  82.1 8.9 %all_to_all.41 = f32[32,1,128]{2,1,0:T(1,128)S(1)} all-to-all(f32[32,1,128]{2,1,0:T(1,128)S(1)} %bitcast.35), channel_id=1, replica_groups=mesh['pts'=8,'cams'=4] {'pts','cams'}, dimensions={0} | all-to-all | bytes 32768 | tf_op jit(solution)/shard_map/all_to_all | solution.py:527
  91.0 1.1 %final.1 = (f32[9,8192]{1,0:T(8,128)}, f32[3,4096]{1,0:T(4,128)}) custom-call(s32[1]{0:T(128)} %bitcast.run_ref, f32[32,128]{1,0:T(8,128)S(1)} %bitcast.27, f32[8,128]{1,0:T(8,128)S(1)} %get-tuple-element.77.product_ref, f32[6,32,128]{2,1,0:T(8,128)S(1)} %get-tuple-element.46.inv_ref, f32[3,32,128]{2,1,0:T(8,128)S(1)} %get-tuple-element.78.grad_ref, ...), custom_call_target="tpu_custom_call" | custom-call | tf_op jit(solution)/shard_map/final/pallas_call | solution.py:503
  (2 shorter events, 0.0 us)
Async XLA Ops:
  64.9 12.1 %collective-permute-start.1 = (f32[216,128]{1,0:T(8,128)S(1)}, f32[216,128]{1,0:T(8,128)S(1)}, u32[]{:S(2)}, u32[]{:S(2)}) collective-permute-start(f32[216,128]{1,0:T(8,128)S(1)} %get-tuple-element.68.own_ref), channel_id=1, source_target_pairs={{0,8},{4,12},{8,0},{12,4},{16,24},{20,28},{24,16},{28,20},{1,9},{5... | collective-permute-start | bytes 331784 | tf_op jit(solution)/shard_map/ppermute | solution.py:530
  65.6 11.4 %collective-permute-start = (f32[216,128]{1,0:T(8,128)S(1)}, f32[216,128]{1,0:T(8,128)S(1)}, u32[]{:S(2)}, u32[]{:S(2)}) collective-permute-start(f32[216,128]{1,0:T(8,128)S(1)} %get-tuple-element.68.own_ref), channel_id=1, source_target_pairs={{0,16},{4,20},{8,24},{12,28},{16,0},{20,4},{24,8},{28,12},{1,17},{... | collective-permute-start | bytes 331784 | tf_op jit(solution)/shard_map/ppermute | solution.py:530
  77.1 4.4 %collective-permute-start.2 = (f32[144,128]{1,0:T(8,128)S(1)}, f32[144,128]{1,0:T(8,128)S(1)}, u32[]{:S(2)}, u32[]{:S(2)}) collective-permute-start(f32[144,128]{1,0:T(8,128)S(1)} %get-tuple-element.69), channel_id=1, source_target_pairs={{0,8},{4,12},{8,0},{12,4},{16,24},{20,28},{24,16},{28,20},{1,9},{5... | collective-permute-start | bytes 221192 | tf_op jit(solution)/shard_map/ppermute | solution.py:530
  77.8 13.2 %collective-permute-start.3 = (f32[432,128]{1,0:T(8,128)S(1)}, f32[432,128]{1,0:T(8,128)S(1)}, u32[]{:S(2)}, u32[]{:S(2)}) collective-permute-start(f32[432,128]{1,0:T(8,128)S(1)} %get-tuple-element.80.refs_0_), channel_id=1, source_target_pairs={{0,4},{4,0},{8,12},{12,8},{16,20},{20,16},{24,28},{28,24},{1,5},{5... | collective-permute-start | bytes 663560 | tf_op jit(solution)/shard_map/ppermute | solution.py:530
  81.5 9.5 %collective-permute-start.4 = (f32[144,128]{1,0:T(8,128)S(1)}, f32[144,128]{1,0:T(8,128)S(1)}, u32[]{:S(2)}, u32[]{:S(2)}) collective-permute-start(f32[144,128]{1,0:T(8,128)S(1)} %collective-permute-done.2.refs_1_), channel_id=1, source_target_pairs={{0,4},{4,0},{8,12},{12,8},{16,20},{20,16},{24,28},{28,24},{1,5},{5... | collective-permute-start | bytes 221192 | tf_op jit(solution)/shard_map/ppermute | solution.py:530
